TPU v7x, 32 devices: a whole 2x2x4 slice. The times are simulated.
32 devices in a mesh: member: 2 (over y), curve: 4 (over z), sub: 4 (over x, core).
Axes of the slice: x: 2, y: 2, z: 4, core: 2. Of those that a mesh axis runs over, the one named last changes fastest.
Arguments:
- old_cells: float32 [768, 4, 128, 128], P(('member', 'curve', 'sub')), parts along dimension 0, as said below
- old_range: int32 [32, 2], P(('member', 'curve', 'sub')), parts along dimension 0, may hold values from 0 to 256, as said below
- neighbours: int32 [512, 4], P(('member', 'curve', 'sub')), parts along dimension 0, may hold values from -1 to 255, as said below
Outputs:
- new_state: float32 [512, 3, 128, 128], P(('member', 'curve', 'sub')), parts along dimension 0
There are 2 independent parts, one for each index of `member`. A program takes and returns all parts, laid end to end along the dimension named above; each array names one. Nothing has to cross between parts.
Inputs may be any that keep to these rules, and one draw needn't show every extreme that they name: `old_range`: consecutive rows adjoin; row 0 starts at 0 and the last row ends at 256; each row's start lies within 4 of its device index times 16, and some start lies exactly 4 above and some exactly 4 below it. `neighbours`: A patch's owner after the regrid is its curve index // 16. Every listed neighbour is owned by the same device or by a device at most 2 positions away along the curve. Among the 64 entries of the rows of one device's patches, no other device is named more than 8 times, and on every device some other device is named exactly 8 times. `old_cells`: depth lies in 0.5 to 1.5, momenta within -0.6 to 0.6, bed within -0.5 to 0.5.
All inputs are finite; a program needn't handle non-finite values.
Results may differ from a plain program's by a relative error of at most 0.00002.
Values sent between devices are 32-bit elements; how exact they have to be, the bound alone decides.
No kernel may reach another device: no remote copies, remote signals or barrier semaphores. Data moves between devices by JAX's collectives and lax.ppermute only.
A program may use at most 128 MiB of HBM per device.

v0:
```python
import jax
import jax.numpy as jnp
from jax import lax
from jax.sharding import PartitionSpec as P

RATE_STEP = 0.1


def padded(value, sides, width):
    for axis, dim in sides:
        peers, length = (lax.axis_size(axis), value.shape[dim])
        up = [(i, (i + 1) % peers) for i in range(peers - 1)]
        down = [(j, i) for i, j in up]
        last = lax.slice_in_dim(value, length - width, length, axis=dim)
        leading = lax.slice_in_dim(value, 0, width, axis=dim)
        before = lax.ppermute(last, axis, up)
        after = lax.ppermute(leading, axis, down)
        value = jnp.concatenate([before, value, after], axis=dim)
    return value


def from_behind(value, axis, steps):
    count = lax.axis_size(axis)
    leading, last = (max(0, -steps), min(count, count - steps))
    return lax.ppermute(value, axis, [(source, source + steps) for source in range(leading, last)])


def side_edges(cells):
    return jnp.stack(
        [cells[:, :, :, 0], cells[:, :, :, -1], cells[:, :, 0, :], cells[:, :, -1, :]], axis=1
    )


def wall_edges(cells):
    signs = jnp.array(
        [
            [1.0, -1.0, 1.0, 1.0],
            [1.0, -1.0, 1.0, 1.0],
            [1.0, 1.0, -1.0, 1.0],
            [1.0, 1.0, -1.0, 1.0],
        ],
        jnp.float32,
    )
    return side_edges(cells) * signs[None, :, :, None]


def rusanov_flux(left, right, normal):
    across = 3 - normal
    height_l = left[:, 0]
    height_r = right[:, 0]
    speed_l = left[:, normal] / height_l
    speed_r = right[:, normal] / height_r
    flux_l = [
        left[:, normal],
        left[:, normal] * speed_l + 0.5 * height_l * height_l,
        left[:, across] * speed_l,
    ]
    flux_r = [
        right[:, normal],
        right[:, normal] * speed_r + 0.5 * height_r * height_r,
        right[:, across] * speed_r,
    ]
    wave_rate = jnp.maximum(
        jnp.abs(speed_l) + jnp.sqrt(height_l), jnp.abs(speed_r) + jnp.sqrt(height_r)
    )
    jumps = [
        right[:, 0] + right[:, 3] - left[:, 0] - left[:, 3],
        right[:, normal] - left[:, normal],
        right[:, across] - left[:, across],
    ]
    parts = []
    for which in range(3):
        parts.append(0.5 * (flux_l[which] + flux_r[which]) - 0.5 * wave_rate * jumps[which])
    if normal == 1:
        return jnp.stack([parts[0], parts[1], parts[2]], axis=1)
    return jnp.stack([parts[0], parts[2], parts[1]], axis=1)


def advance(cells, ghosts):
    side_len = cells.shape[3]
    column = lax.broadcasted_iota(jnp.int32, cells.shape, 3)
    line = lax.broadcasted_iota(jnp.int32, cells.shape, 2)
    west = ghosts[:, 0][:, :, :, None]
    east = ghosts[:, 1][:, :, :, None]
    south = ghosts[:, 2][:, :, None, :]
    north = ghosts[:, 3][:, :, None, :]
    left = jnp.where(column == 0, west, jnp.roll(cells, 1, axis=3))
    right = jnp.where(column == side_len - 1, east, jnp.roll(cells, -1, axis=3))
    below = jnp.where(line == 0, south, jnp.roll(cells, 1, axis=2))
    above = jnp.where(line == side_len - 1, north, jnp.roll(cells, -1, axis=2))
    flux_west = rusanov_flux(left, cells, 1)
    flux_east = rusanov_flux(cells, right, 1)
    flux_south = rusanov_flux(below, cells, 2)
    flux_north = rusanov_flux(cells, above, 2)
    height = cells[:, 0]
    slope_x = 0.5 * (right[:, 3] - left[:, 3])
    slope_y = 0.5 * (above[:, 3] - below[:, 3])
    source = jnp.stack([jnp.zeros_like(height), -height * slope_x, -height * slope_y], axis=1)
    change = flux_east - flux_west + (flux_north - flux_south)
    return cells[:, :3] - RATE_STEP * change + RATE_STEP * source


def local(old_cells, old_range, neighbours):
    per_device = neighbours.shape[0]
    side_len = old_cells.shape[3]
    margin = (old_cells.shape[0] - per_device) // 2
    myself = lax.axis_index(("curve", "sub"))
    offsets = (-2, -1, 1, 2)
    grown = padded(old_cells, ((("curve", "sub"), 0),), margin)
    local_index = jnp.arange(per_device, dtype=jnp.int32)
    curve_index = myself * per_device + local_index
    from_right = (curve_index >= old_range[0, 1]).astype(jnp.int32)
    from_left = (curve_index < old_range[0, 0]).astype(jnp.int32)
    position = local_index + 2 * margin * (1 + from_right - from_left)
    cells = grown[position]
    all_edges = side_edges(cells).reshape(per_device * 4, 4, side_len)
    walls = wall_edges(cells).reshape(per_device * 4, 4, side_len)
    listed = neighbours.reshape(-1)
    opposite = jnp.tile(jnp.array([1, 0, 3, 2], jnp.int32), per_device)
    alive = listed >= 0
    owner = jnp.where(alive, listed // per_device, myself)
    distance = owner - myself
    remote = alive & (distance != 0)
    at_home = alive & (distance == 0)
    peer = jnp.clip(jnp.where(distance < 0, distance + 2, distance + 1), 0, 3)
    source_row = jnp.where(alive, listed % per_device * 4 + opposite, 0)
    local_rows = all_edges[source_row]
    sets = []
    for slot in range(4):
        sets.append(from_behind(all_edges, ("curve", "sub"), -offsets[slot]))
    nearby = jnp.stack(sets, axis=0)
    remote_rows = nearby[peer, source_row]
    chosen = jnp.where(
        remote[:, None, None], remote_rows, jnp.where(at_home[:, None, None], local_rows, walls)
    )
    ghosts = chosen.reshape(per_device, 4, 4, side_len)
    return advance(cells, ghosts)


def solution(mesh):
    placed = (
        P(("member", "curve", "sub"), None, None, None),
        P(("member", "curve", "sub"), None),
        P(("member", "curve", "sub"), None),
    )
    return jax.shard_map(
        local,
        mesh=mesh,
        in_specs=placed,
        out_specs=P(("member", "curve", "sub"), None, None, None),
        check_vma=False,
    )
```

profile of v0, /device:TPU:17, one launch (start us, length us, event | category | flops | bytes accessed | tf_op | source)
XLA Modules:
  0.0 113.3 jit_solution(12681973991127584693)
XLA Ops:
  0.0 0.0 copy-start.9
  0.0 0.0 copy-start.6
  0.0 0.0 copy-start.8
  0.0 2.7 %fusion.37 = (f32[4,4,128,128]{3,2,1,0:T(8,128)}, f32[4,4,128,128]{3,2,1,0:T(8,128)S(1)}) fusion(f32[24,4,128,128]{3,2,1,0:T(8,128)} %param.5), kind=kLoop, calls=%fused_computation.113 | loop fusion | bytes 4194304 | tf_op jit(solution)/shard_map/slice | solution.py:14
  2.7 3.7 %collective-permute-start = (f32[4,4,128,128]{3,2,1,0:T(8,128)}, f32[4,4,128,128]{3,2,1,0:T(8,128)S(1)}, u32[]{:S(2)}, u32[]{:S(2)}) collective-permute-start(f32[4,4,128,128]{3,2,1,0:T(8,128)} %get-tuple-element.23), channel_id=1, source_target_pairs={{0,1},{1,2},{2,3},{3,4},{4,5},{5,6},{6,7},{7,8},{8,9},{9,10},{10,1... | collective-permute-start | bytes 3145736 | tf_op jit(solution)/shard_map/ppermute | solution.py:16
  6.4 1.9 %collective-permute-start.1 = (f32[4,4,128,128]{3,2,1,0:T(8,128)S(1)}, f32[4,4,128,128]{3,2,1,0:T(8,128)S(1)}, u32[]{:S(2)}, u32[]{:S(2)}) collective-permute-start(f32[4,4,128,128]{3,2,1,0:T(8,128)S(1)} %get-tuple-element.24), channel_id=1, source_target_pairs={{1,0},{2,1},{3,2},{4,3},{5,4},{6,5},{7,6},{8,7},{9,8},{10,9},{11,1... | collective-permute-start | bytes 3145736 | tf_op jit(solution)/shard_map/ppermute | solution.py:17
  8.3 0.0 copy-done.6
  8.4 0.1 copy.32
  8.4 0.1 reshape.276
  8.5 0.0 copy-done.9
  8.5 0.1 tile.10
  8.7 0.0 copy-done.8
  8.7 0.7 fusion.42
  9.3 1.3 %fusion.32 = s32[16]{0:T(128)S(1)} fusion(s32[]{:T(128)} %bitcast.1, s32[]{:T(128)} %bitcast, s32[]{:T(128)S(6)} %mul.295), kind=kLoop, calls=%fused_computation.106 | loop fusion | flops 192 | bytes 76 | tf_op jit(solution)/shard_map/select_n | solution.py:115
  10.7 19.0 %collective-permute-done = f32[4,4,128,128]{3,2,1,0:T(8,128)S(1)} collective-permute-done((f32[4,4,128,128]{3,2,1,0:T(8,128)}, f32[4,4,128,128]{3,2,1,0:T(8,128)S(1)}, u32[]{:S(2)}, u32[]{:S(2)}) %collective-permute-start) | collective-permute-done | bytes 1048608 | tf_op jit(solution)/shard_map/ppermute | solution.py:16
  29.7 1.5 %collective-permute-done.1 = f32[4,4,128,128]{3,2,1,0:T(8,128)S(1)} collective-permute-done((f32[4,4,128,128]{3,2,1,0:T(8,128)S(1)}, f32[4,4,128,128]{3,2,1,0:T(8,128)S(1)}, u32[]{:S(2)}, u32[]{:S(2)}) %collective-permute-start.1) | collective-permute-done | bytes 1048608 | tf_op jit(solution)/shard_map/ppermute | solution.py:17
  31.2 5.6 %pad_maximum_fusion = f32[32,4,128,128]{3,2,1,0:T(8,128)} fusion(f32[4,4,128,128]{3,2,1,0:T(8,128)S(1)} %collective-permute-done.1, f32[24,4,128,128]{3,2,1,0:T(8,128)} %param.5, f32[4,4,128,128]{3,2,1,0:T(8,128)S(1)} %collective-permute-done), kind=kLoop, calls=%fused_computation.3 | loop fusion | flops 4194304 | bytes 16777216 | tf_op jit(solution)/shard_map/concatenate | solution.py:18
  36.7 6.2 %gather_fusion = f32[16,4,128,128]{3,2,1,0:T(8,128)} fusion(f32[32,4,128,128]{3,2,1,0:T(8,128)} %pad_maximum_fusion, s32[1024]{0:T(1024)S(1)} %pad_clamp_fusion.1), kind=kCustom, calls=%fused_computation | custom fusion | bytes 8388672 | tf_op jit(solution)/shard_map/gather | solution.py:115
  42.9 8.1 %fusion.40 = (f32[16,4,128,1]{3,2,1,0:T(8,128)}, f32[16,4,128,1]{3,2,1,0:T(8,128)}) fusion(f32[16,4,128,128]{3,2,1,0:T(8,128)} %gather_fusion), kind=kLoop, calls=%fused_computation.116 | loop fusion | bytes 131072 | tf_op jit(solution)/shard_map/slice | solution.py:30
  51.0 1.1 fusion.41
  52.1 2.9 %copy.23 = f32[16,4,128,1]{2,0,3,1:T(8,128)S(1)} copy(f32[16,4,128,1]{3,2,1,0:T(8,128)} %get-tuple-element.32) | data formatting | bytes 65536 | tf_op jit(solution)/shard_map/slice | solution.py:30
  55.0 2.8 %copy.44 = f32[16,4,128,1]{2,1,0,3:T(4,128)S(1)} copy(f32[16,4,128,1]{3,2,1,0:T(8,128)} %get-tuple-element.31) | data formatting | bytes 65536
  57.9 0.1 copy.27
  58.0 0.1 copy.28
  58.1 0.0 copy-start
  58.1 2.2 %collective-permute-start.4 = (f32[64,4,128]{2,1,0:T(4,128)S(1)}, f32[64,4,128]{2,1,0:T(4,128)S(1)}, u32[]{:S(2)}, u32[]{:S(2)}) collective-permute-start(f32[64,4,128]{2,1,0:T(4,128)S(1)} %copy.28), channel_id=1, source_target_pairs={{1,0},{2,1},{3,2},{4,3},{5,4},{6,5},{7,6},{8,7},{9,8},{10,9},{11,1... | collective-permute-start | bytes 393224 | tf_op jit(solution)/shard_map/ppermute | solution.py:25
  60.3 2.8 %collective-permute-start.5 = (f32[64,4,128]{2,1,0:T(4,128)S(1)}, f32[64,4,128]{2,1,0:T(4,128)S(1)}, u32[]{:S(2)}, u32[]{:S(2)}) collective-permute-start(f32[64,4,128]{2,1,0:T(4,128)S(1)} %copy.28), channel_id=1, source_target_pairs={{2,0},{3,1},{4,2},{5,3},{6,4},{7,5},{8,6},{9,7},{10,8},{11,9},{12,... | collective-permute-start | bytes 393224 | tf_op jit(solution)/shard_map/ppermute | solution.py:25
  63.1 2.5 %collective-permute-start.2 = (f32[64,4,128]{2,1,0:T(4,128)S(1)}, f32[64,4,128]{2,1,0:T(4,128)S(1)}, u32[]{:S(2)}, u32[]{:S(2)}) collective-permute-start(f32[64,4,128]{2,1,0:T(4,128)S(1)} %copy.28), channel_id=1, source_target_pairs={{0,2},{1,3},{2,4},{3,5},{4,6},{5,7},{6,8},{7,9},{8,10},{9,11},{10,... | collective-permute-start | bytes 393224 | tf_op jit(solution)/shard_map/ppermute | solution.py:25
  65.6 5.1 %collective-permute-start.3 = (f32[64,4,128]{2,1,0:T(4,128)S(1)}, f32[64,4,128]{2,1,0:T(4,128)S(1)}, u32[]{:S(2)}, u32[]{:S(2)}) collective-permute-start(f32[64,4,128]{2,1,0:T(4,128)S(1)} %copy.28), channel_id=1, source_target_pairs={{0,1},{1,2},{2,3},{3,4},{4,5},{5,6},{6,7},{7,8},{8,9},{9,10},{10,1... | collective-permute-start | bytes 393224 | tf_op jit(solution)/shard_map/ppermute | solution.py:25
  70.7 8.4 %fusion.38 = (f32[16,4,127,128]{3,2,1,0:T(8,128)}, f32[16,4,127,128]{3,2,1,0:T(8,128)}) fusion(f32[16,4,128,128]{3,2,1,0:T(8,128)} %gather_fusion), kind=kLoop, calls=%fused_computation.114 | loop fusion | bytes 16646144 | tf_op jit(solution)/shard_map/jit(_roll_static)/slice | solution.py:90
  79.1 0.0 copy-done
  79.1 0.0 copy-start.7
  79.1 4.8 %fusion.39 = (f32[16,4,128,127]{3,2,1,0:T(8,128)}, f32[16,4,128,127]{3,2,1,0:T(8,128)}) fusion(f32[16,4,128,128]{3,2,1,0:T(8,128)S(1)} %copy-done), kind=kLoop, calls=%fused_computation.115 | loop fusion | bytes 16646144 | tf_op jit(solution)/shard_map/jit(_roll_static)/slice | solution.py:87
  83.9 0.7 gather_fusion.2
  84.5 0.0 collective-permute-done.4
  84.5 0.0 collective-permute-done.5
  84.5 0.0 collective-permute-done.2
  84.5 0.0 collective-permute-done.3
  84.6 0.1 pad_maximum_fusion.1
  84.7 0.8 gather_fusion.1
  85.4 0.0 copy-done.7
  85.5 0.2 fusion.19
  85.7 0.0 copy-start.1
  85.7 6.5 %maximum_select_fusion.3 = (f32[16,4,128,128]{3,2,1,0:T(8,128)S(1)}, f32[16,4,128,128]{3,2,1,0:T(8,128)S(1)}) fusion(f32[16,4,127,128]{3,2,1,0:T(8,128)} %get-tuple-element.28, f32[16,4,1,128]{3,2,1,0:T(1,128)S(1)} %get-tuple-element.34, f32[16,4,128]{2,1,0:T(4,128)S(1)} %get-tuple-element.36, pred[128]{0:T(512)(128)(4,1)S(1)} %iota_compare_fusion, ...), kind=kLoop, calls=%fused_computation.7 | loop fusion | flops 4194304 | bytes 16842880 | tf_op jit(solution)/shard_map/jit(_where)/select_n | solution.py:89
  92.2 0.0 copy-done.1
  92.2 0.0 copy-start.2
  92.2 0.0 copy-start.3
  92.2 1.1 multiply_subtract_fusion.1
  93.3 1.1 copy-done.2
  94.4 1.3 %copy-done.3 = f32[16,4,127,128]{3,2,1,0:T(8,128)S(1)} copy-done((f32[16,4,127,128]{3,2,1,0:T(8,128)S(1)}, f32[16,4,127,128]{3,2,1,0:T(8,128)}, u32[]{:S(2)}) %copy-start.3) | copy-done | bytes 4161560
  95.7 4.8 %maximum_select_fusion.2 = (f32[16,4,128,128]{3,2,1,0:T(8,128)S(1)}, f32[16,4,128,128]{3,2,1,0:T(8,128)S(1)}) fusion(f32[16,4,1,128]{3,2,1,0:T(1,128)S(1)} %get-tuple-element.33, f32[16,4,127,128]{3,2,1,0:T(8,128)S(1)} %copy-done.3, f32[16,4,128]{2,1,0:T(4,128)S(1)} %get-tuple-element.35, pred[128]{0:T(512)(128)(4,1)S(1)} %iota_compare_fusion.1, ...), kind=kLoop, calls=%fused_computation.6 | loop fusion | flops 4194304 | bytes 16842880 | tf_op jit(solution)/shard_map/jit(_where)/select_n | solution.py:90
  100.5 1.9 %multiply_subtract_fusion.3 = (f32[16,1,128,128]{3,2,1,0:T(8,128)S(1)}, f32[16,1,128,128]{3,2,1,0:T(8,128)S(1)}, f32[16,1,128,128]{3,2,1,0:T(8,128)S(1)}, f32[16,1,128,128]{3,2,1,0:T(8,128)S(1)}) fusion(f32[16,4,128,128]{3,2,1,0:T(8,128)S(1)} %get-tuple-element.41, f32[16,4,128,128]{3,2,1,0:T(8,128)S(1)} %copy-done.1, ...), kind=kLoop, calls=%fused_computation.43 | loop fusion | flops 9961472 | bytes 14680064 | tf_op jit(solution)/shard_map/sub | solution.py:73
  102.3 3.4 %multiply_subtract_fusion = (f32[16,1,128,128]{3,2,1,0:T(8,128)}, f32[16,1,128,128]{3,2,1,0:T(8,128)}, f32[16,1,128,128]{3,2,1,0:T(8,128)}, f32[16,1,128,128]{3,2,1,0:T(8,128)S(1)}) fusion(f32[16,4,128,128]{3,2,1,0:T(8,128)S(1)} %get-tuple-element.43, f32[16,4,128,128]{3,2,1,0:T(8,128)S(1)} %copy-done.1, f32[16,1,128,128]{3,2,1,0:T(8,128)S(1)} %get-tuple-element.6, ...), kind=kLoop, calls=%fused_computation.38 | loop fusion | flops 11010048 | bytes 15728640 | tf_op jit(solution)/shard_map/sub | solution.py:73
  105.7 1.4 %fusion.10 = (f32[16,1,128,128]{3,2,1,0:T(8,128)S(1)}, f32[16,1,128,128]{3,2,1,0:T(8,128)S(1)}) fusion(f32[16,1,128,128]{3,2,1,0:T(8,128)S(1)} %get-tuple-element.26, f32[16,4,128,128]{3,2,1,0:T(8,128)S(1)} %get-tuple-element.44, f32[16,4,128,128]{3,2,1,0:T(8,128)S(1)} %copy-done.1), kind=kLoop, calls=%fused_computation.27 | loop fusion | flops 7077888 | bytes 9437184 | tf_op jit(solution)/shard_map/sub | solution.py:73
  107.1 0.0 copy-start.4
  107.1 0.0 copy-start.5
  107.1 1.9 %multiply_subtract_fusion.7 = (f32[16,1,128,128]{3,2,1,0:T(8,128)S(1)}, f32[16,1,128,128]{3,2,1,0:T(8,128)S(1)}, f32[16,1,128,128]{3,2,1,0:T(8,128)S(1)}, f32[16,1,128,128]{3,2,1,0:T(8,128)S(1)}) fusion(f32[16,4,128,128]{3,2,1,0:T(8,128)S(1)} %get-tuple-element.42, f32[16,4,128,128]{3,2,1,0:T(8,128)S(1)} %copy-done.1, ...), kind=kLoop, calls=%fused_computation.51 | loop fusion | flops 9961472 | bytes 14680064 | tf_op jit(solution)/shard_map/sub | solution.py:73
  109.0 0.0 copy-done.4
  109.0 0.0 copy-done.5
  109.0 4.3 %fusion = f32[16,3,128,128]{3,2,1,0:T(8,128)} fusion(f32[16,4,128,128]{3,2,1,0:T(8,128)S(1)} %copy-done.1, f32[16,1,128,128]{3,2,1,0:T(8,128)S(1)} %get-tuple-element.19, f32[16,1,128,128]{3,2,1,0:T(8,128)S(1)} %get-tuple-element.20, f32[16,1,128,128]{3,2,1,0:T(8,128)S(1)} %get-tuple-element.18, f32[16,1,128,128]{3,2,1,0:T(8,128)S(1)} %get-tuple-element.17, ...), kind=kLoop, calls=%fused_computation.9 | loop fusion | flops 13369344 | bytes 20971532 | tf_op jit(solution)/shard_map/add | solution.py:100
  (11 shorter events, 0.1 us)
Async XLA Ops:
  0.0 8.5 %copy-start.9 = (s32[4]{0:T(128)S(1)}, s32[4]{0:T(128)}, u32[]{:S(2)}) copy-start(s32[4]{0:T(128)} %constant.66.clone) | copy-start | bytes 52
  0.0 8.3 %copy-start.6 = (s32[16,4]{0,1:T(4,128)S(1)}, s32[16,4]{0,1:T(4,128)}, u32[]{:S(2)}) copy-start(s32[16,4]{0,1:T(4,128)} %param.7) | copy-start | bytes 772
  0.0 8.7 %copy-start.8 = (s32[1,2]{1,0:T(1,128)S(1)}, s32[1,2]{1,0:T(1,128)}, u32[]{:S(2)}) copy-start(s32[1,2]{1,0:T(1,128)} %param.6) | copy-start | bytes 28
  2.7 26.9 %collective-permute-start = (f32[4,4,128,128]{3,2,1,0:T(8,128)}, f32[4,4,128,128]{3,2,1,0:T(8,128)S(1)}, u32[]{:S(2)}, u32[]{:S(2)}) collective-permute-start(f32[4,4,128,128]{3,2,1,0:T(8,128)} %get-tuple-element.23), channel_id=1, source_target_pairs={{0,1},{1,2},{2,3},{3,4},{4,5},{5,6},{6,7},{7,8},{8,9},{9,10},{10,1... | collective-permute-start | bytes 3145736 | tf_op jit(solution)/shard_map/ppermute | solution.py:16
  6.4 24.8 %collective-permute-start.1 = (f32[4,4,128,128]{3,2,1,0:T(8,128)S(1)}, f32[4,4,128,128]{3,2,1,0:T(8,128)S(1)}, u32[]{:S(2)}, u32[]{:S(2)}) collective-permute-start(f32[4,4,128,128]{3,2,1,0:T(8,128)S(1)} %get-tuple-element.24), channel_id=1, source_target_pairs={{1,0},{2,1},{3,2},{4,3},{5,4},{6,5},{7,6},{8,7},{9,8},{10,9},{11,1... | collective-permute-start | bytes 3145736 | tf_op jit(solution)/shard_map/ppermute | solution.py:17
  58.1 21.0 %copy-start = (f32[16,4,128,128]{3,2,1,0:T(8,128)S(1)}, f32[16,4,128,128]{3,2,1,0:T(8,128)}, u32[]{:S(2)}) copy-start(f32[16,4,128,128]{3,2,1,0:T(8,128)} %gather_fusion) | copy-start | bytes 12582916
  58.1 26.4 %collective-permute-start.4 = (f32[64,4,128]{2,1,0:T(4,128)S(1)}, f32[64,4,128]{2,1,0:T(4,128)S(1)}, u32[]{:S(2)}, u32[]{:S(2)}) collective-permute-start(f32[64,4,128]{2,1,0:T(4,128)S(1)} %copy.28), channel_id=1, source_target_pairs={{1,0},{2,1},{3,2},{4,3},{5,4},{6,5},{7,6},{8,7},{9,8},{10,9},{11,1... | collective-permute-start | bytes 393224 | tf_op jit(solution)/shard_map/ppermute | solution.py:25
  60.3 24.3 %collective-permute-start.5 = (f32[64,4,128]{2,1,0:T(4,128)S(1)}, f32[64,4,128]{2,1,0:T(4,128)S(1)}, u32[]{:S(2)}, u32[]{:S(2)}) collective-permute-start(f32[64,4,128]{2,1,0:T(4,128)S(1)} %copy.28), channel_id=1, source_target_pairs={{2,0},{3,1},{4,2},{5,3},{6,4},{7,5},{8,6},{9,7},{10,8},{11,9},{12,... | collective-permute-start | bytes 393224 | tf_op jit(solution)/shard_map/ppermute | solution.py:25
  63.1 21.5 %collective-permute-start.2 = (f32[64,4,128]{2,1,0:T(4,128)S(1)}, f32[64,4,128]{2,1,0:T(4,128)S(1)}, u32[]{:S(2)}, u32[]{:S(2)}) collective-permute-start(f32[64,4,128]{2,1,0:T(4,128)S(1)} %copy.28), channel_id=1, source_target_pairs={{0,2},{1,3},{2,4},{3,5},{4,6},{5,7},{6,8},{7,9},{8,10},{9,11},{10,... | collective-permute-start | bytes 393224 | tf_op jit(solution)/shard_map/ppermute | solution.py:25
  65.6 19.0 %collective-permute-start.3 = (f32[64,4,128]{2,1,0:T(4,128)S(1)}, f32[64,4,128]{2,1,0:T(4,128)S(1)}, u32[]{:S(2)}, u32[]{:S(2)}) collective-permute-start(f32[64,4,128]{2,1,0:T(4,128)S(1)} %copy.28), channel_id=1, source_target_pairs={{0,1},{1,2},{2,3},{3,4},{4,5},{5,6},{6,7},{7,8},{8,9},{9,10},{10,1... | collective-permute-start | bytes 393224 | tf_op jit(solution)/shard_map/ppermute | solution.py:25
  79.1 6.4 %copy-start.7 = (f32[4,4]{1,0:T(4,128)S(1)}, f32[4,4]{1,0:T(4,128)}, u32[]{:S(2)}) copy-start(f32[4,4]{1,0:T(4,128)} %constant.65.clone) | copy-start | bytes 196
  85.7 6.5 %copy-start.1 = (f32[16,4,128,128]{3,2,1,0:T(8,128)S(1)}, f32[16,4,128,128]{3,2,1,0:T(8,128)}, u32[]{:S(2)}) copy-start(f32[16,4,128,128]{3,2,1,0:T(8,128)} %gather_fusion) | copy-start | bytes 12582916
  92.2 2.2 %copy-start.2 = (f32[16,4,128,1]{3,2,1,0:T(8,128)S(1)}, f32[16,4,128,1]{3,2,1,0:T(8,128)}, u32[]{:S(2)}) copy-start(f32[16,4,128,1]{3,2,1,0:T(8,128)} %get-tuple-element.32) | copy-start | bytes 98308
  92.2 3.5 %copy-start.3 = (f32[16,4,127,128]{3,2,1,0:T(8,128)S(1)}, f32[16,4,127,128]{3,2,1,0:T(8,128)}, u32[]{:S(2)}) copy-start(f32[16,4,127,128]{3,2,1,0:T(8,128)} %get-tuple-element.27) | copy-start | bytes 12484612
  107.1 1.9 %copy-start.4 = (f32[16,1,128,128]{3,2,1,0:T(8,128)S(1)}, f32[16,1,128,128]{3,2,1,0:T(8,128)}, u32[]{:S(2)}) copy-start(f32[16,1,128,128]{3,2,1,0:T(8,128)} %get-tuple-element.11) | copy-start | bytes 3145732
  107.1 1.9 %copy-start.5 = (f32[16,1,128,128]{3,2,1,0:T(8,128)S(1)}, f32[16,1,128,128]{3,2,1,0:T(8,128)}, u32[]{:S(2)}) copy-start(f32[16,1,128,128]{3,2,1,0:T(8,128)} %get-tuple-element.12) | copy-start | bytes 3145732
where the time goes:
time: 114 us; the launch traced here: 113 us
  local copies, waits for them, and re-layouts  41.9 us (37%)
  other arithmetic  32.4 us (28%)
  waiting for transfers between devices  20.5 us (18%)
  starting transfers between devices  18.2 us (16%)
    ppermute x1, waiting for transfers between devices, padded(): before = lax.ppermute(last, axis, up)  19 us
    ppermute x4, starting transfers between devices, from_behind(): lax.ppermute(value, axis, [(source, source + steps) for source in range(l...  12.6 us
    sub x5, other arithmetic, rusanov_flux(): 0.5 * (flux_l[which] + flux_r[which]) - 0.5 * wave_rate * jumps[which]  9.54 us
    slice x1, local copies, waits for them, and re-layouts, advance(): above = jnp.where(line == side_len - 1, north, jnp.roll(cells, -1, axis=2))  8.37 us
    slice x1, local copies, waits for them, and re-layouts, side_edges(): cells[:, :, :, -1]  8.1 us
    select_n x1, other arithmetic, advance(): below = jnp.where(line == 0, south, jnp.roll(cells, 1, axis=2))  6.51 us
    gather x1, local copies, waits for them, and re-layouts, local(): cells = grown[position]  6.19 us
    concatenate x1, other arithmetic, padded(): value = jnp.concatenate([before, value, after], axis=dim)  5.57 us
  transfers between devices with their start and end apart: 6, of which 2 were waited for; matrix products, arithmetic and copies ran while one was open for 14% of the time, Pallas kernels for 0%

commit v1 on v0

v1 whole, which is shorter than its diff:
```python
import functools

import jax
import jax.numpy as jnp
from jax import lax
from jax.experimental import pallas as pl
from jax.experimental.pallas import tpu as pltpu
from jax.sharding import PartitionSpec as P

RATE_STEP = 0.1
HALF = 0.5 * RATE_STEP
AXES = ("curve", "sub")
OFFSETS = (-2, -1, 1, 2)
CAP = 8


def terms(h, mx, my, bed):
    root = lax.rsqrt(h)
    celerity = h * root
    inverse = root * root
    u = mx * inverse
    v = my * inverse
    half_sq = 0.5 * h * h
    cross = my * u
    return dict(
        fx=mx * u + half_sq,
        cross=cross,
        fy=my * v + half_sq,
        rate_x=jnp.abs(u) + celerity,
        rate_y=jnp.abs(v) + celerity,
        eta=h + bed,
    )


def inner_update(h, mx, my, bed):
    t = terms(h, mx, my, bed)
    side = h.shape[0]

    def along(axis, normal, across, flux_n, flux_t, rate):
        place = lax.broadcasted_iota(jnp.int32, h.shape, axis)
        ahead = lambda a: pltpu.roll(a, side - 1, axis)
        behind = lambda a: pltpu.roll(a, 1, axis)
        last = place == side - 1
        top = jnp.maximum(rate, ahead(rate))
        normal_a = ahead(normal)
        q_h = (normal + normal_a) - top * (ahead(t["eta"]) - t["eta"])
        q_n = (flux_n + ahead(flux_n)) - top * (normal_a - normal)
        q_t = (flux_t + ahead(flux_t)) - top * (ahead(across) - across)
        out = []
        for q in (q_h, q_n, q_t):
            q = jnp.where(last, 0.0, q)
            out.append(q - behind(q))
        slope = jnp.where(last, 0.0, ahead(bed)) - jnp.where(place == 0, 0.0, behind(bed))
        return out[0], out[1] + h * slope, out[2]

    xh, xn, xt = along(1, mx, my, t["fx"], t["cross"], t["rate_x"])
    yh, yn, yt = along(0, my, mx, t["fy"], t["cross"], t["rate_y"])
    return h - HALF * (xh + yh), mx - HALF * (xn + yt), my - HALF * (xt + yn)


def patches_kernel(count, cells_ref, out_ref, edge_ref, columns):
    step = pl.program_id(0)
    fields = [cells_ref[0, f] for f in range(4)]
    new = inner_update(*fields)
    for f in range(3):
        out_ref[0, f] = new[f]
    side = fields[0].shape[0]
    lane = lax.broadcasted_iota(jnp.int32, (side, side), 1)
    gathered = columns[...]
    for f in range(4):
        at = 8 * step + 2 * f
        moved = pltpu.roll(fields[f], at + 1, 1)
        gathered = jnp.where((lane == at) | (lane == at + 1), moved, gathered)
        row = 16 * step + 8 + 2 * f
        edge_ref[pl.ds(row, 1), :] = cells_ref[0, f, side - 1 : side, :]
        edge_ref[pl.ds(row + 1, 1), :] = cells_ref[0, f, 0:1, :]
    columns[...] = gathered

    @pl.when(step == count - 1)
    def _():
        turned = jnp.transpose(columns[...])
        for p in range(count):
            edge_ref[16 * p : 16 * p + 8, :] = turned[8 * p : 8 * p + 8, :]


def inner_patches(cells, first, count):
    side = cells.shape[3]
    return pl.pallas_call(
        functools.partial(patches_kernel, count),
        grid=(count,),
        in_specs=[pl.BlockSpec((1, 4, side, side), lambda i: (first + i, 0, 0, 0))],
        out_specs=[
            pl.BlockSpec((1, 3, side, side), lambda i: (i, 0, 0, 0)),
            pl.BlockSpec((16 * count, side), lambda i: (0, 0)),
        ],
        out_shape=[
            jax.ShapeDtypeStruct((count, 3, side, side), jnp.float32),
            jax.ShapeDtypeStruct((16 * count, side), jnp.float32),
        ],
        scratch_shapes=[pltpu.VMEM((side, side), jnp.float32)],
        cost_estimate=pl.CostEstimate(
            flops=count * side * side * 100,
            bytes_accessed=count * side * side * 28,
            transcendentals=count * side * side,
        ),
    )(cells)


def answer_kernel(margin, take_ref, rows_ref, own_ref, left_ref, right_ref, edge_ref, *messages):
    count = own_ref.shape[0] // 16
    edge_ref[...] = own_ref[...]
    for m in range(margin):
        for source, p in ((left_ref, m), (right_ref, count - margin + m)):

            @pl.when(take_ref[p] != 0)
            def _(source=source, p=p, m=m):
                edge_ref[16 * p : 16 * p + 16, :] = source[16 * m : 16 * m + 16, :]

    for k in range(4):
        for j in range(CAP):
            row = rows_ref[k * CAP + j]
            messages[k][pl.ds(8 * (j // 2) + j % 2, 4, stride=2), :] = edge_ref[pl.ds(row, 4, stride=2), :]


def answers(take, rows, own, left, right, margin):
    side = own.shape[1]
    whole = pl.BlockSpec(memory_space=pltpu.VMEM)
    scalars = pl.BlockSpec(memory_space=pltpu.SMEM)
    return pl.pallas_call(
        functools.partial(answer_kernel, margin),
        in_specs=[scalars, scalars, whole, whole, whole],
        out_specs=[whole] * 5,
        out_shape=[jax.ShapeDtypeStruct(own.shape, jnp.float32)]
        + [jax.ShapeDtypeStruct((4 * CAP, side), jnp.float32)] * 4,
    )(take, rows, own, left, right)


def rim_kernel(rows_ref, wall_ref, edge_ref, m0, m1, m2, m3, columns_ref, lines_ref, source, ghost, turn):
    total = edge_ref.shape[0]
    count = total // 16
    source[0:total, :] = edge_ref[...]
    for k, message in enumerate((m0, m1, m2, m3)):
        source[total + 4 * CAP * k : total + 4 * CAP * (k + 1), :] = message[...]
    for p in range(count):
        for s in range(4):
            row = rows_ref[4 * p + s]
            target = 16 * p + 8 * (s // 2) + 1 - s % 2
            ghost[pl.ds(target, 4, stride=2), :] = source[pl.ds(row, 4, stride=2), :]
    turn[...] = jnp.zeros_like(turn)
    for s in range(4):
        parity = 1 - s % 2
        sign = 1.0 - 2.0 * parity
        axis = s // 2
        normal, across = (1, 2) if axis == 0 else (2, 1)

        def pick(ref, f):
            return ref[pl.ds(8 * axis + 2 * f + parity, count, stride=16), :]

        flip = wall_ref[count * s : count * (s + 1), :]
        hc, hg = pick(edge_ref, 0), pick(ghost, 0)
        nc, ng = pick(edge_ref, normal), pick(ghost, normal) * flip
        ac, ag = pick(edge_ref, across), pick(ghost, across)
        bc, bg = pick(edge_ref, 3), pick(ghost, 3)
        rc, rg = lax.rsqrt(hc), lax.rsqrt(hg)
        uc, ug = nc * rc * rc, ng * rg * rg
        top = jnp.maximum(jnp.abs(uc) + hc * rc, jnp.abs(ug) + hg * rg)
        fc, fg = nc * uc + 0.5 * hc * hc, ng * ug + 0.5 * hg * hg
        c_h = -HALF * (sign * (nc + ng) - top * ((hg + bg) - (hc + bc)))
        c_n = -HALF * (sign * (fc + fg + hc * bg) - top * (ng - nc))
        c_t = -HALF * (sign * (ac * uc + ag * ug) - top * (ag - ac))
        for f, value in ((0, c_h), (normal, c_n), (across, c_t)):
            where = pl.ds(2 * f + parity, count, stride=8)
            if axis == 0:
                turn[where, :] = value
            else:
                lines_ref[where, :] = value
    columns_ref[...] = jnp.transpose(turn[...])


def rims(rows, walls, edges, messages):
    total, side = edges.shape
    whole = pl.BlockSpec(memory_space=pltpu.VMEM)
    scalars = pl.BlockSpec(memory_space=pltpu.SMEM)
    return pl.pallas_call(
        rim_kernel,
        in_specs=[scalars] + [whole] * 6,
        out_specs=[whole] * 2,
        out_shape=[jax.ShapeDtypeStruct((side, side), jnp.float32)] * 2,
        scratch_shapes=[
            pltpu.VMEM((total + 16 * CAP, side), jnp.float32),
            pltpu.VMEM((total, side), jnp.float32),
            pltpu.VMEM((side, side), jnp.float32),
        ],
    )(rows, walls, edges, *messages)


def add_rim(p, value, f, columns_ref, lines_ref, lane):
    side = value.shape[0]
    moved = pltpu.roll(columns_ref[...], 2 * side - (8 * p + 2 * f + 1), 1)
    return value + jnp.where((lane == 0) | (lane == side - 1), moved, 0.0)


def finish_patch(p, values, columns_ref, lines_ref, out_ref):
    side = columns_ref.shape[0]
    lane = lax.broadcasted_iota(jnp.int32, (side, side), 1)
    for f in range(3):
        out_ref[0, f] = add_rim(p, values(f), f, columns_ref, lines_ref, lane)
        out_ref[0, f, side - 1 : side, :] += lines_ref[pl.ds(8 * p + 2 * f, 1), :]
        out_ref[0, f, 0:1, :] += lines_ref[pl.ds(8 * p + 2 * f + 1, 1), :]


def middle_kernel(margin, own_ref, columns_ref, lines_ref, out_ref):
    p = pl.program_id(0) + margin
    finish_patch(p, lambda f: own_ref[0, f], columns_ref, lines_ref, out_ref)


def middle(own, columns, lines, margin):
    count, _, side, _ = own.shape
    block = pl.BlockSpec((1, 3, side, side), lambda i: (i + margin, 0, 0, 0))
    whole = pl.BlockSpec(memory_space=pltpu.VMEM)
    return pl.pallas_call(
        functools.partial(middle_kernel, margin),
        grid=(count - 2 * margin,),
        in_specs=[block, whole, whole],
        out_specs=block,
        out_shape=jax.ShapeDtypeStruct(own.shape, jnp.float32),
    )(own, columns, lines)


def ends_kernel(margin, count, take_ref, own_ref, left_ref, right_ref, columns_ref, lines_ref, _, out_ref):
    i = pl.program_id(0)
    p = jnp.where(i < margin, i, count - 2 * margin + i)
    taken = take_ref[p] != 0

    def values(f):
        moved = jnp.where(i < margin, left_ref[0, f], right_ref[0, f])
        return jnp.where(taken, moved, own_ref[0, f])

    finish_patch(p, values, columns_ref, lines_ref, out_ref)


def ends(take, own, left, right, columns, lines, filled, margin):
    count, _, side, _ = own.shape
    at = lambda i: jnp.where(i < margin, i, count - 2 * margin + i)
    block = pl.BlockSpec((1, 3, side, side), lambda i: (at(i), 0, 0, 0))
    whole = pl.BlockSpec(memory_space=pltpu.VMEM)
    return pl.pallas_call(
        functools.partial(ends_kernel, margin, count),
        grid=(2 * margin,),
        in_specs=[
            pl.BlockSpec(memory_space=pltpu.SMEM),
            block,
            pl.BlockSpec((1, 3, side, side), lambda i: (jnp.minimum(i, margin - 1), 0, 0, 0)),
            pl.BlockSpec((1, 3, side, side), lambda i: (jnp.maximum(i - margin, 0), 0, 0, 0)),
            whole,
            whole,
            pl.BlockSpec(memory_space=pl.ANY),
        ],
        out_specs=block,
        out_shape=jax.ShapeDtypeStruct(own.shape, jnp.float32),
        input_output_aliases={6: 0},
    )(take, own, left, right, columns, lines, filled)


def shifted(value, steps):
    count = lax.axis_size(AXES)
    first, last = max(0, -steps), min(count, count - steps)
    return lax.ppermute(value, AXES, [(i, i + steps) for i in range(first, last)])


def ranks(named):
    size = named.shape[-1]
    earlier = jnp.arange(size)[:, None] < jnp.arange(size)[None, :]
    return jnp.sum(jnp.where(named[..., :, None] & earlier, 1, 0), axis=-2)


def local(old_cells, old_range, neighbours):
    per_device = neighbours.shape[0]
    slots = old_cells.shape[0]
    side = old_cells.shape[3]
    margin = (slots - per_device) // 2
    devices = lax.axis_size(AXES)
    me = lax.axis_index(AXES)

    tables = lax.all_gather(neighbours, AXES, tiled=True)

    down, down_edges = inner_patches(old_cells, 0, margin)
    from_right = shifted(down, -1)
    up, up_edges = inner_patches(old_cells, slots - margin, margin)
    from_left = shifted(up, 1)
    edges_right = shifted(down_edges, -1)
    edges_left = shifted(up_edges, 1)
    own, own_edges = inner_patches(old_cells, margin, per_device)

    curve_index = me * per_device + jnp.arange(per_device, dtype=jnp.int32)
    take = ((curve_index < old_range[0, 0]) | (curve_index >= old_range[0, 1])).astype(jnp.int32)

    entry = jnp.arange(4 * per_device, dtype=jnp.int32)
    entry_side = entry % 4
    offsets = jnp.array(OFFSETS, jnp.int32)
    asking = me - offsets
    present = (asking >= 0) & (asking < devices)
    listed_by = tables.reshape(devices, 4 * per_device)[jnp.clip(asking, 0, devices - 1)]
    asked = present[:, None] & (listed_by >= 0) & (listed_by // per_device == me)
    order = ranks(asked)
    edge_row = 16 * (listed_by % per_device) + 8 * (entry_side // 2) + entry_side % 2
    chosen = asked[:, None, :] & (order[:, None, :] == jnp.arange(CAP)[None, :, None])
    send_rows = jnp.sum(jnp.where(chosen, edge_row[:, None, :], 0), axis=2).reshape(-1)

    edges, *outgoing = answers(take, send_rows, own_edges, edges_left, edges_right, margin)
    messages = [shifted(outgoing[k], -OFFSETS[k]) for k in range(4)]

    listed = neighbours.reshape(-1)
    alive = listed >= 0
    distance = jnp.where(alive, listed // per_device - me, 0)
    named = distance[None, :] == offsets[:, None]
    place = ranks(named)
    total = 16 * per_device
    base = total + 4 * CAP * jnp.arange(4, dtype=jnp.int32)[:, None]
    remote = jnp.sum(jnp.where(named, base + 8 * (place // 2) + place % 2, 0), axis=0)
    home = 16 * (listed % per_device) + 8 * (entry_side // 2) + entry_side % 2
    wall = 16 * (entry // 4) + 8 * (entry_side // 2) + 1 - entry_side % 2
    ghost_rows = jnp.where(alive, jnp.where(distance == 0, home, remote), wall)
    flips = jnp.where(neighbours >= 0, 1.0, -1.0).astype(jnp.float32).T.reshape(-1, 1)
    walls = jnp.broadcast_to(flips, (4 * per_device, side))

    columns, lines = rims(ghost_rows, walls, edges, messages)
    filled = middle(own, columns, lines, margin)
    return ends(take, own, from_left, from_right, columns, lines, filled, margin)


def solution(mesh):
    placed = (
        P(("member", "curve", "sub"), None, None, None),
        P(("member", "curve", "sub"), None),
        P(("member", "curve", "sub"), None),
    )
    return jax.shard_map(
        local,
        mesh=mesh,
        in_specs=placed,
        out_specs=P(("member", "curve", "sub"), None, None, None),
        check_vma=False,
    )
```

time: 114 us -> 89.8 us (0.79)
  the two profiles are of different devices: /device:TPU:17 before, /device:TPU:0 now
where the time goes in v1:
time: 89.8 us; the launch traced here: 88.8 us
  Pallas kernels  36.6 us (41%)
  blocking collectives  21.9 us (24%)
  starting transfers between devices  16.9 us (19%)
  local copies, waits for them, and re-layouts  5.38 us (6%)
  waiting for transfers between devices  4.79 us (5%)
  other arithmetic  2.94 us (3%)
    all_gather x1, blocking collectives, local(): tables = lax.all_gather(neighbours, AXES, tiled=True)  21.9 us
    pallas_call x3, Pallas kernels, inner_patches(): pl.pallas_call(functools.partial(patches_kernel, count), grid=(count,), i...  20.9 us
    ppermute x8, starting transfers between devices, shifted(): lax.ppermute(value, AXES, [(i, i + steps) for i in range(first, last)])  16.9 us
    pallas_call x1, Pallas kernels, ends(): pl.pallas_call(functools.partial(ends_kernel, margin, count), grid=(2 * m...  6.45 us
    pallas_call x1, Pallas kernels, middle(): pl.pallas_call(functools.partial(middle_kernel, margin), grid=(count - 2...  5.86 us
    ppermute x8, waiting for transfers between devices, shifted(): lax.ppermute(value, AXES, [(i, i + steps) for i in range(first, last)])  4.79 us
    unnamed x25, local copies, waits for them, and re-layouts  2.5 us
  transfers between devices with their start and end apart: 8, of which 2 were waited for; matrix products, arithmetic and copies ran while one was open for 7% of the time, Pallas kernels for 29%

profile of v1, /device:TPU:0, one launch (start us, length us, event | category | flops | bytes accessed | tf_op | source)
XLA Modules:
  0.0 88.8 jit_solution(1890367477547648610)
XLA Ops:
  0.0 4.1 %shard_map.48 = (f32[4,3,128,128]{3,2,1,0:T(8,128)}, f32[64,128]{1,0:T(8,128)}) custom-call(f32[24,4,128,128]{3,2,1,0:T(8,128)} %cells_ref.5), custom_call_target="tpu_custom_call" | custom-call | flops 6553600 | bytes 1835008 | tf_op jit(solution)/shard_map/pallas_call | solution.py:88
  4.1 1.3 %collective-permute-start.3 = (f32[64,128]{1,0:T(8,128)}, f32[64,128]{1,0:T(8,128)S(1)}, u32[]{:S(2)}, u32[]{:S(2)}) collective-permute-start(f32[64,128]{1,0:T(8,128)} %get-tuple-element.23), channel_id=1, source_target_pairs={{1,0},{2,1},{3,2},{4,3},{5,4},{6,5},{7,6},{8,7},{9,8},{10,9},{11,1... | collective-permute-start | bytes 98312 | tf_op jit(solution)/shard_map/ppermute | solution.py:268
  5.4 0.0 copy-start.11
  5.4 0.0 copy-start.9
  5.4 0.0 copy-start.4
  5.4 0.0 copy-start.10
  5.4 1.4 %collective-permute-start.1 = (f32[4,3,128,128]{3,2,1,0:T(8,128)}, f32[4,3,128,128]{3,2,1,0:T(8,128)S(1)}, u32[]{:S(2)}, u32[]{:S(2)}) collective-permute-start(f32[4,3,128,128]{3,2,1,0:T(8,128)} %get-tuple-element.20), channel_id=1, source_target_pairs={{1,0},{2,1},{3,2},{4,3},{5,4},{6,5},{7,6},{8,7},{9,8},{10,9},{11,1... | collective-permute-start | bytes 2359304 | tf_op jit(solution)/shard_map/ppermute | solution.py:268
  6.9 4.1 %shard_map.47 = (f32[4,3,128,128]{3,2,1,0:T(8,128)}, f32[64,128]{1,0:T(8,128)}) custom-call(f32[24,4,128,128]{3,2,1,0:T(8,128)} %cells_ref.5), custom_call_target="tpu_custom_call" | custom-call | flops 6553600 | bytes 1835008 | tf_op jit(solution)/shard_map/pallas_call | solution.py:88
  11.0 3.6 %collective-permute-start.2 = (f32[64,128]{1,0:T(8,128)}, f32[64,128]{1,0:T(8,128)S(1)}, u32[]{:S(2)}, u32[]{:S(2)}) collective-permute-start(f32[64,128]{1,0:T(8,128)} %get-tuple-element.22), channel_id=1, source_target_pairs={{0,1},{1,2},{2,3},{3,4},{4,5},{5,6},{6,7},{7,8},{8,9},{9,10},{10,1... | collective-permute-start | bytes 98312 | tf_op jit(solution)/shard_map/ppermute | solution.py:268
  14.6 4.5 %collective-permute-start = (f32[4,3,128,128]{3,2,1,0:T(8,128)}, f32[4,3,128,128]{3,2,1,0:T(8,128)S(1)}, u32[]{:S(2)}, u32[]{:S(2)}) collective-permute-start(f32[4,3,128,128]{3,2,1,0:T(8,128)} %get-tuple-element.19), channel_id=1, source_target_pairs={{0,1},{1,2},{2,3},{3,4},{4,5},{5,6},{6,7},{7,8},{8,9},{9,10},{10,1... | collective-permute-start | bytes 2359304 | tf_op jit(solution)/shard_map/ppermute | solution.py:268
  19.2 0.0 copy-done.11
  19.2 0.0 copy-done.9
  19.2 0.6 fusion.19
  19.9 0.0 copy-done.4
  19.9 0.1 copy.14
  20.0 0.1 reshape.234
  20.1 21.9 %all-gather = s32[16,16,4]{1,2,0:T(4,128)S(1)} all-gather(s32[1,16,4]{1,2,0:T(4,128)S(1)} %bitcast.7), channel_id=1, replica_groups=mesh['member'=2,'curve'=4,'sub'=4] {'curve','sub'}, dimensions={0}, use_global_device_ids=true | all-gather | bytes 4352 | tf_op jit(solution)/shard_map/all_gather | solution.py:285
  42.0 0.1 copy.15
  42.1 0.1 copy.16
  42.1 0.6 gather_fusion
  42.7 0.0 copy-done.10
  42.7 0.1 and_and_fusion
  42.8 0.2 select_reduce_fusion
  42.9 0.1 select_reduce_fusion.2
  43.1 1.8 %or_convert_fusion.take_ref = s32[16]{0:T(128)} fusion(s32[]{:T(128)} %bitcast.1, s32[]{:T(128)} %bitcast, s32[]{:T(128)S(6)} %mul.48), kind=kLoop, calls=%fused_computation.43 | loop fusion | flops 80 | bytes 76 | tf_op jit(solution)/shard_map/convert_element_type | solution.py:296
  44.9 0.7 reshape.236.rows_ref
  45.6 12.7 %shard_map.46 = (f32[16,3,128,128]{3,2,1,0:T(8,128)}, f32[256,128]{1,0:T(8,128)}) custom-call(f32[24,4,128,128]{3,2,1,0:T(8,128)} %cells_ref.5), custom_call_target="tpu_custom_call" | custom-call | flops 26214400 | bytes 7340032 | tf_op jit(solution)/shard_map/pallas_call | solution.py:88
  58.3 0.0 collective-permute-done.3.right_ref
  58.3 0.0 copy-start.2
  58.3 0.0 collective-permute-done.2.left_ref
  58.3 0.0 copy-start.3
  58.3 0.6 copy-done.2
  58.9 0.0 copy-done.3
  58.9 1.7 %shard_map.49 = (f32[256,128]{1,0:T(8,128)}, f32[32,128]{1,0:T(8,128)}, f32[32,128]{1,0:T(8,128)}, f32[32,128]{1,0:T(8,128)}, f32[32,128]{1,0:T(8,128)}) custom-call(s32[16]{0:T(128)} %or_convert_fusion.take_ref, s32[32]{0:T(128)} %reshape.236.rows_ref, f32[256,128]{1,0:T(8,128)} %get-tuple-element.21.own_ref, f32[64,128]{1,0:T(8,128)} %copy-done.3, ...), custom_call_target="tpu_custom_call" | custom-call | tf_op jit(solution)/shard_map/pallas_call | solution.py:129
  60.6 1.7 %collective-permute-start.4 = (f32[32,128]{1,0:T(8,128)}, f32[32,128]{1,0:T(8,128)S(1)}, u32[]{:S(2)}, u32[]{:S(2)}) collective-permute-start(f32[32,128]{1,0:T(8,128)} %get-tuple-element.25), channel_id=1, source_target_pairs={{0,2},{1,3},{2,4},{3,5},{4,6},{5,7},{6,8},{7,9},{8,10},{9,11},{10,... | collective-permute-start | bytes 49160 | tf_op jit(solution)/shard_map/ppermute | solution.py:268
  62.3 0.1 fusion.12
  62.4 1.8 %collective-permute-start.5 = (f32[32,128]{1,0:T(8,128)}, f32[32,128]{1,0:T(8,128)S(1)}, u32[]{:S(2)}, u32[]{:S(2)}) collective-permute-start(f32[32,128]{1,0:T(8,128)} %get-tuple-element.26), channel_id=1, source_target_pairs={{0,1},{1,2},{2,3},{3,4},{4,5},{5,6},{6,7},{7,8},{8,9},{9,10},{10,1... | collective-permute-start | bytes 49160 | tf_op jit(solution)/shard_map/ppermute | solution.py:268
  64.2 1.3 %collective-permute-start.6 = (f32[32,128]{1,0:T(8,128)}, f32[32,128]{1,0:T(8,128)S(1)}, u32[]{:S(2)}, u32[]{:S(2)}) collective-permute-start(f32[32,128]{1,0:T(8,128)} %get-tuple-element.27), channel_id=1, source_target_pairs={{1,0},{2,1},{3,2},{4,3},{5,4},{6,5},{7,6},{8,7},{9,8},{10,9},{11,1... | collective-permute-start | bytes 49160 | tf_op jit(solution)/shard_map/ppermute | solution.py:268
  65.5 0.0 collective-permute-done.4.m0
  65.5 0.0 copy-start.5
  65.5 1.3 %collective-permute-start.7 = (f32[32,128]{1,0:T(8,128)}, f32[32,128]{1,0:T(8,128)S(1)}, u32[]{:S(2)}, u32[]{:S(2)}) collective-permute-start(f32[32,128]{1,0:T(8,128)} %get-tuple-element.28), channel_id=1, source_target_pairs={{2,0},{3,1},{4,2},{5,3},{6,4},{7,5},{8,6},{9,7},{10,8},{11,9},{12,... | collective-permute-start | bytes 49160 | tf_op jit(solution)/shard_map/ppermute | solution.py:268
  66.8 0.6 compare_select_fusion.8.rows_ref
  67.4 0.1 broadcast_in_dim.66
  67.5 0.0 collective-permute-done.5.m1
  67.5 0.0 copy-start.6
  67.5 0.2 collective-permute-done.6.m2
  67.7 0.0 copy-start.7
  67.7 4.6 %collective-permute-done.7.m3 = f32[32,128]{1,0:T(8,128)S(1)} collective-permute-done((f32[32,128]{1,0:T(8,128)}, f32[32,128]{1,0:T(8,128)S(1)}, u32[]{:S(2)}, u32[]{:S(2)}) %collective-permute-start.7) | collective-permute-done | bytes 16416 | tf_op jit(solution)/shard_map/ppermute | solution.py:268
  72.3 0.0 copy-start.8
  72.3 0.7 broadcast_in_dim.67.wall_ref
  72.9 0.0 copy-done.5
  73.0 0.0 copy-done.6
  73.0 0.0 copy-done.7
  73.0 0.0 copy-done.8
  73.0 1.7 %shard_map.50 = (f32[128,128]{1,0:T(8,128)}, f32[128,128]{1,0:T(8,128)}) custom-call(s32[64]{0:T(128)} %compare_select_fusion.8.rows_ref, f32[64,128]{1,0:T(8,128)} %broadcast_in_dim.67.wall_ref, f32[256,128]{1,0:T(8,128)} %get-tuple-element.24.edge_ref, f32[32,128]{1,0:T(8,128)} %copy-done.5, f32[32,128]{1,0:T(8,128)} %copy-done.6, f32[32,128]{1,0:T(8,128)} %copy-done.7, ...), custom_call_target="tpu_custom_call" | custom-call | tf_op jit(solution)/shard_map/pallas_call | solution.py:184
  74.7 5.9 %shard_map.51._ = f32[16,3,128,128]{3,2,1,0:T(8,128)} custom-call(f32[16,3,128,128]{3,2,1,0:T(8,128)} %get-tuple-element.18.own_ref, f32[128,128]{1,0:T(8,128)} %get-tuple-element.29.columns_ref, f32[128,128]{1,0:T(8,128)} %get-tuple-element.30.lines_ref), custom_call_target="tpu_custom_call" | custom-call | tf_op jit(solution)/shard_map/pallas_call | solution.py:221
  80.6 0.0 collective-permute-done.1.right_ref
  80.6 0.0 copy-start
  80.6 0.0 collective-permute-done.left_ref
  80.6 0.9 copy-done
  81.4 0.0 copy-start.1
  81.4 0.9 %copy-done.1 = f32[4,3,128,128]{3,2,1,0:T(8,128)} copy-done((f32[4,3,128,128]{3,2,1,0:T(8,128)}, f32[4,3,128,128]{3,2,1,0:T(8,128)S(1)}, u32[]{:S(2)}) %copy-start.1) | copy-done | bytes 786456
  82.3 6.5 %shard_map.52 = f32[16,3,128,128]{3,2,1,0:T(8,128)} custom-call(s32[16]{0:T(128)} %or_convert_fusion.take_ref, f32[16,3,128,128]{3,2,1,0:T(8,128)} %get-tuple-element.18.own_ref, f32[4,3,128,128]{3,2,1,0:T(8,128)} %copy-done.1, f32[4,3,128,128]{3,2,1,0:T(8,128)} %copy-done, ...), custom_call_target="tpu_custom_call", output_to_operand_aliasing={{}: (6, {})} | custom-call | tf_op jit(solution)/shard_map/pallas_call | solution.py:247
  (9 shorter events, 0.1 us)
Async XLA Ops:
  4.1 54.2 %collective-permute-start.3 = (f32[64,128]{1,0:T(8,128)}, f32[64,128]{1,0:T(8,128)S(1)}, u32[]{:S(2)}, u32[]{:S(2)}) collective-permute-start(f32[64,128]{1,0:T(8,128)} %get-tuple-element.23), channel_id=1, source_target_pairs={{1,0},{2,1},{3,2},{4,3},{5,4},{6,5},{7,6},{8,7},{9,8},{10,9},{11,1... | collective-permute-start | bytes 98312 | tf_op jit(solution)/shard_map/ppermute | solution.py:268
  5.4 13.8 %copy-start.11 = (s32[4]{0:T(128)S(1)}, s32[4]{0:T(128)}, u32[]{:S(2)}) copy-start(s32[4]{0:T(128)} %constant.146) | copy-start | bytes 52
  5.4 13.8 %copy-start.9 = (s32[1,2]{1,0:T(1,128)S(1)}, s32[1,2]{1,0:T(1,128)}, u32[]{:S(2)}) copy-start(s32[1,2]{1,0:T(1,128)} %param.5) | copy-start | bytes 28
  5.4 14.5 %copy-start.4 = (s32[16,4]{0,1:T(4,128)S(1)}, s32[16,4]{0,1:T(4,128)}, u32[]{:S(2)}) copy-start(s32[16,4]{0,1:T(4,128)} %param.6) | copy-start | bytes 772
  5.4 37.3 %copy-start.10 = (s32[4]{0:T(128)S(1)}, s32[4]{0:T(128)}, u32[]{:S(2)}) copy-start(s32[4]{0:T(128)} %constant.142.clone) | copy-start | bytes 52
  5.4 75.1 %collective-permute-start.1 = (f32[4,3,128,128]{3,2,1,0:T(8,128)}, f32[4,3,128,128]{3,2,1,0:T(8,128)S(1)}, u32[]{:S(2)}, u32[]{:S(2)}) collective-permute-start(f32[4,3,128,128]{3,2,1,0:T(8,128)} %get-tuple-element.20), channel_id=1, source_target_pairs={{1,0},{2,1},{3,2},{4,3},{5,4},{6,5},{7,6},{8,7},{9,8},{10,9},{11,1... | collective-permute-start | bytes 2359304 | tf_op jit(solution)/shard_map/ppermute | solution.py:268
  11.0 47.3 %collective-permute-start.2 = (f32[64,128]{1,0:T(8,128)}, f32[64,128]{1,0:T(8,128)S(1)}, u32[]{:S(2)}, u32[]{:S(2)}) collective-permute-start(f32[64,128]{1,0:T(8,128)} %get-tuple-element.22), channel_id=1, source_target_pairs={{0,1},{1,2},{2,3},{3,4},{4,5},{5,6},{6,7},{7,8},{8,9},{9,10},{10,1... | collective-permute-start | bytes 98312 | tf_op jit(solution)/shard_map/ppermute | solution.py:268
  14.6 65.9 %collective-permute-start = (f32[4,3,128,128]{3,2,1,0:T(8,128)}, f32[4,3,128,128]{3,2,1,0:T(8,128)S(1)}, u32[]{:S(2)}, u32[]{:S(2)}) collective-permute-start(f32[4,3,128,128]{3,2,1,0:T(8,128)} %get-tuple-element.19), channel_id=1, source_target_pairs={{0,1},{1,2},{2,3},{3,4},{4,5},{5,6},{6,7},{7,8},{8,9},{9,10},{10,1... | collective-permute-start | bytes 2359304 | tf_op jit(solution)/shard_map/ppermute | solution.py:268
  58.3 0.6 copy-start.2
  58.3 0.6 copy-start.3
  60.6 4.9 %collective-permute-start.4 = (f32[32,128]{1,0:T(8,128)}, f32[32,128]{1,0:T(8,128)S(1)}, u32[]{:S(2)}, u32[]{:S(2)}) collective-permute-start(f32[32,128]{1,0:T(8,128)} %get-tuple-element.25), channel_id=1, source_target_pairs={{0,2},{1,3},{2,4},{3,5},{4,6},{5,7},{6,8},{7,9},{8,10},{9,11},{10,... | collective-permute-start | bytes 49160 | tf_op jit(solution)/shard_map/ppermute | solution.py:268
  62.4 5.1 %collective-permute-start.5 = (f32[32,128]{1,0:T(8,128)}, f32[32,128]{1,0:T(8,128)S(1)}, u32[]{:S(2)}, u32[]{:S(2)}) collective-permute-start(f32[32,128]{1,0:T(8,128)} %get-tuple-element.26), channel_id=1, source_target_pairs={{0,1},{1,2},{2,3},{3,4},{4,5},{5,6},{6,7},{7,8},{8,9},{9,10},{10,1... | collective-permute-start | bytes 49160 | tf_op jit(solution)/shard_map/ppermute | solution.py:268
  64.2 3.5 %collective-permute-start.6 = (f32[32,128]{1,0:T(8,128)}, f32[32,128]{1,0:T(8,128)S(1)}, u32[]{:S(2)}, u32[]{:S(2)}) collective-permute-start(f32[32,128]{1,0:T(8,128)} %get-tuple-element.27), channel_id=1, source_target_pairs={{1,0},{2,1},{3,2},{4,3},{5,4},{6,5},{7,6},{8,7},{9,8},{10,9},{11,1... | collective-permute-start | bytes 49160 | tf_op jit(solution)/shard_map/ppermute | solution.py:268
  65.5 7.5 %copy-start.5 = (f32[32,128]{1,0:T(8,128)}, f32[32,128]{1,0:T(8,128)S(1)}, u32[]{:S(2)}) copy-start(f32[32,128]{1,0:T(8,128)S(1)} %collective-permute-done.4.m0) | copy-start | bytes 49156
  65.5 6.8 %collective-permute-start.7 = (f32[32,128]{1,0:T(8,128)}, f32[32,128]{1,0:T(8,128)S(1)}, u32[]{:S(2)}, u32[]{:S(2)}) collective-permute-start(f32[32,128]{1,0:T(8,128)} %get-tuple-element.28), channel_id=1, source_target_pairs={{2,0},{3,1},{4,2},{5,3},{6,4},{7,5},{8,6},{9,7},{10,8},{11,9},{12,... | collective-permute-start | bytes 49160 | tf_op jit(solution)/shard_map/ppermute | solution.py:268
  67.5 5.5 %copy-start.6 = (f32[32,128]{1,0:T(8,128)}, f32[32,128]{1,0:T(8,128)S(1)}, u32[]{:S(2)}) copy-start(f32[32,128]{1,0:T(8,128)S(1)} %collective-permute-done.5.m1) | copy-start | bytes 49156
  67.7 5.3 %copy-start.7 = (f32[32,128]{1,0:T(8,128)}, f32[32,128]{1,0:T(8,128)S(1)}, u32[]{:S(2)}) copy-start(f32[32,128]{1,0:T(8,128)S(1)} %collective-permute-done.6.m2) | copy-start | bytes 49156
  72.3 0.7 copy-start.8
  80.6 0.9 copy-start
  81.4 0.9 %copy-start.1 = (f32[4,3,128,128]{3,2,1,0:T(8,128)}, f32[4,3,128,128]{3,2,1,0:T(8,128)S(1)}, u32[]{:S(2)}) copy-start(f32[4,3,128,128]{3,2,1,0:T(8,128)S(1)} %collective-permute-done.left_ref) | copy-start | bytes 2359300

commit v2 on v0

v2 whole, which is shorter than its diff:
```python
import functools

import jax
import jax.numpy as jnp
from jax import lax
from jax.experimental import pallas as pl
from jax.experimental.pallas import tpu as pltpu
from jax.sharding import PartitionSpec as P

RATE_STEP = 0.1
HALF = 0.5 * RATE_STEP
AXES = ("curve", "sub")
CAP = 8
ROWS = 8
VMEM = pl.BlockSpec(memory_space=pltpu.VMEM)
SMEM = pl.BlockSpec(memory_space=pltpu.SMEM)
HBM = pl.BlockSpec(memory_space=pltpu.HBM)


def position():
    me = lax.axis_index(AXES)
    return me, lax.rem(me, 2)


def iota(axis, side):
    return lax.broadcasted_iota(jnp.int32, (ROWS, side), axis)


def inner_update(load, store, columns, at, side):
    lane, line = iota(1, side), iota(0, side)
    pair = lane // 2
    west, east = lane == 0, lane == side - 1
    first, last = line == 0, line == ROWS - 1
    strips = side // ROWS
    ahead = lambda a: pltpu.roll(a, side - 1, 1)
    behind = lambda a: pltpu.roll(a, 1, 1)
    below = None
    pending = None

    def finish(k, held, ups):
        h, part_h, part_x, part_y, lows, bed_low, up_own = held
        north = [jnp.where(last, u, o) for u, o in zip(ups, up_own)]
        part_y = part_y + h * (north[3] - bed_low)
        store(0, k, h - HALF * (part_h + (north[0] - lows[0])))
        mx, my = load(1, k), load(2, k)
        store(1, k, mx - HALF * (part_x + (north[1] - lows[1])))
        store(2, k, my - HALF * (part_y + (north[2] - lows[2])))

    for k in range(strips):
        h, mx, my, bed = (load(f, k) for f in range(4))
        held = columns[ROWS * k : ROWS * (k + 1), :]
        for f, value in enumerate((h, mx, my, bed)):
            held = jnp.where(pair == at // 2 + f, pltpu.roll(value, at + 2 * f + 1, 1), held)
        columns[ROWS * k : ROWS * (k + 1), :] = held
        root = lax.rsqrt(h)
        celerity = h * root
        inverse = root * root
        u = mx * inverse
        v = my * inverse
        half_sq = 0.5 * h * h
        cross = my * u
        fx = mx * u + half_sq
        fy = my * v + half_sq
        rate_x = jnp.abs(u) + celerity
        rate_y = jnp.abs(v) + celerity
        eta = h + bed
        top = jnp.maximum(rate_x, ahead(rate_x))
        mx_e, my_e, bed_e = ahead(mx), ahead(my), ahead(bed)
        q = [
            (mx + mx_e) - top * (ahead(eta) - eta),
            (fx + ahead(fx)) - top * (mx_e - mx),
            (cross + ahead(cross)) - top * (my_e - my),
        ]
        q = [jnp.where(east, 0.0, each) for each in q]
        slope = jnp.where(east, 0.0, bed_e) - jnp.where(west, 0.0, behind(bed))
        part_h = q[0] - behind(q[0])
        part_x = q[1] - behind(q[1]) + h * slope
        part_y = q[2] - behind(q[2])
        values = (rate_y, eta, mx, my, cross, fy, bed)
        turned = [pltpu.roll(each, 1, 0) for each in values]
        if below is None:
            south = turned[:6] + [jnp.where(first, 0.0, turned[6])]
        else:
            south = [jnp.where(first, b, t) for b, t in zip(below, turned)]
        below = turned
        top = jnp.maximum(rate_y, south[0])
        q = [
            (my + south[3]) - top * (eta - south[1]),
            (cross + south[4]) - top * (mx - south[2]),
            (fy + south[5]) - top * (my - south[3]),
        ]
        if k == 0:
            q = [jnp.where(first, 0.0, each) for each in q]
        ups = [pltpu.roll(each, ROWS - 1, 0) for each in q + [bed]]
        if pending is not None:
            finish(k - 1, pending, ups)
        pending = (h, part_h, part_x, part_y, q, south[6], ups)
    finish(strips - 1, pending, [0.0] * 4)


def take_edges(count, cells, slot_of, columns, edges, base):
    side = columns.shape[0]
    turned = jnp.transpose(columns[...])
    for p in range(count):
        edges[base + 16 * p : base + 16 * p + 8, :] = turned[8 * p : 8 * p + 8, :]
        for f in range(4):
            row = base + 16 * p + 8 + 2 * f
            edges[row : row + 1, :] = cells[slot_of(p), f, side - 1 : side, :]
            edges[row + 1 : row + 2, :] = cells[slot_of(p), f, 0:1, :]


def update_one(cells, i, columns, lane_at, side, put):
    inner_update(
        lambda f, k: cells[i, f, ROWS * k : ROWS * (k + 1), :],
        lambda f, k, value: put(f, ROWS * k, value),
        columns,
        lane_at,
        side,
    )


def fetch(cells_hbm, first, cells, sems, count):
    def copy(i):
        return pltpu.make_async_copy(cells_hbm.at[first + i], cells.at[i], sems.at[i])

    for i in range(count):
        copy(i).start()
    return copy


def outer_kernel(margin, cells_hbm, out, edges, cells, columns, sems):
    side = columns.shape[0]
    _, odd = position()
    copy = fetch(cells_hbm, odd * (cells_hbm.shape[0] - margin), cells, sems, margin)

    @pl.loop(0, margin)
    def _(i):
        copy(i).wait()

        def put(f, row, value):
            out[i, f, row : row + ROWS, :] = value

        update_one(cells, i, columns, 8 * i, side, put)

    take_edges(margin, cells, lambda p: p, columns, edges, 0)


def cost(patches, side):
    return pl.CostEstimate(
        flops=patches * side * side * 800,
        bytes_accessed=patches * side * side * 28,
        transcendentals=patches * side * side,
    )


def outer_patches(old_cells, margin):
    side = old_cells.shape[3]
    return pl.pallas_call(
        functools.partial(outer_kernel, margin),
        in_specs=[HBM],
        out_specs=[VMEM, VMEM],
        out_shape=[
            jax.ShapeDtypeStruct((margin, 3, side, side), jnp.float32),
            jax.ShapeDtypeStruct((16 * margin, side), jnp.float32),
        ],
        scratch_shapes=[
            pltpu.VMEM((margin, 4, side, side), jnp.float32),
            pltpu.VMEM((side, side), jnp.float32),
            pltpu.SemaphoreType.DMA((margin,)),
        ],
        cost_estimate=cost(margin, side),
        name="outer",
    )(old_cells)


def layout(margin, per_device, side):
    inner = 3 * side * margin
    home = inner + 16 * margin
    limit = home + 16 * per_device
    brought = limit + 8
    return inner, home, limit, brought, brought + 16 * margin + 8


def home_kernel(margin, range_ref, cells_hbm, shared, own, cells, columns, sems):
    side = columns.shape[0]
    count = own.shape[0]
    inner, home, limit, _, _ = layout(margin, count, side)
    _, odd = position()
    copy = fetch(cells_hbm, (1 - odd) * margin, cells, sems, margin + count)
    inner_at = (1 - odd) * count
    home_at = odd * margin

    @pl.loop(0, margin)
    def _(i):
        copy(inner_at + i).wait()

        def put(f, row, value):
            at = pl.multiple_of(i * (3 * side) + (f * side + row), ROWS)
            shared[pl.ds(at, ROWS), :] = value

        update_one(cells, inner_at + i, columns, 8 * i, side, put)

    take_edges(margin, cells, lambda p: inner_at + p, columns, shared, inner)

    @pl.loop(0, count)
    def _(i):
        copy(home_at + i).wait()

        def put(f, row, value):
            own[i, f, row : row + ROWS, :] = value

        update_one(cells, home_at + i, columns, 8 * i, side, put)

    take_edges(count, cells, lambda p: home_at + p, columns, shared, home)
    outer_limit = jnp.where(odd == 1, range_ref[0, 1], range_ref[0, 0])
    shared[limit : limit + 8, :] = jnp.full((8, side), outer_limit, jnp.int32).astype(jnp.float32)


def home_patches(old_range, old_cells, margin, per_device):
    side = old_cells.shape[3]
    total = layout(margin, per_device, side)[-1]
    return pl.pallas_call(
        functools.partial(home_kernel, margin),
        in_specs=[SMEM, HBM],
        out_specs=[VMEM, VMEM],
        out_shape=[
            jax.ShapeDtypeStruct((total, side), jnp.float32),
            jax.ShapeDtypeStruct((per_device, 3, side, side), jnp.float32),
        ],
        scratch_shapes=[
            pltpu.VMEM((margin + per_device, 4, side, side), jnp.float32),
            pltpu.VMEM((side, side), jnp.float32),
            pltpu.SemaphoreType.DMA((margin + per_device,)),
        ],
        cost_estimate=cost(margin + per_device, side),
        compiler_params=pltpu.CompilerParams(vmem_limit_bytes=24 << 20),
        name="home",
    )(old_range, old_cells)


def answer_kernel(margin, count, range_ref, rows_ref, mine, theirs, edges, message):
    side = edges.shape[1]
    inner, home, limit, brought, _ = layout(margin, count, side)
    me, odd = position()
    start, stop = range_ref[0, 0], range_ref[0, 1]
    even = odd == 0
    at_me = pl.multiple_of(16 * count * odd, 16)
    at_them = pl.multiple_of(16 * count * (1 - odd), 16)
    edges[pl.ds(at_me, 16 * count), :] = mine[home : home + 16 * count, :]
    edges[pl.ds(at_them, 16 * count), :] = theirs[home : home + 16 * count, :]
    their_limit = theirs[limit : limit + 8, :]
    low, high = 0, count - margin
    for m in range(margin):
        l = jnp.where(even, high, low) + m
        g = me * count + l
        taken = jnp.where(even, g >= stop, g < start)
        to = pl.multiple_of(at_me + 16 * l, 16)
        from_pair = theirs[inner + 16 * m : inner + 16 * (m + 1), :]
        edges[pl.ds(to, 16), :] = jnp.where(taken, from_pair, edges[pl.ds(to, 16), :])
        l = jnp.where(even, low, high) + m
        g = (me + 1 - 2 * odd) * count + l
        taken = jnp.where(even, g < stop, g >= start)
        to = pl.multiple_of(at_them + 16 * l, 16)
        from_pair = mine[inner + 16 * m : inner + 16 * (m + 1), :]
        edges[pl.ds(to, 16), :] = jnp.where(taken, from_pair, edges[pl.ds(to, 16), :])
        l = jnp.where(even, low, high) + m
        g = me * count + l
        taken = jnp.where(even, g < start, g >= stop)
        to = pl.multiple_of(at_me + 16 * l, 16)
        crossed = mine[brought + 16 * m : brought + 16 * (m + 1), :]
        edges[pl.ds(to, 16), :] = jnp.where(taken, crossed, edges[pl.ds(to, 16), :])
        l = jnp.where(even, high, low) + m
        g = ((me + 1 - 2 * odd) * count + l).astype(jnp.float32)
        to = pl.multiple_of(at_them + 16 * l, 16)
        taken = jnp.where(even, g - their_limit, their_limit - g - 1.0) >= 0.0
        for half in range(2):
            crossed = theirs[brought + 16 * m + 8 * half : brought + 16 * m + 8 * half + 8, :]
            at = pl.multiple_of(to + 8 * half, 8)
            edges[pl.ds(at, 8), :] = jnp.where(taken, crossed, edges[pl.ds(at, 8), :])
    for n in range(3 * CAP):
        message[pl.ds(8 * (n // 2) + n % 2, 4, stride=2), :] = edges[pl.ds(rows_ref[n], 4, stride=2), :]


def answers(old_range, rows, mine, theirs, margin, per_device):
    side = mine.shape[1]
    return pl.pallas_call(
        functools.partial(answer_kernel, margin, per_device),
        in_specs=[SMEM, SMEM, VMEM, VMEM],
        out_specs=[VMEM, VMEM],
        out_shape=[
            jax.ShapeDtypeStruct((32 * per_device, side), jnp.float32),
            jax.ShapeDtypeStruct((12 * CAP, side), jnp.float32),
        ],
        name="answers",
    )(old_range, rows, mine, theirs)


def add_rim(p, load, store, columns, lines):
    side = columns.shape[0]
    lane, line = iota(1, side), iota(0, side)
    rim = (lane == 0) | (lane == side - 1)
    south = [lines[pl.ds(8 * p + 2 * f + 1, 1), :] for f in range(3)]
    north = [lines[pl.ds(8 * p + 2 * f, 1), :] for f in range(3)]
    strips = side // ROWS
    for k in range(strips):
        held = columns[ROWS * k : ROWS * (k + 1), :]
        for f in range(3):
            value = load(f, k) + jnp.where(rim, pltpu.roll(held, side - 1 - 8 * p - 2 * f, 1), 0.0)
            if k == 0:
                value = value + jnp.where(line == 0, south[f], 0.0)
            if k == strips - 1:
                value = value + jnp.where(line == ROWS - 1, north[f], 0.0)
            store(f, k, value)


def rim_terms(rows_ref, edges, crossed, passed, columns, lines, source, ghost, turn, count, odd):
    total = edges.shape[0]
    step = crossed.shape[0]
    source[0:total, :] = edges[...]
    source[total : total + step, :] = crossed[...]
    source[total + step : total + 2 * step, :] = passed[...]
    field = lax.broadcasted_iota(jnp.int32, (4, edges.shape[1]), 0)
    for p in range(count):
        for s in range(4):
            row = rows_ref[4 * p + s]
            wall = row < 0
            value = source[pl.ds(jnp.where(wall, -1 - row, row), 4, stride=2), :]
            value = jnp.where((field == 1 + s // 2) & wall, -value, value)
            ghost[pl.ds(16 * p + 8 * (s // 2) + 1 - s % 2, 4, stride=2), :] = value
    turn[...] = jnp.zeros_like(turn)
    lines[...] = jnp.zeros_like(lines)
    for s in range(4):
        parity = 1 - s % 2
        sign = 1.0 - 2.0 * parity
        axis = s // 2
        normal, across = (1, 2) if axis == 0 else (2, 1)

        def both(f):
            row = 8 * axis + 2 * f + parity
            own = source[pl.ds(16 * count * odd + row, count, stride=16), :]
            return own, ghost[pl.ds(row, count, stride=16), :]

        hc, hg = both(0)
        nc, ng = both(normal)
        ac, ag = both(across)
        bc, bg = both(3)
        rc, rg = lax.rsqrt(hc), lax.rsqrt(hg)
        uc, ug = nc * rc * rc, ng * rg * rg
        top = jnp.maximum(jnp.abs(uc) + hc * rc, jnp.abs(ug) + hg * rg)
        fc, fg = nc * uc + 0.5 * hc * hc, ng * ug + 0.5 * hg * hg
        c_h = -HALF * (sign * (nc + ng) - top * ((hg + bg) - (hc + bc)))
        c_n = -HALF * (sign * (fc + fg + hc * bg) - top * (ng - nc))
        c_t = -HALF * (sign * (ac * uc + ag * ug) - top * (ag - ac))
        for f, value in ((0, c_h), (normal, c_n), (across, c_t)):
            target = turn if axis == 0 else lines
            target[pl.ds(2 * f + parity, count, stride=8), :] = value
    columns[...] = jnp.transpose(turn[...])


def most_kernel(
    margin, range_ref, rows_ref, edges, crossed, passed, own, theirs, out, columns, lines, result, source, ghost, turn, sems
):
    count, side = own.shape[0], columns.shape[0]
    me, odd = position()
    even = odd == 0
    rim_terms(rows_ref, edges, crossed, passed, columns, lines, source, ghost, turn, count, odd)
    start, stop = range_ref[0, 0], range_ref[0, 1]
    first = (1 - odd) * margin
    many = count - margin

    def copy(i):
        return pltpu.make_async_copy(result.at[i], out.at[first + i], sems.at[i])

    @pl.loop(0, many)
    def _(i):
        p = first + i
        g = me * count + p
        taken = jnp.where(even, g >= stop, g < start)
        m = jnp.clip(jnp.where(even, p - (count - margin), p), 0, margin - 1)

        def load(f, k):
            at = pl.multiple_of(m * (3 * side) + (f * side + ROWS * k), ROWS)
            return jnp.where(taken, theirs[pl.ds(at, ROWS), :], own[p, f, ROWS * k : ROWS * (k + 1), :])

        def store(f, k, value):
            result[i, f, ROWS * k : ROWS * (k + 1), :] = value

        add_rim(p, load, store, columns, lines)
        copy(i).start()

    for i in range(many):
        copy(i).wait()


def most(old_range, rows, edges, crossed, passed, own, theirs, margin):
    count, _, side, _ = own.shape
    many = count - margin
    return pl.pallas_call(
        functools.partial(most_kernel, margin),
        in_specs=[SMEM, SMEM] + [VMEM] * 5,
        out_specs=[HBM, VMEM, VMEM],
        out_shape=[
            jax.ShapeDtypeStruct(own.shape, jnp.float32),
            jax.ShapeDtypeStruct((side, side), jnp.float32),
            jax.ShapeDtypeStruct((side, side), jnp.float32),
        ],
        scratch_shapes=[
            pltpu.VMEM((many, 3, side, side), jnp.float32),
            pltpu.VMEM((edges.shape[0] + 2 * crossed.shape[0], side), jnp.float32),
            pltpu.VMEM((16 * count, side), jnp.float32),
            pltpu.VMEM((side, side), jnp.float32),
            pltpu.SemaphoreType.DMA((many,)),
        ],
        compiler_params=pltpu.CompilerParams(vmem_limit_bytes=24 << 20),
        name="most",
    )(old_range, rows, edges, crossed, passed, own, theirs)


def rest_kernel(margin, range_ref, own, arrived, columns, lines, _, out, result, sems):
    count, side = own.shape[0], columns.shape[0]
    me, odd = position()
    even = odd == 0
    start, stop = range_ref[0, 0], range_ref[0, 1]
    first = odd * (count - margin)

    def copy(i):
        return pltpu.make_async_copy(result.at[i], out.at[first + i], sems.at[i])

    @pl.loop(0, margin)
    def _(i):
        p = first + i
        g = me * count + p
        taken = jnp.where(even, g < start, g >= stop)

        def load(f, k):
            at = slice(ROWS * k, ROWS * (k + 1))
            return jnp.where(taken, arrived[i, f, at, :], own[p, f, at, :])

        def store(f, k, value):
            result[i, f, ROWS * k : ROWS * (k + 1), :] = value

        add_rim(p, load, store, columns, lines)
        copy(i).start()

    for i in range(margin):
        copy(i).wait()


def rest(old_range, own, arrived, columns, lines, filled, margin):
    count, _, side, _ = own.shape
    return pl.pallas_call(
        functools.partial(rest_kernel, margin),
        in_specs=[SMEM] + [VMEM] * 4 + [HBM],
        out_specs=HBM,
        out_shape=jax.ShapeDtypeStruct(own.shape, jnp.float32),
        scratch_shapes=[
            pltpu.VMEM((margin, 3, side, side), jnp.float32),
            pltpu.SemaphoreType.DMA((margin,)),
        ],
        input_output_aliases={5: 0},
        name="rest",
    )(old_range, own, arrived, columns, lines, filled)


def swapped(value, first):
    pairs = [(i, i + 1) for i in range(first, lax.axis_size(AXES) - 1, 2)]
    return lax.ppermute(value, AXES, pairs + [(j, i) for i, j in pairs])


def ranks(named):
    size = named.shape[-1]
    earlier = jnp.arange(size)[:, None] < jnp.arange(size)[None, :]
    return jnp.sum(jnp.where(named[..., :, None] & earlier, 1, 0), axis=-2)


def local(old_cells, old_range, neighbours):
    per_device = neighbours.shape[0]
    side = old_cells.shape[3]
    margin = (old_cells.shape[0] - per_device) // 2
    entries = 4 * per_device
    me, odd = position()
    brought = layout(margin, per_device, side)[3]

    their_table = swapped(neighbours, 0)
    leaving, leaving_edges = outer_patches(old_cells, margin)
    arrived = swapped(leaving, 1)

    tables = jnp.where(
        odd == 0,
        jnp.concatenate([neighbours.reshape(1, -1), their_table.reshape(1, -1)], axis=1),
        jnp.concatenate([their_table.reshape(1, -1), neighbours.reshape(1, -1)], axis=1),
    ).astype(jnp.float32)
    tables = jnp.pad(tables, ((0, 7), (0, side - 2 * entries)))
    came = swapped(jnp.concatenate([leaving_edges, tables], axis=0), 1)

    shared, own = home_patches(old_range, old_cells, margin, per_device)
    shared = lax.dynamic_update_slice(shared, came, (brought, 0))
    theirs = swapped(shared, 0)

    entry = jnp.arange(entries, dtype=jnp.int32)
    entry_side = entry % 4
    at_side = 8 * (entry_side // 2) + entry_side % 2
    asked_by = came[16 * margin, : 2 * entries].astype(jnp.int32).reshape(2, entries)
    middle = jnp.where(odd == 0, asked_by[1], asked_by[0])
    listed = jnp.stack([asked_by[0], middle, asked_by[1]])
    owners = me + jnp.where(odd == 0, jnp.array([0, 0, 1], jnp.int32), jnp.array([-1, 0, 0], jnp.int32))
    asked = (listed >= 0) & (listed // per_device == owners[:, None])
    rows = 16 * (listed - 2 * per_device * (me // 2)) + at_side
    chosen = asked[:, None, :] & (ranks(asked)[:, None, :] == jnp.arange(CAP)[None, :, None])
    send_rows = jnp.sum(jnp.where(chosen, rows[:, None, :], 0), axis=2).reshape(-1)

    edges, message = answers(old_range, send_rows, shared, theirs, margin, per_device)
    crossed = swapped(message, 1)
    passed = swapped(crossed, 0)

    listed = neighbours.reshape(-1)
    owner = listed // per_device
    mine, total, step = 32 * per_device, 16 * per_device, 12 * CAP
    lists = jnp.where(
        odd == 0,
        jnp.array([[-2, mine], [-1, mine + 4 * CAP], [2, mine + step]], jnp.int32),
        jnp.array([[-2, mine + step + 8 * CAP], [1, mine + 4 * CAP], [2, mine + 8 * CAP]], jnp.int32),
    )
    named = (listed >= 0) & (owner - me == lists[:, :1])
    place = ranks(named)
    across = jnp.sum(jnp.where(named, lists[:, 1:] + 8 * (place // 2) + place % 2, 0), axis=0)
    within = 16 * (listed - 2 * per_device * (me // 2)) + at_side
    wall = total * odd + 16 * (entry // 4) + 8 * (entry_side // 2) + 1 - entry_side % 2
    ghost_rows = jnp.where(listed < 0, -1 - wall, jnp.where(owner // 2 == me // 2, within, across))

    filled, columns, lines = most(old_range, ghost_rows, edges, crossed, passed, own, theirs, margin)
    return rest(old_range, own, arrived, columns, lines, filled, margin)


def solution(mesh):
    placed = (
        P(("member", "curve", "sub"), None, None, None),
        P(("member", "curve", "sub"), None),
        P(("member", "curve", "sub"), None),
    )
    return jax.shard_map(
        local,
        mesh=mesh,
        in_specs=placed,
        out_specs=P(("member", "curve", "sub"), None, None, None),
        check_vma=False,
    )
```

time: 114 us -> 58.6 us (0.51)
  local copies, waits for them, and re-layouts: 41.9 us -> 6.71 us
  Pallas kernels: 0 us -> 33.1 us
  other arithmetic: 32.4 us -> 1.45 us
  waiting for transfers between devices: 20.5 us -> 4.38 us
  starting transfers between devices: 18.2 us -> 12 us
    pallas_call x0 -> x5, Pallas kernels: none -> 33.1 us  [the longest x1 18.5 us: home_patches(): pl.pallas_call(functools.partial(home_kernel, margin), in_specs=[SMEM, HB...]
    slice x7 -> x0, local copies, waits for them, and re-layouts: 28.6 us -> none  [the longest x1 8.37 us: advance(): above = jnp.where(line == side_len - 1, north, jnp.roll(cells, -1, axis=2))]
    ppermute x6, waiting for transfers between devices: 20.5 us -> 4.38 us  [swapped(): return lax.ppermute(value, AXES, pairs + [(j, i) for i, j in pairs])]
    select_n x4 -> x2, other arithmetic: 12.7 us -> 0.02 us  [the longest x1 0.01 us: local(): jnp.where(listed < 0, -1 - wall, jnp.where(owner // 2 == me // 2, within,...]
    sub x5 -> x1, other arithmetic: 9.54 us -> 0.01 us  [local(): named = (listed >= 0) & (owner - me == lists[:, :1])]
    gather x3 -> x0, local copies, waits for them, and re-layouts: 7.6 us -> none  [the longest x1 6.19 us: local(): cells = grown[position]]
    ppermute x6, starting transfers between devices: 18.2 us -> 12 us  [swapped(): return lax.ppermute(value, AXES, pairs + [(j, i) for i, j in pairs])]
    concatenate x2 -> x1, other arithmetic: 5.59 us -> 0.77 us  [local(): came = swapped(jnp.concatenate([leaving_edges, tables], axis=0), 1)]
  transfers between devices with their start and end apart: 6 -> 6, of which waited for: 2 -> 3; matrix products, arithmetic and copies ran while one was open for 14% -> 5% of each run, Pallas kernels for 0% -> 51%
where the time goes in v2:
time: 58.6 us; the launch traced here: 57.9 us
  Pallas kernels  33.1 us (56%)
  starting transfers between devices  12 us (20%)
  local copies, waits for them, and re-layouts  6.71 us (11%)
  waiting for transfers between devices  4.38 us (7%)
  other arithmetic  1.45 us (2%)
    pallas_call x1, Pallas kernels, home_patches(): pl.pallas_call(functools.partial(home_kernel, margin), in_specs=[SMEM, HB...  18.5 us
    ppermute x6, starting transfers between devices, swapped(): return lax.ppermute(value, AXES, pairs + [(j, i) for i, j in pairs])  12 us
    pallas_call x1, Pallas kernels, outer_patches(): pl.pallas_call(functools.partial(outer_kernel, margin), in_specs=[HBM], o...  5.13 us
    unnamed x25, local copies, waits for them, and re-layouts  5.08 us
    ppermute x6, waiting for transfers between devices, swapped(): return lax.ppermute(value, AXES, pairs + [(j, i) for i, j in pairs])  4.38 us
    pallas_call x1, Pallas kernels, most(): pl.pallas_call(functools.partial(most_kernel, margin), in_specs=[SMEM, SM...  3.76 us
    pallas_call x1, Pallas kernels, rest(): pl.pallas_call(functools.partial(rest_kernel, margin), in_specs=[SMEM] +...  3.36 us
    pallas_call x1, Pallas kernels, answers(): pl.pallas_call(functools.partial(answer_kernel, margin, per_device), in_s...  2.33 us
  transfers between devices with their start and end apart: 6, of which 3 were waited for; matrix products, arithmetic and copies ran while one was open for 5% of the time, Pallas kernels for 51%

profile of v2, /device:TPU:17, one launch (start us, length us, event | category | flops | bytes accessed | tf_op | source)
XLA Modules:
  0.0 57.9 jit_solution(16165273039315455672)
XLA Ops:
  0.0 0.0 copy-start.8
  0.0 0.0 copy-start.9
  0.0 0.0 copy-start.10
  0.0 0.0 copy-start.11
  0.0 0.0 copy-start.7
  0.0 0.0 copy-start.5
  0.0 0.7 %collective-permute-start.1 = (s32[16,4]{0,1:T(4,128)}, s32[16,4]{0,1:T(4,128)S(1)}, u32[]{:S(2)}, u32[]{:S(2)}) collective-permute-start(s32[16,4]{0,1:T(4,128)} %param.9), channel_id=1, source_target_pairs={{0,1},{2,3},{4,5},{6,7},{8,9},{10,11},{12,13},{14,15},{1,0},{3,2},... | collective-permute-start | bytes 776 | tf_op jit(solution)/shard_map/ppermute | solution.py:467
  0.8 5.1 %outer.1 = (f32[4,3,128,128]{3,2,1,0:T(8,128)}, f32[64,128]{1,0:T(8,128)}) custom-call(f32[24,4,128,128]{3,2,1,0:T(8,128)} %cells_hbm.3), custom_call_target="tpu_custom_call" | custom-call | flops 52428800 | bytes 1835008 | tf_op jit(solution)/shard_map/outer/pallas_call | solution.py:158
  5.9 3.0 %collective-permute-start = (f32[4,3,128,128]{3,2,1,0:T(8,128)}, f32[4,3,128,128]{3,2,1,0:T(8,128)}, u32[]{:S(2)}, u32[]{:S(2)}) collective-permute-start(f32[4,3,128,128]{3,2,1,0:T(8,128)} %get-tuple-element.15), channel_id=1, source_target_pairs={{1,2},{3,4},{5,6},{7,8},{9,10},{11,12},{13,14},{2,1},{4,3},{6,5},{... | collective-permute-start | bytes 2359304 | tf_op jit(solution)/shard_map/ppermute | solution.py:467
  9.0 0.0 copy-done.7
  9.0 0.1 copy.15
  9.1 0.1 reshape.513
  9.2 0.0 copy-done.8
  9.2 0.0 copy-done.9
  9.2 0.0 copy-done.10
  9.2 0.0 copy-done.11
  9.3 0.1 concatenate.65
  9.4 0.0 collective-permute-done.1
  9.4 0.1 copy.17
  9.5 0.1 concatenate.66
  9.6 0.1 fusion.11
  9.6 0.8 %select_maximum_fusion = f32[72,128]{1,0:T(8,128)S(1)} fusion(f32[1,128]{1,0:T(1,128)S(1)} %fusion.11, f32[64,128]{1,0:T(8,128)} %get-tuple-element.16), kind=kLoop, calls=%fused_computation.2 | loop fusion | flops 27648 | bytes 70144 | tf_op jit(solution)/shard_map/concatenate | solution.py:494
  10.4 2.5 %collective-permute-start.2 = (f32[72,128]{1,0:T(8,128)S(1)}, f32[72,128]{1,0:T(8,128)S(1)}, u32[]{:S(2)}, u32[]{:S(2)}) collective-permute-start(f32[72,128]{1,0:T(8,128)S(1)} %select_maximum_fusion), channel_id=1, source_target_pairs={{1,2},{3,4},{5,6},{7,8},{9,10},{11,12},{13,14},{2,1},{4,3},{6,5},{... | collective-permute-start | bytes 110600 | tf_op jit(solution)/shard_map/ppermute | solution.py:467
  13.0 0.0 copy-done.5
  13.0 0.0 copy-start
  13.0 2.8 %copy-done = f32[24,4,128,128]{3,2,1,0:T(8,128)S(1)} copy-done((f32[24,4,128,128]{3,2,1,0:T(8,128)S(1)}, f32[24,4,128,128]{3,2,1,0:T(8,128)}, u32[]{:S(2)}) %copy-start) | copy-done | bytes 6291480
  15.8 0.0 copy-start.6
  15.8 18.5 %home.1 = (f32[1936,128]{1,0:T(8,128)}, f32[16,3,128,128]{3,2,1,0:T(8,128)S(1)}) custom-call(s32[1,2]{1,0:T(1,128)S(1)} %copy-done.5, f32[24,4,128,128]{3,2,1,0:T(8,128)S(1)} %copy-done), custom_call_target="tpu_custom_call" | custom-call | flops 262144000 | bytes 9175040 | tf_op jit(solution)/shard_map/home/pallas_call | solution.py:222
  34.3 0.0 copy-start.1
  34.3 0.0 collective-permute-done.2
  34.3 0.7 %constant_dynamic-update-slice_fusion.mine = f32[1936,128]{1,0:T(8,128)} fusion(f32[1936,128]{1,0:T(8,128)} %get-tuple-element.17, f32[72,128]{1,0:T(8,128)S(1)} %collective-permute-done.2), kind=kLoop, calls=%fused_computation.65 | loop fusion | bytes 73728 | tf_op jit(solution)/shard_map/dynamic_update_slice | solution.py:497
  35.0 0.9 %collective-permute-start.3 = (f32[1936,128]{1,0:T(8,128)}, f32[1936,128]{1,0:T(8,128)}, u32[]{:S(2)}, u32[]{:S(2)}) collective-permute-start(f32[1936,128]{1,0:T(8,128)} %constant_dynamic-update-slice_fusion.mine), channel_id=1, source_target_pairs={{0,1},{2,3},{4,5},{6,7},{8,9},{10,11},{12,13},{14,15},{1,0},{3,2},... | collective-permute-start | bytes 2973704 | tf_op jit(solution)/shard_map/ppermute | solution.py:467
  35.9 0.1 fusion.20
  36.0 0.1 compare_and_fusion
  36.1 0.1 select_reduce_fusion
  36.3 0.1 select_reduce_fusion.2
  36.4 0.6 %reshape.514.rows_ref = s32[24]{0:T(128)} reshape(s32[3,8]{1,0:T(4,128)S(1)} %select_reduce_fusion.2) | data formatting | bytes 192 | tf_op jit(solution)/shard_map/reshape | solution.py:510
  37.0 1.5 %collective-permute-done.3.theirs = f32[1936,128]{1,0:T(8,128)} collective-permute-done((f32[1936,128]{1,0:T(8,128)}, f32[1936,128]{1,0:T(8,128)}, u32[]{:S(2)}, u32[]{:S(2)}) %collective-permute-start.3) | collective-permute-done | bytes 991264 | tf_op jit(solution)/shard_map/ppermute | solution.py:467
  38.5 2.3 %answers.1 = (f32[512,128]{1,0:T(8,128)}, f32[96,128]{1,0:T(8,128)}) custom-call(s32[1,2]{1,0:T(1,128)} %range_ref.7, s32[24]{0:T(128)} %reshape.514.rows_ref, f32[1936,128]{1,0:T(8,128)} %constant_dynamic-update-slice_fusion.mine, f32[1936,128]{1,0:T(8,128)} %collective-permute-done.3.theirs), custom_call_target="tpu_custom_call" | custom-call | tf_op jit(solution)/shard_map/answers/pallas_call | solution.py:286
  40.8 3.5 %collective-permute-start.4 = (f32[96,128]{1,0:T(8,128)}, f32[96,128]{1,0:T(8,128)S(1)}, u32[]{:S(2)}, u32[]{:S(2)}) collective-permute-start(f32[96,128]{1,0:T(8,128)} %get-tuple-element.19), channel_id=1, source_target_pairs={{1,2},{3,4},{5,6},{7,8},{9,10},{11,12},{13,14},{2,1},{4,3},{6,5},{... | collective-permute-start | bytes 147464 | tf_op jit(solution)/shard_map/ppermute | solution.py:467
  44.3 0.1 fusion.10
  44.4 2.0 %collective-permute-done.4.crossed = f32[96,128]{1,0:T(8,128)S(1)} collective-permute-done((f32[96,128]{1,0:T(8,128)}, f32[96,128]{1,0:T(8,128)S(1)}, u32[]{:S(2)}, u32[]{:S(2)}) %collective-permute-start.4) | collective-permute-done | bytes 49184 | tf_op jit(solution)/shard_map/ppermute | solution.py:467
  46.4 1.3 %collective-permute-start.5 = (f32[96,128]{1,0:T(8,128)S(1)}, f32[96,128]{1,0:T(8,128)S(1)}, u32[]{:S(2)}, u32[]{:S(2)}) collective-permute-start(f32[96,128]{1,0:T(8,128)S(1)} %collective-permute-done.4.crossed), channel_id=1, source_target_pairs={{0,1},{2,3},{4,5},{6,7},{8,9},{10,11},{12,13},{14,15},{1,0},{3,2},... | collective-permute-start | bytes 147464 | tf_op jit(solution)/shard_map/ppermute | solution.py:467
  47.7 0.9 %collective-permute-done.5.passed = f32[96,128]{1,0:T(8,128)S(1)} collective-permute-done((f32[96,128]{1,0:T(8,128)S(1)}, f32[96,128]{1,0:T(8,128)S(1)}, u32[]{:S(2)}, u32[]{:S(2)}) %collective-permute-start.5) | collective-permute-done | bytes 49184 | tf_op jit(solution)/shard_map/ppermute | solution.py:467
  48.6 0.0 copy-done.6
  48.6 0.0 copy-start.2
  48.6 0.9 %copy-done.2 = f32[512,128]{1,0:T(8,128)S(1)} copy-done((f32[512,128]{1,0:T(8,128)S(1)}, f32[512,128]{1,0:T(8,128)}, u32[]{:S(2)}) %copy-start.2) | copy-done | bytes 262168
  49.5 3.8 %most.1 = (f32[16,3,128,128]{3,2,1,0:T(8,128)}, f32[128,128]{1,0:T(8,128)S(1)}, f32[128,128]{1,0:T(8,128)S(1)}) custom-call(s32[1,2]{1,0:T(1,128)S(1)} %copy-done.6, s32[64]{0:T(128)S(1)} %compare_select_fusion.7.rows_ref, f32[512,128]{1,0:T(8,128)S(1)} %copy-done.2, f32[96,128]{1,0:T(8,128)S(1)} %collective-permute-done.4.crossed, ...), custom_call_target="tpu_custom_call" | custom-call | tf_op jit(solution)/shard_map/most/pallas_call | solution.py:398
  53.3 0.0 copy-done.1
  53.3 0.0 copy-start.3
  53.3 0.6 %copy-done.3 = f32[128,128]{1,0:T(8,128)} copy-done((f32[128,128]{1,0:T(8,128)}, f32[128,128]{1,0:T(8,128)S(1)}, u32[]{:S(2)}) %copy-start.3) | copy-done | bytes 65560
  53.9 0.0 copy-start.4
  53.9 0.6 %copy-done.4 = f32[128,128]{1,0:T(8,128)} copy-done((f32[128,128]{1,0:T(8,128)}, f32[128,128]{1,0:T(8,128)S(1)}, u32[]{:S(2)}) %copy-start.4) | copy-done | bytes 65560
  54.5 0.0 collective-permute-done.arrived
  54.5 3.4 %rest.1 = f32[16,3,128,128]{3,2,1,0:T(8,128)} custom-call(s32[1,2]{1,0:T(1,128)} %range_ref.7, f32[16,3,128,128]{3,2,1,0:T(8,128)} %copy-done.1, f32[4,3,128,128]{3,2,1,0:T(8,128)} %collective-permute-done.arrived, f32[128,128]{1,0:T(8,128)} %copy-done.3, f32[128,128]{1,0:T(8,128)} %copy-done.4, ...), custom_call_target="tpu_custom_call", output_to_operand_aliasing={{}: (5, {})} | custom-call | tf_op jit(solution)/shard_map/rest/pallas_call | solution.py:451
  (10 shorter events, 0.1 us)
Async XLA Ops:
  0.0 9.2 %copy-start.8 = (s32[3,2]{0,1:T(2,128)S(1)}, s32[3,2]{0,1:T(2,128)}, u32[]{:S(2)}) copy-start(s32[3,2]{0,1:T(2,128)} %constant.150.clone) | copy-start | bytes 76
  0.0 9.2 %copy-start.9 = (s32[3,2]{0,1:T(2,128)S(1)}, s32[3,2]{0,1:T(2,128)}, u32[]{:S(2)}) copy-start(s32[3,2]{0,1:T(2,128)} %constant.149.clone) | copy-start | bytes 76
  0.0 9.2 %copy-start.10 = (s32[3]{0:T(128)S(1)}, s32[3]{0:T(128)}, u32[]{:S(2)}) copy-start(s32[3]{0:T(128)} %constant.148.clone) | copy-start | bytes 40
  0.0 9.2 %copy-start.11 = (s32[3]{0:T(128)S(1)}, s32[3]{0:T(128)}, u32[]{:S(2)}) copy-start(s32[3]{0:T(128)} %constant.147.clone) | copy-start | bytes 40
  0.0 9.0 %copy-start.7 = (s32[16,4]{0,1:T(4,128)S(1)}, s32[16,4]{0,1:T(4,128)}, u32[]{:S(2)}) copy-start(s32[16,4]{0,1:T(4,128)} %param.9) | copy-start | bytes 772
  0.0 12.9 %copy-start.5 = (s32[1,2]{1,0:T(1,128)S(1)}, s32[1,2]{1,0:T(1,128)}, u32[]{:S(2)}) copy-start(s32[1,2]{1,0:T(1,128)} %range_ref.7) | copy-start | bytes 28
  0.0 9.3 %collective-permute-start.1 = (s32[16,4]{0,1:T(4,128)}, s32[16,4]{0,1:T(4,128)S(1)}, u32[]{:S(2)}, u32[]{:S(2)}) collective-permute-start(s32[16,4]{0,1:T(4,128)} %param.9), channel_id=1, source_target_pairs={{0,1},{2,3},{4,5},{6,7},{8,9},{10,11},{12,13},{14,15},{1,0},{3,2},... | collective-permute-start | bytes 776 | tf_op jit(solution)/shard_map/ppermute | solution.py:467
  5.9 48.6 %collective-permute-start = (f32[4,3,128,128]{3,2,1,0:T(8,128)}, f32[4,3,128,128]{3,2,1,0:T(8,128)}, u32[]{:S(2)}, u32[]{:S(2)}) collective-permute-start(f32[4,3,128,128]{3,2,1,0:T(8,128)} %get-tuple-element.15), channel_id=1, source_target_pairs={{1,2},{3,4},{5,6},{7,8},{9,10},{11,12},{13,14},{2,1},{4,3},{6,5},{... | collective-permute-start | bytes 2359304 | tf_op jit(solution)/shard_map/ppermute | solution.py:467
  10.4 23.9 %collective-permute-start.2 = (f32[72,128]{1,0:T(8,128)S(1)}, f32[72,128]{1,0:T(8,128)S(1)}, u32[]{:S(2)}, u32[]{:S(2)}) collective-permute-start(f32[72,128]{1,0:T(8,128)S(1)} %select_maximum_fusion), channel_id=1, source_target_pairs={{1,2},{3,4},{5,6},{7,8},{9,10},{11,12},{13,14},{2,1},{4,3},{6,5},{... | collective-permute-start | bytes 110600 | tf_op jit(solution)/shard_map/ppermute | solution.py:467
  13.0 2.8 %copy-start = (f32[24,4,128,128]{3,2,1,0:T(8,128)S(1)}, f32[24,4,128,128]{3,2,1,0:T(8,128)}, u32[]{:S(2)}) copy-start(f32[24,4,128,128]{3,2,1,0:T(8,128)} %cells_hbm.3) | copy-start | bytes 18874372
  15.8 32.8 %copy-start.6 = (s32[1,2]{1,0:T(1,128)S(1)}, s32[1,2]{1,0:T(1,128)}, u32[]{:S(2)}) copy-start(s32[1,2]{1,0:T(1,128)} %range_ref.7) | copy-start | bytes 28
  34.3 19.0 %copy-start.1 = (f32[16,3,128,128]{3,2,1,0:T(8,128)}, f32[16,3,128,128]{3,2,1,0:T(8,128)S(1)}, u32[]{:S(2)}) copy-start(f32[16,3,128,128]{3,2,1,0:T(8,128)S(1)} %get-tuple-element.14.own) | copy-start | bytes 9437188
  35.0 3.5 %collective-permute-start.3 = (f32[1936,128]{1,0:T(8,128)}, f32[1936,128]{1,0:T(8,128)}, u32[]{:S(2)}, u32[]{:S(2)}) collective-permute-start(f32[1936,128]{1,0:T(8,128)} %constant_dynamic-update-slice_fusion.mine), channel_id=1, source_target_pairs={{0,1},{2,3},{4,5},{6,7},{8,9},{10,11},{12,13},{14,15},{1,0},{3,2},... | collective-permute-start | bytes 2973704 | tf_op jit(solution)/shard_map/ppermute | solution.py:467
  40.8 5.6 %collective-permute-start.4 = (f32[96,128]{1,0:T(8,128)}, f32[96,128]{1,0:T(8,128)S(1)}, u32[]{:S(2)}, u32[]{:S(2)}) collective-permute-start(f32[96,128]{1,0:T(8,128)} %get-tuple-element.19), channel_id=1, source_target_pairs={{1,2},{3,4},{5,6},{7,8},{9,10},{11,12},{13,14},{2,1},{4,3},{6,5},{... | collective-permute-start | bytes 147464 | tf_op jit(solution)/shard_map/ppermute | solution.py:467
  46.4 2.2 %collective-permute-start.5 = (f32[96,128]{1,0:T(8,128)S(1)}, f32[96,128]{1,0:T(8,128)S(1)}, u32[]{:S(2)}, u32[]{:S(2)}) collective-permute-start(f32[96,128]{1,0:T(8,128)S(1)} %collective-permute-done.4.crossed), channel_id=1, source_target_pairs={{0,1},{2,3},{4,5},{6,7},{8,9},{10,11},{12,13},{14,15},{1,0},{3,2},... | collective-permute-start | bytes 147464 | tf_op jit(solution)/shard_map/ppermute | solution.py:467
  48.6 1.0 %copy-start.2 = (f32[512,128]{1,0:T(8,128)S(1)}, f32[512,128]{1,0:T(8,128)}, u32[]{:S(2)}) copy-start(f32[512,128]{1,0:T(8,128)} %get-tuple-element.18.edges) | copy-start | bytes 786436
  53.3 0.6 %copy-start.3 = (f32[128,128]{1,0:T(8,128)}, f32[128,128]{1,0:T(8,128)S(1)}, u32[]{:S(2)}) copy-start(f32[128,128]{1,0:T(8,128)S(1)} %get-tuple-element.20.columns) | copy-start | bytes 196612
  53.9 0.6 %copy-start.4 = (f32[128,128]{1,0:T(8,128)}, f32[128,128]{1,0:T(8,128)S(1)}, u32[]{:S(2)}) copy-start(f32[128,128]{1,0:T(8,128)S(1)} %get-tuple-element.21.lines) | copy-start | bytes 196612

commit v3 on v2

--- a/solution.py
+++ b/solution.py
@@ -26,32 +26,21 @@
     return lax.broadcasted_iota(jnp.int32, (ROWS, side), axis)
 
 
+def spread(j, side):
+    return pl.ds(j, ROWS, stride=side // ROWS)
+
+
 def inner_update(load, store, columns, at, side):
     lane, line = iota(1, side), iota(0, side)
     pair = lane // 2
     west, east = lane == 0, lane == side - 1
     first, last = line == 0, line == ROWS - 1
-    strips = side // ROWS
+    steps = side // ROWS
     ahead = lambda a: pltpu.roll(a, side - 1, 1)
     behind = lambda a: pltpu.roll(a, 1, 1)
-    below = None
-    pending = None
-
-    def finish(k, held, ups):
-        h, part_h, part_x, part_y, lows, bed_low, up_own = held
-        north = [jnp.where(last, u, o) for u, o in zip(ups, up_own)]
-        part_y = part_y + h * (north[3] - bed_low)
-        store(0, k, h - HALF * (part_h + (north[0] - lows[0])))
-        mx, my = load(1, k), load(2, k)
-        store(1, k, mx - HALF * (part_x + (north[1] - lows[1])))
-        store(2, k, my - HALF * (part_y + (north[2] - lows[2])))
-
-    for k in range(strips):
-        h, mx, my, bed = (load(f, k) for f in range(4))
-        held = columns[ROWS * k : ROWS * (k + 1), :]
-        for f, value in enumerate((h, mx, my, bed)):
-            held = jnp.where(pair == at // 2 + f, pltpu.roll(value, at + 2 * f + 1, 1), held)
-        columns[ROWS * k : ROWS * (k + 1), :] = held
+    marks = [pair == at // 2 + f for f in range(4)]
+
+    def cell(h, mx, my, bed):
         root = lax.rsqrt(h)
         celerity = h * root
         inverse = root * root
@@ -59,11 +48,50 @@
         v = my * inverse
         half_sq = 0.5 * h * h
         cross = my * u
-        fx = mx * u + half_sq
-        fy = my * v + half_sq
+        rate_y = jnp.abs(v) + celerity
         rate_x = jnp.abs(u) + celerity
-        rate_y = jnp.abs(v) + celerity
-        eta = h + bed
+        return (rate_y, h + bed, mx, my, cross, my * v + half_sq, bed), rate_x, mx * u + half_sq
+
+    def face_y(low, high):
+        top = jnp.maximum(low[0], high[0])
+        return [
+            (high[3] + low[3]) - top * (high[1] - low[1]),
+            (high[4] + low[4]) - top * (high[2] - low[2]),
+            (high[5] + low[5]) - top * (high[3] - low[3]),
+        ]
+
+    def fields(j):
+        return [load(f, j) for f in range(4)]
+
+    def finish(held, north, bed_north):
+        h, mx, my, part_h, part_x, part_y, south, bed_south = held
+        return (
+            h - HALF * (part_h + (north[0] - south[0])),
+            mx - HALF * (part_x + (north[1] - south[1])),
+            my - HALF * (part_y + (north[2] - south[2]) + h * (bed_north - bed_south)),
+        )
+
+    top_fields = fields(steps - 1)
+    loaded = [fields(0), fields(1)]
+    low = [pltpu.roll(each, 1, 0) for each in cell(*top_fields)[0]]
+    pending, ready = None, []
+
+    moved_of = {}
+    for j in range(steps):
+        if j + 2 < steps:
+            loaded.append(top_fields if j + 2 == steps - 1 else fields(j + 2))
+        h, mx, my, bed = loaded[j]
+        while ready and ready[0][0] <= j - 3:
+            at_j, values = ready.pop(0)
+            for f in range(3):
+                store(f, at_j, values[f])
+            columns.store(at_j, moved_of.pop(at_j))
+        held = columns.load(j)
+        for f, value in enumerate((h, mx, my, bed)):
+            held = jnp.where(marks[f], pltpu.roll(value, at + 2 * f + 1, 1), held)
+        moved_of[j] = held
+        high, rate_x, fx = cell(h, mx, my, bed)
+        cross, eta = high[4], high[1]
         top = jnp.maximum(rate_x, ahead(rate_x))
         mx_e, my_e, bed_e = ahead(mx), ahead(my), ahead(bed)
         q = [
@@ -76,26 +104,32 @@
         part_h = q[0] - behind(q[0])
         part_x = q[1] - behind(q[1]) + h * slope
         part_y = q[2] - behind(q[2])
-        values = (rate_y, eta, mx, my, cross, fy, bed)
-        turned = [pltpu.roll(each, 1, 0) for each in values]
-        if below is None:
-            south = turned[:6] + [jnp.where(first, 0.0, turned[6])]
-        else:
-            south = [jnp.where(first, b, t) for b, t in zip(below, turned)]
-        below = turned
-        top = jnp.maximum(rate_y, south[0])
-        q = [
-            (my + south[3]) - top * (eta - south[1]),
-            (cross + south[4]) - top * (mx - south[2]),
-            (fy + south[5]) - top * (my - south[3]),
-        ]
-        if k == 0:
-            q = [jnp.where(first, 0.0, each) for each in q]
-        ups = [pltpu.roll(each, ROWS - 1, 0) for each in q + [bed]]
+        south = face_y(low, high)
+        bed_south = low[6]
+        if j == 0:
+            south = [jnp.where(first, 0.0, each) for each in south]
+            bed_south = jnp.where(first, 0.0, bed_south)
+            seam = [jnp.where(last, 0.0, pltpu.roll(each, ROWS - 1, 0)) for each in south + [bed]]
         if pending is not None:
-            finish(k - 1, pending, ups)
-        pending = (h, part_h, part_x, part_y, q, south[6], ups)
-    finish(strips - 1, pending, [0.0] * 4)
+            ready.append((j - 1, finish(pending, south, bed)))
+        pending = (h, mx, my, part_h, part_x, part_y, south, bed_south)
+        low = high
+    ready.append((steps - 1, finish(pending, seam[:3], seam[3])))
+    for at_j, values in ready:
+        for f in range(3):
+            store(f, at_j, values[f])
+        columns.store(at_j, moved_of.pop(at_j))
+
+
+class Columns:
+    def __init__(self, ref):
+        self.ref, self.side = ref, ref.shape[0]
+
+    def load(self, j):
+        return self.ref[spread(j, self.side), :]
+
+    def store(self, j, value):
+        self.ref[spread(j, self.side), :] = value
 
 
 def take_edges(count, cells, slot_of, columns, edges, base):
@@ -111,9 +145,9 @@
 
 def update_one(cells, i, columns, lane_at, side, put):
     inner_update(
-        lambda f, k: cells[i, f, ROWS * k : ROWS * (k + 1), :],
-        lambda f, k, value: put(f, ROWS * k, value),
-        columns,
+        lambda f, j: cells[i, f, spread(j, side), :],
+        lambda f, j, value: put(f, ROWS * j, value),
+        Columns(columns),
         lane_at,
         side,
     )
@@ -151,6 +185,10 @@
         bytes_accessed=patches * side * side * 28,
         transcendentals=patches * side * side,
     )
+
+
+def room(mebibytes):
+    return pltpu.CompilerParams(vmem_limit_bytes=mebibytes << 20)
 
 
 def outer_patches(old_cells, margin):
@@ -169,6 +207,7 @@
             pltpu.SemaphoreType.DMA((margin,)),
         ],
         cost_estimate=cost(margin, side),
+        compiler_params=room(48),
         name="outer",
     )(old_cells)
 
@@ -233,7 +272,7 @@
             pltpu.SemaphoreType.DMA((margin + per_device,)),
         ],
         cost_estimate=cost(margin + per_device, side),
-        compiler_params=pltpu.CompilerParams(vmem_limit_bytes=24 << 20),
+        compiler_params=room(48),
         name="home",
     )(old_range, old_cells)
 
@@ -277,8 +316,11 @@
             crossed = theirs[brought + 16 * m + 8 * half : brought + 16 * m + 8 * half + 8, :]
             at = pl.multiple_of(to + 8 * half, 8)
             edges[pl.ds(at, 8), :] = jnp.where(taken, crossed, edges[pl.ds(at, 8), :])
-    for n in range(3 * CAP):
-        message[pl.ds(8 * (n // 2) + n % 2, 4, stride=2), :] = edges[pl.ds(rows_ref[n], 4, stride=2), :]
+    for k in range(3):
+        asked = range(k * CAP, (k + 1) * CAP)
+        values = [edges[pl.ds(rows_ref[n], 4, stride=2), :] for n in asked]
+        for n, value in zip(asked, values):
+            message[pl.ds(8 * (n // 2) + n % 2, 4, stride=2), :] = value
 
 
 def answers(old_range, rows, mine, theirs, margin, per_device):
@@ -291,6 +333,7 @@
             jax.ShapeDtypeStruct((32 * per_device, side), jnp.float32),
             jax.ShapeDtypeStruct((12 * CAP, side), jnp.float32),
         ],
+        compiler_params=room(4),
         name="answers",
     )(old_range, rows, mine, theirs)
 
@@ -301,16 +344,21 @@
     rim = (lane == 0) | (lane == side - 1)
     south = [lines[pl.ds(8 * p + 2 * f + 1, 1), :] for f in range(3)]
     north = [lines[pl.ds(8 * p + 2 * f, 1), :] for f in range(3)]
-    strips = side // ROWS
-    for k in range(strips):
-        held = columns[ROWS * k : ROWS * (k + 1), :]
-        for f in range(3):
-            value = load(f, k) + jnp.where(rim, pltpu.roll(held, side - 1 - 8 * p - 2 * f, 1), 0.0)
-            if k == 0:
-                value = value + jnp.where(line == 0, south[f], 0.0)
-            if k == strips - 1:
-                value = value + jnp.where(line == ROWS - 1, north[f], 0.0)
-            store(f, k, value)
+    steps = side // ROWS
+    group = 4
+    for start in range(0, steps, group):
+        done = []
+        for j in range(start, start + group):
+            held = columns[spread(j, side), :]
+            for f in range(3):
+                value = load(f, j) + jnp.where(rim, pltpu.roll(held, side - 1 - 8 * p - 2 * f, 1), 0.0)
+                if j == 0:
+                    value = value + jnp.where(line == 0, south[f], 0.0)
+                if j == steps - 1:
+                    value = value + jnp.where(line == ROWS - 1, north[f], 0.0)
+                done.append((f, j, value))
+        for f, j, value in done:
+            store(f, j, value)
 
 
 def rim_terms(rows_ref, edges, crossed, passed, columns, lines, source, ghost, turn, count, odd):
@@ -320,13 +368,18 @@
     source[total : total + step, :] = crossed[...]
     source[total + step : total + 2 * step, :] = passed[...]
     field = lax.broadcasted_iota(jnp.int32, (4, edges.shape[1]), 0)
-    for p in range(count):
-        for s in range(4):
-            row = rows_ref[4 * p + s]
-            wall = row < 0
-            value = source[pl.ds(jnp.where(wall, -1 - row, row), 4, stride=2), :]
-            value = jnp.where((field == 1 + s // 2) & wall, -value, value)
-            ghost[pl.ds(16 * p + 8 * (s // 2) + 1 - s % 2, 4, stride=2), :] = value
+    group = 4
+    for start in range(0, count, group):
+        fetched = []
+        for p in range(start, start + group):
+            for s in range(4):
+                row = rows_ref[4 * p + s]
+                wall = row < 0
+                value = source[pl.ds(jnp.where(wall, -1 - row, row), 4, stride=2), :]
+                value = jnp.where((field == 1 + s // 2) & wall, -value, value)
+                fetched.append((16 * p + 8 * (s // 2) + 1 - s % 2, value))
+        for target, value in fetched:
+            ghost[pl.ds(target, 4, stride=2), :] = value
     turn[...] = jnp.zeros_like(turn)
     lines[...] = jnp.zeros_like(lines)
     for s in range(4):
@@ -383,7 +436,7 @@
             return jnp.where(taken, theirs[pl.ds(at, ROWS), :], own[p, f, ROWS * k : ROWS * (k + 1), :])
 
         def store(f, k, value):
-            result[i, f, ROWS * k : ROWS * (k + 1), :] = value
+            result[i, f, spread(k, side), :] = value
 
         add_rim(p, load, store, columns, lines)
         copy(i).start()
@@ -411,7 +464,7 @@
             pltpu.VMEM((side, side), jnp.float32),
             pltpu.SemaphoreType.DMA((many,)),
         ],
-        compiler_params=pltpu.CompilerParams(vmem_limit_bytes=24 << 20),
+        compiler_params=room(6),
         name="most",
     )(old_range, rows, edges, crossed, passed, own, theirs)
 
@@ -437,7 +490,7 @@
             return jnp.where(taken, arrived[i, f, at, :], own[p, f, at, :])
 
         def store(f, k, value):
-            result[i, f, ROWS * k : ROWS * (k + 1), :] = value
+            result[i, f, spread(k, side), :] = value
 
         add_rim(p, load, store, columns, lines)
         copy(i).start()
@@ -458,6 +511,7 @@
             pltpu.SemaphoreType.DMA((margin,)),
         ],
         input_output_aliases={5: 0},
+        compiler_params=room(4),
         name="rest",
     )(old_range, own, arrived, columns, lines, filled)
 

time: 58.6 us -> 51.3 us (0.88)
  local copies, waits for them, and re-layouts: 6.71 us -> 1.16 us
  Pallas kernels: 33.1 us -> 31 us
  waiting for transfers between devices: 4.38 us -> 5.71 us
  other arithmetic: 1.45 us -> 0.69 us
    unnamed x25 -> x13, local copies, waits for them, and re-layouts: 5.08 us -> 0.11 us
    ppermute x6, waiting for transfers between devices: 4.38 us -> 5.71 us  [swapped(): return lax.ppermute(value, AXES, pairs + [(j, i) for i, j in pairs])]
    pallas_call x1, Pallas kernels: 3.36 us -> 2.47 us  [rest(): pl.pallas_call(functools.partial(rest_kernel, margin), in_specs=[SMEM] +...]
    concatenate x1, other arithmetic: 0.77 us -> 0.01 us  [local(): came = swapped(jnp.concatenate([leaving_edges, tables], axis=0), 1)]
    pallas_call x1, Pallas kernels: 2.33 us -> 1.62 us  [answers(): pl.pallas_call(functools.partial(answer_kernel, margin, per_device), in_s...]
  transfers between devices with their start and end apart: 6 -> 6, of which waited for: 3 -> 3; matrix products, arithmetic and copies ran while one was open for 5% -> 4% of each run, Pallas kernels for 51% -> 56%
where the time goes in v3:
time: 51.3 us; the launch traced here: 51 us
  Pallas kernels  31 us (60%)
  starting transfers between devices  12.2 us (24%)
  waiting for transfers between devices  5.71 us (11%)
  local copies, waits for them, and re-layouts  1.16 us (2%)
  other arithmetic  0.69 us (1%)
    pallas_call x1, Pallas kernels, home_patches(): pl.pallas_call(functools.partial(home_kernel, margin), in_specs=[SMEM, HB...  18 us
    ppermute x6, starting transfers between devices, swapped(): return lax.ppermute(value, AXES, pairs + [(j, i) for i, j in pairs])  12.2 us
    ppermute x6, waiting for transfers between devices, swapped(): return lax.ppermute(value, AXES, pairs + [(j, i) for i, j in pairs])  5.71 us
    pallas_call x1, Pallas kernels, outer_patches(): pl.pallas_call(functools.partial(outer_kernel, margin), in_specs=[HBM], o...  4.89 us
    pallas_call x1, Pallas kernels, most(): pl.pallas_call(functools.partial(most_kernel, margin), in_specs=[SMEM, SM...  4 us
    pallas_call x1, Pallas kernels, rest(): pl.pallas_call(functools.partial(rest_kernel, margin), in_specs=[SMEM] +...  2.47 us
    pallas_call x1, Pallas kernels, answers(): pl.pallas_call(functools.partial(answer_kernel, margin, per_device), in_s...  1.62 us
  transfers between devices with their start and end apart: 6, of which 3 were waited for; matrix products, arithmetic and copies ran while one was open for 4% of the time, Pallas kernels for 56%

profile of v3, /device:TPU:17, one launch (start us, length us, event | category | flops | bytes accessed | tf_op | source)
XLA Modules:
  0.0 51.0 jit_solution(769764340106380043)
XLA Ops:
  0.0 0.0 copy-start.2
  0.0 0.0 copy-start.3
  0.0 0.0 copy-start.4
  0.0 0.0 copy-start.5
  0.0 0.0 copy-start.1
  0.0 0.0 copy-start
  0.0 0.7 %collective-permute-start.1 = (s32[16,4]{0,1:T(4,128)}, s32[16,4]{0,1:T(4,128)S(1)}, u32[]{:S(2)}, u32[]{:S(2)}) collective-permute-start(s32[16,4]{0,1:T(4,128)} %param.9), channel_id=1, source_target_pairs={{0,1},{2,3},{4,5},{6,7},{8,9},{10,11},{12,13},{14,15},{1,0},{3,2},... | collective-permute-start | bytes 776 | tf_op jit(solution)/shard_map/ppermute | solution.py:521
  0.8 4.9 %outer.1 = (f32[4,3,128,128]{3,2,1,0:T(8,128)}, f32[64,128]{1,0:T(8,128)S(1)}) custom-call(f32[24,4,128,128]{3,2,1,0:T(8,128)} %cells_hbm.3), custom_call_target="tpu_custom_call" | custom-call | flops 52428800 | bytes 1835008 | tf_op jit(solution)/shard_map/outer/pallas_call | solution.py:196
  5.7 3.0 %collective-permute-start = (f32[4,3,128,128]{3,2,1,0:T(8,128)}, f32[4,3,128,128]{3,2,1,0:T(8,128)}, u32[]{:S(2)}, u32[]{:S(2)}) collective-permute-start(f32[4,3,128,128]{3,2,1,0:T(8,128)} %get-tuple-element.15), channel_id=1, source_target_pairs={{1,2},{3,4},{5,6},{7,8},{9,10},{11,12},{13,14},{2,1},{4,3},{6,5},{... | collective-permute-start | bytes 2359304 | tf_op jit(solution)/shard_map/ppermute | solution.py:521
  8.7 0.0 copy-done.1
  8.7 0.1 copy.15
  8.8 0.1 reshape.513
  9.0 0.0 copy-done.2
  9.0 0.0 copy-done.3
  9.0 0.0 copy-done.4
  9.0 0.0 copy-done.5
  9.0 0.1 concatenate.65
  9.1 0.0 collective-permute-done.1
  9.1 0.1 copy.17
  9.2 0.1 concatenate.66
  9.3 0.1 fusion.11
  9.4 2.5 %collective-permute-start.2 = (f32[72,128]{1,0:T(8,128)S(1)}, f32[72,128]{1,0:T(8,128)S(1)}, u32[]{:S(2)}, u32[]{:S(2)}) collective-permute-start(f32[72,128]{1,0:T(8,128)S(1)} %select_maximum_fusion), channel_id=1, source_target_pairs={{1,2},{3,4},{5,6},{7,8},{9,10},{11,12},{13,14},{2,1},{4,3},{6,5},{... | collective-permute-start | bytes 110600 | tf_op jit(solution)/shard_map/ppermute | solution.py:521
  12.0 0.0 copy-done
  12.0 18.0 %home.1 = (f32[1936,128]{1,0:T(8,128)}, f32[16,3,128,128]{3,2,1,0:T(8,128)S(1)}) custom-call(s32[1,2]{1,0:T(1,128)S(1)} %copy-done, f32[24,4,128,128]{3,2,1,0:T(8,128)} %cells_hbm.3), custom_call_target="tpu_custom_call" | custom-call | flops 262144000 | bytes 9175040 | tf_op jit(solution)/shard_map/home/pallas_call | solution.py:261
  30.0 0.0 collective-permute-done.2
  30.0 0.6 %constant_dynamic-update-slice_fusion.mine = f32[1936,128]{1,0:T(8,128)} fusion(f32[1936,128]{1,0:T(8,128)} %get-tuple-element.17, f32[72,128]{1,0:T(8,128)S(1)} %collective-permute-done.2), kind=kLoop, calls=%fused_computation.65 | loop fusion | bytes 73728 | tf_op jit(solution)/shard_map/dynamic_update_slice | solution.py:551
  30.6 2.2 %collective-permute-start.3 = (f32[1936,128]{1,0:T(8,128)}, f32[1936,128]{1,0:T(8,128)}, u32[]{:S(2)}, u32[]{:S(2)}) collective-permute-start(f32[1936,128]{1,0:T(8,128)} %constant_dynamic-update-slice_fusion.mine), channel_id=1, source_target_pairs={{0,1},{2,3},{4,5},{6,7},{8,9},{10,11},{12,13},{14,15},{1,0},{3,2},... | collective-permute-start | bytes 2973704 | tf_op jit(solution)/shard_map/ppermute | solution.py:521
  32.8 0.1 fusion.20
  32.9 0.1 compare_and_fusion
  33.0 0.1 select_reduce_fusion
  33.1 0.1 select_reduce_fusion.2
  33.3 0.1 reshape.514.rows_ref
  33.4 2.0 %collective-permute-done.3.theirs = f32[1936,128]{1,0:T(8,128)} collective-permute-done((f32[1936,128]{1,0:T(8,128)}, f32[1936,128]{1,0:T(8,128)}, u32[]{:S(2)}, u32[]{:S(2)}) %collective-permute-start.3) | collective-permute-done | bytes 991264 | tf_op jit(solution)/shard_map/ppermute | solution.py:521
  35.4 1.6 %answers.1 = (f32[512,128]{1,0:T(8,128)S(1)}, f32[96,128]{1,0:T(8,128)S(1)}) custom-call(s32[1,2]{1,0:T(1,128)S(1)} %copy-done, s32[24]{0:T(128)S(1)} %reshape.514.rows_ref, f32[1936,128]{1,0:T(8,128)} %constant_dynamic-update-slice_fusion.mine, f32[1936,128]{1,0:T(8,128)} %collective-permute-done.3.theirs), custom_call_target="tpu_custom_call" | custom-call | tf_op jit(solution)/shard_map/answers/pallas_call | solution.py:328
  37.0 2.5 %collective-permute-start.4 = (f32[96,128]{1,0:T(8,128)S(1)}, f32[96,128]{1,0:T(8,128)S(1)}, u32[]{:S(2)}, u32[]{:S(2)}) collective-permute-start(f32[96,128]{1,0:T(8,128)S(1)} %get-tuple-element.19), channel_id=1, source_target_pairs={{1,2},{3,4},{5,6},{7,8},{9,10},{11,12},{13,14},{2,1},{4,3},{6,5},{... | collective-permute-start | bytes 147464 | tf_op jit(solution)/shard_map/ppermute | solution.py:521
  39.5 0.1 fusion.10
  39.6 2.8 %collective-permute-done.4.crossed = f32[96,128]{1,0:T(8,128)S(1)} collective-permute-done((f32[96,128]{1,0:T(8,128)S(1)}, f32[96,128]{1,0:T(8,128)S(1)}, u32[]{:S(2)}, u32[]{:S(2)}) %collective-permute-start.4) | collective-permute-done | bytes 49184 | tf_op jit(solution)/shard_map/ppermute | solution.py:521
  42.4 1.3 %collective-permute-start.5 = (f32[96,128]{1,0:T(8,128)S(1)}, f32[96,128]{1,0:T(8,128)S(1)}, u32[]{:S(2)}, u32[]{:S(2)}) collective-permute-start(f32[96,128]{1,0:T(8,128)S(1)} %collective-permute-done.4.crossed), channel_id=1, source_target_pairs={{0,1},{2,3},{4,5},{6,7},{8,9},{10,11},{12,13},{14,15},{1,0},{3,2},... | collective-permute-start | bytes 147464 | tf_op jit(solution)/shard_map/ppermute | solution.py:521
  43.7 0.9 %collective-permute-done.5.passed = f32[96,128]{1,0:T(8,128)S(1)} collective-permute-done((f32[96,128]{1,0:T(8,128)S(1)}, f32[96,128]{1,0:T(8,128)S(1)}, u32[]{:S(2)}, u32[]{:S(2)}) %collective-permute-start.5) | collective-permute-done | bytes 49184 | tf_op jit(solution)/shard_map/ppermute | solution.py:521
  44.6 4.0 %most.1 = (f32[16,3,128,128]{3,2,1,0:T(8,128)}, f32[128,128]{1,0:T(8,128)S(1)}, f32[128,128]{1,0:T(8,128)S(1)}) custom-call(s32[1,2]{1,0:T(1,128)S(1)} %copy-done, s32[64]{0:T(128)S(1)} %compare_select_fusion.7.rows_ref, f32[512,128]{1,0:T(8,128)S(1)} %get-tuple-element.18.edges, f32[96,128]{1,0:T(8,128)S(1)} %collective-permute-done.4.crossed, ...), custom_call_target="tpu_custom_call" | custom-call | tf_op jit(solution)/shard_map/most/pallas_call | solution.py:451
  48.6 0.0 collective-permute-done.arrived
  48.6 2.5 %rest.1 = f32[16,3,128,128]{3,2,1,0:T(8,128)} custom-call(s32[1,2]{1,0:T(1,128)S(1)} %copy-done, f32[16,3,128,128]{3,2,1,0:T(8,128)S(1)} %get-tuple-element.14.own, f32[4,3,128,128]{3,2,1,0:T(8,128)} %collective-permute-done.arrived, f32[128,128]{1,0:T(8,128)S(1)} %get-tuple-element.20.columns, ...), custom_call_target="tpu_custom_call", output_to_operand_aliasing={{}: (5, {})} | custom-call | tf_op jit(solution)/shard_map/rest/pallas_call | solution.py:504
  (11 shorter events, 0.1 us)
Async XLA Ops:
  0.0 9.0 %copy-start.2 = (s32[3,2]{0,1:T(2,128)S(1)}, s32[3,2]{0,1:T(2,128)}, u32[]{:S(2)}) copy-start(s32[3,2]{0,1:T(2,128)} %constant.150.clone) | copy-start | bytes 76
  0.0 9.0 %copy-start.3 = (s32[3,2]{0,1:T(2,128)S(1)}, s32[3,2]{0,1:T(2,128)}, u32[]{:S(2)}) copy-start(s32[3,2]{0,1:T(2,128)} %constant.149.clone) | copy-start | bytes 76
  0.0 9.0 %copy-start.4 = (s32[3]{0:T(128)S(1)}, s32[3]{0:T(128)}, u32[]{:S(2)}) copy-start(s32[3]{0:T(128)} %constant.148.clone) | copy-start | bytes 40
  0.0 9.0 %copy-start.5 = (s32[3]{0:T(128)S(1)}, s32[3]{0:T(128)}, u32[]{:S(2)}) copy-start(s32[3]{0:T(128)} %constant.147.clone) | copy-start | bytes 40
  0.0 8.7 %copy-start.1 = (s32[16,4]{0,1:T(4,128)S(1)}, s32[16,4]{0,1:T(4,128)}, u32[]{:S(2)}) copy-start(s32[16,4]{0,1:T(4,128)} %param.9) | copy-start | bytes 772
  0.0 11.9 %copy-start = (s32[1,2]{1,0:T(1,128)S(1)}, s32[1,2]{1,0:T(1,128)}, u32[]{:S(2)}) copy-start(s32[1,2]{1,0:T(1,128)} %range_ref.7) | copy-start | bytes 28
  0.0 9.1 %collective-permute-start.1 = (s32[16,4]{0,1:T(4,128)}, s32[16,4]{0,1:T(4,128)S(1)}, u32[]{:S(2)}, u32[]{:S(2)}) collective-permute-start(s32[16,4]{0,1:T(4,128)} %param.9), channel_id=1, source_target_pairs={{0,1},{2,3},{4,5},{6,7},{8,9},{10,11},{12,13},{14,15},{1,0},{3,2},... | collective-permute-start | bytes 776 | tf_op jit(solution)/shard_map/ppermute | solution.py:521
  5.7 42.9 %collective-permute-start = (f32[4,3,128,128]{3,2,1,0:T(8,128)}, f32[4,3,128,128]{3,2,1,0:T(8,128)}, u32[]{:S(2)}, u32[]{:S(2)}) collective-permute-start(f32[4,3,128,128]{3,2,1,0:T(8,128)} %get-tuple-element.15), channel_id=1, source_target_pairs={{1,2},{3,4},{5,6},{7,8},{9,10},{11,12},{13,14},{2,1},{4,3},{6,5},{... | collective-permute-start | bytes 2359304 | tf_op jit(solution)/shard_map/ppermute | solution.py:521
  9.4 20.6 %collective-permute-start.2 = (f32[72,128]{1,0:T(8,128)S(1)}, f32[72,128]{1,0:T(8,128)S(1)}, u32[]{:S(2)}, u32[]{:S(2)}) collective-permute-start(f32[72,128]{1,0:T(8,128)S(1)} %select_maximum_fusion), channel_id=1, source_target_pairs={{1,2},{3,4},{5,6},{7,8},{9,10},{11,12},{13,14},{2,1},{4,3},{6,5},{... | collective-permute-start | bytes 110600 | tf_op jit(solution)/shard_map/ppermute | solution.py:521
  30.6 4.7 %collective-permute-start.3 = (f32[1936,128]{1,0:T(8,128)}, f32[1936,128]{1,0:T(8,128)}, u32[]{:S(2)}, u32[]{:S(2)}) collective-permute-start(f32[1936,128]{1,0:T(8,128)} %constant_dynamic-update-slice_fusion.mine), channel_id=1, source_target_pairs={{0,1},{2,3},{4,5},{6,7},{8,9},{10,11},{12,13},{14,15},{1,0},{3,2},... | collective-permute-start | bytes 2973704 | tf_op jit(solution)/shard_map/ppermute | solution.py:521
  37.0 5.4 %collective-permute-start.4 = (f32[96,128]{1,0:T(8,128)S(1)}, f32[96,128]{1,0:T(8,128)S(1)}, u32[]{:S(2)}, u32[]{:S(2)}) collective-permute-start(f32[96,128]{1,0:T(8,128)S(1)} %get-tuple-element.19), channel_id=1, source_target_pairs={{1,2},{3,4},{5,6},{7,8},{9,10},{11,12},{13,14},{2,1},{4,3},{6,5},{... | collective-permute-start | bytes 147464 | tf_op jit(solution)/shard_map/ppermute | solution.py:521
  42.4 2.2 %collective-permute-start.5 = (f32[96,128]{1,0:T(8,128)S(1)}, f32[96,128]{1,0:T(8,128)S(1)}, u32[]{:S(2)}, u32[]{:S(2)}) collective-permute-start(f32[96,128]{1,0:T(8,128)S(1)} %collective-permute-done.4.crossed), channel_id=1, source_target_pairs={{0,1},{2,3},{4,5},{6,7},{8,9},{10,11},{12,13},{14,15},{1,0},{3,2},... | collective-permute-start | bytes 147464 | tf_op jit(solution)/shard_map/ppermute | solution.py:521

commit v4 on v3

--- a/solution.py
+++ b/solution.py
@@ -30,14 +30,46 @@
     return pl.ds(j, ROWS, stride=side // ROWS)
 
 
-def inner_update(load, store, columns, at, side):
+def pieces(x):
+    high = x.astype(jnp.bfloat16)
+    low = (x - high.astype(jnp.float32)).astype(jnp.bfloat16)
+    return jnp.concatenate([high, low], axis=1)
+
+
+def product(parts, weights):
+    return jnp.dot(parts, weights, preferred_element_type=jnp.float32)
+
+
+AHEAD, EAST, SUMS, SLOPE = slice(0, 2), slice(2, 4), slice(4, 5), slice(5, 6)
+
+
+def fill_weights(weights):
+    side = weights.shape[0] // 2
+    row = lax.broadcasted_iota(jnp.int32, (side, side), 0)
+    lane = lax.broadcasted_iota(jnp.int32, (side, side), 1)
+    one = lambda where: jnp.where(where, 1.0, 0.0)
+    after, here, before = one(row == lane + 1), one(row == lane), one(row == lane - 1)
+    inner_e, inner_w = lane != side - 1, lane != 0
+    east = jnp.where(inner_e, after + here, 0.0)
+    west = jnp.where(inner_w, here + before, 0.0)
+    blocks = (
+        after,
+        before,
+        jnp.where(inner_e, after - here, 0.0),
+        jnp.where(inner_w, here - before, 0.0),
+        east - west,
+        after - before,
+    )
+    for n, block in enumerate(blocks):
+        for half in range(2):
+            weights[half * side : (half + 1) * side, n * side : (n + 1) * side] = block.astype(jnp.bfloat16)
+
+
+def inner_update(load, store, columns, at, side, weights):
     lane, line = iota(1, side), iota(0, side)
     pair = lane // 2
-    west, east = lane == 0, lane == side - 1
     first, last = line == 0, line == ROWS - 1
     steps = side // ROWS
-    ahead = lambda a: pltpu.roll(a, side - 1, 1)
-    behind = lambda a: pltpu.roll(a, 1, 1)
     marks = [pair == at // 2 + f for f in range(4)]
 
     def cell(h, mx, my, bed):
@@ -50,7 +82,7 @@
         cross = my * u
         rate_y = jnp.abs(v) + celerity
         rate_x = jnp.abs(u) + celerity
-        return (rate_y, h + bed, mx, my, cross, my * v + half_sq, bed), rate_x, mx * u + half_sq
+        return (rate_y, h + bed, mx, my, cross, my * v + half_sq, bed), rate_x, mx * u + half_sq, h
 
     def face_y(low, high):
         top = jnp.maximum(low[0], high[0])
@@ -60,65 +92,46 @@
             (high[5] + low[5]) - top * (high[3] - low[3]),
         ]
 
-    def fields(j):
-        return [load(f, j) for f in range(4)]
-
-    def finish(held, north, bed_north):
-        h, mx, my, part_h, part_x, part_y, south, bed_south = held
-        return (
-            h - HALF * (part_h + (north[0] - south[0])),
-            mx - HALF * (part_x + (north[1] - south[1])),
-            my - HALF * (part_y + (north[2] - south[2]) + h * (bed_north - bed_south)),
-        )
-
-    top_fields = fields(steps - 1)
-    loaded = [fields(0), fields(1)]
-    low = [pltpu.roll(each, 1, 0) for each in cell(*top_fields)[0]]
-    pending, ready = None, []
-
-    moved_of = {}
+    def taken(block):
+        return weights[:, block.start * side : block.stop * side]
+
+    cells = [cell(*[load(f, j) for f in range(4)]) for j in range(steps)]
+    stack = lambda pick: jnp.concatenate([pick(c) for c in cells], axis=0)
+    rates = product(pieces(stack(lambda c: c[1])), taken(AHEAD))
+    eta, mx, my, cross, bed = (pieces(stack(lambda c, n=n: c[0][n])) for n in (1, 2, 3, 4, 6))
+    fx = pieces(stack(lambda c: c[2]))
+    jumps = [product(each, taken(EAST)) for each in (eta, mx, my)]
+    sums = [product(each, taken(SUMS)) for each in (mx, fx, cross)]
+    slopes = product(bed, taken(SLOPE))
+
     for j in range(steps):
-        if j + 2 < steps:
-            loaded.append(top_fields if j + 2 == steps - 1 else fields(j + 2))
-        h, mx, my, bed = loaded[j]
-        while ready and ready[0][0] <= j - 3:
-            at_j, values = ready.pop(0)
-            for f in range(3):
-                store(f, at_j, values[f])
-            columns.store(at_j, moved_of.pop(at_j))
         held = columns.load(j)
-        for f, value in enumerate((h, mx, my, bed)):
+        _, _, mx, my, _, _, bed = cells[j][0]
+        for f, value in enumerate((cells[j][3], mx, my, bed)):
             held = jnp.where(marks[f], pltpu.roll(value, at + 2 * f + 1, 1), held)
-        moved_of[j] = held
-        high, rate_x, fx = cell(h, mx, my, bed)
-        cross, eta = high[4], high[1]
-        top = jnp.maximum(rate_x, ahead(rate_x))
-        mx_e, my_e, bed_e = ahead(mx), ahead(my), ahead(bed)
-        q = [
-            (mx + mx_e) - top * (ahead(eta) - eta),
-            (fx + ahead(fx)) - top * (mx_e - mx),
-            (cross + ahead(cross)) - top * (my_e - my),
-        ]
-        q = [jnp.where(east, 0.0, each) for each in q]
-        slope = jnp.where(east, 0.0, bed_e) - jnp.where(west, 0.0, behind(bed))
-        part_h = q[0] - behind(q[0])
-        part_x = q[1] - behind(q[1]) + h * slope
-        part_y = q[2] - behind(q[2])
-        south = face_y(low, high)
-        bed_south = low[6]
-        if j == 0:
-            south = [jnp.where(first, 0.0, each) for each in south]
-            bed_south = jnp.where(first, 0.0, bed_south)
-            seam = [jnp.where(last, 0.0, pltpu.roll(each, ROWS - 1, 0)) for each in south + [bed]]
-        if pending is not None:
-            ready.append((j - 1, finish(pending, south, bed)))
-        pending = (h, mx, my, part_h, part_x, part_y, south, bed_south)
-        low = high
-    ready.append((steps - 1, finish(pending, seam[:3], seam[3])))
-    for at_j, values in ready:
-        for f in range(3):
-            store(f, at_j, values[f])
-        columns.store(at_j, moved_of.pop(at_j))
+        columns.store(j, held)
+
+    low = [pltpu.roll(each, 1, 0) for each in cells[steps - 1][0]]
+    faces = []
+    for j in range(steps):
+        faces.append(face_y(low, cells[j][0]))
+        low = cells[j][0]
+    faces[0] = [jnp.where(first, 0.0, each) for each in faces[0]]
+    beds = [c[0][6] for c in cells]
+    under = jnp.where(first, 0.0, pltpu.roll(beds[-1], 1, 0))
+    over = jnp.where(last, 0.0, pltpu.roll(beds[0], ROWS - 1, 0))
+    faces.append([jnp.where(last, 0.0, pltpu.roll(each, ROWS - 1, 0)) for each in faces[0]])
+    for j in range(steps):
+        (_, _, mx, my, _, _, _), rate, _, h = cells[j]
+        rows = slice(ROWS * j, ROWS * (j + 1))
+        top_e = jnp.maximum(rate, rates[rows, :side])
+        top_w = jnp.maximum(rate, rates[rows, side:])
+        x = [s[rows] - (top_e * d[rows, :side] - top_w * d[rows, side:]) for s, d in zip(sums, jumps)]
+        south, north = faces[j], faces[j + 1]
+        slope_y = (beds[j + 1] if j + 1 < steps else over) - (beds[j - 1] if j else under)
+        store(0, j, h - HALF * (x[0] + (north[0] - south[0])))
+        store(1, j, mx - HALF * (x[1] + h * slopes[rows] + (north[1] - south[1])))
+        store(2, j, my - HALF * (x[2] + h * slope_y + (north[2] - south[2])))
 
 
 class Columns:
@@ -143,29 +156,32 @@
             edges[row + 1 : row + 2, :] = cells[slot_of(p), f, 0:1, :]
 
 
-def update_one(cells, i, columns, lane_at, side, put):
+def update_one(cells, i, columns, lane_at, side, weights, put):
     inner_update(
         lambda f, j: cells[i, f, spread(j, side), :],
         lambda f, j, value: put(f, ROWS * j, value),
         Columns(columns),
         lane_at,
         side,
+        weights,
     )
 
 
-def fetch(cells_hbm, first, cells, sems, count):
+def fetch(cells_hbm, first, cells, sems, parts):
     def copy(i):
         return pltpu.make_async_copy(cells_hbm.at[first + i], cells.at[i], sems.at[i])
 
-    for i in range(count):
-        copy(i).start()
+    for start, count in parts:
+        for i in range(count):
+            copy(start + i).start()
     return copy
 
 
-def outer_kernel(margin, cells_hbm, out, edges, cells, columns, sems):
+def outer_kernel(margin, cells_hbm, out, edges, cells, columns, weights, sems):
     side = columns.shape[0]
     _, odd = position()
-    copy = fetch(cells_hbm, odd * (cells_hbm.shape[0] - margin), cells, sems, margin)
+    copy = fetch(cells_hbm, odd * (cells_hbm.shape[0] - margin), cells, sems, [(0, margin)])
+    fill_weights(weights)
 
     @pl.loop(0, margin)
     def _(i):
@@ -174,7 +190,7 @@
         def put(f, row, value):
             out[i, f, row : row + ROWS, :] = value
 
-        update_one(cells, i, columns, 8 * i, side, put)
+        update_one(cells, i, columns, 8 * i, side, weights, put)
 
     take_edges(margin, cells, lambda p: p, columns, edges, 0)
 
@@ -204,6 +220,7 @@
         scratch_shapes=[
             pltpu.VMEM((margin, 4, side, side), jnp.float32),
             pltpu.VMEM((side, side), jnp.float32),
+            pltpu.VMEM((2 * side, 6 * side), jnp.bfloat16),
             pltpu.SemaphoreType.DMA((margin,)),
         ],
         cost_estimate=cost(margin, side),
@@ -220,14 +237,16 @@
     return inner, home, limit, brought, brought + 16 * margin + 8
 
 
-def home_kernel(margin, range_ref, cells_hbm, shared, own, cells, columns, sems):
+def home_kernel(margin, range_ref, cells_hbm, shared, own, cells, columns, weights, sems):
     side = columns.shape[0]
     count = own.shape[0]
     inner, home, limit, _, _ = layout(margin, count, side)
     _, odd = position()
-    copy = fetch(cells_hbm, (1 - odd) * margin, cells, sems, margin + count)
     inner_at = (1 - odd) * count
     home_at = odd * margin
+    parts = [(inner_at, margin), (home_at, count)]
+    copy = fetch(cells_hbm, (1 - odd) * margin, cells, sems, parts)
+    fill_weights(weights)
 
     @pl.loop(0, margin)
     def _(i):
@@ -237,7 +256,7 @@
             at = pl.multiple_of(i * (3 * side) + (f * side + row), ROWS)
             shared[pl.ds(at, ROWS), :] = value
 
-        update_one(cells, inner_at + i, columns, 8 * i, side, put)
+        update_one(cells, inner_at + i, columns, 8 * i, side, weights, put)
 
     take_edges(margin, cells, lambda p: inner_at + p, columns, shared, inner)
 
@@ -248,7 +267,7 @@
         def put(f, row, value):
             own[i, f, row : row + ROWS, :] = value
 
-        update_one(cells, home_at + i, columns, 8 * i, side, put)
+        update_one(cells, home_at + i, columns, 8 * i, side, weights, put)
 
     take_edges(count, cells, lambda p: home_at + p, columns, shared, home)
     outer_limit = jnp.where(odd == 1, range_ref[0, 1], range_ref[0, 0])
@@ -269,6 +288,7 @@
         scratch_shapes=[
             pltpu.VMEM((margin + per_device, 4, side, side), jnp.float32),
             pltpu.VMEM((side, side), jnp.float32),
+            pltpu.VMEM((2 * side, 6 * side), jnp.bfloat16),
             pltpu.SemaphoreType.DMA((margin + per_device,)),
         ],
         cost_estimate=cost(margin + per_device, side),
@@ -339,9 +359,14 @@
 
 
 def add_rim(p, load, store, columns, lines):
-    side = columns.shape[0]
-    lane, line = iota(1, side), iota(0, side)
-    rim = (lane == 0) | (lane == side - 1)
+    side = lines.shape[1]
+    line = iota(0, side)
+    row = lax.broadcasted_iota(jnp.int32, (side, side), 0)
+    lane = lax.broadcasted_iota(jnp.int32, (side, side), 1)
+    source = row - jnp.where(lane == 0, 1, jnp.where(lane == side - 1, 0, 1024))
+    places = [jnp.where(source == 8 * p + 2 * f, 1.0, 0.0).astype(jnp.bfloat16) for f in range(3)]
+    place = jnp.concatenate(places, axis=1)
+    terms = product(columns[...], jnp.concatenate([place, place], axis=0))
     south = [lines[pl.ds(8 * p + 2 * f + 1, 1), :] for f in range(3)]
     north = [lines[pl.ds(8 * p + 2 * f, 1), :] for f in range(3)]
     steps = side // ROWS
@@ -349,9 +374,8 @@
     for start in range(0, steps, group):
         done = []
         for j in range(start, start + group):
-            held = columns[spread(j, side), :]
             for f in range(3):
-                value = load(f, j) + jnp.where(rim, pltpu.roll(held, side - 1 - 8 * p - 2 * f, 1), 0.0)
+                value = load(f, j) + terms[ROWS * j : ROWS * (j + 1), f * side : (f + 1) * side]
                 if j == 0:
                     value = value + jnp.where(line == 0, south[f], 0.0)
                 if j == steps - 1:
@@ -407,7 +431,9 @@
         for f, value in ((0, c_h), (normal, c_n), (across, c_t)):
             target = turn if axis == 0 else lines
             target[pl.ds(2 * f + parity, count, stride=8), :] = value
-    columns[...] = jnp.transpose(turn[...])
+    turn[...] = jnp.transpose(turn[...])
+    side = turn.shape[0]
+    columns[...] = pieces(jnp.concatenate([turn[spread(j, side), :] for j in range(side // ROWS)], axis=0))
 
 
 def most_kernel(
@@ -454,7 +480,7 @@
         out_specs=[HBM, VMEM, VMEM],
         out_shape=[
             jax.ShapeDtypeStruct(own.shape, jnp.float32),
-            jax.ShapeDtypeStruct((side, side), jnp.float32),
+            jax.ShapeDtypeStruct((side, 2 * side), jnp.bfloat16),
             jax.ShapeDtypeStruct((side, side), jnp.float32),
         ],
         scratch_shapes=[

time: 51.3 us -> 47.4 us (0.924)
  Pallas kernels: 31 us -> 22.5 us
  waiting for transfers between devices: 5.71 us -> 12.7 us
  starting transfers between devices: 12.2 us -> 9.83 us
    pallas_call x1, Pallas kernels: 18 us -> 9.95 us  [home_patches(): pl.pallas_call(functools.partial(home_kernel, margin), in_specs=[SMEM, HB...]
    ppermute x6, waiting for transfers between devices: 5.71 us -> 12.7 us  [swapped(): return lax.ppermute(value, AXES, pairs + [(j, i) for i, j in pairs])]
    ppermute x6, starting transfers between devices: 12.2 us -> 9.83 us  [swapped(): return lax.ppermute(value, AXES, pairs + [(j, i) for i, j in pairs])]
    pallas_call x1, Pallas kernels: 4.89 us -> 3.32 us  [outer_patches(): pl.pallas_call(functools.partial(outer_kernel, margin), in_specs=[HBM], o...]
    pallas_call x1, Pallas kernels: 4 us -> 4.89 us  [most(): pl.pallas_call(functools.partial(most_kernel, margin), in_specs=[SMEM, SM...]
  transfers between devices with their start and end apart: 6 -> 6, of which waited for: 3 -> 4; matrix products, arithmetic and copies ran while one was open for 4% -> 4% of each run, Pallas kernels for 56% -> 42%
where the time goes in v4:
time: 47.4 us; the launch traced here: 47.1 us
  Pallas kernels  22.5 us (47%)
  waiting for transfers between devices  12.7 us (27%)
  starting transfers between devices  9.83 us (21%)
  local copies, waits for them, and re-layouts  1.16 us (2%)
  other arithmetic  0.69 us (1%)
    ppermute x6, waiting for transfers between devices, swapped(): return lax.ppermute(value, AXES, pairs + [(j, i) for i, j in pairs])  12.7 us
    pallas_call x1, Pallas kernels, home_patches(): pl.pallas_call(functools.partial(home_kernel, margin), in_specs=[SMEM, HB...  9.95 us
    ppermute x6, starting transfers between devices, swapped(): return lax.ppermute(value, AXES, pairs + [(j, i) for i, j in pairs])  9.83 us
    pallas_call x1, Pallas kernels, most(): pl.pallas_call(functools.partial(most_kernel, margin), in_specs=[SMEM, SM...  4.89 us
    pallas_call x1, Pallas kernels, outer_patches(): pl.pallas_call(functools.partial(outer_kernel, margin), in_specs=[HBM], o...  3.32 us
    pallas_call x1, Pallas kernels, rest(): pl.pallas_call(functools.partial(rest_kernel, margin), in_specs=[SMEM] +...  2.73 us
    pallas_call x1, Pallas kernels, answers(): pl.pallas_call(functools.partial(answer_kernel, margin, per_device), in_s...  1.62 us
  transfers between devices with their start and end apart: 6, of which 4 were waited for; matrix products, arithmetic and copies ran while one was open for 4% of the time, Pallas kernels for 42%

profile of v4, /device:TPU:17, one launch (start us, length us, event | category | flops | bytes accessed | tf_op | source)
XLA Modules:
  0.0 47.1 jit_solution(5291675390924941608)
XLA Ops:
  0.0 0.0 copy-start.2
  0.0 0.0 copy-start.3
  0.0 0.0 copy-start.4
  0.0 0.0 copy-start.5
  0.0 0.0 copy-start.1
  0.0 0.0 copy-start
  0.0 0.7 %collective-permute-start.1 = (s32[16,4]{0,1:T(4,128)}, s32[16,4]{0,1:T(4,128)S(1)}, u32[]{:S(2)}, u32[]{:S(2)}) collective-permute-start(s32[16,4]{0,1:T(4,128)} %param.9), channel_id=1, source_target_pairs={{0,1},{2,3},{4,5},{6,7},{8,9},{10,11},{12,13},{14,15},{1,0},{3,2},... | collective-permute-start | bytes 776 | tf_op jit(solution)/shard_map/ppermute | solution.py:547
  0.8 3.3 %outer.1 = (f32[4,3,128,128]{3,2,1,0:T(8,128)}, f32[64,128]{1,0:T(8,128)S(1)}) custom-call(f32[24,4,128,128]{3,2,1,0:T(8,128)} %cells_hbm.3), custom_call_target="tpu_custom_call" | custom-call | flops 52428800 | bytes 1835008 | tf_op jit(solution)/shard_map/outer/pallas_call | solution.py:212
  4.1 3.0 %collective-permute-start = (f32[4,3,128,128]{3,2,1,0:T(8,128)}, f32[4,3,128,128]{3,2,1,0:T(8,128)}, u32[]{:S(2)}, u32[]{:S(2)}) collective-permute-start(f32[4,3,128,128]{3,2,1,0:T(8,128)} %get-tuple-element.15), channel_id=1, source_target_pairs={{1,2},{3,4},{5,6},{7,8},{9,10},{11,12},{13,14},{2,1},{4,3},{6,5},{... | collective-permute-start | bytes 2359304 | tf_op jit(solution)/shard_map/ppermute | solution.py:547
  7.1 0.0 copy-done.1
  7.2 0.1 copy.15
  7.2 0.1 reshape.513
  7.4 0.0 copy-done.2
  7.4 0.0 copy-done.3
  7.4 0.0 copy-done.4
  7.4 0.0 copy-done.5
  7.5 0.1 concatenate.65
  7.5 0.0 collective-permute-done.1
  7.6 0.1 copy.17
  7.6 0.1 concatenate.66
  7.7 0.1 fusion.11
  7.8 2.5 %collective-permute-start.2 = (f32[72,128]{1,0:T(8,128)S(1)}, f32[72,128]{1,0:T(8,128)S(1)}, u32[]{:S(2)}, u32[]{:S(2)}) collective-permute-start(f32[72,128]{1,0:T(8,128)S(1)} %select_maximum_fusion), channel_id=1, source_target_pairs={{1,2},{3,4},{5,6},{7,8},{9,10},{11,12},{13,14},{2,1},{4,3},{6,5},{... | collective-permute-start | bytes 110600 | tf_op jit(solution)/shard_map/ppermute | solution.py:547
  10.4 0.0 copy-done
  10.4 9.9 %home.1 = (f32[1936,128]{1,0:T(8,128)}, f32[16,3,128,128]{3,2,1,0:T(8,128)S(1)}) custom-call(s32[1,2]{1,0:T(1,128)S(1)} %copy-done, f32[24,4,128,128]{3,2,1,0:T(8,128)} %cells_hbm.3), custom_call_target="tpu_custom_call" | custom-call | flops 262144000 | bytes 9175040 | tf_op jit(solution)/shard_map/home/pallas_call | solution.py:280
  20.4 6.5 %collective-permute-done.2 = f32[72,128]{1,0:T(8,128)S(1)} collective-permute-done((f32[72,128]{1,0:T(8,128)S(1)}, f32[72,128]{1,0:T(8,128)S(1)}, u32[]{:S(2)}, u32[]{:S(2)}) %collective-permute-start.2) | collective-permute-done | bytes 36896 | tf_op jit(solution)/shard_map/ppermute | solution.py:547
  26.8 0.6 %constant_dynamic-update-slice_fusion.mine = f32[1936,128]{1,0:T(8,128)} fusion(f32[1936,128]{1,0:T(8,128)} %get-tuple-element.17, f32[72,128]{1,0:T(8,128)S(1)} %collective-permute-done.2), kind=kLoop, calls=%fused_computation.65 | loop fusion | bytes 73728 | tf_op jit(solution)/shard_map/dynamic_update_slice | solution.py:577
  27.5 0.0 collective-permute-start.3
  27.5 0.1 fusion.20
  27.5 0.1 compare_and_fusion
  27.6 0.1 select_reduce_fusion
  27.8 0.1 select_reduce_fusion.2
  27.9 0.1 reshape.514.rows_ref
  28.0 2.4 %collective-permute-done.3.theirs = f32[1936,128]{1,0:T(8,128)} collective-permute-done((f32[1936,128]{1,0:T(8,128)}, f32[1936,128]{1,0:T(8,128)}, u32[]{:S(2)}, u32[]{:S(2)}) %collective-permute-start.3) | collective-permute-done | bytes 991264 | tf_op jit(solution)/shard_map/ppermute | solution.py:547
  30.4 1.6 %answers.1 = (f32[512,128]{1,0:T(8,128)S(1)}, f32[96,128]{1,0:T(8,128)S(1)}) custom-call(s32[1,2]{1,0:T(1,128)S(1)} %copy-done, s32[24]{0:T(128)S(1)} %reshape.514.rows_ref, f32[1936,128]{1,0:T(8,128)} %constant_dynamic-update-slice_fusion.mine, f32[1936,128]{1,0:T(8,128)} %collective-permute-done.3.theirs), custom_call_target="tpu_custom_call" | custom-call | tf_op jit(solution)/shard_map/answers/pallas_call | solution.py:348
  32.0 3.0 %collective-permute-start.4 = (f32[96,128]{1,0:T(8,128)S(1)}, f32[96,128]{1,0:T(8,128)S(1)}, u32[]{:S(2)}, u32[]{:S(2)}) collective-permute-start(f32[96,128]{1,0:T(8,128)S(1)} %get-tuple-element.19), channel_id=1, source_target_pairs={{1,2},{3,4},{5,6},{7,8},{9,10},{11,12},{13,14},{2,1},{4,3},{6,5},{... | collective-permute-start | bytes 147464 | tf_op jit(solution)/shard_map/ppermute | solution.py:547
  35.0 0.1 fusion.10
  35.1 2.9 %collective-permute-done.4.crossed = f32[96,128]{1,0:T(8,128)S(1)} collective-permute-done((f32[96,128]{1,0:T(8,128)S(1)}, f32[96,128]{1,0:T(8,128)S(1)}, u32[]{:S(2)}, u32[]{:S(2)}) %collective-permute-start.4) | collective-permute-done | bytes 49184 | tf_op jit(solution)/shard_map/ppermute | solution.py:547
  38.1 0.5 %collective-permute-start.5 = (f32[96,128]{1,0:T(8,128)S(1)}, f32[96,128]{1,0:T(8,128)S(1)}, u32[]{:S(2)}, u32[]{:S(2)}) collective-permute-start(f32[96,128]{1,0:T(8,128)S(1)} %collective-permute-done.4.crossed), channel_id=1, source_target_pairs={{0,1},{2,3},{4,5},{6,7},{8,9},{10,11},{12,13},{14,15},{1,0},{3,2},... | collective-permute-start | bytes 147464 | tf_op jit(solution)/shard_map/ppermute | solution.py:547
  38.6 0.9 %collective-permute-done.5.passed = f32[96,128]{1,0:T(8,128)S(1)} collective-permute-done((f32[96,128]{1,0:T(8,128)S(1)}, f32[96,128]{1,0:T(8,128)S(1)}, u32[]{:S(2)}, u32[]{:S(2)}) %collective-permute-start.5) | collective-permute-done | bytes 49184 | tf_op jit(solution)/shard_map/ppermute | solution.py:547
  39.4 4.9 %most.1 = (f32[16,3,128,128]{3,2,1,0:T(8,128)}, bf16[128,256]{1,0:T(8,128)(2,1)S(1)}, f32[128,128]{1,0:T(8,128)S(1)}) custom-call(s32[1,2]{1,0:T(1,128)S(1)} %copy-done, s32[64]{0:T(128)S(1)} %compare_select_fusion.7.rows_ref, f32[512,128]{1,0:T(8,128)S(1)} %get-tuple-element.18.edges, f32[96,128]{1,0:T(8,128)S(1)} %collective-permute-done.4.crossed, ...), custom_call_target="tpu_custom_call" | custom-call | tf_op jit(solution)/shard_map/most/pallas_call | solution.py:477
  44.3 0.0 collective-permute-done.arrived
  44.4 2.7 %rest.1 = f32[16,3,128,128]{3,2,1,0:T(8,128)} custom-call(s32[1,2]{1,0:T(1,128)S(1)} %copy-done, f32[16,3,128,128]{3,2,1,0:T(8,128)S(1)} %get-tuple-element.14.own, f32[4,3,128,128]{3,2,1,0:T(8,128)} %collective-permute-done.arrived, bf16[128,256]{1,0:T(8,128)(2,1)S(1)} %get-tuple-element.20.columns, ...), custom_call_target="tpu_custom_call", output_to_operand_aliasing={{}: (5, {})} | custom-call | tf_op jit(solution)/shard_map/rest/pallas_call | solution.py:530
  (11 shorter events, 0.1 us)
Async XLA Ops:
  0.0 7.4 %copy-start.2 = (s32[3,2]{0,1:T(2,128)S(1)}, s32[3,2]{0,1:T(2,128)}, u32[]{:S(2)}) copy-start(s32[3,2]{0,1:T(2,128)} %constant.150.clone) | copy-start | bytes 76
  0.0 7.4 %copy-start.3 = (s32[3,2]{0,1:T(2,128)S(1)}, s32[3,2]{0,1:T(2,128)}, u32[]{:S(2)}) copy-start(s32[3,2]{0,1:T(2,128)} %constant.149.clone) | copy-start | bytes 76
  0.0 7.4 %copy-start.4 = (s32[3]{0:T(128)S(1)}, s32[3]{0:T(128)}, u32[]{:S(2)}) copy-start(s32[3]{0:T(128)} %constant.148.clone) | copy-start | bytes 40
  0.0 7.4 %copy-start.5 = (s32[3]{0:T(128)S(1)}, s32[3]{0:T(128)}, u32[]{:S(2)}) copy-start(s32[3]{0:T(128)} %constant.147.clone) | copy-start | bytes 40
  0.0 7.1 %copy-start.1 = (s32[16,4]{0,1:T(4,128)S(1)}, s32[16,4]{0,1:T(4,128)}, u32[]{:S(2)}) copy-start(s32[16,4]{0,1:T(4,128)} %param.9) | copy-start | bytes 772
  0.0 10.4 %copy-start = (s32[1,2]{1,0:T(1,128)S(1)}, s32[1,2]{1,0:T(1,128)}, u32[]{:S(2)}) copy-start(s32[1,2]{1,0:T(1,128)} %range_ref.7) | copy-start | bytes 28
  0.0 7.5 %collective-permute-start.1 = (s32[16,4]{0,1:T(4,128)}, s32[16,4]{0,1:T(4,128)S(1)}, u32[]{:S(2)}, u32[]{:S(2)}) collective-permute-start(s32[16,4]{0,1:T(4,128)} %param.9), channel_id=1, source_target_pairs={{0,1},{2,3},{4,5},{6,7},{8,9},{10,11},{12,13},{14,15},{1,0},{3,2},... | collective-permute-start | bytes 776 | tf_op jit(solution)/shard_map/ppermute | solution.py:547
  4.1 40.2 %collective-permute-start = (f32[4,3,128,128]{3,2,1,0:T(8,128)}, f32[4,3,128,128]{3,2,1,0:T(8,128)}, u32[]{:S(2)}, u32[]{:S(2)}) collective-permute-start(f32[4,3,128,128]{3,2,1,0:T(8,128)} %get-tuple-element.15), channel_id=1, source_target_pairs={{1,2},{3,4},{5,6},{7,8},{9,10},{11,12},{13,14},{2,1},{4,3},{6,5},{... | collective-permute-start | bytes 2359304 | tf_op jit(solution)/shard_map/ppermute | solution.py:547
  7.8 19.0 %collective-permute-start.2 = (f32[72,128]{1,0:T(8,128)S(1)}, f32[72,128]{1,0:T(8,128)S(1)}, u32[]{:S(2)}, u32[]{:S(2)}) collective-permute-start(f32[72,128]{1,0:T(8,128)S(1)} %select_maximum_fusion), channel_id=1, source_target_pairs={{1,2},{3,4},{5,6},{7,8},{9,10},{11,12},{13,14},{2,1},{4,3},{6,5},{... | collective-permute-start | bytes 110600 | tf_op jit(solution)/shard_map/ppermute | solution.py:547
  27.5 2.9 %collective-permute-start.3 = (f32[1936,128]{1,0:T(8,128)}, f32[1936,128]{1,0:T(8,128)}, u32[]{:S(2)}, u32[]{:S(2)}) collective-permute-start(f32[1936,128]{1,0:T(8,128)} %constant_dynamic-update-slice_fusion.mine), channel_id=1, source_target_pairs={{0,1},{2,3},{4,5},{6,7},{8,9},{10,11},{12,13},{14,15},{1,0},{3,2},... | collective-permute-start | bytes 2973704 | tf_op jit(solution)/shard_map/ppermute | solution.py:547
  32.0 6.0 %collective-permute-start.4 = (f32[96,128]{1,0:T(8,128)S(1)}, f32[96,128]{1,0:T(8,128)S(1)}, u32[]{:S(2)}, u32[]{:S(2)}) collective-permute-start(f32[96,128]{1,0:T(8,128)S(1)} %get-tuple-element.19), channel_id=1, source_target_pairs={{1,2},{3,4},{5,6},{7,8},{9,10},{11,12},{13,14},{2,1},{4,3},{6,5},{... | collective-permute-start | bytes 147464 | tf_op jit(solution)/shard_map/ppermute | solution.py:547
  38.1 1.4 %collective-permute-start.5 = (f32[96,128]{1,0:T(8,128)S(1)}, f32[96,128]{1,0:T(8,128)S(1)}, u32[]{:S(2)}, u32[]{:S(2)}) collective-permute-start(f32[96,128]{1,0:T(8,128)S(1)} %collective-permute-done.4.crossed), channel_id=1, source_target_pairs={{0,1},{2,3},{4,5},{6,7},{8,9},{10,11},{12,13},{14,15},{1,0},{3,2},... | collective-permute-start | bytes 147464 | tf_op jit(solution)/shard_map/ppermute | solution.py:547

commit v5 on v4

--- a/solution.py
+++ b/solution.py
@@ -12,6 +12,7 @@
 AXES = ("curve", "sub")
 CAP = 8
 ROWS = 8
+PAIR = 2
 VMEM = pl.BlockSpec(memory_space=pltpu.VMEM)
 SMEM = pl.BlockSpec(memory_space=pltpu.SMEM)
 HBM = pl.BlockSpec(memory_space=pltpu.HBM)
@@ -65,12 +66,10 @@
             weights[half * side : (half + 1) * side, n * side : (n + 1) * side] = block.astype(jnp.bfloat16)
 
 
-def inner_update(load, store, columns, at, side, weights):
-    lane, line = iota(1, side), iota(0, side)
-    pair = lane // 2
+def inner_update(load, store, side, weights):
+    line = iota(0, side)
     first, last = line == 0, line == ROWS - 1
     steps = side // ROWS
-    marks = [pair == at // 2 + f for f in range(4)]
 
     def cell(h, mx, my, bed):
         root = lax.rsqrt(h)
@@ -103,14 +102,6 @@
     jumps = [product(each, taken(EAST)) for each in (eta, mx, my)]
     sums = [product(each, taken(SUMS)) for each in (mx, fx, cross)]
     slopes = product(bed, taken(SLOPE))
-
-    for j in range(steps):
-        held = columns.load(j)
-        _, _, mx, my, _, _, bed = cells[j][0]
-        for f, value in enumerate((cells[j][3], mx, my, bed)):
-            held = jnp.where(marks[f], pltpu.roll(value, at + 2 * f + 1, 1), held)
-        columns.store(j, held)
-
     low = [pltpu.roll(each, 1, 0) for each in cells[steps - 1][0]]
     faces = []
     for j in range(steps):
@@ -134,15 +125,15 @@
         store(2, j, my - HALF * (x[2] + h * slope_y + (north[2] - south[2])))
 
 
-class Columns:
-    def __init__(self, ref):
-        self.ref, self.side = ref, ref.shape[0]
-
-    def load(self, j):
-        return self.ref[spread(j, self.side), :]
-
-    def store(self, j, value):
-        self.ref[spread(j, self.side), :] = value
+def gather_columns(loads, columns, first_at, side):
+    pair = iota(1, side) // 2
+    for j in range(side // ROWS):
+        held = columns[spread(j, side), :]
+        for n, load in enumerate(loads):
+            at = first_at + 8 * n
+            for f in range(4):
+                held = jnp.where(pair == at // 2 + f, pltpu.roll(load(f, j), at + 2 * f + 1, 1), held)
+        columns[spread(j, side), :] = held
 
 
 def take_edges(count, cells, slot_of, columns, edges, base):
@@ -156,15 +147,15 @@
             edges[row + 1 : row + 2, :] = cells[slot_of(p), f, 0:1, :]
 
 
-def update_one(cells, i, columns, lane_at, side, weights, put):
-    inner_update(
-        lambda f, j: cells[i, f, spread(j, side), :],
-        lambda f, j, value: put(f, ROWS * j, value),
-        Columns(columns),
-        lane_at,
-        side,
-        weights,
-    )
+def loader(cells, i):
+    side = cells.shape[3]
+    return lambda f, j: cells[i, f, spread(j, side), :]
+
+
+def update(cells, first, many, weights, put):
+    for n in range(many):
+        store = lambda f, j, value, n=n: put(n, f, ROWS * j, value)
+        inner_update(loader(cells, first + n), store, cells.shape[3], weights)
 
 
 def fetch(cells_hbm, first, cells, sems, parts):
@@ -177,22 +168,33 @@
     return copy
 
 
-def outer_kernel(margin, cells_hbm, out, edges, cells, columns, weights, sems):
-    side = columns.shape[0]
+def outer_slot(cells_hbm, margin):
     _, odd = position()
-    copy = fetch(cells_hbm, odd * (cells_hbm.shape[0] - margin), cells, sems, [(0, margin)])
+    return odd * (cells_hbm.shape[0] - margin)
+
+
+def outer_edges_kernel(margin, cells_hbm, edges, cells, columns, sems):
+    copy = fetch(cells_hbm, outer_slot(cells_hbm, margin), cells, sems, [(0, margin)])
+    for i in range(margin):
+        copy(i).wait()
+    gather_columns([loader(cells, i) for i in range(margin)], columns, 0, columns.shape[0])
+    take_edges(margin, cells, lambda p: p, columns, edges, 0)
+
+
+def outer_kernel(margin, cells_hbm, _, out, cells, weights, sems):
+    copy = fetch(cells_hbm, outer_slot(cells_hbm, margin), cells, sems, [(0, margin)])
     fill_weights(weights)
 
-    @pl.loop(0, margin)
-    def _(i):
-        copy(i).wait()
-
-        def put(f, row, value):
-            out[i, f, row : row + ROWS, :] = value
-
-        update_one(cells, i, columns, 8 * i, side, weights, put)
-
-    take_edges(margin, cells, lambda p: p, columns, edges, 0)
+    @pl.loop(0, margin // PAIR)
+    def _(step):
+        i = step * PAIR
+        for n in range(PAIR):
+            copy(i + n).wait()
+
+        def put(n, f, row, value):
+            out[i + n, f, row : row + ROWS, :] = value
+
+        update(cells, i, PAIR, weights, put)
 
 
 def cost(patches, side):
@@ -207,40 +209,52 @@
     return pltpu.CompilerParams(vmem_limit_bytes=mebibytes << 20)
 
 
-def outer_patches(old_cells, margin):
+def outer_edges(old_cells, margin):
+    side = old_cells.shape[3]
+    return pl.pallas_call(
+        functools.partial(outer_edges_kernel, margin),
+        in_specs=[HBM],
+        out_specs=VMEM,
+        out_shape=jax.ShapeDtypeStruct((16 * margin, side), jnp.float32),
+        scratch_shapes=[
+            pltpu.VMEM((margin, 4, side, side), jnp.float32),
+            pltpu.VMEM((side, side), jnp.float32),
+            pltpu.SemaphoreType.DMA((margin,)),
+        ],
+        compiler_params=room(48),
+        name="outer_edges",
+    )(old_cells)
+
+
+def outer_patches(old_cells, before, margin):
     side = old_cells.shape[3]
     return pl.pallas_call(
         functools.partial(outer_kernel, margin),
-        in_specs=[HBM],
-        out_specs=[VMEM, VMEM],
-        out_shape=[
-            jax.ShapeDtypeStruct((margin, 3, side, side), jnp.float32),
-            jax.ShapeDtypeStruct((16 * margin, side), jnp.float32),
-        ],
+        in_specs=[HBM, HBM],
+        out_specs=VMEM,
+        out_shape=jax.ShapeDtypeStruct((margin, 3, side, side), jnp.float32),
         scratch_shapes=[
             pltpu.VMEM((margin, 4, side, side), jnp.float32),
-            pltpu.VMEM((side, side), jnp.float32),
             pltpu.VMEM((2 * side, 6 * side), jnp.bfloat16),
             pltpu.SemaphoreType.DMA((margin,)),
         ],
         cost_estimate=cost(margin, side),
         compiler_params=room(48),
         name="outer",
-    )(old_cells)
-
-
-def layout(margin, per_device, side):
-    inner = 3 * side * margin
-    home = inner + 16 * margin
+    )(old_cells, before)
+
+
+def layout(margin, per_device):
+    home = 16 * margin
     limit = home + 16 * per_device
     brought = limit + 8
-    return inner, home, limit, brought, brought + 16 * margin + 8
-
-
-def home_kernel(margin, range_ref, cells_hbm, shared, own, cells, columns, weights, sems):
+    return home, limit, brought, brought + 16 * margin
+
+
+def home_kernel(margin, range_ref, cells_hbm, came, shared, inner, own, cells, columns, weights, sems):
     side = columns.shape[0]
     count = own.shape[0]
-    inner, home, limit, _, _ = layout(margin, count, side)
+    home, limit, brought, total = layout(margin, count)
     _, odd = position()
     inner_at = (1 - odd) * count
     home_at = odd * margin
@@ -248,41 +262,37 @@
     copy = fetch(cells_hbm, (1 - odd) * margin, cells, sems, parts)
     fill_weights(weights)
 
-    @pl.loop(0, margin)
-    def _(i):
-        copy(inner_at + i).wait()
-
-        def put(f, row, value):
-            at = pl.multiple_of(i * (3 * side) + (f * side + row), ROWS)
-            shared[pl.ds(at, ROWS), :] = value
-
-        update_one(cells, inner_at + i, columns, 8 * i, side, weights, put)
-
-    take_edges(margin, cells, lambda p: inner_at + p, columns, shared, inner)
-
-    @pl.loop(0, count)
-    def _(i):
-        copy(home_at + i).wait()
-
-        def put(f, row, value):
-            own[i, f, row : row + ROWS, :] = value
-
-        update_one(cells, home_at + i, columns, 8 * i, side, weights, put)
-
-    take_edges(count, cells, lambda p: home_at + p, columns, shared, home)
+    for at, many, out, row in ((inner_at, margin, inner, 0), (home_at, count, own, home)):
+
+        @pl.loop(0, many // PAIR)
+        def _(step, at=at, out=out):
+            i = step * PAIR
+            for n in range(PAIR):
+                copy(at + i + n).wait()
+
+            def put(n, f, row, value):
+                out[i + n, f, row : row + ROWS, :] = value
+
+            gather_columns([loader(cells, at + i + n) for n in range(PAIR)], columns, 8 * i, side)
+            update(cells, at + i, PAIR, weights, put)
+
+        take_edges(many, cells, lambda p, at=at: at + p, columns, shared, row)
+
     outer_limit = jnp.where(odd == 1, range_ref[0, 1], range_ref[0, 0])
     shared[limit : limit + 8, :] = jnp.full((8, side), outer_limit, jnp.int32).astype(jnp.float32)
-
-
-def home_patches(old_range, old_cells, margin, per_device):
+    shared[brought:total, :] = came[0 : total - brought, :]
+
+
+def home_patches(old_range, old_cells, came, margin, per_device):
     side = old_cells.shape[3]
-    total = layout(margin, per_device, side)[-1]
+    total = layout(margin, per_device)[-1]
     return pl.pallas_call(
         functools.partial(home_kernel, margin),
-        in_specs=[SMEM, HBM],
-        out_specs=[VMEM, VMEM],
+        in_specs=[SMEM, HBM, VMEM],
+        out_specs=[VMEM] * 3,
         out_shape=[
             jax.ShapeDtypeStruct((total, side), jnp.float32),
+            jax.ShapeDtypeStruct((margin, 3, side, side), jnp.float32),
             jax.ShapeDtypeStruct((per_device, 3, side, side), jnp.float32),
         ],
         scratch_shapes=[
@@ -294,12 +304,13 @@
         cost_estimate=cost(margin + per_device, side),
         compiler_params=room(48),
         name="home",
-    )(old_range, old_cells)
+    )(old_range, old_cells, came)
 
 
 def answer_kernel(margin, count, range_ref, rows_ref, mine, theirs, edges, message):
     side = edges.shape[1]
-    inner, home, limit, brought, _ = layout(margin, count, side)
+    home, limit, brought, _ = layout(margin, count)
+    inner = 0
     me, odd = position()
     start, stop = range_ref[0, 0], range_ref[0, 1]
     even = odd == 0
@@ -358,33 +369,6 @@
     )(old_range, rows, mine, theirs)
 
 
-def add_rim(p, load, store, columns, lines):
-    side = lines.shape[1]
-    line = iota(0, side)
-    row = lax.broadcasted_iota(jnp.int32, (side, side), 0)
-    lane = lax.broadcasted_iota(jnp.int32, (side, side), 1)
-    source = row - jnp.where(lane == 0, 1, jnp.where(lane == side - 1, 0, 1024))
-    places = [jnp.where(source == 8 * p + 2 * f, 1.0, 0.0).astype(jnp.bfloat16) for f in range(3)]
-    place = jnp.concatenate(places, axis=1)
-    terms = product(columns[...], jnp.concatenate([place, place], axis=0))
-    south = [lines[pl.ds(8 * p + 2 * f + 1, 1), :] for f in range(3)]
-    north = [lines[pl.ds(8 * p + 2 * f, 1), :] for f in range(3)]
-    steps = side // ROWS
-    group = 4
-    for start in range(0, steps, group):
-        done = []
-        for j in range(start, start + group):
-            for f in range(3):
-                value = load(f, j) + terms[ROWS * j : ROWS * (j + 1), f * side : (f + 1) * side]
-                if j == 0:
-                    value = value + jnp.where(line == 0, south[f], 0.0)
-                if j == steps - 1:
-                    value = value + jnp.where(line == ROWS - 1, north[f], 0.0)
-                done.append((f, j, value))
-        for f, j, value in done:
-            store(f, j, value)
-
-
 def rim_terms(rows_ref, edges, crossed, passed, columns, lines, source, ghost, turn, count, odd):
     total = edges.shape[0]
     step = crossed.shape[0]
@@ -436,110 +420,88 @@
     columns[...] = pieces(jnp.concatenate([turn[spread(j, side), :] for j in range(side // ROWS)], axis=0))
 
 
-def most_kernel(
-    margin, range_ref, rows_ref, edges, crossed, passed, own, theirs, out, columns, lines, result, source, ghost, turn, sems
+def fill_places(places):
+    side = places.shape[0] // 2
+    row = lax.broadcasted_iota(jnp.int32, (side, side), 0) % 8
+    lane = lax.broadcasted_iota(jnp.int32, (side, side), 1)
+    source = row - jnp.where(lane == 0, 1, jnp.where(lane == side - 1, 0, 1024))
+    for f in range(3):
+        block = jnp.where(source == 2 * f, 1.0, 0.0).astype(jnp.bfloat16)
+        for half in range(2):
+            places[half * side : (half + 1) * side, f * side : (f + 1) * side] = block
+
+
+def final_kernel(
+    margin, range_ref, rows_ref, edges, crossed, passed, own, theirs, arrived, out,
+    result, source, ghost, turn, columns, lines, places, sems,
 ):
-    count, side = own.shape[0], columns.shape[0]
+    count, side = own.shape[0], lines.shape[1]
     me, odd = position()
     even = odd == 0
+    fill_places(places)
     rim_terms(rows_ref, edges, crossed, passed, columns, lines, source, ghost, turn, count, odd)
     start, stop = range_ref[0, 0], range_ref[0, 1]
-    first = (1 - odd) * margin
-    many = count - margin
-
-    def copy(i):
-        return pltpu.make_async_copy(result.at[i], out.at[first + i], sems.at[i])
-
-    @pl.loop(0, many)
-    def _(i):
-        p = first + i
-        g = me * count + p
-        taken = jnp.where(even, g >= stop, g < start)
-        m = jnp.clip(jnp.where(even, p - (count - margin), p), 0, margin - 1)
-
-        def load(f, k):
-            at = pl.multiple_of(m * (3 * side) + (f * side + ROWS * k), ROWS)
-            return jnp.where(taken, theirs[pl.ds(at, ROWS), :], own[p, f, ROWS * k : ROWS * (k + 1), :])
-
-        def store(f, k, value):
-            result[i, f, spread(k, side), :] = value
-
-        add_rim(p, load, store, columns, lines)
-        copy(i).start()
-
-    for i in range(many):
-        copy(i).wait()
-
-
-def most(old_range, rows, edges, crossed, passed, own, theirs, margin):
+    line = iota(0, side)
+    lane = lax.broadcasted_iota(jnp.int32, (side, 2 * side), 1) % side
+    steps = side // ROWS
+
+    def copy(p):
+        return pltpu.make_async_copy(result.at[p], out.at[p], sems.at[p])
+
+    for group in range(0, count, margin):
+        patches = range(group, group + margin)
+        held = columns[...]
+        masked = [held * jnp.where(lane // 8 == p, 1.0, 0.0).astype(jnp.bfloat16) for p in patches]
+        terms = product(jnp.concatenate(masked, axis=0), places[...])
+        for m, p in enumerate(patches):
+            if group == 0:
+                taken = me * count + p < start
+            elif group == count - margin:
+                taken = me * count + p >= stop
+            else:
+                taken = None
+            near = even if group else odd == 1
+            for f in range(3):
+                for j in range(steps):
+                    rows = slice(ROWS * j, ROWS * (j + 1))
+                    value = own[p, f, rows, :]
+                    if taken is not None:
+                        moved = jnp.where(near, theirs[m, f, rows, :], arrived[m, f, rows, :])
+                        value = jnp.where(taken, moved, value)
+                    at = side * m + ROWS * j
+                    value = value + terms[at : at + ROWS, f * side : (f + 1) * side]
+                    if j == 0:
+                        south = lines[8 * p + 2 * f + 1 : 8 * p + 2 * f + 2, :]
+                        value = value + jnp.where(line == 0, south, 0.0)
+                    if j == steps - 1:
+                        north = lines[8 * p + 2 * f : 8 * p + 2 * f + 1, :]
+                        value = value + jnp.where(line == ROWS - 1, north, 0.0)
+                    result[p, f, spread(j, side), :] = value
+            copy(p).start()
+    for p in range(count):
+        copy(p).wait()
+
+
+def finished(old_range, rows, edges, crossed, passed, own, theirs, arrived, margin):
     count, _, side, _ = own.shape
-    many = count - margin
     return pl.pallas_call(
-        functools.partial(most_kernel, margin),
-        in_specs=[SMEM, SMEM] + [VMEM] * 5,
-        out_specs=[HBM, VMEM, VMEM],
-        out_shape=[
-            jax.ShapeDtypeStruct(own.shape, jnp.float32),
-            jax.ShapeDtypeStruct((side, 2 * side), jnp.bfloat16),
-            jax.ShapeDtypeStruct((side, side), jnp.float32),
-        ],
+        functools.partial(final_kernel, margin),
+        in_specs=[SMEM, SMEM] + [VMEM] * 6,
+        out_specs=HBM,
+        out_shape=jax.ShapeDtypeStruct(own.shape, jnp.float32),
         scratch_shapes=[
-            pltpu.VMEM((many, 3, side, side), jnp.float32),
+            pltpu.VMEM(own.shape, jnp.float32),
             pltpu.VMEM((edges.shape[0] + 2 * crossed.shape[0], side), jnp.float32),
             pltpu.VMEM((16 * count, side), jnp.float32),
             pltpu.VMEM((side, side), jnp.float32),
-            pltpu.SemaphoreType.DMA((many,)),
+            pltpu.VMEM((side, 2 * side), jnp.bfloat16),
+            pltpu.VMEM((side, side), jnp.float32),
+            pltpu.VMEM((2 * side, 3 * side), jnp.bfloat16),
+            pltpu.SemaphoreType.DMA((count,)),
         ],
-        compiler_params=room(6),
-        name="most",
-    )(old_range, rows, edges, crossed, passed, own, theirs)
-
-
-def rest_kernel(margin, range_ref, own, arrived, columns, lines, _, out, result, sems):
-    count, side = own.shape[0], columns.shape[0]
-    me, odd = position()
-    even = odd == 0
-    start, stop = range_ref[0, 0], range_ref[0, 1]
-    first = odd * (count - margin)
-
-    def copy(i):
-        return pltpu.make_async_copy(result.at[i], out.at[first + i], sems.at[i])
-
-    @pl.loop(0, margin)
-    def _(i):
-        p = first + i
-        g = me * count + p
-        taken = jnp.where(even, g < start, g >= stop)
-
-        def load(f, k):
-            at = slice(ROWS * k, ROWS * (k + 1))
-            return jnp.where(taken, arrived[i, f, at, :], own[p, f, at, :])
-
-        def store(f, k, value):
-            result[i, f, spread(k, side), :] = value
-
-        add_rim(p, load, store, columns, lines)
-        copy(i).start()
-
-    for i in range(margin):
-        copy(i).wait()
-
-
-def rest(old_range, own, arrived, columns, lines, filled, margin):
-    count, _, side, _ = own.shape
-    return pl.pallas_call(
-        functools.partial(rest_kernel, margin),
-        in_specs=[SMEM] + [VMEM] * 4 + [HBM],
-        out_specs=HBM,
-        out_shape=jax.ShapeDtypeStruct(own.shape, jnp.float32),
-        scratch_shapes=[
-            pltpu.VMEM((margin, 3, side, side), jnp.float32),
-            pltpu.SemaphoreType.DMA((margin,)),
-        ],
-        input_output_aliases={5: 0},
-        compiler_params=room(4),
-        name="rest",
-    )(old_range, own, arrived, columns, lines, filled)
+        compiler_params=room(12),
+        name="final",
+    )(old_range, rows, edges, crossed, passed, own, theirs, arrived)
 
 
 def swapped(value, first):
@@ -559,11 +521,9 @@
     margin = (old_cells.shape[0] - per_device) // 2
     entries = 4 * per_device
     me, odd = position()
-    brought = layout(margin, per_device, side)[3]
 
     their_table = swapped(neighbours, 0)
-    leaving, leaving_edges = outer_patches(old_cells, margin)
-    arrived = swapped(leaving, 1)
+    leaving_edges = outer_edges(old_cells, margin)
 
     tables = jnp.where(
         odd == 0,
@@ -571,11 +531,14 @@
         jnp.concatenate([their_table.reshape(1, -1), neighbours.reshape(1, -1)], axis=1),
     ).astype(jnp.float32)
     tables = jnp.pad(tables, ((0, 7), (0, side - 2 * entries)))
-    came = swapped(jnp.concatenate([leaving_edges, tables], axis=0), 1)
-
-    shared, own = home_patches(old_range, old_cells, margin, per_device)
-    shared = lax.dynamic_update_slice(shared, came, (brought, 0))
-    theirs = swapped(shared, 0)
+    bundle = jnp.concatenate([leaving_edges, tables], axis=0)
+    came = swapped(bundle, 1)
+
+    arrived = swapped(outer_patches(old_cells, bundle, margin), 1)
+
+    shared, inner, own = home_patches(old_range, old_cells, came, margin, per_device)
+    their_edges = swapped(shared, 0)
+    theirs = swapped(inner, 0)
 
     entry = jnp.arange(entries, dtype=jnp.int32)
     entry_side = entry % 4
@@ -589,7 +552,7 @@
     chosen = asked[:, None, :] & (ranks(asked)[:, None, :] == jnp.arange(CAP)[None, :, None])
     send_rows = jnp.sum(jnp.where(chosen, rows[:, None, :], 0), axis=2).reshape(-1)
 
-    edges, message = answers(old_range, send_rows, shared, theirs, margin, per_device)
+    edges, message = answers(old_range, send_rows, shared, their_edges, margin, per_device)
     crossed = swapped(message, 1)
     passed = swapped(crossed, 0)
 
@@ -608,8 +571,7 @@
     wall = total * odd + 16 * (entry // 4) + 8 * (entry_side // 2) + 1 - entry_side % 2
     ghost_rows = jnp.where(listed < 0, -1 - wall, jnp.where(owner // 2 == me // 2, within, across))
 
-    filled, columns, lines = most(old_range, ghost_rows, edges, crossed, passed, own, theirs, margin)
-    return rest(old_range, own, arrived, columns, lines, filled, margin)
+    return finished(old_range, ghost_rows, edges, crossed, passed, own, theirs, arrived, margin)
 
 
 def solution(mesh):

time: 47.4 us -> 43.5 us (0.918)
  waiting for transfers between devices: 12.7 us -> 1.38 us
  other arithmetic: 0.69 us -> 6.65 us
  Pallas kernels: 22.5 us -> 20.1 us
  starting transfers between devices: 9.83 us -> 12.1 us
  local copies, waits for them, and re-layouts: 1.16 us -> 2.43 us
    ppermute x6 -> x7, waiting for transfers between devices: 12.7 us -> 1.38 us  [swapped(): return lax.ppermute(value, AXES, pairs + [(j, i) for i, j in pairs])]
    ppermute x6 -> x7, starting transfers between devices: 9.83 us -> 12.1 us  [swapped(): return lax.ppermute(value, AXES, pairs + [(j, i) for i, j in pairs])]
    pallas_call x3, Pallas kernels: 10.9 us -> 9 us  [the longest x1 4.07 us: finished(): pl.pallas_call(functools.partial(final_kernel, margin), in_specs=[SMEM, S...]
    pallas_call x1, Pallas kernels: 1.62 us -> 0.65 us  [answers(): pl.pallas_call(functools.partial(answer_kernel, margin, per_device), in_s...]
    select_n x1, other arithmetic: 0.01 us -> 0.68 us  [local(): jnp.where(odd == 0, jnp.array([[-2, mine], [-1, mine + 4 * CAP], [2, mine...]
    unnamed x13 -> x17, local copies, waits for them, and re-layouts: 0.11 us -> 0.79 us
    reduce_sum x1, other arithmetic: 0.09 us -> 0.76 us  [local(): jnp.sum(jnp.where(named, lists[:, 1:] + 8 * (place // 2) + place % 2, 0),...]
    add x1, other arithmetic: 0.01 us -> 0.66 us  [local(): me + jnp.where(odd == 0, jnp.array([0, 0, 1], jnp.int32), jnp.array([-1,...]
  transfers between devices with their start and end apart: 6 -> 7, of which waited for: 4 -> 2; matrix products, arithmetic and copies ran while one was open for 4% -> 20% of each run, Pallas kernels for 42% -> 37%
where the time goes in v5:
time: 43.5 us; the launch traced here: 42.9 us
  Pallas kernels  20.1 us (46%)
  starting transfers between devices  12.1 us (28%)
  other arithmetic  6.65 us (15%)
  local copies, waits for them, and re-layouts  2.43 us (6%)
  waiting for transfers between devices  1.38 us (3%)
    ppermute x7, starting transfers between devices, swapped(): return lax.ppermute(value, AXES, pairs + [(j, i) for i, j in pairs])  12.1 us
    pallas_call x1, Pallas kernels, home_patches(): pl.pallas_call(functools.partial(home_kernel, margin), in_specs=[SMEM, HB...  10.5 us
    pallas_call x1, Pallas kernels, finished(): pl.pallas_call(functools.partial(final_kernel, margin), in_specs=[SMEM, S...  4.07 us
    pallas_call x1, Pallas kernels, outer_patches(): pl.pallas_call(functools.partial(outer_kernel, margin), in_specs=[HBM, HB...  3.2 us
    pallas_call x1, Pallas kernels, outer_edges(): pl.pallas_call(functools.partial(outer_edges_kernel, margin), in_specs=[H...  1.73 us
    ppermute x7, waiting for transfers between devices, swapped(): return lax.ppermute(value, AXES, pairs + [(j, i) for i, j in pairs])  1.38 us
  transfers between devices with their start and end apart: 7, of which 2 were waited for; matrix products, arithmetic and copies ran while one was open for 20% of the time, Pallas kernels for 37%

profile of v5, /device:TPU:17, one launch (start us, length us, event | category | flops | bytes accessed | tf_op | source)
XLA Modules:
  0.0 42.9 jit_solution(16038883336828726079)
XLA Ops:
  0.0 0.7 %collective-permute-start = (s32[16,4]{0,1:T(4,128)}, s32[16,4]{0,1:T(4,128)S(1)}, u32[]{:S(2)}, u32[]{:S(2)}) collective-permute-start(s32[16,4]{0,1:T(4,128)} %param.9), channel_id=1, source_target_pairs={{0,1},{2,3},{4,5},{6,7},{8,9},{10,11},{12,13},{14,15},{1,0},{3,2},... | collective-permute-start | bytes 776 | tf_op jit(solution)/shard_map/ppermute | solution.py:509
  0.7 0.8 %copy.14 = s32[16,4]{1,0:T(8,128)S(1)} copy(s32[16,4]{0,1:T(4,128)} %param.9) | data formatting | bytes 512 | tf_op args[2]
  1.4 0.1 reshape.513
  1.5 0.0 copy-start.2
  1.5 0.0 copy-start.5
  1.6 0.5 %broadcast_subtract_fusion = (s32[64]{0:T(128)S(1)}, s32[64]{0:T(128)}) fusion(s32[]{:T(128)S(6)} %add.120, s32[64]{0:T(128)S(1)} %reshape.513), kind=kLoop, calls=%fused_computation.68 | loop fusion | flops 1024 | bytes 772 | tf_op jit(solution)/shard_map/sub | solution.py:567
  2.1 0.0 copy-start.3
  2.1 0.7 %broadcast_select_fusion.3 = s32[3,2]{0,1:T(2,128)S(1)} fusion(s32[3,2]{0,1:T(2,128)} %constant.147.clone, s32[3,2]{0,1:T(2,128)} %constant.148.clone, pred[]{:T(512)S(6)} %eq.69), kind=kLoop, calls=%fused_computation.52 | loop fusion | flops 6 | bytes 73 | tf_op jit(solution)/shard_map/jit(_where)/select_n | solution.py:562
  2.8 0.6 %slice_bitcast_fusion = (s32[3]{0:T(128)}, s32[3]{0:T(128)S(1)}) fusion(s32[3,2]{0,1:T(2,128)S(1)} %broadcast_select_fusion.3), kind=kLoop, calls=%fused_computation.65 | loop fusion | bytes 48 | tf_op jit(solution)/shard_map/add | solution.py:569
  3.4 0.0 copy-start.4
  3.4 0.7 %fusion.12 = s32[3]{0:T(128)S(1)} fusion(s32[3]{0:T(128)} %constant.145.clone, s32[3]{0:T(128)} %constant.146.clone, pred[]{:T(512)S(6)} %eq.69, s32[]{:T(128)S(6)} %add.120), kind=kLoop, calls=%fused_computation.58 | loop fusion | flops 6 | bytes 41 | tf_op jit(solution)/shard_map/add | solution.py:549
  4.0 0.0 copy-done.4
  4.0 0.6 %compare_and_fusion.1 = pred[3,64]{1,0:T(4,128)(4,1)} fusion(s32[64]{0:T(128)S(1)} %get-tuple-element.17, s32[3]{0:T(128)S(1)} %get-tuple-element.20, pred[64]{0:T(512)(128)(4,1)S(1)} %broadcast_compare_fusion), kind=kLoop, calls=%fused_computation.32 | loop fusion | flops 384 | bytes 524 | tf_op jit(solution)/shard_map/and | solution.py:567
  4.6 0.6 %iota_compare_fusion.1 = pred[64,64]{1,0:T(8,128)(4,1)} fusion(), kind=kLoop, calls=%fused_computation.4 | loop fusion | flops 4096 | bytes 4096 | tf_op jit(solution)/shard_map/lt | solution.py:514
  5.2 0.1 concatenate.65
  5.3 1.7 %outer_edges.1 = f32[64,128]{1,0:T(8,128)S(1)} custom-call(f32[24,4,128,128]{3,2,1,0:T(8,128)} %cells_hbm.5), custom_call_target="tpu_custom_call" | custom-call | tf_op jit(solution)/shard_map/outer_edges/pallas_call | solution.py:214
  7.0 0.0 copy-done.5
  7.1 0.0 collective-permute-done
  7.1 0.1 copy.16
  7.1 0.1 concatenate.66
  7.2 0.0 copy-done.2
  7.2 0.0 copy-done.3
  7.3 0.1 fusion.11
  7.3 3.0 %collective-permute-start.1 = (f32[72,128]{1,0:T(8,128)S(1)}, f32[72,128]{1,0:T(8,128)S(1)}, u32[]{:S(2)}, u32[]{:S(2)}) collective-permute-start(f32[72,128]{1,0:T(8,128)S(1)} %select_maximum_fusion._), channel_id=1, source_target_pairs={{1,2},{3,4},{5,6},{7,8},{9,10},{11,12},{13,14},{2,1},{4,3},{6,5},{... | collective-permute-start | bytes 110600 | tf_op jit(solution)/shard_map/ppermute | solution.py:509
  10.4 0.5 %fusion.19 = s32[64]{0:T(128)} fusion(), kind=kLoop, calls=%fused_computation.70 | loop fusion | flops 1728 | bytes 256 | tf_op jit(solution)/shard_map/add | solution.py:545
  10.9 0.0 copy-start
  10.9 3.2 %outer.1 = f32[4,3,128,128]{3,2,1,0:T(8,128)} custom-call(f32[24,4,128,128]{3,2,1,0:T(8,128)} %cells_hbm.5, f32[72,128]{1,0:T(8,128)S(1)} %select_maximum_fusion._), custom_call_target="tpu_custom_call" | custom-call | flops 52428800 | bytes 1835008 | tf_op jit(solution)/shard_map/outer/pallas_call | solution.py:231
  14.1 2.5 %collective-permute-start.6 = (f32[4,3,128,128]{3,2,1,0:T(8,128)}, f32[4,3,128,128]{3,2,1,0:T(8,128)}, u32[]{:S(2)}, u32[]{:S(2)}) collective-permute-start(f32[4,3,128,128]{3,2,1,0:T(8,128)} %outer.1), channel_id=1, source_target_pairs={{1,2},{3,4},{5,6},{7,8},{9,10},{11,12},{13,14},{2,1},{4,3},{6,5},{... | collective-permute-start | bytes 2359304 | tf_op jit(solution)/shard_map/ppermute | solution.py:509
  16.6 0.0 collective-permute-done.1.came
  16.7 0.1 fusion.20
  16.7 0.0 copy-done
  16.7 0.0 copy-start.7
  16.7 0.0 copy-start.1
  16.7 0.0 copy-start.6
  16.8 10.5 %home.1 = (f32[392,128]{1,0:T(8,128)S(1)}, f32[4,3,128,128]{3,2,1,0:T(8,128)}, f32[16,3,128,128]{3,2,1,0:T(8,128)S(1)}) custom-call(s32[1,2]{1,0:T(1,128)S(1)} %copy-done, f32[24,4,128,128]{3,2,1,0:T(8,128)} %cells_hbm.5, f32[72,128]{1,0:T(8,128)S(1)} %collective-permute-done.1.came), custom_call_target="tpu_custom_call" | custom-call | flops 262144000 | bytes 9175040 | tf_op jit(solution)/shard_map/home/pallas_call | solution.py:289
  27.2 1.0 %collective-permute-start.2 = (f32[392,128]{1,0:T(8,128)S(1)}, f32[392,128]{1,0:T(8,128)S(1)}, u32[]{:S(2)}, u32[]{:S(2)}) collective-permute-start(f32[392,128]{1,0:T(8,128)S(1)} %get-tuple-element.10.mine), channel_id=1, source_target_pairs={{0,1},{2,3},{4,5},{6,7},{8,9},{10,11},{12,13},{14,15},{1,0},{3,2},... | collective-permute-start | bytes 602120 | tf_op jit(solution)/shard_map/ppermute | solution.py:509
  28.2 0.1 collective-permute-start.5
  28.3 0.0 copy-done.7
  28.3 0.1 compare_and_fusion
  28.4 0.0 copy-done.1
  28.4 0.0 copy-done.6
  28.4 0.7 %select_reduce_fusion = (s32[3,64]{1,0:T(4,128)S(1)}, s32[3,64]{1,0:T(4,128)}) fusion(pred[3,64]{1,0:T(4,128)(4,1)S(1)} %compare_and_fusion, pred[64,64]{1,0:T(8,128)(4,1)S(1)} %copy-done.1, pred[3,64]{1,0:T(4,128)(4,1)S(1)} %copy-done.6), kind=kLoop, calls=%fused_computation | loop fusion | flops 73344 | bytes 6016 | tf_op jit(solution)/shard_map/reduce_sum | solution.py:515
  29.1 0.7 %select_reduce_fusion.2 = s32[3,8]{1,0:T(4,128)} fusion(s32[3,64]{1,0:T(4,128)S(1)} %multiply_add_fusion, s32[3,64]{1,0:T(4,128)S(1)} %get-tuple-element.15, pred[3,64]{1,0:T(4,128)(4,1)S(1)} %compare_and_fusion), kind=kLoop, calls=%fused_computation.5 | loop fusion | flops 6120 | bytes 1824 | tf_op jit(solution)/shard_map/reduce_sum | solution.py:553
  29.8 0.7 %reshape.514.rows_ref = s32[24]{0:T(128)S(1)} reshape(s32[3,8]{1,0:T(4,128)} %select_reduce_fusion.2) | data formatting | bytes 192 | tf_op jit(solution)/shard_map/reshape | solution.py:553
  30.5 0.0 collective-permute-done.2.theirs
  30.5 0.7 %answers.1 = (f32[512,128]{1,0:T(8,128)S(1)}, f32[96,128]{1,0:T(8,128)S(1)}) custom-call(s32[1,2]{1,0:T(1,128)S(1)} %copy-done, s32[24]{0:T(128)S(1)} %reshape.514.rows_ref, f32[392,128]{1,0:T(8,128)S(1)} %get-tuple-element.10.mine, f32[392,128]{1,0:T(8,128)S(1)} %collective-permute-done.2.theirs), custom_call_target="tpu_custom_call" | custom-call | tf_op jit(solution)/shard_map/answers/pallas_call | solution.py:359
  31.2 3.5 %collective-permute-start.3 = (f32[96,128]{1,0:T(8,128)S(1)}, f32[96,128]{1,0:T(8,128)S(1)}, u32[]{:S(2)}, u32[]{:S(2)}) collective-permute-start(f32[96,128]{1,0:T(8,128)S(1)} %get-tuple-element.12), channel_id=1, source_target_pairs={{1,2},{3,4},{5,6},{7,8},{9,10},{11,12},{13,14},{2,1},{4,3},{6,5},{... | collective-permute-start | bytes 147464 | tf_op jit(solution)/shard_map/ppermute | solution.py:509
  34.7 0.8 %fusion.10 = s32[64]{0:T(128)S(1)} fusion(s32[3,64]{1,0:T(4,128)} %get-tuple-element.16, s32[3]{0:T(128)} %get-tuple-element.19, s32[3]{0:T(128)} %copy-done.4, s32[64]{0:T(128)} %copy-done.3, pred[64]{0:T(512)(128)(4,1)} %copy-done.5), kind=kLoop, calls=%fused_computation.31 | loop fusion | flops 4928 | bytes 1368 | tf_op jit(solution)/shard_map/reduce_sum | solution.py:569
  35.4 1.1 %collective-permute-done.3.crossed = f32[96,128]{1,0:T(8,128)S(1)} collective-permute-done((f32[96,128]{1,0:T(8,128)S(1)}, f32[96,128]{1,0:T(8,128)S(1)}, u32[]{:S(2)}, u32[]{:S(2)}) %collective-permute-start.3) | collective-permute-done | bytes 49184 | tf_op jit(solution)/shard_map/ppermute | solution.py:509
  36.6 1.3 %collective-permute-start.4 = (f32[96,128]{1,0:T(8,128)S(1)}, f32[96,128]{1,0:T(8,128)S(1)}, u32[]{:S(2)}, u32[]{:S(2)}) collective-permute-start(f32[96,128]{1,0:T(8,128)S(1)} %collective-permute-done.3.crossed), channel_id=1, source_target_pairs={{0,1},{2,3},{4,5},{6,7},{8,9},{10,11},{12,13},{14,15},{1,0},{3,2},... | collective-permute-start | bytes 147464 | tf_op jit(solution)/shard_map/ppermute | solution.py:509
  37.9 0.7 %compare_select_fusion.7.rows_ref = s32[64]{0:T(128)S(1)} fusion(s32[64]{0:T(128)} %copy-done.2, s32[64]{0:T(128)S(1)} %fusion.10, s32[64]{0:T(128)} %get-tuple-element.18, s32[]{:T(128)S(6)} %mul.42, s32[]{:T(128)S(6)} %select_n.156, s32[]{:T(128)S(6)} %mul_shard_map.3), kind=kLoop, calls=%fused_computation.56 | loop fusion | flops 3904 | bytes 1036 | tf_op jit(solution)/shard_map/jit(_where)/select_n | solution.py:572
  38.6 0.2 collective-permute-done.4.passed
  38.8 0.0 collective-permute-done.6.arrived
  38.8 0.0 collective-permute-done.5.theirs
  38.8 4.1 %final.1 = f32[16,3,128,128]{3,2,1,0:T(8,128)} custom-call(s32[1,2]{1,0:T(1,128)S(1)} %copy-done, s32[64]{0:T(128)S(1)} %compare_select_fusion.7.rows_ref, f32[512,128]{1,0:T(8,128)S(1)} %get-tuple-element.11.edges, f32[96,128]{1,0:T(8,128)S(1)} %collective-permute-done.3.crossed, f32[96,128]{1,0:T(8,128)S(1)} %collective-permute-done.4.passed, ...), custom_call_target="tpu_custom_call" | custom-call | tf_op jit(solution)/shard_map/final/pallas_call | solution.py:487
  (4 shorter events, 0.0 us)
Async XLA Ops:
  0.0 7.1 %collective-permute-start = (s32[16,4]{0,1:T(4,128)}, s32[16,4]{0,1:T(4,128)S(1)}, u32[]{:S(2)}, u32[]{:S(2)}) collective-permute-start(s32[16,4]{0,1:T(4,128)} %param.9), channel_id=1, source_target_pairs={{0,1},{2,3},{4,5},{6,7},{8,9},{10,11},{12,13},{14,15},{1,0},{3,2},... | collective-permute-start | bytes 776 | tf_op jit(solution)/shard_map/ppermute | solution.py:509
  1.5 5.7 %copy-start.2 = (s32[64]{0:T(128)}, s32[64]{0:T(128)S(1)}, u32[]{:S(2)}) copy-start(s32[64]{0:T(128)S(1)} %reshape.513) | copy-start | bytes 772
  1.5 5.5 %copy-start.5 = (pred[64]{0:T(512)(128)(4,1)}, pred[64]{0:T(512)(128)(4,1)S(1)}, u32[]{:S(2)}) copy-start(pred[64]{0:T(512)(128)(4,1)S(1)} %broadcast_compare_fusion) | copy-start | bytes 196
  2.1 5.2 %copy-start.3 = (s32[64]{0:T(128)}, s32[64]{0:T(128)S(1)}, u32[]{:S(2)}) copy-start(s32[64]{0:T(128)S(1)} %get-tuple-element.17) | copy-start | bytes 772
  3.4 0.7 %copy-start.4 = (s32[3]{0:T(128)}, s32[3]{0:T(128)S(1)}, u32[]{:S(2)}) copy-start(s32[3]{0:T(128)S(1)} %get-tuple-element.20) | copy-start | bytes 40
  7.3 9.3 %collective-permute-start.1 = (f32[72,128]{1,0:T(8,128)S(1)}, f32[72,128]{1,0:T(8,128)S(1)}, u32[]{:S(2)}, u32[]{:S(2)}) collective-permute-start(f32[72,128]{1,0:T(8,128)S(1)} %select_maximum_fusion._), channel_id=1, source_target_pairs={{1,2},{3,4},{5,6},{7,8},{9,10},{11,12},{13,14},{2,1},{4,3},{6,5},{... | collective-permute-start | bytes 110600 | tf_op jit(solution)/shard_map/ppermute | solution.py:509
  10.9 5.9 %copy-start = (s32[1,2]{1,0:T(1,128)S(1)}, s32[1,2]{1,0:T(1,128)}, u32[]{:S(2)}) copy-start(s32[1,2]{1,0:T(1,128)} %range_ref.5) | copy-start | bytes 28
  14.1 24.7 %collective-permute-start.6 = (f32[4,3,128,128]{3,2,1,0:T(8,128)}, f32[4,3,128,128]{3,2,1,0:T(8,128)}, u32[]{:S(2)}, u32[]{:S(2)}) collective-permute-start(f32[4,3,128,128]{3,2,1,0:T(8,128)} %outer.1), channel_id=1, source_target_pairs={{1,2},{3,4},{5,6},{7,8},{9,10},{11,12},{13,14},{2,1},{4,3},{6,5},{... | collective-permute-start | bytes 2359304 | tf_op jit(solution)/shard_map/ppermute | solution.py:509
  16.7 11.6 %copy-start.7 = (s32[64]{0:T(128)S(1)}, s32[64]{0:T(128)}, u32[]{:S(2)}) copy-start(s32[64]{0:T(128)} %fusion.19) | copy-start | bytes 772
  16.7 11.7 %copy-start.1 = (pred[64,64]{1,0:T(8,128)(4,1)S(1)}, pred[64,64]{1,0:T(8,128)(4,1)}, u32[]{:S(2)}) copy-start(pred[64,64]{1,0:T(8,128)(4,1)} %iota_compare_fusion.1) | copy-start | bytes 12292
  16.7 11.7 %copy-start.6 = (pred[3,64]{1,0:T(4,128)(4,1)S(1)}, pred[3,64]{1,0:T(4,128)(4,1)}, u32[]{:S(2)}) copy-start(pred[3,64]{1,0:T(4,128)(4,1)} %compare_and_fusion.1) | copy-start | bytes 580
  27.2 3.3 %collective-permute-start.2 = (f32[392,128]{1,0:T(8,128)S(1)}, f32[392,128]{1,0:T(8,128)S(1)}, u32[]{:S(2)}, u32[]{:S(2)}) collective-permute-start(f32[392,128]{1,0:T(8,128)S(1)} %get-tuple-element.10.mine), channel_id=1, source_target_pairs={{0,1},{2,3},{4,5},{6,7},{8,9},{10,11},{12,13},{14,15},{1,0},{3,2},... | collective-permute-start | bytes 602120 | tf_op jit(solution)/shard_map/ppermute | solution.py:509
  28.2 10.6 %collective-permute-start.5 = (f32[4,3,128,128]{3,2,1,0:T(8,128)}, f32[4,3,128,128]{3,2,1,0:T(8,128)}, u32[]{:S(2)}, u32[]{:S(2)}) collective-permute-start(f32[4,3,128,128]{3,2,1,0:T(8,128)} %get-tuple-element.14), channel_id=1, source_target_pairs={{0,1},{2,3},{4,5},{6,7},{8,9},{10,11},{12,13},{14,15},{1,0},{3,2},... | collective-permute-start | bytes 2359304 | tf_op jit(solution)/shard_map/ppermute | solution.py:509
  31.2 5.4 %collective-permute-start.3 = (f32[96,128]{1,0:T(8,128)S(1)}, f32[96,128]{1,0:T(8,128)S(1)}, u32[]{:S(2)}, u32[]{:S(2)}) collective-permute-start(f32[96,128]{1,0:T(8,128)S(1)} %get-tuple-element.12), channel_id=1, source_target_pairs={{1,2},{3,4},{5,6},{7,8},{9,10},{11,12},{13,14},{2,1},{4,3},{6,5},{... | collective-permute-start | bytes 147464 | tf_op jit(solution)/shard_map/ppermute | solution.py:509
  36.6 2.2 %collective-permute-start.4 = (f32[96,128]{1,0:T(8,128)S(1)}, f32[96,128]{1,0:T(8,128)S(1)}, u32[]{:S(2)}, u32[]{:S(2)}) collective-permute-start(f32[96,128]{1,0:T(8,128)S(1)} %collective-permute-done.3.crossed), channel_id=1, source_target_pairs={{0,1},{2,3},{4,5},{6,7},{8,9},{10,11},{12,13},{14,15},{1,0},{3,2},... | collective-permute-start | bytes 147464 | tf_op jit(solution)/shard_map/ppermute | solution.py:509

commit v6 on v5

--- a/solution.py
+++ b/solution.py
@@ -66,10 +66,11 @@
             weights[half * side : (half + 1) * side, n * side : (n + 1) * side] = block.astype(jnp.bfloat16)
 
 
-def inner_update(load, store, side, weights):
+def inner_update(loads, store, side, weights):
     line = iota(0, side)
     first, last = line == 0, line == ROWS - 1
     steps = side // ROWS
+    many = len(loads)
 
     def cell(h, mx, my, bed):
         root = lax.rsqrt(h)
@@ -94,35 +95,38 @@
     def taken(block):
         return weights[:, block.start * side : block.stop * side]
 
-    cells = [cell(*[load(f, j) for f in range(4)]) for j in range(steps)]
-    stack = lambda pick: jnp.concatenate([pick(c) for c in cells], axis=0)
-    rates = product(pieces(stack(lambda c: c[1])), taken(AHEAD))
-    eta, mx, my, cross, bed = (pieces(stack(lambda c, n=n: c[0][n])) for n in (1, 2, 3, 4, 6))
-    fx = pieces(stack(lambda c: c[2]))
-    jumps = [product(each, taken(EAST)) for each in (eta, mx, my)]
-    sums = [product(each, taken(SUMS)) for each in (mx, fx, cross)]
+    cells = [cell(*[load(f, j) for f in range(4)]) for load in loads for j in range(steps)]
+    stack = lambda pick: pieces(jnp.concatenate([pick(c) for c in cells], axis=0))
+    eta, mx, my, cross, bed = (stack(lambda c, n=n: c[0][n]) for n in (1, 2, 3, 4, 6))
+    fx = stack(lambda c: c[2])
+    rates = product(stack(lambda c: c[1]), taken(AHEAD))
+    jumps = product(jnp.concatenate([eta, mx, my], axis=0), taken(EAST))
+    sums = product(jnp.concatenate([mx, fx, cross], axis=0), taken(SUMS))
     slopes = product(bed, taken(SLOPE))
-    low = [pltpu.roll(each, 1, 0) for each in cells[steps - 1][0]]
-    faces = []
-    for j in range(steps):
-        faces.append(face_y(low, cells[j][0]))
-        low = cells[j][0]
-    faces[0] = [jnp.where(first, 0.0, each) for each in faces[0]]
-    beds = [c[0][6] for c in cells]
-    under = jnp.where(first, 0.0, pltpu.roll(beds[-1], 1, 0))
-    over = jnp.where(last, 0.0, pltpu.roll(beds[0], ROWS - 1, 0))
-    faces.append([jnp.where(last, 0.0, pltpu.roll(each, ROWS - 1, 0)) for each in faces[0]])
-    for j in range(steps):
-        (_, _, mx, my, _, _, _), rate, _, h = cells[j]
-        rows = slice(ROWS * j, ROWS * (j + 1))
-        top_e = jnp.maximum(rate, rates[rows, :side])
-        top_w = jnp.maximum(rate, rates[rows, side:])
-        x = [s[rows] - (top_e * d[rows, :side] - top_w * d[rows, side:]) for s, d in zip(sums, jumps)]
-        south, north = faces[j], faces[j + 1]
-        slope_y = (beds[j + 1] if j + 1 < steps else over) - (beds[j - 1] if j else under)
-        store(0, j, h - HALF * (x[0] + (north[0] - south[0])))
-        store(1, j, mx - HALF * (x[1] + h * slopes[rows] + (north[1] - south[1])))
-        store(2, j, my - HALF * (x[2] + h * slope_y + (north[2] - south[2])))
+    for n in range(many):
+        mine = cells[n * steps : (n + 1) * steps]
+        low = [pltpu.roll(each, 1, 0) for each in mine[steps - 1][0]]
+        faces = []
+        for j in range(steps):
+            faces.append(face_y(low, mine[j][0]))
+            low = mine[j][0]
+        faces[0] = [jnp.where(first, 0.0, each) for each in faces[0]]
+        beds = [c[0][6] for c in mine]
+        under = jnp.where(first, 0.0, pltpu.roll(beds[-1], 1, 0))
+        over = jnp.where(last, 0.0, pltpu.roll(beds[0], ROWS - 1, 0))
+        faces.append([jnp.where(last, 0.0, pltpu.roll(each, ROWS - 1, 0)) for each in faces[0]])
+        for j in range(steps):
+            (_, _, mx, my, _, _, _), rate, _, h = mine[j]
+            at = [(q * many + n) * side + ROWS * j for q in range(3)]
+            rows = [slice(r, r + ROWS) for r in at]
+            top_e = jnp.maximum(rate, rates[rows[0], :side])
+            top_w = jnp.maximum(rate, rates[rows[0], side:])
+            x = [sums[r] - (top_e * jumps[r, :side] - top_w * jumps[r, side:]) for r in rows]
+            south, north = faces[j], faces[j + 1]
+            slope_y = (beds[j + 1] if j + 1 < steps else over) - (beds[j - 1] if j else under)
+            store(n, 0, j, h - HALF * (x[0] + (north[0] - south[0])))
+            store(n, 1, j, mx - HALF * (x[1] + h * slopes[rows[0]] + (north[1] - south[1])))
+            store(n, 2, j, my - HALF * (x[2] + h * slope_y + (north[2] - south[2])))
 
 
 def gather_columns(loads, columns, first_at, side):
@@ -153,9 +157,8 @@
 
 
 def update(cells, first, many, weights, put):
-    for n in range(many):
-        store = lambda f, j, value, n=n: put(n, f, ROWS * j, value)
-        inner_update(loader(cells, first + n), store, cells.shape[3], weights)
+    loads = [loader(cells, first + n) for n in range(many)]
+    inner_update(loads, lambda n, f, j, value: put(n, f, ROWS * j, value), cells.shape[3], weights)
 
 
 def fetch(cells_hbm, first, cells, sems, parts):
@@ -173,15 +176,8 @@
     return odd * (cells_hbm.shape[0] - margin)
 
 
-def outer_edges_kernel(margin, cells_hbm, edges, cells, columns, sems):
-    copy = fetch(cells_hbm, outer_slot(cells_hbm, margin), cells, sems, [(0, margin)])
-    for i in range(margin):
-        copy(i).wait()
-    gather_columns([loader(cells, i) for i in range(margin)], columns, 0, columns.shape[0])
-    take_edges(margin, cells, lambda p: p, columns, edges, 0)
-
-
-def outer_kernel(margin, cells_hbm, _, out, cells, weights, sems):
+def outer_kernel(margin, cells_hbm, out, edges, cells, columns, weights, sems):
+    side = columns.shape[0]
     copy = fetch(cells_hbm, outer_slot(cells_hbm, margin), cells, sems, [(0, margin)])
     fill_weights(weights)
 
@@ -194,7 +190,10 @@
         def put(n, f, row, value):
             out[i + n, f, row : row + ROWS, :] = value
 
+        gather_columns([loader(cells, i + n) for n in range(PAIR)], columns, 8 * i, side)
         update(cells, i, PAIR, weights, put)
+
+    take_edges(margin, cells, lambda p: p, columns, edges, 0)
 
 
 def cost(patches, side):
@@ -209,39 +208,39 @@
     return pltpu.CompilerParams(vmem_limit_bytes=mebibytes << 20)
 
 
-def outer_edges(old_cells, margin):
+def outer_patches(old_cells, margin):
     side = old_cells.shape[3]
     return pl.pallas_call(
-        functools.partial(outer_edges_kernel, margin),
+        functools.partial(outer_kernel, margin),
         in_specs=[HBM],
-        out_specs=VMEM,
-        out_shape=jax.ShapeDtypeStruct((16 * margin, side), jnp.float32),
+        out_specs=[VMEM, VMEM],
+        out_shape=[
+            jax.ShapeDtypeStruct((margin, 3, side, side), jnp.float32),
+            jax.ShapeDtypeStruct((16 * margin, side), jnp.float32),
+        ],
         scratch_shapes=[
             pltpu.VMEM((margin, 4, side, side), jnp.float32),
             pltpu.VMEM((side, side), jnp.float32),
-            pltpu.SemaphoreType.DMA((margin,)),
-        ],
-        compiler_params=room(48),
-        name="outer_edges",
-    )(old_cells)
-
-
-def outer_patches(old_cells, before, margin):
-    side = old_cells.shape[3]
-    return pl.pallas_call(
-        functools.partial(outer_kernel, margin),
-        in_specs=[HBM, HBM],
-        out_specs=VMEM,
-        out_shape=jax.ShapeDtypeStruct((margin, 3, side, side), jnp.float32),
-        scratch_shapes=[
-            pltpu.VMEM((margin, 4, side, side), jnp.float32),
             pltpu.VMEM((2 * side, 6 * side), jnp.bfloat16),
             pltpu.SemaphoreType.DMA((margin,)),
         ],
         cost_estimate=cost(margin, side),
         compiler_params=room(48),
         name="outer",
-    )(old_cells, before)
+    )(old_cells)
+
+
+def after(value, other):
+    any_place = pl.BlockSpec(memory_space=pl.ANY)
+    return pl.pallas_call(
+        lambda value_ref, other_ref, out_ref: None,
+        in_specs=[any_place, any_place],
+        out_specs=any_place,
+        out_shape=jax.ShapeDtypeStruct(value.shape, value.dtype),
+        input_output_aliases={0: 0},
+        compiler_params=room(4),
+        name="after",
+    )(value, other)
 
 
 def layout(margin, per_device):
@@ -523,7 +522,7 @@
     me, odd = position()
 
     their_table = swapped(neighbours, 0)
-    leaving_edges = outer_edges(old_cells, margin)
+    leaving, leaving_edges = outer_patches(old_cells, margin)
 
     tables = jnp.where(
         odd == 0,
@@ -534,7 +533,7 @@
     bundle = jnp.concatenate([leaving_edges, tables], axis=0)
     came = swapped(bundle, 1)
 
-    arrived = swapped(outer_patches(old_cells, bundle, margin), 1)
+    arrived = swapped(after(leaving, bundle), 1)
 
     shared, inner, own = home_patches(old_range, old_cells, came, margin, per_device)
     their_edges = swapped(shared, 0)

time: 43.5 us -> 41.6 us (0.956)
  Pallas kernels: 20.1 us -> 18.1 us
  waiting for transfers between devices: 1.38 us -> 2.34 us
  starting transfers between devices: 12.1 us -> 11.3 us
    pallas_call x2, Pallas kernels: 4.93 us -> 3.41 us  [the longest x1 3.41 us: outer_patches(): pl.pallas_call(functools.partial(outer_kernel, margin), in_specs=[HBM], o...]
    ppermute x7, waiting for transfers between devices: 1.38 us -> 2.34 us  [swapped(): return lax.ppermute(value, AXES, pairs + [(j, i) for i, j in pairs])]
    ppermute x7, starting transfers between devices: 12.1 us -> 11.3 us  [swapped(): return lax.ppermute(value, AXES, pairs + [(j, i) for i, j in pairs])]
    pallas_call x1, Pallas kernels: 10.5 us -> 10 us  [home_patches(): pl.pallas_call(functools.partial(home_kernel, margin), in_specs=[SMEM, HB...]
  transfers between devices with their start and end apart: 7 -> 7, of which waited for: 2 -> 2; matrix products, arithmetic and copies ran while one was open for 20% -> 22% of each run, Pallas kernels for 37% -> 34%
where the time goes in v6:
time: 41.6 us; the launch traced here: 41.1 us
  Pallas kernels  18.1 us (44%)
  starting transfers between devices  11.3 us (27%)
  other arithmetic  6.73 us (16%)
  local copies, waits for them, and re-layouts  2.46 us (6%)
  waiting for transfers between devices  2.34 us (6%)
    ppermute x7, starting transfers between devices, swapped(): return lax.ppermute(value, AXES, pairs + [(j, i) for i, j in pairs])  11.3 us
    pallas_call x1, Pallas kernels, home_patches(): pl.pallas_call(functools.partial(home_kernel, margin), in_specs=[SMEM, HB...  10 us
    pallas_call x1, Pallas kernels, finished(): pl.pallas_call(functools.partial(final_kernel, margin), in_specs=[SMEM, S...  4.07 us
    pallas_call x1, Pallas kernels, outer_patches(): pl.pallas_call(functools.partial(outer_kernel, margin), in_specs=[HBM], o...  3.41 us
    ppermute x7, waiting for transfers between devices, swapped(): return lax.ppermute(value, AXES, pairs + [(j, i) for i, j in pairs])  2.34 us
  transfers between devices with their start and end apart: 7, of which 2 were waited for; matrix products, arithmetic and copies ran while one was open for 22% of the time, Pallas kernels for 34%

profile of v6, /device:TPU:17, one launch (start us, length us, event | category | flops | bytes accessed | tf_op | source)
XLA Modules:
  0.0 41.1 jit_solution(8118180489244909762)
XLA Ops:
  0.0 0.7 %collective-permute-start = (s32[16,4]{0,1:T(4,128)}, s32[16,4]{0,1:T(4,128)S(1)}, u32[]{:S(2)}, u32[]{:S(2)}) collective-permute-start(s32[16,4]{0,1:T(4,128)} %param.9), channel_id=1, source_target_pairs={{0,1},{2,3},{4,5},{6,7},{8,9},{10,11},{12,13},{14,15},{1,0},{3,2},... | collective-permute-start | bytes 776 | tf_op jit(solution)/shard_map/ppermute | solution.py:508
  0.7 0.8 %copy.15 = s32[16,4]{1,0:T(8,128)S(1)} copy(s32[16,4]{0,1:T(4,128)} %param.9) | data formatting | bytes 512 | tf_op args[2]
  1.4 0.1 reshape.513
  1.5 0.0 copy-start.2
  1.5 0.0 copy-start.5
  1.6 0.5 %broadcast_subtract_fusion = (s32[64]{0:T(128)S(1)}, s32[64]{0:T(128)}) fusion(s32[]{:T(128)S(6)} %add.120, s32[64]{0:T(128)S(1)} %reshape.513), kind=kLoop, calls=%fused_computation.68 | loop fusion | flops 1024 | bytes 772 | tf_op jit(solution)/shard_map/sub | solution.py:566
  2.1 0.0 copy-start.3
  2.1 0.6 %iota_compare_fusion.1 = pred[64,64]{1,0:T(8,128)(4,1)} fusion(), kind=kLoop, calls=%fused_computation.4 | loop fusion | flops 4096 | bytes 4096 | tf_op jit(solution)/shard_map/lt | solution.py:513
  2.7 0.7 %broadcast_select_fusion.3 = s32[3,2]{0,1:T(2,128)S(1)} fusion(s32[3,2]{0,1:T(2,128)} %constant.147.clone, s32[3,2]{0,1:T(2,128)} %constant.148.clone, pred[]{:T(512)S(6)} %eq.69), kind=kLoop, calls=%fused_computation.52 | loop fusion | flops 6 | bytes 73 | tf_op jit(solution)/shard_map/jit(_where)/select_n | solution.py:561
  3.4 0.6 %slice_bitcast_fusion = (s32[3]{0:T(128)}, s32[3]{0:T(128)S(1)}) fusion(s32[3,2]{0,1:T(2,128)S(1)} %broadcast_select_fusion.3), kind=kLoop, calls=%fused_computation.65 | loop fusion | bytes 48 | tf_op jit(solution)/shard_map/add | solution.py:568
  3.9 0.0 copy-start.4
  3.9 0.7 %fusion.12 = s32[3]{0:T(128)S(1)} fusion(s32[3]{0:T(128)} %constant.145.clone, s32[3]{0:T(128)} %constant.146.clone, pred[]{:T(512)S(6)} %eq.69, s32[]{:T(128)S(6)} %add.120), kind=kLoop, calls=%fused_computation.58 | loop fusion | flops 6 | bytes 41 | tf_op jit(solution)/shard_map/add | solution.py:548
  4.6 0.0 copy-done.4
  4.6 0.6 %compare_and_fusion.1 = pred[3,64]{1,0:T(4,128)(4,1)} fusion(s32[64]{0:T(128)S(1)} %get-tuple-element.21, s32[3]{0:T(128)S(1)} %get-tuple-element.24, pred[64]{0:T(512)(128)(4,1)S(1)} %broadcast_compare_fusion), kind=kLoop, calls=%fused_computation.32 | loop fusion | flops 384 | bytes 524 | tf_op jit(solution)/shard_map/and | solution.py:566
  5.2 0.0 copy-start
  5.2 3.4 %outer.1 = (f32[4,3,128,128]{3,2,1,0:T(8,128)}, f32[64,128]{1,0:T(8,128)S(1)}) custom-call(f32[24,4,128,128]{3,2,1,0:T(8,128)} %cells_hbm.3), custom_call_target="tpu_custom_call" | custom-call | flops 52428800 | bytes 1835008 | tf_op jit(solution)/shard_map/outer/pallas_call | solution.py:213
  8.6 0.0 copy-done.5
  8.7 0.1 concatenate.65
  8.7 0.0 collective-permute-done
  8.8 0.1 copy.17
  8.8 0.1 concatenate.66
  8.9 0.1 fusion.11
  9.0 0.0 copy-done.2
  9.0 0.0 copy-done.3
  9.0 3.0 %collective-permute-start.1 = (f32[72,128]{1,0:T(8,128)S(1)}, f32[72,128]{1,0:T(8,128)S(1)}, u32[]{:S(2)}, u32[]{:S(2)}) collective-permute-start(f32[72,128]{1,0:T(8,128)S(1)} %select_maximum_fusion.other_ref), channel_id=1, source_target_pairs={{1,2},{3,4},{5,6},{7,8},{9,10},{11,12},{13,14},{2,1},{4,3},{6,5},{... | collective-permute-start | bytes 110600 | tf_op jit(solution)/shard_map/ppermute | solution.py:508
  12.0 0.6 %fusion.19 = s32[64]{0:T(128)} fusion(), kind=kLoop, calls=%fused_computation.70 | loop fusion | flops 1728 | bytes 256 | tf_op jit(solution)/shard_map/add | solution.py:544
  12.6 2.5 %collective-permute-start.6 = (f32[4,3,128,128]{3,2,1,0:T(8,128)}, f32[4,3,128,128]{3,2,1,0:T(8,128)}, u32[]{:S(2)}, u32[]{:S(2)}) collective-permute-start(f32[4,3,128,128]{3,2,1,0:T(8,128)} %after.1), channel_id=1, source_target_pairs={{1,2},{3,4},{5,6},{7,8},{9,10},{11,12},{13,14},{2,1},{4,3},{6,5},{... | collective-permute-start | bytes 2359304 | tf_op jit(solution)/shard_map/ppermute | solution.py:508
  15.2 0.0 collective-permute-done.1.came
  15.2 0.1 fusion.20
  15.3 0.0 copy-done
  15.3 0.0 copy-start.7
  15.3 0.0 copy-start.1
  15.3 0.0 copy-start.6
  15.3 10.0 %home.1 = (f32[392,128]{1,0:T(8,128)S(1)}, f32[4,3,128,128]{3,2,1,0:T(8,128)}, f32[16,3,128,128]{3,2,1,0:T(8,128)S(1)}) custom-call(s32[1,2]{1,0:T(1,128)S(1)} %copy-done, f32[24,4,128,128]{3,2,1,0:T(8,128)} %cells_hbm.3, f32[72,128]{1,0:T(8,128)S(1)} %collective-permute-done.1.came), custom_call_target="tpu_custom_call" | custom-call | flops 262144000 | bytes 9175040 | tf_op jit(solution)/shard_map/home/pallas_call | solution.py:288
  25.3 1.0 %collective-permute-start.2 = (f32[392,128]{1,0:T(8,128)S(1)}, f32[392,128]{1,0:T(8,128)S(1)}, u32[]{:S(2)}, u32[]{:S(2)}) collective-permute-start(f32[392,128]{1,0:T(8,128)S(1)} %get-tuple-element.13.mine), channel_id=1, source_target_pairs={{0,1},{2,3},{4,5},{6,7},{8,9},{10,11},{12,13},{14,15},{1,0},{3,2},... | collective-permute-start | bytes 602120 | tf_op jit(solution)/shard_map/ppermute | solution.py:508
  26.3 0.1 collective-permute-start.5
  26.3 0.0 copy-done.7
  26.3 0.1 compare_and_fusion
  26.4 0.0 copy-done.1
  26.4 0.0 copy-done.6
  26.4 0.7 %select_reduce_fusion = (s32[3,64]{1,0:T(4,128)S(1)}, s32[3,64]{1,0:T(4,128)}) fusion(pred[3,64]{1,0:T(4,128)(4,1)S(1)} %compare_and_fusion, pred[64,64]{1,0:T(8,128)(4,1)S(1)} %copy-done.1, pred[3,64]{1,0:T(4,128)(4,1)S(1)} %copy-done.6), kind=kLoop, calls=%fused_computation | loop fusion | flops 73344 | bytes 6016 | tf_op jit(solution)/shard_map/reduce_sum | solution.py:514
  27.1 0.7 %select_reduce_fusion.2 = s32[3,8]{1,0:T(4,128)} fusion(s32[3,64]{1,0:T(4,128)S(1)} %multiply_add_fusion, s32[3,64]{1,0:T(4,128)S(1)} %get-tuple-element.19, pred[3,64]{1,0:T(4,128)(4,1)S(1)} %compare_and_fusion), kind=kLoop, calls=%fused_computation.5 | loop fusion | flops 6120 | bytes 1824 | tf_op jit(solution)/shard_map/reduce_sum | solution.py:552
  27.8 0.8 %reshape.514.rows_ref = s32[24]{0:T(128)S(1)} reshape(s32[3,8]{1,0:T(4,128)} %select_reduce_fusion.2) | data formatting | bytes 192 | tf_op jit(solution)/shard_map/reshape | solution.py:552
  28.6 0.0 collective-permute-done.2.theirs
  28.6 0.7 %answers.1 = (f32[512,128]{1,0:T(8,128)S(1)}, f32[96,128]{1,0:T(8,128)S(1)}) custom-call(s32[1,2]{1,0:T(1,128)S(1)} %copy-done, s32[24]{0:T(128)S(1)} %reshape.514.rows_ref, f32[392,128]{1,0:T(8,128)S(1)} %get-tuple-element.13.mine, f32[392,128]{1,0:T(8,128)S(1)} %collective-permute-done.2.theirs), custom_call_target="tpu_custom_call" | custom-call | tf_op jit(solution)/shard_map/answers/pallas_call | solution.py:358
  29.3 3.5 %collective-permute-start.3 = (f32[96,128]{1,0:T(8,128)S(1)}, f32[96,128]{1,0:T(8,128)S(1)}, u32[]{:S(2)}, u32[]{:S(2)}) collective-permute-start(f32[96,128]{1,0:T(8,128)S(1)} %get-tuple-element.15), channel_id=1, source_target_pairs={{1,2},{3,4},{5,6},{7,8},{9,10},{11,12},{13,14},{2,1},{4,3},{6,5},{... | collective-permute-start | bytes 147464 | tf_op jit(solution)/shard_map/ppermute | solution.py:508
  32.8 0.8 %fusion.10 = s32[64]{0:T(128)S(1)} fusion(s32[3,64]{1,0:T(4,128)} %get-tuple-element.20, s32[3]{0:T(128)} %get-tuple-element.23, s32[3]{0:T(128)} %copy-done.4, s32[64]{0:T(128)} %copy-done.3, pred[64]{0:T(512)(128)(4,1)} %copy-done.5), kind=kLoop, calls=%fused_computation.31 | loop fusion | flops 4928 | bytes 1368 | tf_op jit(solution)/shard_map/reduce_sum | solution.py:568
  33.5 2.1 %collective-permute-done.3.crossed = f32[96,128]{1,0:T(8,128)S(1)} collective-permute-done((f32[96,128]{1,0:T(8,128)S(1)}, f32[96,128]{1,0:T(8,128)S(1)}, u32[]{:S(2)}, u32[]{:S(2)}) %collective-permute-start.3) | collective-permute-done | bytes 49184 | tf_op jit(solution)/shard_map/ppermute | solution.py:508
  35.6 0.5 %collective-permute-start.4 = (f32[96,128]{1,0:T(8,128)S(1)}, f32[96,128]{1,0:T(8,128)S(1)}, u32[]{:S(2)}, u32[]{:S(2)}) collective-permute-start(f32[96,128]{1,0:T(8,128)S(1)} %collective-permute-done.3.crossed), channel_id=1, source_target_pairs={{0,1},{2,3},{4,5},{6,7},{8,9},{10,11},{12,13},{14,15},{1,0},{3,2},... | collective-permute-start | bytes 147464 | tf_op jit(solution)/shard_map/ppermute | solution.py:508
  36.1 0.6 %compare_select_fusion.7.rows_ref = s32[64]{0:T(128)S(1)} fusion(s32[64]{0:T(128)} %copy-done.2, s32[64]{0:T(128)S(1)} %fusion.10, s32[64]{0:T(128)} %get-tuple-element.22, s32[]{:T(128)S(6)} %mul.42, s32[]{:T(128)S(6)} %select_n.156, s32[]{:T(128)S(6)} %mul_shard_map.3), kind=kLoop, calls=%fused_computation.56 | loop fusion | flops 3904 | bytes 1036 | tf_op jit(solution)/shard_map/jit(_where)/select_n | solution.py:571
  36.7 0.3 collective-permute-done.4.passed
  37.0 0.0 collective-permute-done.6.arrived
  37.0 0.0 collective-permute-done.5.theirs
  37.0 4.1 %final.1 = f32[16,3,128,128]{3,2,1,0:T(8,128)} custom-call(s32[1,2]{1,0:T(1,128)S(1)} %copy-done, s32[64]{0:T(128)S(1)} %compare_select_fusion.7.rows_ref, f32[512,128]{1,0:T(8,128)S(1)} %get-tuple-element.14.edges, f32[96,128]{1,0:T(8,128)S(1)} %collective-permute-done.3.crossed, f32[96,128]{1,0:T(8,128)S(1)} %collective-permute-done.4.passed, ...), custom_call_target="tpu_custom_call" | custom-call | tf_op jit(solution)/shard_map/final/pallas_call | solution.py:486
  (5 shorter events, 0.0 us)
Async XLA Ops:
  0.0 8.7 %collective-permute-start = (s32[16,4]{0,1:T(4,128)}, s32[16,4]{0,1:T(4,128)S(1)}, u32[]{:S(2)}, u32[]{:S(2)}) collective-permute-start(s32[16,4]{0,1:T(4,128)} %param.9), channel_id=1, source_target_pairs={{0,1},{2,3},{4,5},{6,7},{8,9},{10,11},{12,13},{14,15},{1,0},{3,2},... | collective-permute-start | bytes 776 | tf_op jit(solution)/shard_map/ppermute | solution.py:508
  1.5 7.5 %copy-start.2 = (s32[64]{0:T(128)}, s32[64]{0:T(128)S(1)}, u32[]{:S(2)}) copy-start(s32[64]{0:T(128)S(1)} %reshape.513) | copy-start | bytes 772
  1.5 7.1 %copy-start.5 = (pred[64]{0:T(512)(128)(4,1)}, pred[64]{0:T(512)(128)(4,1)S(1)}, u32[]{:S(2)}) copy-start(pred[64]{0:T(512)(128)(4,1)S(1)} %broadcast_compare_fusion) | copy-start | bytes 196
  2.1 6.9 %copy-start.3 = (s32[64]{0:T(128)}, s32[64]{0:T(128)S(1)}, u32[]{:S(2)}) copy-start(s32[64]{0:T(128)S(1)} %get-tuple-element.21) | copy-start | bytes 772
  3.9 0.7 %copy-start.4 = (s32[3]{0:T(128)}, s32[3]{0:T(128)S(1)}, u32[]{:S(2)}) copy-start(s32[3]{0:T(128)S(1)} %get-tuple-element.24) | copy-start | bytes 40
  5.2 10.0 %copy-start = (s32[1,2]{1,0:T(1,128)S(1)}, s32[1,2]{1,0:T(1,128)}, u32[]{:S(2)}) copy-start(s32[1,2]{1,0:T(1,128)} %range_ref.5) | copy-start | bytes 28
  9.0 6.2 %collective-permute-start.1 = (f32[72,128]{1,0:T(8,128)S(1)}, f32[72,128]{1,0:T(8,128)S(1)}, u32[]{:S(2)}, u32[]{:S(2)}) collective-permute-start(f32[72,128]{1,0:T(8,128)S(1)} %select_maximum_fusion.other_ref), channel_id=1, source_target_pairs={{1,2},{3,4},{5,6},{7,8},{9,10},{11,12},{13,14},{2,1},{4,3},{6,5},{... | collective-permute-start | bytes 110600 | tf_op jit(solution)/shard_map/ppermute | solution.py:508
  12.6 24.4 %collective-permute-start.6 = (f32[4,3,128,128]{3,2,1,0:T(8,128)}, f32[4,3,128,128]{3,2,1,0:T(8,128)}, u32[]{:S(2)}, u32[]{:S(2)}) collective-permute-start(f32[4,3,128,128]{3,2,1,0:T(8,128)} %after.1), channel_id=1, source_target_pairs={{1,2},{3,4},{5,6},{7,8},{9,10},{11,12},{13,14},{2,1},{4,3},{6,5},{... | collective-permute-start | bytes 2359304 | tf_op jit(solution)/shard_map/ppermute | solution.py:508
  15.3 11.1 %copy-start.7 = (s32[64]{0:T(128)S(1)}, s32[64]{0:T(128)}, u32[]{:S(2)}) copy-start(s32[64]{0:T(128)} %fusion.19) | copy-start | bytes 772
  15.3 11.2 %copy-start.1 = (pred[64,64]{1,0:T(8,128)(4,1)S(1)}, pred[64,64]{1,0:T(8,128)(4,1)}, u32[]{:S(2)}) copy-start(pred[64,64]{1,0:T(8,128)(4,1)} %iota_compare_fusion.1) | copy-start | bytes 12292
  15.3 11.2 %copy-start.6 = (pred[3,64]{1,0:T(4,128)(4,1)S(1)}, pred[3,64]{1,0:T(4,128)(4,1)}, u32[]{:S(2)}) copy-start(pred[3,64]{1,0:T(4,128)(4,1)} %compare_and_fusion.1) | copy-start | bytes 580
  25.3 3.3 %collective-permute-start.2 = (f32[392,128]{1,0:T(8,128)S(1)}, f32[392,128]{1,0:T(8,128)S(1)}, u32[]{:S(2)}, u32[]{:S(2)}) collective-permute-start(f32[392,128]{1,0:T(8,128)S(1)} %get-tuple-element.13.mine), channel_id=1, source_target_pairs={{0,1},{2,3},{4,5},{6,7},{8,9},{10,11},{12,13},{14,15},{1,0},{3,2},... | collective-permute-start | bytes 602120 | tf_op jit(solution)/shard_map/ppermute | solution.py:508
  26.3 10.7 %collective-permute-start.5 = (f32[4,3,128,128]{3,2,1,0:T(8,128)}, f32[4,3,128,128]{3,2,1,0:T(8,128)}, u32[]{:S(2)}, u32[]{:S(2)}) collective-permute-start(f32[4,3,128,128]{3,2,1,0:T(8,128)} %get-tuple-element.17), channel_id=1, source_target_pairs={{0,1},{2,3},{4,5},{6,7},{8,9},{10,11},{12,13},{14,15},{1,0},{3,2},... | collective-permute-start | bytes 2359304 | tf_op jit(solution)/shard_map/ppermute | solution.py:508
  29.3 6.4 %collective-permute-start.3 = (f32[96,128]{1,0:T(8,128)S(1)}, f32[96,128]{1,0:T(8,128)S(1)}, u32[]{:S(2)}, u32[]{:S(2)}) collective-permute-start(f32[96,128]{1,0:T(8,128)S(1)} %get-tuple-element.15), channel_id=1, source_target_pairs={{1,2},{3,4},{5,6},{7,8},{9,10},{11,12},{13,14},{2,1},{4,3},{6,5},{... | collective-permute-start | bytes 147464 | tf_op jit(solution)/shard_map/ppermute | solution.py:508
  35.6 1.4 %collective-permute-start.4 = (f32[96,128]{1,0:T(8,128)S(1)}, f32[96,128]{1,0:T(8,128)S(1)}, u32[]{:S(2)}, u32[]{:S(2)}) collective-permute-start(f32[96,128]{1,0:T(8,128)S(1)} %collective-permute-done.3.crossed), channel_id=1, source_target_pairs={{0,1},{2,3},{4,5},{6,7},{8,9},{10,11},{12,13},{14,15},{1,0},{3,2},... | collective-permute-start | bytes 147464 | tf_op jit(solution)/shard_map/ppermute | solution.py:508

commit v7 on v6

--- a/solution.py
+++ b/solution.py
@@ -508,9 +508,12 @@
     return lax.ppermute(value, AXES, pairs + [(j, i) for i, j in pairs])
 
 
-def ranks(named):
-    size = named.shape[-1]
-    earlier = jnp.arange(size)[:, None] < jnp.arange(size)[None, :]
+def late(value, anchor):
+    return lax.optimization_barrier((value, anchor))[0]
+
+
+def ranks(named, entry):
+    earlier = entry[:, None] < entry[None, :]
     return jnp.sum(jnp.where(named[..., :, None] & earlier, 1, 0), axis=-2)
 
 
@@ -524,10 +527,12 @@
     their_table = swapped(neighbours, 0)
     leaving, leaving_edges = outer_patches(old_cells, margin)
 
+    table = late(neighbours, leaving_edges).reshape(1, -1)
+    their_table = their_table.reshape(1, -1)
     tables = jnp.where(
         odd == 0,
-        jnp.concatenate([neighbours.reshape(1, -1), their_table.reshape(1, -1)], axis=1),
-        jnp.concatenate([their_table.reshape(1, -1), neighbours.reshape(1, -1)], axis=1),
+        jnp.concatenate([table, their_table], axis=1),
+        jnp.concatenate([their_table, table], axis=1),
     ).astype(jnp.float32)
     tables = jnp.pad(tables, ((0, 7), (0, side - 2 * entries)))
     bundle = jnp.concatenate([leaving_edges, tables], axis=0)
@@ -539,23 +544,28 @@
     their_edges = swapped(shared, 0)
     theirs = swapped(inner, 0)
 
-    entry = jnp.arange(entries, dtype=jnp.int32)
+    me, entry, asked_by = late((me, jnp.arange(entries, dtype=jnp.int32), came), shared)
+    odd = lax.rem(me, 2)
     entry_side = entry % 4
     at_side = 8 * (entry_side // 2) + entry_side % 2
-    asked_by = came[16 * margin, : 2 * entries].astype(jnp.int32).reshape(2, entries)
+    asked_by = asked_by[16 * margin, : 2 * entries].astype(jnp.int32).reshape(2, entries)
     middle = jnp.where(odd == 0, asked_by[1], asked_by[0])
     listed = jnp.stack([asked_by[0], middle, asked_by[1]])
     owners = me + jnp.where(odd == 0, jnp.array([0, 0, 1], jnp.int32), jnp.array([-1, 0, 0], jnp.int32))
     asked = (listed >= 0) & (listed // per_device == owners[:, None])
     rows = 16 * (listed - 2 * per_device * (me // 2)) + at_side
-    chosen = asked[:, None, :] & (ranks(asked)[:, None, :] == jnp.arange(CAP)[None, :, None])
+    chosen = asked[:, None, :] & (ranks(asked, entry)[:, None, :] == jnp.arange(CAP)[None, :, None])
     send_rows = jnp.sum(jnp.where(chosen, rows[:, None, :], 0), axis=2).reshape(-1)
 
     edges, message = answers(old_range, send_rows, shared, their_edges, margin, per_device)
     crossed = swapped(message, 1)
     passed = swapped(crossed, 0)
 
-    listed = neighbours.reshape(-1)
+    me, entry, listed = late((me, entry, neighbours), message)
+    odd = lax.rem(me, 2)
+    entry_side = entry % 4
+    at_side = 8 * (entry_side // 2) + entry_side % 2
+    listed = listed.reshape(-1)
     owner = listed // per_device
     mine, total, step = 32 * per_device, 16 * per_device, 12 * CAP
     lists = jnp.where(
@@ -564,7 +574,7 @@
         jnp.array([[-2, mine + step + 8 * CAP], [1, mine + 4 * CAP], [2, mine + 8 * CAP]], jnp.int32),
     )
     named = (listed >= 0) & (owner - me == lists[:, :1])
-    place = ranks(named)
+    place = ranks(named, entry)
     across = jnp.sum(jnp.where(named, lists[:, 1:] + 8 * (place // 2) + place % 2, 0), axis=0)
     within = 16 * (listed - 2 * per_device * (me // 2)) + at_side
     wall = total * odd + 16 * (entry // 4) + 8 * (entry_side // 2) + 1 - entry_side % 2

time: 41.6 us -> 45.8 us (1.10)
  local copies, waits for them, and re-layouts: 2.46 us -> 6.08 us
  waiting for transfers between devices: 2.34 us -> 0.55 us
  Pallas kernels: 18.1 us -> 18.9 us
  other arithmetic: 6.73 us -> 7.47 us
  starting transfers between devices: 11.3 us -> 11.9 us
    unnamed x17 -> x18, local copies, waits for them, and re-layouts: 0.79 us -> 4.14 us
    ppermute x7, waiting for transfers between devices: 2.34 us -> 0.55 us  [swapped(): return lax.ppermute(value, AXES, pairs + [(j, i) for i, j in pairs])]
    lt x1 -> x2, other arithmetic: 0.61 us -> 1.46 us  [ranks(): earlier = entry[:, None] < entry[None, :]]
    optimization_barrier x0 -> x2, local copies, waits for them, and re-layouts: none -> 0.84 us  [late(): return lax.optimization_barrier((value, anchor))[0]]
    reduce_sum x1, other arithmetic: 0.78 us -> 0.09 us  [local(): jnp.sum(jnp.where(named, lists[:, 1:] + 8 * (place // 2) + place % 2, 0),...]
    convert_element_type x2, other arithmetic: 0.08 us -> 0.75 us  [the longest x1 0.67 us: local(): asked_by[16 * margin, :2 * entries].astype(jnp.int32).reshape(2, entries)]
    add x1, other arithmetic: 0.01 us -> 0.68 us  [local(): rows = 16 * (listed - 2 * per_device * (me // 2)) + at_side]
    ppermute x7, starting transfers between devices: 11.3 us -> 11.9 us  [swapped(): return lax.ppermute(value, AXES, pairs + [(j, i) for i, j in pairs])]
  transfers between devices with their start and end apart: 7 -> 7, of which waited for: 2 -> 3; matrix products, arithmetic and copies ran while one was open for 22% -> 20% of each run, Pallas kernels for 34% -> 33%
where the time goes in v7:
time: 45.8 us; the launch traced here: 45 us
  Pallas kernels  18.9 us (41%)
  starting transfers between devices  11.9 us (26%)
  other arithmetic  7.47 us (16%)
  local copies, waits for them, and re-layouts  6.08 us (13%)
  waiting for transfers between devices  0.55 us (1%)
    ppermute x7, starting transfers between devices, swapped(): return lax.ppermute(value, AXES, pairs + [(j, i) for i, j in pairs])  11.9 us
    pallas_call x1, Pallas kernels, home_patches(): pl.pallas_call(functools.partial(home_kernel, margin), in_specs=[SMEM, HB...  10.3 us
    pallas_call x1, Pallas kernels, finished(): pl.pallas_call(functools.partial(final_kernel, margin), in_specs=[SMEM, S...  4.24 us
    unnamed x18, local copies, waits for them, and re-layouts  4.14 us
    pallas_call x1, Pallas kernels, outer_patches(): pl.pallas_call(functools.partial(outer_kernel, margin), in_specs=[HBM], o...  3.64 us
    lt x2, other arithmetic, ranks(): earlier = entry[:, None] < entry[None, :]  1.46 us
  transfers between devices with their start and end apart: 7, of which 3 were waited for; matrix products, arithmetic and copies ran while one was open for 20% of the time, Pallas kernels for 33%

profile of v7, /device:TPU:17, one launch (start us, length us, event | category | flops | bytes accessed | tf_op | source)
XLA Modules:
  0.0 45.0 jit_solution(7576143678240045763)
XLA Ops:
  0.0 0.7 %collective-permute-start = (s32[16,4]{0,1:T(4,128)}, s32[16,4]{0,1:T(4,128)S(1)}, u32[]{:S(2)}, u32[]{:S(2)}) collective-permute-start(s32[16,4]{0,1:T(4,128)} %param.9), channel_id=1, source_target_pairs={{0,1},{2,3},{4,5},{6,7},{8,9},{10,11},{12,13},{14,15},{1,0},{3,2},... | collective-permute-start | bytes 776 | tf_op jit(solution)/shard_map/ppermute | solution.py:508
  0.7 0.0 copy-start.8
  0.7 0.0 copy-start.5
  0.7 3.6 %outer.1 = (f32[4,3,128,128]{3,2,1,0:T(8,128)}, f32[64,128]{1,0:T(8,128)S(1)}) custom-call(f32[24,4,128,128]{3,2,1,0:T(8,128)} %cells_hbm.3), custom_call_target="tpu_custom_call" | custom-call | flops 52428800 | bytes 1835008 | tf_op jit(solution)/shard_map/outer/pallas_call | solution.py:213
  4.3 0.0 copy-done.8
  4.3 0.1 copy.15
  4.4 0.1 concatenate.65
  4.5 0.0 collective-permute-done
  4.5 0.1 copy.16
  4.6 0.1 concatenate.66
  4.7 0.1 fusion.12
  4.8 3.0 %collective-permute-start.1 = (f32[72,128]{1,0:T(8,128)S(1)}, f32[72,128]{1,0:T(8,128)S(1)}, u32[]{:S(2)}, u32[]{:S(2)}) collective-permute-start(f32[72,128]{1,0:T(8,128)S(1)} %select_maximum_fusion.other_ref), channel_id=1, source_target_pairs={{1,2},{3,4},{5,6},{7,8},{9,10},{11,12},{13,14},{2,1},{4,3},{6,5},{... | collective-permute-start | bytes 110600 | tf_op jit(solution)/shard_map/ppermute | solution.py:508
  7.8 2.6 %collective-permute-start.6 = (f32[4,3,128,128]{3,2,1,0:T(8,128)}, f32[4,3,128,128]{3,2,1,0:T(8,128)}, u32[]{:S(2)}, u32[]{:S(2)}) collective-permute-start(f32[4,3,128,128]{3,2,1,0:T(8,128)} %after.1), channel_id=1, source_target_pairs={{1,2},{3,4},{5,6},{7,8},{9,10},{11,12},{13,14},{2,1},{4,3},{6,5},{... | collective-permute-start | bytes 2359304 | tf_op jit(solution)/shard_map/ppermute | solution.py:508
  10.4 0.2 collective-permute-done.1.came
  10.6 0.0 copy-done.5
  10.6 0.0 copy-start.4
  10.6 10.3 %home.1 = (f32[392,128]{1,0:T(8,128)S(1)}, f32[4,3,128,128]{3,2,1,0:T(8,128)S(1)}, f32[16,3,128,128]{3,2,1,0:T(8,128)S(1)}) custom-call(s32[1,2]{1,0:T(1,128)S(1)} %copy-done.5, f32[24,4,128,128]{3,2,1,0:T(8,128)} %cells_hbm.3, f32[72,128]{1,0:T(8,128)S(1)} %collective-permute-done.1.came), custom_call_target="tpu_custom_call" | custom-call | flops 262144000 | bytes 9175040 | tf_op jit(solution)/shard_map/home/pallas_call | solution.py:288
  20.9 0.0 copy-done.4
  20.9 0.0 copy-start.6
  20.9 0.9 %copy-done.6 = f32[4,3,128,128]{3,2,1,0:T(8,128)} copy-done((f32[4,3,128,128]{3,2,1,0:T(8,128)}, f32[4,3,128,128]{3,2,1,0:T(8,128)S(1)}, u32[]{:S(2)}) %copy-start.6) | copy-done | bytes 786456
  21.8 0.0 copy-start.7
  21.8 0.6 %fusion.11 = s32[64]{0:T(128)} fusion(s32[64]{0:T(128)S(1)} %iota.7), kind=kLoop, calls=%fused_computation.65 | loop fusion | flops 2048 | bytes 512 | tf_op jit(solution)/shard_map/add | solution.py:550
  22.4 0.0 copy-done.7
  22.4 0.7 %broadcast_compare_fusion.1 = pred[64,64]{1,0:T(8,128)(4,1)} fusion(s32[64]{0:T(128)S(1)} %iota.7), kind=kLoop, calls=%fused_computation.5 | loop fusion | flops 4096 | bytes 4352 | tf_op jit(solution)/shard_map/lt | solution.py:516
  23.1 0.7 %collective-permute-start.2 = (f32[392,128]{1,0:T(8,128)S(1)}, f32[392,128]{1,0:T(8,128)S(1)}, u32[]{:S(2)}, u32[]{:S(2)}) collective-permute-start(f32[392,128]{1,0:T(8,128)S(1)} %get-tuple-element.21.mine), channel_id=1, source_target_pairs={{0,1},{2,3},{4,5},{6,7},{8,9},{10,11},{12,13},{14,15},{1,0},{3,2},... | collective-permute-start | bytes 602120 | tf_op jit(solution)/shard_map/ppermute | solution.py:508
  23.9 0.0 copy-start
  23.9 0.7 %copy-done = f32[392,128]{1,0:T(8,128)} copy-done((f32[392,128]{1,0:T(8,128)}, f32[392,128]{1,0:T(8,128)S(1)}, u32[]{:S(2)}) %copy-start) | copy-done | bytes 200728
  24.5 0.7 %slice_convert_fusion = s32[1,128]{1,0:T(1,128)S(1)} fusion(f32[72,128]{1,0:T(8,128)} %copy-done.4), kind=kLoop, calls=%fused_computation.72 | loop fusion | flops 128 | bytes 1024 | tf_op jit(solution)/shard_map/convert_element_type | solution.py:551
  25.2 0.1 fusion.15
  25.3 0.7 %fusion.13 = s32[3]{0:T(128)S(1)} fusion(s32[3]{0:T(128)} %constant.161.clone, s32[3]{0:T(128)} %constant.162.clone, pred[]{:T(512)S(6)} %eq.73, s32[]{:T(128)S(6)} %add.105), kind=kLoop, calls=%fused_computation.68 | loop fusion | flops 6 | bytes 41 | tf_op jit(solution)/shard_map/add | solution.py:554
  26.0 0.1 compare_and_fusion.1
  26.0 0.7 %multiply_add_fusion = s32[3,64]{1,0:T(4,128)S(1)} fusion(s32[1,64]{1,0:T(1,128)S(1)} %get-tuple-element.39, s32[1,64]{1,0:T(1,128)S(1)} %get-tuple-element.38, s32[1,64]{1,0:T(1,128)S(1)} %get-tuple-element.37, s32[64]{0:T(128)} %fusion.11, s32[]{:T(128)S(6)} %mul.37), kind=kLoop, calls=%fused_computation.28 | loop fusion | flops 960 | bytes 1796 | tf_op jit(solution)/shard_map/add | solution.py:556
  26.7 0.8 %select_reduce_fusion.1 = s32[3,64]{1,0:T(4,128)S(1)} fusion(pred[64,64]{1,0:T(8,128)(4,1)} %broadcast_compare_fusion.1, pred[3,64]{1,0:T(4,128)(4,1)S(1)} %compare_and_fusion.1), kind=kLoop, calls=%fused_computation.1 | loop fusion | flops 36672 | bytes 5056 | tf_op jit(solution)/shard_map/reduce_sum | solution.py:517
  27.5 0.7 %select_reduce_fusion.2 = s32[3,8]{1,0:T(4,128)} fusion(s32[3,64]{1,0:T(4,128)S(1)} %multiply_add_fusion, s32[3,64]{1,0:T(4,128)S(1)} %select_reduce_fusion.1, pred[3,64]{1,0:T(4,128)(4,1)S(1)} %compare_and_fusion.1), kind=kLoop, calls=%fused_computation.6 | loop fusion | flops 6120 | bytes 1824 | tf_op jit(solution)/shard_map/reduce_sum | solution.py:558
  28.2 0.7 %reshape.516.rows_ref = s32[24]{0:T(128)S(1)} reshape(s32[3,8]{1,0:T(4,128)} %select_reduce_fusion.2) | data formatting | bytes 192 | tf_op jit(solution)/shard_map/reshape | solution.py:558
  29.0 0.0 collective-permute-start.5
  29.0 0.0 collective-permute-done.2.theirs
  29.0 0.0 copy-start.2
  29.0 0.7 %copy-done.2 = f32[392,128]{1,0:T(8,128)} copy-done((f32[392,128]{1,0:T(8,128)}, f32[392,128]{1,0:T(8,128)S(1)}, u32[]{:S(2)}) %copy-start.2) | copy-done | bytes 200728
  29.7 0.0 copy-start.1
  29.7 0.9 %copy-done.1 = f32[392,128]{1,0:T(8,128)S(1)} copy-done((f32[392,128]{1,0:T(8,128)S(1)}, f32[392,128]{1,0:T(8,128)}, u32[]{:S(2)}) %copy-start.1) | copy-done | bytes 200728
  30.6 0.0 copy-start.3
  30.6 0.9 %copy-done.3 = f32[392,128]{1,0:T(8,128)S(1)} copy-done((f32[392,128]{1,0:T(8,128)S(1)}, f32[392,128]{1,0:T(8,128)}, u32[]{:S(2)}) %copy-start.3) | copy-done | bytes 200728
  31.5 0.6 %answers.1 = (f32[512,128]{1,0:T(8,128)S(1)}, f32[96,128]{1,0:T(8,128)S(1)}) custom-call(s32[1,2]{1,0:T(1,128)S(1)} %copy-done.5, s32[24]{0:T(128)S(1)} %reshape.516.rows_ref, f32[392,128]{1,0:T(8,128)S(1)} %copy-done.1, f32[392,128]{1,0:T(8,128)S(1)} %copy-done.3), custom_call_target="tpu_custom_call" | custom-call | tf_op jit(solution)/shard_map/answers/pallas_call | solution.py:358
  32.2 0.8 %copy.17 = s32[16,4]{1,0:T(8,128)S(1)} copy(s32[16,4]{0,1:T(4,128)} %param.9) | data formatting | bytes 512 | tf_op jit(solution)/shard_map/optimization_barrier | solution.py:512
  33.0 0.1 reshape.517
  33.1 3.5 %collective-permute-start.3 = (f32[96,128]{1,0:T(8,128)S(1)}, f32[96,128]{1,0:T(8,128)S(1)}, u32[]{:S(2)}, u32[]{:S(2)}) collective-permute-start(f32[96,128]{1,0:T(8,128)S(1)} %get-tuple-element.25), channel_id=1, source_target_pairs={{1,2},{3,4},{5,6},{7,8},{9,10},{11,12},{13,14},{2,1},{4,3},{6,5},{... | collective-permute-start | bytes 147464 | tf_op jit(solution)/shard_map/ppermute | solution.py:508
  36.6 0.7 %broadcast_select_fusion = s32[3,2]{0,1:T(2,128)S(1)} fusion(s32[3,2]{0,1:T(2,128)} %constant.163.clone, s32[3,2]{0,1:T(2,128)} %constant.164.clone, pred[]{:T(512)S(6)} %eq.82), kind=kLoop, calls=%fused_computation.58 | loop fusion | flops 6 | bytes 73 | tf_op jit(solution)/shard_map/jit(_where)/select_n | solution.py:571
  37.3 0.1 compare_and_fusion
  37.4 0.8 %broadcast_compare_fusion = pred[64,64]{1,0:T(8,128)(4,1)S(1)} fusion(s32[64]{0:T(128)} %copy-done.7), kind=kLoop, calls=%fused_computation.4 | loop fusion | flops 4096 | bytes 4352 | tf_op jit(solution)/shard_map/lt | solution.py:516
  38.2 0.1 select_reduce_fusion
  38.3 0.1 fusion.10
  38.4 0.1 collective-permute-done.3.crossed
  38.5 1.4 %collective-permute-start.4 = (f32[96,128]{1,0:T(8,128)S(1)}, f32[96,128]{1,0:T(8,128)S(1)}, u32[]{:S(2)}, u32[]{:S(2)}) collective-permute-start(f32[96,128]{1,0:T(8,128)S(1)} %collective-permute-done.3.crossed), channel_id=1, source_target_pairs={{0,1},{2,3},{4,5},{6,7},{8,9},{10,11},{12,13},{14,15},{1,0},{3,2},... | collective-permute-start | bytes 147464 | tf_op jit(solution)/shard_map/ppermute | solution.py:508
  39.9 0.6 %compare_select_fusion.15.rows_ref = s32[64]{0:T(128)S(1)} fusion(s32[64]{0:T(128)S(1)} %reshape.517, s32[64]{0:T(128)S(1)} %fusion.10, s32[64]{0:T(128)S(1)} %get-tuple-element.34, s32[64]{0:T(128)} %copy-done.7, s32[]{:T(128)S(6)} %mul.42, s32[]{:T(128)S(6)} %select_n.156, s32[]{:T(128)S(6)} %mul_shard_map.3), kind=kLoop, calls=%fused_computation.66 | loop fusion | flops 4352 | bytes 1292 | tf_op jit(solution)/shard_map/jit(_where)/select_n | solution.py:581
  40.5 0.2 collective-permute-done.4.passed
  40.8 0.0 collective-permute-done.6.arrived
  40.8 0.0 collective-permute-done.5.theirs
  40.8 4.2 %final.1 = f32[16,3,128,128]{3,2,1,0:T(8,128)} custom-call(s32[1,2]{1,0:T(1,128)S(1)} %copy-done.5, s32[64]{0:T(128)S(1)} %compare_select_fusion.15.rows_ref, f32[512,128]{1,0:T(8,128)S(1)} %get-tuple-element.29.edges, f32[96,128]{1,0:T(8,128)S(1)} %collective-permute-done.3.crossed, f32[96,128]{1,0:T(8,128)S(1)} %collective-permute-done.4.passed, ...), custom_call_target="tpu_custom_call" | custom-call | tf_op jit(solution)/shard_map/final/pallas_call | solution.py:486
  (6 shorter events, 0.0 us)
Async XLA Ops:
  0.0 4.5 %collective-permute-start = (s32[16,4]{0,1:T(4,128)}, s32[16,4]{0,1:T(4,128)S(1)}, u32[]{:S(2)}, u32[]{:S(2)}) collective-permute-start(s32[16,4]{0,1:T(4,128)} %param.9), channel_id=1, source_target_pairs={{0,1},{2,3},{4,5},{6,7},{8,9},{10,11},{12,13},{14,15},{1,0},{3,2},... | collective-permute-start | bytes 776 | tf_op jit(solution)/shard_map/ppermute | solution.py:508
  0.7 3.7 %copy-start.8 = (s32[16,4]{0,1:T(4,128)S(1)}, s32[16,4]{0,1:T(4,128)}, u32[]{:S(2)}) copy-start(s32[16,4]{0,1:T(4,128)} %param.9) | copy-start | bytes 772
  0.7 9.9 %copy-start.5 = (s32[1,2]{1,0:T(1,128)S(1)}, s32[1,2]{1,0:T(1,128)}, u32[]{:S(2)}) copy-start(s32[1,2]{1,0:T(1,128)} %range_ref.5) | copy-start | bytes 28
  4.8 5.8 %collective-permute-start.1 = (f32[72,128]{1,0:T(8,128)S(1)}, f32[72,128]{1,0:T(8,128)S(1)}, u32[]{:S(2)}, u32[]{:S(2)}) collective-permute-start(f32[72,128]{1,0:T(8,128)S(1)} %select_maximum_fusion.other_ref), channel_id=1, source_target_pairs={{1,2},{3,4},{5,6},{7,8},{9,10},{11,12},{13,14},{2,1},{4,3},{6,5},{... | collective-permute-start | bytes 110600 | tf_op jit(solution)/shard_map/ppermute | solution.py:508
  7.8 33.0 %collective-permute-start.6 = (f32[4,3,128,128]{3,2,1,0:T(8,128)}, f32[4,3,128,128]{3,2,1,0:T(8,128)}, u32[]{:S(2)}, u32[]{:S(2)}) collective-permute-start(f32[4,3,128,128]{3,2,1,0:T(8,128)} %after.1), channel_id=1, source_target_pairs={{1,2},{3,4},{5,6},{7,8},{9,10},{11,12},{13,14},{2,1},{4,3},{6,5},{... | collective-permute-start | bytes 2359304 | tf_op jit(solution)/shard_map/ppermute | solution.py:508
  10.6 10.3 %copy-start.4 = (f32[72,128]{1,0:T(8,128)}, f32[72,128]{1,0:T(8,128)S(1)}, u32[]{:S(2)}) copy-start(f32[72,128]{1,0:T(8,128)S(1)} %collective-permute-done.1.came) | copy-start | bytes 110596
  20.9 0.9 %copy-start.6 = (f32[4,3,128,128]{3,2,1,0:T(8,128)}, f32[4,3,128,128]{3,2,1,0:T(8,128)S(1)}, u32[]{:S(2)}) copy-start(f32[4,3,128,128]{3,2,1,0:T(8,128)S(1)} %get-tuple-element.31) | copy-start | bytes 2359300
  21.8 0.6 %copy-start.7 = (s32[64]{0:T(128)}, s32[64]{0:T(128)S(1)}, u32[]{:S(2)}) copy-start(s32[64]{0:T(128)S(1)} %iota.7) | copy-start | bytes 772
  23.1 5.9 %collective-permute-start.2 = (f32[392,128]{1,0:T(8,128)S(1)}, f32[392,128]{1,0:T(8,128)S(1)}, u32[]{:S(2)}, u32[]{:S(2)}) collective-permute-start(f32[392,128]{1,0:T(8,128)S(1)} %get-tuple-element.21.mine), channel_id=1, source_target_pairs={{0,1},{2,3},{4,5},{6,7},{8,9},{10,11},{12,13},{14,15},{1,0},{3,2},... | collective-permute-start | bytes 602120 | tf_op jit(solution)/shard_map/ppermute | solution.py:508
  23.9 0.7 %copy-start = (f32[392,128]{1,0:T(8,128)}, f32[392,128]{1,0:T(8,128)S(1)}, u32[]{:S(2)}) copy-start(f32[392,128]{1,0:T(8,128)S(1)} %get-tuple-element.21.mine) | copy-start | bytes 602116
  29.0 11.8 %collective-permute-start.5 = (f32[4,3,128,128]{3,2,1,0:T(8,128)}, f32[4,3,128,128]{3,2,1,0:T(8,128)}, u32[]{:S(2)}, u32[]{:S(2)}) collective-permute-start(f32[4,3,128,128]{3,2,1,0:T(8,128)} %copy-done.6), channel_id=1, source_target_pairs={{0,1},{2,3},{4,5},{6,7},{8,9},{10,11},{12,13},{14,15},{1,0},{3,2},... | collective-permute-start | bytes 2359304 | tf_op jit(solution)/shard_map/ppermute | solution.py:508
  29.0 0.7 %copy-start.2 = (f32[392,128]{1,0:T(8,128)}, f32[392,128]{1,0:T(8,128)S(1)}, u32[]{:S(2)}) copy-start(f32[392,128]{1,0:T(8,128)S(1)} %collective-permute-done.2.theirs) | copy-start | bytes 602116
  29.7 0.9 %copy-start.1 = (f32[392,128]{1,0:T(8,128)S(1)}, f32[392,128]{1,0:T(8,128)}, u32[]{:S(2)}) copy-start(f32[392,128]{1,0:T(8,128)} %copy-done) | copy-start | bytes 602116
  30.6 0.9 %copy-start.3 = (f32[392,128]{1,0:T(8,128)S(1)}, f32[392,128]{1,0:T(8,128)}, u32[]{:S(2)}) copy-start(f32[392,128]{1,0:T(8,128)} %copy-done.2) | copy-start | bytes 602116
  33.1 5.4 %collective-permute-start.3 = (f32[96,128]{1,0:T(8,128)S(1)}, f32[96,128]{1,0:T(8,128)S(1)}, u32[]{:S(2)}, u32[]{:S(2)}) collective-permute-start(f32[96,128]{1,0:T(8,128)S(1)} %get-tuple-element.25), channel_id=1, source_target_pairs={{1,2},{3,4},{5,6},{7,8},{9,10},{11,12},{13,14},{2,1},{4,3},{6,5},{... | collective-permute-start | bytes 147464 | tf_op jit(solution)/shard_map/ppermute | solution.py:508
  38.5 2.3 %collective-permute-start.4 = (f32[96,128]{1,0:T(8,128)S(1)}, f32[96,128]{1,0:T(8,128)S(1)}, u32[]{:S(2)}, u32[]{:S(2)}) collective-permute-start(f32[96,128]{1,0:T(8,128)S(1)} %collective-permute-done.3.crossed), channel_id=1, source_target_pairs={{0,1},{2,3},{4,5},{6,7},{8,9},{10,11},{12,13},{14,15},{1,0},{3,2},... | collective-permute-start | bytes 147464 | tf_op jit(solution)/shard_map/ppermute | solution.py:508

commit v8 on v6

--- a/solution.py
+++ b/solution.py
@@ -176,10 +176,17 @@
     return odd * (cells_hbm.shape[0] - margin)
 
 
-def outer_kernel(margin, cells_hbm, out, edges, cells, columns, weights, sems):
+def outer_kernel(margin, cells_hbm, table, their_table, out, bundle, cells, columns, weights, sems):
     side = columns.shape[0]
+    _, odd = position()
     copy = fetch(cells_hbm, outer_slot(cells_hbm, margin), cells, sems, [(0, margin)])
     fill_weights(weights)
+    count, sides = table.shape
+    at = 16 * margin
+    bundle[at : at + 2 * count, :] = jnp.zeros((2 * count, side), jnp.float32)
+    for which, ref in ((odd, table), (1 - odd, their_table)):
+        start = pl.multiple_of(at + which * count, 8)
+        bundle[pl.ds(start, count), 0:sides] = ref[...].astype(jnp.float32)
 
     @pl.loop(0, margin // PAIR)
     def _(step):
@@ -193,7 +200,7 @@
         gather_columns([loader(cells, i + n) for n in range(PAIR)], columns, 8 * i, side)
         update(cells, i, PAIR, weights, put)
 
-    take_edges(margin, cells, lambda p: p, columns, edges, 0)
+    take_edges(margin, cells, lambda p: p, columns, bundle, 0)
 
 
 def cost(patches, side):
@@ -208,15 +215,15 @@
     return pltpu.CompilerParams(vmem_limit_bytes=mebibytes << 20)
 
 
-def outer_patches(old_cells, margin):
+def outer_patches(old_cells, table, their_table, margin):
     side = old_cells.shape[3]
     return pl.pallas_call(
         functools.partial(outer_kernel, margin),
-        in_specs=[HBM],
+        in_specs=[HBM, VMEM, VMEM],
         out_specs=[VMEM, VMEM],
         out_shape=[
             jax.ShapeDtypeStruct((margin, 3, side, side), jnp.float32),
-            jax.ShapeDtypeStruct((16 * margin, side), jnp.float32),
+            jax.ShapeDtypeStruct((16 * margin + 2 * table.shape[0], side), jnp.float32),
         ],
         scratch_shapes=[
             pltpu.VMEM((margin, 4, side, side), jnp.float32),
@@ -227,7 +234,7 @@
         cost_estimate=cost(margin, side),
         compiler_params=room(48),
         name="outer",
-    )(old_cells)
+    )(old_cells, table, their_table)
 
 
 def after(value, other):
@@ -306,7 +313,40 @@
     )(old_range, old_cells, came)
 
 
-def answer_kernel(margin, count, range_ref, rows_ref, mine, theirs, edges, message):
+def entries_of(table, sides, lanes):
+    count = table.shape[0]
+    return jnp.concatenate([jnp.broadcast_to(table[:, s : s + 1], (count, lanes)) for s in range(sides)], axis=0)
+
+
+def grid_iota(rows, lanes, axis):
+    return lax.broadcasted_iota(jnp.int32, (rows, lanes), axis)
+
+
+def flag(where):
+    return jnp.where(where, 1.0, 0.0)
+
+
+def ranks(masks):
+    rows, lanes = masks[0].shape
+    earlier = flag(grid_iota(rows, lanes, 1) < grid_iota(rows, lanes, 0)).astype(jnp.bfloat16)
+    stacked = jnp.concatenate(masks, axis=1).astype(jnp.bfloat16)
+    if rows < lanes:
+        stacked = jnp.concatenate([stacked, jnp.zeros((lanes - rows, stacked.shape[1]), jnp.bfloat16)], axis=0)
+    counted = product(earlier, stacked)
+    return [counted[:, n * lanes : (n + 1) * lanes] for n in range(len(masks))]
+
+
+def edge_places(row, count, patch):
+    s = row // count
+    return 4 * count * (s % 2) + s // 2, 2.0 * patch
+
+
+def edges_of_field(edges, f):
+    tiles = edges.shape[0] // 8
+    return [edges[pl.ds(2 * f + parity, tiles, stride=8), :] for parity in range(2)]
+
+
+def answer_kernel(margin, count, range_ref, mine, theirs, came, edges, message):
     side = edges.shape[1]
     home, limit, brought, _ = layout(margin, count)
     inner = 0
@@ -346,18 +386,44 @@
             crossed = theirs[brought + 16 * m + 8 * half : brought + 16 * m + 8 * half + 8, :]
             at = pl.multiple_of(to + 8 * half, 8)
             edges[pl.ds(at, 8), :] = jnp.where(taken, crossed, edges[pl.ds(at, 8), :])
-    for k in range(3):
-        asked = range(k * CAP, (k + 1) * CAP)
-        values = [edges[pl.ds(rows_ref[n], 4, stride=2), :] for n in asked]
-        for n, value in zip(asked, values):
-            message[pl.ds(8 * (n // 2) + n % 2, 4, stride=2), :] = value
-
-
-def answers(old_range, rows, mine, theirs, margin, per_device):
+    sides, total = 4, 8 * count
+    row = grid_iota(total, side, 0)
+    lane = grid_iota(total, side, 1)
+    which, within = row // (sides * count), row % (sides * count)
+    at = 16 * margin
+    tables = [came[at + n * count : at + (n + 1) * count, :] for n in range(2)]
+    listed = jnp.concatenate([entries_of(table, sides, side) for table in tables], axis=0)
+    patch = listed - (2 * count * (me // 2)).astype(jnp.float32)
+    held = [(patch >= n * count) & (patch < (n + 1) * count) for n in range(2)]
+    masks = [
+        flag((which == 0) & held[0]),
+        jnp.where(even, flag((which == 1) & held[0]), flag((which == 0) & held[1])),
+        flag((which == 1) & held[1]),
+    ]
+    chosen = jnp.zeros((total, side), jnp.float32)
+    for k, (mask, rank) in enumerate(zip(masks, ranks(masks))):
+        slot = (lane - k * CAP).astype(jnp.float32)
+        chosen = chosen + jnp.where((lane // CAP == k) & (rank == slot), mask, 0.0)
+    place, twice = edge_places(within, count, patch)
+    hot = flag(lane.astype(jnp.float32) == place.astype(jnp.float32) + twice).astype(jnp.bfloat16)
+    slots = jnp.transpose(chosen)[0:32, :].astype(jnp.bfloat16)
+    picked = product(slots, hot).astype(jnp.bfloat16)
+    picked = jnp.concatenate([picked] * 3, axis=1)
+    for f in range(4):
+        values = jnp.concatenate(edges_of_field(edges, f), axis=0)
+        high = values.astype(jnp.bfloat16)
+        left = values - high.astype(jnp.float32)
+        mid = left.astype(jnp.bfloat16)
+        low = (left - mid.astype(jnp.float32)).astype(jnp.bfloat16)
+        taken = product(picked, jnp.concatenate([high, mid, low], axis=0))
+        message[3 * CAP * f : 3 * CAP * (f + 1), :] = taken[0 : 3 * CAP, :]
+
+
+def answers(old_range, mine, theirs, came, margin, per_device):
     side = mine.shape[1]
     return pl.pallas_call(
         functools.partial(answer_kernel, margin, per_device),
-        in_specs=[SMEM, SMEM, VMEM, VMEM],
+        in_specs=[SMEM, VMEM, VMEM, VMEM],
         out_specs=[VMEM, VMEM],
         out_shape=[
             jax.ShapeDtypeStruct((32 * per_device, side), jnp.float32),
@@ -365,28 +431,58 @@
         ],
         compiler_params=room(4),
         name="answers",
-    )(old_range, rows, mine, theirs)
-
-
-def rim_terms(rows_ref, edges, crossed, passed, columns, lines, source, ghost, turn, count, odd):
-    total = edges.shape[0]
-    step = crossed.shape[0]
-    source[0:total, :] = edges[...]
-    source[total : total + step, :] = crossed[...]
-    source[total + step : total + 2 * step, :] = passed[...]
-    field = lax.broadcasted_iota(jnp.int32, (4, edges.shape[1]), 0)
-    group = 4
-    for start in range(0, count, group):
-        fetched = []
-        for p in range(start, start + group):
-            for s in range(4):
-                row = rows_ref[4 * p + s]
-                wall = row < 0
-                value = source[pl.ds(jnp.where(wall, -1 - row, row), 4, stride=2), :]
-                value = jnp.where((field == 1 + s // 2) & wall, -value, value)
-                fetched.append((16 * p + 8 * (s // 2) + 1 - s % 2, value))
-        for target, value in fetched:
-            ghost[pl.ds(target, 4, stride=2), :] = value
+    )(old_range, mine, theirs, came)
+
+
+def ghosts(table, edges, crossed, passed, me, odd):
+    count, sides = table.shape
+    side = edges.shape[1]
+    total = sides * count
+    even = odd == 0
+    row, lane = grid_iota(total, side, 0), grid_iota(total, side, 1)
+    s, p = row // count, row % count
+    listed = entries_of(table[...].astype(jnp.float32), sides, side)
+    wall = listed < 0.0
+    patch = listed - (2 * count * (me // 2)).astype(jnp.float32)
+    distance = listed - (count * me).astype(jnp.float32)
+    first = 4 * count * 2
+    step = 3 * CAP
+    lists = (
+        (-2, -2, first, first + step + 2 * CAP),
+        (-1, 1, first + CAP, first + CAP),
+        (2, 2, first + step, first + 2 * CAP),
+    )
+    masks, starts = [], []
+    for far_even, far_odd, at_even, at_odd in lists:
+        low = (count * jnp.where(even, far_even, far_odd)).astype(jnp.float32)
+        masks.append(flag(~wall & (distance >= low) & (distance < low + count)))
+        starts.append(jnp.where(even, at_even, at_odd).astype(jnp.float32))
+    across = jnp.zeros((total, side), jnp.float32)
+    for mask, rank, start in zip(masks, ranks(masks), starts):
+        across = across + mask * (rank + start)
+    place, twice = edge_places(row, count, patch)
+    own = 4 * count * (1 - s % 2) + 2 * (count * odd + p) + s // 2
+    inside = (patch >= 0.0) & (patch < 2.0 * count)
+    index = jnp.where(inside, place.astype(jnp.float32) + twice, across)
+    index = jnp.where(wall, own.astype(jnp.float32), index)
+    lane = lane.astype(jnp.float32)
+    hot = jnp.concatenate([flag(lane == index), flag(lane + side == index)], axis=1).astype(jnp.bfloat16)
+    hot = jnp.concatenate([hot, hot], axis=1)
+    fields = []
+    for f in range(4):
+        parts = edges_of_field(edges, f)
+        parts += [ref[step * f : step * (f + 1), :] for ref in (crossed, passed)]
+        parts.append(jnp.zeros((2 * side - first - 2 * step, side), jnp.float32))
+        values = jnp.concatenate(parts, axis=0)
+        high = values.astype(jnp.bfloat16)
+        low = (values - high.astype(jnp.float32)).astype(jnp.bfloat16)
+        fields.append(product(hot, jnp.concatenate([high, low], axis=0)))
+    return fields, wall
+
+
+def rim_terms(table, edges, crossed, passed, columns, lines, turn, me, odd):
+    count = table.shape[0]
+    outside, wall = ghosts(table, edges, crossed, passed, me, odd)
     turn[...] = jnp.zeros_like(turn)
     lines[...] = jnp.zeros_like(lines)
     for s in range(4):
@@ -395,13 +491,15 @@
         axis = s // 2
         normal, across = (1, 2) if axis == 0 else (2, 1)
 
+        at = slice(count * s, count * (s + 1))
+
         def both(f):
             row = 8 * axis + 2 * f + parity
-            own = source[pl.ds(16 * count * odd + row, count, stride=16), :]
-            return own, ghost[pl.ds(row, count, stride=16), :]
+            return edges[pl.ds(16 * count * odd + row, count, stride=16), :], outside[f][at]
 
         hc, hg = both(0)
         nc, ng = both(normal)
+        ng = jnp.where(wall[at], -ng, ng)
         ac, ag = both(across)
         bc, bg = both(3)
         rc, rg = lax.rsqrt(hc), lax.rsqrt(hg)
@@ -431,14 +529,14 @@
 
 
 def final_kernel(
-    margin, range_ref, rows_ref, edges, crossed, passed, own, theirs, arrived, out,
-    result, source, ghost, turn, columns, lines, places, sems,
+    margin, range_ref, table, edges, crossed, passed, own, theirs, arrived, out,
+    result, turn, columns, lines, places, sems,
 ):
     count, side = own.shape[0], lines.shape[1]
     me, odd = position()
     even = odd == 0
     fill_places(places)
-    rim_terms(rows_ref, edges, crossed, passed, columns, lines, source, ghost, turn, count, odd)
+    rim_terms(table, edges, crossed, passed, columns, lines, turn, me, odd)
     start, stop = range_ref[0, 0], range_ref[0, 1]
     line = iota(0, side)
     lane = lax.broadcasted_iota(jnp.int32, (side, 2 * side), 1) % side
@@ -481,17 +579,15 @@
         copy(p).wait()
 
 
-def finished(old_range, rows, edges, crossed, passed, own, theirs, arrived, margin):
+def finished(old_range, table, edges, crossed, passed, own, theirs, arrived, margin):
     count, _, side, _ = own.shape
     return pl.pallas_call(
         functools.partial(final_kernel, margin),
-        in_specs=[SMEM, SMEM] + [VMEM] * 6,
+        in_specs=[SMEM] + [VMEM] * 7,
         out_specs=HBM,
         out_shape=jax.ShapeDtypeStruct(own.shape, jnp.float32),
         scratch_shapes=[
             pltpu.VMEM(own.shape, jnp.float32),
-            pltpu.VMEM((edges.shape[0] + 2 * crossed.shape[0], side), jnp.float32),
-            pltpu.VMEM((16 * count, side), jnp.float32),
             pltpu.VMEM((side, side), jnp.float32),
             pltpu.VMEM((side, 2 * side), jnp.bfloat16),
             pltpu.VMEM((side, side), jnp.float32),
@@ -500,7 +596,7 @@
         ],
         compiler_params=room(12),
         name="final",
-    )(old_range, rows, edges, crossed, passed, own, theirs, arrived)
+    )(old_range, table, edges, crossed, passed, own, theirs, arrived)
 
 
 def swapped(value, first):
@@ -508,69 +604,20 @@
     return lax.ppermute(value, AXES, pairs + [(j, i) for i, j in pairs])
 
 
-def ranks(named):
-    size = named.shape[-1]
-    earlier = jnp.arange(size)[:, None] < jnp.arange(size)[None, :]
-    return jnp.sum(jnp.where(named[..., :, None] & earlier, 1, 0), axis=-2)
-
-
 def local(old_cells, old_range, neighbours):
     per_device = neighbours.shape[0]
-    side = old_cells.shape[3]
     margin = (old_cells.shape[0] - per_device) // 2
-    entries = 4 * per_device
-    me, odd = position()
-
     their_table = swapped(neighbours, 0)
-    leaving, leaving_edges = outer_patches(old_cells, margin)
-
-    tables = jnp.where(
-        odd == 0,
-        jnp.concatenate([neighbours.reshape(1, -1), their_table.reshape(1, -1)], axis=1),
-        jnp.concatenate([their_table.reshape(1, -1), neighbours.reshape(1, -1)], axis=1),
-    ).astype(jnp.float32)
-    tables = jnp.pad(tables, ((0, 7), (0, side - 2 * entries)))
-    bundle = jnp.concatenate([leaving_edges, tables], axis=0)
+    leaving, bundle = outer_patches(old_cells, neighbours, their_table, margin)
     came = swapped(bundle, 1)
-
     arrived = swapped(after(leaving, bundle), 1)
-
     shared, inner, own = home_patches(old_range, old_cells, came, margin, per_device)
     their_edges = swapped(shared, 0)
     theirs = swapped(inner, 0)
-
-    entry = jnp.arange(entries, dtype=jnp.int32)
-    entry_side = entry % 4
-    at_side = 8 * (entry_side // 2) + entry_side % 2
-    asked_by = came[16 * margin, : 2 * entries].astype(jnp.int32).reshape(2, entries)
-    middle = jnp.where(odd == 0, asked_by[1], asked_by[0])
-    listed = jnp.stack([asked_by[0], middle, asked_by[1]])
-    owners = me + jnp.where(odd == 0, jnp.array([0, 0, 1], jnp.int32), jnp.array([-1, 0, 0], jnp.int32))
-    asked = (listed >= 0) & (listed // per_device == owners[:, None])
-    rows = 16 * (listed - 2 * per_device * (me // 2)) + at_side
-    chosen = asked[:, None, :] & (ranks(asked)[:, None, :] == jnp.arange(CAP)[None, :, None])
-    send_rows = jnp.sum(jnp.where(chosen, rows[:, None, :], 0), axis=2).reshape(-1)
-
-    edges, message = answers(old_range, send_rows, shared, their_edges, margin, per_device)
+    edges, message = answers(old_range, shared, their_edges, came, margin, per_device)
     crossed = swapped(message, 1)
     passed = swapped(crossed, 0)
-
-    listed = neighbours.reshape(-1)
-    owner = listed // per_device
-    mine, total, step = 32 * per_device, 16 * per_device, 12 * CAP
-    lists = jnp.where(
-        odd == 0,
-        jnp.array([[-2, mine], [-1, mine + 4 * CAP], [2, mine + step]], jnp.int32),
-        jnp.array([[-2, mine + step + 8 * CAP], [1, mine + 4 * CAP], [2, mine + 8 * CAP]], jnp.int32),
-    )
-    named = (listed >= 0) & (owner - me == lists[:, :1])
-    place = ranks(named)
-    across = jnp.sum(jnp.where(named, lists[:, 1:] + 8 * (place // 2) + place % 2, 0), axis=0)
-    within = 16 * (listed - 2 * per_device * (me // 2)) + at_side
-    wall = total * odd + 16 * (entry // 4) + 8 * (entry_side // 2) + 1 - entry_side % 2
-    ghost_rows = jnp.where(listed < 0, -1 - wall, jnp.where(owner // 2 == me // 2, within, across))
-
-    return finished(old_range, ghost_rows, edges, crossed, passed, own, theirs, arrived, margin)
+    return finished(old_range, neighbours, edges, crossed, passed, own, theirs, arrived, margin)
 
 
 def solution(mesh):

time: 41.6 us -> 36 us (0.87)
  other arithmetic: 6.73 us -> 0 us
  waiting for transfers between devices: 2.34 us -> 7.71 us
  Pallas kernels: 18.1 us -> 16.4 us
  local copies, waits for them, and re-layouts: 2.46 us -> 0.76 us
  starting transfers between devices: 11.3 us -> 10.8 us
    ppermute x7, waiting for transfers between devices: 2.34 us -> 7.71 us  [swapped(): return lax.ppermute(value, AXES, pairs + [(j, i) for i, j in pairs])]
    reduce_sum x3 -> x0, other arithmetic: 2.19 us -> none  [the longest x1 0.78 us: local(): jnp.sum(jnp.where(named, lists[:, 1:] + 8 * (place // 2) + place % 2, 0),...]
    pallas_call x2, Pallas kernels: 7.48 us -> 6.13 us  [the longest x1 3.54 us: finished(): pl.pallas_call(functools.partial(final_kernel, margin), in_specs=[SMEM] +...]
    select_n x2 -> x0, other arithmetic: 1.31 us -> none  [the longest x1 0.68 us: local(): jnp.where(odd == 0, jnp.array([[-2, mine], [-1, mine + 4 * CAP], [2, mine...]
    add x3 -> x0, other arithmetic: 1.25 us -> none  [the longest x1 0.66 us: local(): me + jnp.where(odd == 0, jnp.array([0, 0, 1], jnp.int32), jnp.array([-1,...]
    reshape x2 -> x0, local copies, waits for them, and re-layouts: 0.84 us -> none  [the longest x1 0.75 us: local(): jnp.sum(jnp.where(chosen, rows[:, None, :], 0), axis=2).reshape(-1)]
    pallas_call x1, Pallas kernels: 10 us -> 9.16 us  [home_patches(): pl.pallas_call(functools.partial(home_kernel, margin), in_specs=[SMEM, HB...]
    and x2 -> x0, other arithmetic: 0.69 us -> none  [the longest x1 0.62 us: local(): named = (listed >= 0) & (owner - me == lists[:, :1])]
  transfers between devices with their start and end apart: 7 -> 7, of which waited for: 2 -> 4; matrix products, arithmetic and copies ran while one was open for 22% -> 0% of each run, Pallas kernels for 34% -> 29%
where the time goes in v8:
time: 36 us; the launch traced here: 35.8 us
  Pallas kernels  16.4 us (46%)
  starting transfers between devices  10.8 us (30%)
  waiting for transfers between devices  7.71 us (21%)
  local copies, waits for them, and re-layouts  0.76 us (2%)
    ppermute x7, starting transfers between devices, swapped(): return lax.ppermute(value, AXES, pairs + [(j, i) for i, j in pairs])  10.8 us
    pallas_call x1, Pallas kernels, home_patches(): pl.pallas_call(functools.partial(home_kernel, margin), in_specs=[SMEM, HB...  9.16 us
    ppermute x7, waiting for transfers between devices, swapped(): return lax.ppermute(value, AXES, pairs + [(j, i) for i, j in pairs])  7.71 us
    pallas_call x1, Pallas kernels, finished(): pl.pallas_call(functools.partial(final_kernel, margin), in_specs=[SMEM] +...  3.54 us
    pallas_call x1, Pallas kernels, outer_patches(): pl.pallas_call(functools.partial(outer_kernel, margin), in_specs=[HBM, VM...  2.59 us
    pallas_call x1, Pallas kernels, answers(): pl.pallas_call(functools.partial(answer_kernel, margin, per_device), in_s...  1.12 us
    unnamed x3, local copies, waits for them, and re-layouts  0.76 us
  transfers between devices with their start and end apart: 7, of which 4 were waited for; matrix products, arithmetic and copies ran while one was open for 0% of the time, Pallas kernels for 29%

profile of v8, /device:TPU:17, one launch (start us, length us, event | category | flops | bytes accessed | tf_op | source)
XLA Modules:
  0.0 35.8 jit_solution(17503213045901736649)
XLA Ops:
  0.0 0.8 %copy.7.table = s32[16,4]{1,0:T(8,128)S(1)} copy(s32[16,4]{0,1:T(4,128)} %param.5) | data formatting | bytes 512 | tf_op args[2]
  0.8 0.0 copy-start
  0.8 0.7 %collective-permute-start = (s32[16,4]{1,0:T(8,128)S(1)}, s32[16,4]{1,0:T(8,128)S(1)}, u32[]{:S(2)}, u32[]{:S(2)}) collective-permute-start(s32[16,4]{1,0:T(8,128)S(1)} %copy.7.table), channel_id=1, source_target_pairs={{0,1},{2,3},{4,5},{6,7},{8,9},{10,11},{12,13},{14,15},{1,0},{3,2},... | collective-permute-start | bytes 776 | tf_op jit(solution)/shard_map/ppermute | solution.py:604
  1.4 0.8 %collective-permute-done.their_table = s32[16,4]{1,0:T(8,128)S(1)} collective-permute-done((s32[16,4]{1,0:T(8,128)S(1)}, s32[16,4]{1,0:T(8,128)S(1)}, u32[]{:S(2)}, u32[]{:S(2)}) %collective-permute-start) | collective-permute-done | bytes 288 | tf_op jit(solution)/shard_map/ppermute | solution.py:604
  2.3 2.6 %outer.1 = (f32[4,3,128,128]{3,2,1,0:T(8,128)S(1)}, f32[96,128]{1,0:T(8,128)S(1)}) custom-call(f32[24,4,128,128]{3,2,1,0:T(8,128)} %cells_hbm.3, s32[16,4]{1,0:T(8,128)S(1)} %copy.7.table, s32[16,4]{1,0:T(8,128)S(1)} %collective-permute-done.their_table), custom_call_target="tpu_custom_call" | custom-call | flops 52428800 | bytes 1835008 | tf_op jit(solution)/shard_map/outer/pallas_call | solution.py:220
  4.9 3.3 %collective-permute-start.1 = (f32[96,128]{1,0:T(8,128)S(1)}, f32[96,128]{1,0:T(8,128)S(1)}, u32[]{:S(2)}, u32[]{:S(2)}) collective-permute-start(f32[96,128]{1,0:T(8,128)S(1)} %get-tuple-element.12.other_ref), channel_id=1, source_target_pairs={{1,2},{3,4},{5,6},{7,8},{9,10},{11,12},{13,14},{2,1},{4,3},{6,5},{... | collective-permute-start | bytes 147464 | tf_op jit(solution)/shard_map/ppermute | solution.py:604
  8.2 2.2 %collective-permute-start.6 = (f32[4,3,128,128]{3,2,1,0:T(8,128)S(1)}, f32[4,3,128,128]{3,2,1,0:T(8,128)S(1)}, u32[]{:S(2)}, u32[]{:S(2)}) collective-permute-start(f32[4,3,128,128]{3,2,1,0:T(8,128)S(1)} %after.1), channel_id=1, source_target_pairs={{1,2},{3,4},{5,6},{7,8},{9,10},{11,12},{13,14},{2,1},{4,3},{6,5},{... | collective-permute-start | bytes 2359304 | tf_op jit(solution)/shard_map/ppermute | solution.py:604
  10.5 0.0 collective-permute-done.1.came
  10.5 0.0 copy-done
  10.5 9.2 %home.1 = (f32[392,128]{1,0:T(8,128)S(1)}, f32[4,3,128,128]{3,2,1,0:T(8,128)S(1)}, f32[16,3,128,128]{3,2,1,0:T(8,128)S(1)}) custom-call(s32[1,2]{1,0:T(1,128)S(1)} %copy-done, f32[24,4,128,128]{3,2,1,0:T(8,128)} %cells_hbm.3, f32[96,128]{1,0:T(8,128)S(1)} %collective-permute-done.1.came), custom_call_target="tpu_custom_call" | custom-call | flops 262144000 | bytes 9175040 | tf_op jit(solution)/shard_map/home/pallas_call | solution.py:295
  19.6 1.3 %collective-permute-start.5 = (f32[4,3,128,128]{3,2,1,0:T(8,128)S(1)}, f32[4,3,128,128]{3,2,1,0:T(8,128)S(1)}, u32[]{:S(2)}, u32[]{:S(2)}) collective-permute-start(f32[4,3,128,128]{3,2,1,0:T(8,128)S(1)} %get-tuple-element.17), channel_id=1, source_target_pairs={{0,1},{2,3},{4,5},{6,7},{8,9},{10,11},{12,13},{14,15},{1,0},{3,2},... | collective-permute-start | bytes 2359304 | tf_op jit(solution)/shard_map/ppermute | solution.py:604
  20.9 0.1 collective-permute-start.2
  21.0 2.1 %collective-permute-done.2.theirs = f32[392,128]{1,0:T(8,128)S(1)} collective-permute-done((f32[392,128]{1,0:T(8,128)S(1)}, f32[392,128]{1,0:T(8,128)S(1)}, u32[]{:S(2)}, u32[]{:S(2)}) %collective-permute-start.2) | collective-permute-done | bytes 200736 | tf_op jit(solution)/shard_map/ppermute | solution.py:604
  23.1 1.1 %answers.1 = (f32[512,128]{1,0:T(8,128)S(1)}, f32[96,128]{1,0:T(8,128)S(1)}) custom-call(s32[1,2]{1,0:T(1,128)S(1)} %copy-done, f32[392,128]{1,0:T(8,128)S(1)} %get-tuple-element.13.mine, f32[392,128]{1,0:T(8,128)S(1)} %collective-permute-done.2.theirs, f32[96,128]{1,0:T(8,128)S(1)} %collective-permute-done.1.came), custom_call_target="tpu_custom_call" | custom-call | tf_op jit(solution)/shard_map/answers/pallas_call | solution.py:424
  24.3 3.2 %collective-permute-start.3 = (f32[96,128]{1,0:T(8,128)S(1)}, f32[96,128]{1,0:T(8,128)S(1)}, u32[]{:S(2)}, u32[]{:S(2)}) collective-permute-start(f32[96,128]{1,0:T(8,128)S(1)} %get-tuple-element.15), channel_id=1, source_target_pairs={{1,2},{3,4},{5,6},{7,8},{9,10},{11,12},{13,14},{2,1},{4,3},{6,5},{... | collective-permute-start | bytes 147464 | tf_op jit(solution)/shard_map/ppermute | solution.py:604
  27.5 3.6 %collective-permute-done.3.crossed = f32[96,128]{1,0:T(8,128)S(1)} collective-permute-done((f32[96,128]{1,0:T(8,128)S(1)}, f32[96,128]{1,0:T(8,128)S(1)}, u32[]{:S(2)}, u32[]{:S(2)}) %collective-permute-start.3) | collective-permute-done | bytes 49184 | tf_op jit(solution)/shard_map/ppermute | solution.py:604
  31.0 0.0 collective-permute-start.4
  31.1 1.2 %collective-permute-done.4.passed = f32[96,128]{1,0:T(8,128)S(1)} collective-permute-done((f32[96,128]{1,0:T(8,128)S(1)}, f32[96,128]{1,0:T(8,128)S(1)}, u32[]{:S(2)}, u32[]{:S(2)}) %collective-permute-start.4) | collective-permute-done | bytes 49184 | tf_op jit(solution)/shard_map/ppermute | solution.py:604
  32.3 0.0 collective-permute-done.6.arrived
  32.3 0.0 collective-permute-done.5.theirs
  32.3 3.5 %final.1 = f32[16,3,128,128]{3,2,1,0:T(8,128)} custom-call(s32[1,2]{1,0:T(1,128)S(1)} %copy-done, s32[16,4]{1,0:T(8,128)S(1)} %copy.7.table, f32[512,128]{1,0:T(8,128)S(1)} %get-tuple-element.14.edges, f32[96,128]{1,0:T(8,128)S(1)} %collective-permute-done.3.crossed, f32[96,128]{1,0:T(8,128)S(1)} %collective-permute-done.4.passed, ...), custom_call_target="tpu_custom_call" | custom-call | tf_op jit(solution)/shard_map/final/pallas_call | solution.py:584
  (1 shorter events, 0.0 us)
Async XLA Ops:
  0.8 9.7 %copy-start = (s32[1,2]{1,0:T(1,128)S(1)}, s32[1,2]{1,0:T(1,128)}, u32[]{:S(2)}) copy-start(s32[1,2]{1,0:T(1,128)} %range_ref.5) | copy-start | bytes 28
  0.8 1.5 %collective-permute-start = (s32[16,4]{1,0:T(8,128)S(1)}, s32[16,4]{1,0:T(8,128)S(1)}, u32[]{:S(2)}, u32[]{:S(2)}) collective-permute-start(s32[16,4]{1,0:T(8,128)S(1)} %copy.7.table), channel_id=1, source_target_pairs={{0,1},{2,3},{4,5},{6,7},{8,9},{10,11},{12,13},{14,15},{1,0},{3,2},... | collective-permute-start | bytes 776 | tf_op jit(solution)/shard_map/ppermute | solution.py:604
  4.9 5.6 %collective-permute-start.1 = (f32[96,128]{1,0:T(8,128)S(1)}, f32[96,128]{1,0:T(8,128)S(1)}, u32[]{:S(2)}, u32[]{:S(2)}) collective-permute-start(f32[96,128]{1,0:T(8,128)S(1)} %get-tuple-element.12.other_ref), channel_id=1, source_target_pairs={{1,2},{3,4},{5,6},{7,8},{9,10},{11,12},{13,14},{2,1},{4,3},{6,5},{... | collective-permute-start | bytes 147464 | tf_op jit(solution)/shard_map/ppermute | solution.py:604
  8.2 24.0 %collective-permute-start.6 = (f32[4,3,128,128]{3,2,1,0:T(8,128)S(1)}, f32[4,3,128,128]{3,2,1,0:T(8,128)S(1)}, u32[]{:S(2)}, u32[]{:S(2)}) collective-permute-start(f32[4,3,128,128]{3,2,1,0:T(8,128)S(1)} %after.1), channel_id=1, source_target_pairs={{1,2},{3,4},{5,6},{7,8},{9,10},{11,12},{13,14},{2,1},{4,3},{6,5},{... | collective-permute-start | bytes 2359304 | tf_op jit(solution)/shard_map/ppermute | solution.py:604
  19.6 12.6 %collective-permute-start.5 = (f32[4,3,128,128]{3,2,1,0:T(8,128)S(1)}, f32[4,3,128,128]{3,2,1,0:T(8,128)S(1)}, u32[]{:S(2)}, u32[]{:S(2)}) collective-permute-start(f32[4,3,128,128]{3,2,1,0:T(8,128)S(1)} %get-tuple-element.17), channel_id=1, source_target_pairs={{0,1},{2,3},{4,5},{6,7},{8,9},{10,11},{12,13},{14,15},{1,0},{3,2},... | collective-permute-start | bytes 2359304 | tf_op jit(solution)/shard_map/ppermute | solution.py:604
  20.9 2.2 %collective-permute-start.2 = (f32[392,128]{1,0:T(8,128)S(1)}, f32[392,128]{1,0:T(8,128)S(1)}, u32[]{:S(2)}, u32[]{:S(2)}) collective-permute-start(f32[392,128]{1,0:T(8,128)S(1)} %get-tuple-element.13.mine), channel_id=1, source_target_pairs={{0,1},{2,3},{4,5},{6,7},{8,9},{10,11},{12,13},{14,15},{1,0},{3,2},... | collective-permute-start | bytes 602120 | tf_op jit(solution)/shard_map/ppermute | solution.py:604
  24.3 6.7 %collective-permute-start.3 = (f32[96,128]{1,0:T(8,128)S(1)}, f32[96,128]{1,0:T(8,128)S(1)}, u32[]{:S(2)}, u32[]{:S(2)}) collective-permute-start(f32[96,128]{1,0:T(8,128)S(1)} %get-tuple-element.15), channel_id=1, source_target_pairs={{1,2},{3,4},{5,6},{7,8},{9,10},{11,12},{13,14},{2,1},{4,3},{6,5},{... | collective-permute-start | bytes 147464 | tf_op jit(solution)/shard_map/ppermute | solution.py:604
  31.0 1.2 %collective-permute-start.4 = (f32[96,128]{1,0:T(8,128)S(1)}, f32[96,128]{1,0:T(8,128)S(1)}, u32[]{:S(2)}, u32[]{:S(2)}) collective-permute-start(f32[96,128]{1,0:T(8,128)S(1)} %collective-permute-done.3.crossed), channel_id=1, source_target_pairs={{0,1},{2,3},{4,5},{6,7},{8,9},{10,11},{12,13},{14,15},{1,0},{3,2},... | collective-permute-start | bytes 147464 | tf_op jit(solution)/shard_map/ppermute | solution.py:604

commit v9 on v8

--- a/solution.py
+++ b/solution.py
@@ -13,6 +13,7 @@
 CAP = 8
 ROWS = 8
 PAIR = 2
+FIRST = 0
 VMEM = pl.BlockSpec(memory_space=pltpu.VMEM)
 SMEM = pl.BlockSpec(memory_space=pltpu.SMEM)
 HBM = pl.BlockSpec(memory_space=pltpu.HBM)
@@ -67,8 +68,9 @@
 
 
 def inner_update(loads, store, side, weights):
-    line = iota(0, side)
+    line, lane = iota(0, side), iota(1, side)
     first, last = line == 0, line == ROWS - 1
+    rim = jnp.where(lane == 0, 2.0, jnp.where(lane == side - 1, -2.0, 0.0))
     steps = side // ROWS
     many = len(loads)
 
@@ -101,7 +103,7 @@
     fx = stack(lambda c: c[2])
     rates = product(stack(lambda c: c[1]), taken(AHEAD))
     jumps = product(jnp.concatenate([eta, mx, my], axis=0), taken(EAST))
-    sums = product(jnp.concatenate([mx, fx, cross], axis=0), taken(SUMS))
+    sums = product(jnp.concatenate([fx, cross], axis=0), taken(SUMS))
     slopes = product(bed, taken(SLOPE))
     for n in range(many):
         mine = cells[n * steps : (n + 1) * steps]
@@ -121,7 +123,8 @@
             rows = [slice(r, r + ROWS) for r in at]
             top_e = jnp.maximum(rate, rates[rows[0], :side])
             top_w = jnp.maximum(rate, rates[rows[0], side:])
-            x = [sums[r] - (top_e * jumps[r, :side] - top_w * jumps[r, side:]) for r in rows]
+            total = [jumps[rows[1], :side] + jumps[rows[1], side:] + rim * mx, sums[rows[0]], sums[rows[1]]]
+            x = [t - (top_e * jumps[r, :side] - top_w * jumps[r, side:]) for t, r in zip(total, rows)]
             south, north = faces[j], faces[j + 1]
             slope_y = (beds[j + 1] if j + 1 < steps else over) - (beds[j - 1] if j else under)
             store(n, 0, j, h - HALF * (x[0] + (north[0] - south[0])))
@@ -176,26 +179,30 @@
     return odd * (cells_hbm.shape[0] - margin)
 
 
-def outer_kernel(margin, cells_hbm, table, their_table, out, bundle, cells, columns, weights, sems):
+def bundle_layout(margin):
+    tables = 16 * margin
+    return tables, tables + 16
+
+
+def outer_kernel(margin, cells_hbm, table, rest, bundle, cells, columns, weights, sems):
     side = columns.shape[0]
     _, odd = position()
     copy = fetch(cells_hbm, outer_slot(cells_hbm, margin), cells, sems, [(0, margin)])
     fill_weights(weights)
-    count, sides = table.shape
-    at = 16 * margin
-    bundle[at : at + 2 * count, :] = jnp.zeros((2 * count, side), jnp.float32)
-    for which, ref in ((odd, table), (1 - odd, their_table)):
-        start = pl.multiple_of(at + which * count, 8)
-        bundle[pl.ds(start, count), 0:sides] = ref[...].astype(jnp.float32)
-
-    @pl.loop(0, margin // PAIR)
-    def _(step):
-        i = step * PAIR
+    tables, results = bundle_layout(margin)
+    sides, count = table.shape
+    bundle[tables:results, :] = jnp.zeros((results - tables, side), jnp.float32)
+    bundle[pl.ds(pl.multiple_of(tables + 8 * odd, 8), sides), 0:count] = table[...].astype(jnp.float32)
+    for i in range(0, margin, PAIR):
         for n in range(PAIR):
             copy(i + n).wait()
 
-        def put(n, f, row, value):
-            out[i + n, f, row : row + ROWS, :] = value
+        def put(n, f, row, value, i=i):
+            if i + n < FIRST:
+                at = results + (3 * (i + n) + f) * side + row
+                bundle[at : at + ROWS, :] = value
+            else:
+                rest[i + n - FIRST, f, row : row + ROWS, :] = value
 
         gather_columns([loader(cells, i + n) for n in range(PAIR)], columns, 8 * i, side)
         update(cells, i, PAIR, weights, put)
@@ -204,26 +211,22 @@
 
 
 def cost(patches, side):
-    return pl.CostEstimate(
-        flops=patches * side * side * 800,
-        bytes_accessed=patches * side * side * 28,
-        transcendentals=patches * side * side,
-    )
+    return pl.CostEstimate(flops=patches * side, bytes_accessed=patches * side, transcendentals=0)
 
 
 def room(mebibytes):
     return pltpu.CompilerParams(vmem_limit_bytes=mebibytes << 20)
 
 
-def outer_patches(old_cells, table, their_table, margin):
+def outer_patches(old_cells, table, margin):
     side = old_cells.shape[3]
     return pl.pallas_call(
         functools.partial(outer_kernel, margin),
-        in_specs=[HBM, VMEM, VMEM],
+        in_specs=[HBM, VMEM],
         out_specs=[VMEM, VMEM],
         out_shape=[
-            jax.ShapeDtypeStruct((margin, 3, side, side), jnp.float32),
-            jax.ShapeDtypeStruct((16 * margin + 2 * table.shape[0], side), jnp.float32),
+            jax.ShapeDtypeStruct((margin - FIRST, 3, side, side), jnp.float32),
+            jax.ShapeDtypeStruct((bundle_layout(margin)[1] + 3 * FIRST * side, side), jnp.float32),
         ],
         scratch_shapes=[
             pltpu.VMEM((margin, 4, side, side), jnp.float32),
@@ -234,7 +237,34 @@
         cost_estimate=cost(margin, side),
         compiler_params=room(48),
         name="outer",
-    )(old_cells, table, their_table)
+    )(old_cells, table)
+
+
+def placed_rows(rows, start_of, bundle, extra, name):
+    any_place = pl.BlockSpec(memory_space=pl.ANY)
+    small = rows == 8
+
+    def kernel(bundle_ref, extra_ref, out_ref, held, sem):
+        source = extra_ref
+        if small:
+            held[...] = jnp.zeros_like(held)
+            held[0 : extra_ref.shape[0], 0 : extra_ref.shape[1]] = extra_ref[...].astype(jnp.float32)
+            source = held
+        start = pl.multiple_of(start_of(), 8)
+        copy = pltpu.make_async_copy(source.at[pl.ds(0, rows), :], out_ref.at[pl.ds(start, rows), :], sem)
+        copy.start()
+        copy.wait()
+
+    return pl.pallas_call(
+        kernel,
+        in_specs=[any_place, VMEM if small else any_place],
+        out_specs=any_place,
+        out_shape=jax.ShapeDtypeStruct(bundle.shape, bundle.dtype),
+        scratch_shapes=[pltpu.VMEM((8, bundle.shape[1]), jnp.float32), pltpu.SemaphoreType.DMA],
+        input_output_aliases={0: 0},
+        compiler_params=room(4),
+        name=name,
+    )(bundle, extra)
 
 
 def after(value, other):
@@ -391,7 +421,8 @@
     lane = grid_iota(total, side, 1)
     which, within = row // (sides * count), row % (sides * count)
     at = 16 * margin
-    tables = [came[at + n * count : at + (n + 1) * count, :] for n in range(2)]
+    turned = jnp.transpose(jnp.concatenate([came[at : at + 16, :], jnp.zeros((side - 16, side), jnp.float32)], axis=0))
+    tables = [turned[0:count, 8 * n : 8 * n + sides] for n in range(2)]
     listed = jnp.concatenate([entries_of(table, sides, side) for table in tables], axis=0)
     patch = listed - (2 * count * (me // 2)).astype(jnp.float32)
     held = [(patch >= n * count) & (patch < (n + 1) * count) for n in range(2)]
@@ -434,14 +465,16 @@
     )(old_range, mine, theirs, came)
 
 
-def ghosts(table, edges, crossed, passed, me, odd):
-    count, sides = table.shape
+def ghosts(table, edges, crossed, passed, turn, me, odd):
+    sides, count = table.shape
     side = edges.shape[1]
     total = sides * count
     even = odd == 0
     row, lane = grid_iota(total, side, 0), grid_iota(total, side, 1)
     s, p = row // count, row % count
-    listed = entries_of(table[...].astype(jnp.float32), sides, side)
+    turn[...] = jnp.zeros_like(turn)
+    turn[0:sides, 0:count] = table[...].astype(jnp.float32)
+    listed = entries_of(jnp.transpose(turn[...])[0:count, :], sides, side)
     wall = listed < 0.0
     patch = listed - (2 * count * (me // 2)).astype(jnp.float32)
     distance = listed - (count * me).astype(jnp.float32)
@@ -481,8 +514,8 @@
 
 
 def rim_terms(table, edges, crossed, passed, columns, lines, turn, me, odd):
-    count = table.shape[0]
-    outside, wall = ghosts(table, edges, crossed, passed, me, odd)
+    count = table.shape[1]
+    outside, wall = ghosts(table, edges, crossed, passed, turn, me, odd)
     turn[...] = jnp.zeros_like(turn)
     lines[...] = jnp.zeros_like(lines)
     for s in range(4):
@@ -529,7 +562,7 @@
 
 
 def final_kernel(
-    margin, range_ref, table, edges, crossed, passed, own, theirs, arrived, out,
+    margin, range_ref, table, edges, crossed, passed, own, theirs, came, arrived, out,
     result, turn, columns, lines, places, sems,
 ):
     count, side = own.shape[0], lines.shape[1]
@@ -541,6 +574,7 @@
     line = iota(0, side)
     lane = lax.broadcasted_iota(jnp.int32, (side, 2 * side), 1) % side
     steps = side // ROWS
+    results = bundle_layout(margin)[1]
 
     def copy(p):
         return pltpu.make_async_copy(result.at[p], out.at[p], sems.at[p])
@@ -563,7 +597,12 @@
                     rows = slice(ROWS * j, ROWS * (j + 1))
                     value = own[p, f, rows, :]
                     if taken is not None:
-                        moved = jnp.where(near, theirs[m, f, rows, :], arrived[m, f, rows, :])
+                        if m < FIRST:
+                            at = results + (3 * m + f) * side + ROWS * j
+                            crossing = came[at : at + ROWS, :]
+                        else:
+                            crossing = arrived[m - FIRST, f, rows, :]
+                        moved = jnp.where(near, theirs[m, f, rows, :], crossing)
                         value = jnp.where(taken, moved, value)
                     at = side * m + ROWS * j
                     value = value + terms[at : at + ROWS, f * side : (f + 1) * side]
@@ -579,11 +618,11 @@
         copy(p).wait()
 
 
-def finished(old_range, table, edges, crossed, passed, own, theirs, arrived, margin):
+def finished(old_range, table, edges, crossed, passed, own, theirs, came, arrived, margin):
     count, _, side, _ = own.shape
     return pl.pallas_call(
         functools.partial(final_kernel, margin),
-        in_specs=[SMEM] + [VMEM] * 7,
+        in_specs=[SMEM] + [VMEM] * 8,
         out_specs=HBM,
         out_shape=jax.ShapeDtypeStruct(own.shape, jnp.float32),
         scratch_shapes=[
@@ -596,7 +635,7 @@
         ],
         compiler_params=room(12),
         name="final",
-    )(old_range, table, edges, crossed, passed, own, theirs, arrived)
+    )(old_range, table, edges, crossed, passed, own, theirs, came, arrived)
 
 
 def swapped(value, first):
@@ -607,17 +646,20 @@
 def local(old_cells, old_range, neighbours):
     per_device = neighbours.shape[0]
     margin = (old_cells.shape[0] - per_device) // 2
-    their_table = swapped(neighbours, 0)
-    leaving, bundle = outer_patches(old_cells, neighbours, their_table, margin)
+    table = neighbours.T
+    their_table = swapped(table, 0)
+    rest, bundle = outer_patches(old_cells, table, margin)
+    their_row = lambda: bundle_layout(margin)[0] + 8 * (1 - position()[1])
+    bundle = placed_rows(8, their_row, bundle, their_table, "tables")
     came = swapped(bundle, 1)
-    arrived = swapped(after(leaving, bundle), 1)
+    arrived = swapped(after(rest, bundle), 1)
     shared, inner, own = home_patches(old_range, old_cells, came, margin, per_device)
     their_edges = swapped(shared, 0)
-    theirs = swapped(inner, 0)
+    theirs = swapped(after(inner, their_edges), 0)
     edges, message = answers(old_range, shared, their_edges, came, margin, per_device)
     crossed = swapped(message, 1)
     passed = swapped(crossed, 0)
-    return finished(old_range, neighbours, edges, crossed, passed, own, theirs, arrived, margin)
+    return finished(old_range, table, edges, crossed, passed, own, theirs, came, arrived, margin)
 
 
 def solution(mesh):

time: 36 us -> 47.3 us (1.31)
  waiting for transfers between devices: 7.71 us -> 18.9 us
    ppermute x7, waiting for transfers between devices: 7.71 us -> 18.9 us  [swapped(): return lax.ppermute(value, AXES, pairs + [(j, i) for i, j in pairs])]
  transfers between devices with their start and end apart: 7 -> 7, of which waited for: 4 -> 3; matrix products, arithmetic and copies ran while one was open for 0% -> 0% of each run, Pallas kernels for 29% -> 8%
where the time goes in v9:
time: 47.3 us; the launch traced here: 47.1 us
  waiting for transfers between devices  18.9 us (40%)
  Pallas kernels  16.4 us (35%)
  starting transfers between devices  10.9 us (23%)
  local copies, waits for them, and re-layouts  0.69 us (1%)
    ppermute x7, waiting for transfers between devices, swapped(): return lax.ppermute(value, AXES, pairs + [(j, i) for i, j in pairs])  18.9 us
    ppermute x7, starting transfers between devices, swapped(): return lax.ppermute(value, AXES, pairs + [(j, i) for i, j in pairs])  10.9 us
    pallas_call x1, Pallas kernels, home_patches(): pl.pallas_call(functools.partial(home_kernel, margin), in_specs=[SMEM, HB...  9.12 us
    pallas_call x1, Pallas kernels, finished(): pl.pallas_call(functools.partial(final_kernel, margin), in_specs=[SMEM] +...  3.56 us
    pallas_call x1, Pallas kernels, outer_patches(): pl.pallas_call(functools.partial(outer_kernel, margin), in_specs=[HBM, VM...  2.51 us
    pallas_call x1, Pallas kernels, answers(): pl.pallas_call(functools.partial(answer_kernel, margin, per_device), in_s...  1.19 us
  transfers between devices with their start and end apart: 7, of which 3 were waited for; matrix products, arithmetic and copies ran while one was open for 0% of the time, Pallas kernels for 8%

profile of v9, /device:TPU:17, one launch (start us, length us, event | category | flops | bytes accessed | tf_op | source)
XLA Modules:
  0.0 47.1 jit_solution(7546299120741146410)
XLA Ops:
  0.0 0.7 %collective-permute-start = (s32[4,16]{1,0:T(4,128)}, s32[4,16]{1,0:T(4,128)S(1)}, u32[]{:S(2)}, u32[]{:S(2)}) collective-permute-start(s32[4,16]{1,0:T(4,128)} %bitcast.1), channel_id=1, source_target_pairs={{0,1},{2,3},{4,5},{6,7},{8,9},{10,11},{12,13},{14,15},{1,0},{3,2},... | collective-permute-start | bytes 776 | tf_op jit(solution)/shard_map/ppermute | solution.py:643
  0.7 0.0 copy-start
  0.7 0.7 %copy-done = s32[16,4]{0,1:T(4,128)S(1)} copy-done((s32[16,4]{0,1:T(4,128)S(1)}, s32[16,4]{0,1:T(4,128)}, u32[]{:S(2)}) %copy-start) | copy-done | bytes 280
  1.4 0.0 copy-start.2
  1.4 2.5 %outer.1 = (f32[4,3,128,128]{3,2,1,0:T(8,128)S(1)}, f32[80,128]{1,0:T(8,128)S(1)}) custom-call(f32[24,4,128,128]{3,2,1,0:T(8,128)} %cells_hbm.3, s32[4,16]{1,0:T(4,128)S(1)} %bitcast.2), custom_call_target="tpu_custom_call" | custom-call | flops 512 | bytes 512 | tf_op jit(solution)/shard_map/outer/pallas_call | solution.py:223
  3.9 0.0 collective-permute-done.extra_ref
  3.9 3.0 %collective-permute-start.1 = (f32[80,128]{1,0:T(8,128)S(1)}, f32[80,128]{1,0:T(8,128)S(1)}, u32[]{:S(2)}, u32[]{:S(2)}) collective-permute-start(f32[80,128]{1,0:T(8,128)S(1)} %tables.1.other_ref), channel_id=1, source_target_pairs={{1,2},{3,4},{5,6},{7,8},{9,10},{11,12},{13,14},{2,1},{4,3},{6,5},{... | collective-permute-start | bytes 122888 | tf_op jit(solution)/shard_map/ppermute | solution.py:643
  6.9 2.8 %collective-permute-done.1.came = f32[80,128]{1,0:T(8,128)S(1)} collective-permute-done((f32[80,128]{1,0:T(8,128)S(1)}, f32[80,128]{1,0:T(8,128)S(1)}, u32[]{:S(2)}, u32[]{:S(2)}) %collective-permute-start.1) | collective-permute-done | bytes 40992 | tf_op jit(solution)/shard_map/ppermute | solution.py:643
  9.8 0.0 copy-done.2
  9.8 9.1 %home.1 = (f32[392,128]{1,0:T(8,128)S(1)}, f32[4,3,128,128]{3,2,1,0:T(8,128)S(1)}, f32[16,3,128,128]{3,2,1,0:T(8,128)S(1)}) custom-call(s32[1,2]{1,0:T(1,128)S(1)} %copy-done.2, f32[24,4,128,128]{3,2,1,0:T(8,128)} %cells_hbm.3, f32[80,128]{1,0:T(8,128)S(1)} %collective-permute-done.1.came), custom_call_target="tpu_custom_call" | custom-call | flops 2560 | bytes 2560 | tf_op jit(solution)/shard_map/home/pallas_call | solution.py:325
  18.9 0.0 copy-start.1
  18.9 0.6 %collective-permute-start.2 = (f32[392,128]{1,0:T(8,128)S(1)}, f32[392,128]{1,0:T(8,128)S(1)}, u32[]{:S(2)}, u32[]{:S(2)}) collective-permute-start(f32[392,128]{1,0:T(8,128)S(1)} %get-tuple-element.13.mine), channel_id=1, source_target_pairs={{0,1},{2,3},{4,5},{6,7},{8,9},{10,11},{12,13},{14,15},{1,0},{3,2},... | collective-permute-start | bytes 602120 | tf_op jit(solution)/shard_map/ppermute | solution.py:643
  19.5 3.4 %collective-permute-start.6 = (f32[4,3,128,128]{3,2,1,0:T(8,128)S(1)}, f32[4,3,128,128]{3,2,1,0:T(8,128)S(1)}, u32[]{:S(2)}, u32[]{:S(2)}) collective-permute-start(f32[4,3,128,128]{3,2,1,0:T(8,128)S(1)} %after.3), channel_id=1, source_target_pairs={{1,2},{3,4},{5,6},{7,8},{9,10},{11,12},{13,14},{2,1},{4,3},{6,5},{... | collective-permute-start | bytes 2359304 | tf_op jit(solution)/shard_map/ppermute | solution.py:643
  22.9 0.0 collective-permute-done.2.theirs.other_ref
  22.9 0.1 collective-permute-start.5
  23.0 1.2 %answers.1 = (f32[512,128]{1,0:T(8,128)S(1)}, f32[96,128]{1,0:T(8,128)S(1)}) custom-call(s32[1,2]{1,0:T(1,128)S(1)} %copy-done.2, f32[392,128]{1,0:T(8,128)S(1)} %get-tuple-element.13.mine, f32[392,128]{1,0:T(8,128)S(1)} %collective-permute-done.2.theirs.other_ref, f32[80,128]{1,0:T(8,128)S(1)} %collective-permute-done.1.came), custom_call_target="tpu_custom_call" | custom-call | tf_op jit(solution)/shard_map/answers/pallas_call | solution.py:455
  24.2 3.2 %collective-permute-start.3 = (f32[96,128]{1,0:T(8,128)S(1)}, f32[96,128]{1,0:T(8,128)S(1)}, u32[]{:S(2)}, u32[]{:S(2)}) collective-permute-start(f32[96,128]{1,0:T(8,128)S(1)} %get-tuple-element.15), channel_id=1, source_target_pairs={{1,2},{3,4},{5,6},{7,8},{9,10},{11,12},{13,14},{2,1},{4,3},{6,5},{... | collective-permute-start | bytes 147464 | tf_op jit(solution)/shard_map/ppermute | solution.py:643
  27.4 14.9 %collective-permute-done.3.crossed = f32[96,128]{1,0:T(8,128)S(1)} collective-permute-done((f32[96,128]{1,0:T(8,128)S(1)}, f32[96,128]{1,0:T(8,128)S(1)}, u32[]{:S(2)}, u32[]{:S(2)}) %collective-permute-start.3) | collective-permute-done | bytes 49184 | tf_op jit(solution)/shard_map/ppermute | solution.py:643
  42.2 0.0 collective-permute-start.4
  42.2 1.2 %collective-permute-done.4.passed = f32[96,128]{1,0:T(8,128)S(1)} collective-permute-done((f32[96,128]{1,0:T(8,128)S(1)}, f32[96,128]{1,0:T(8,128)S(1)}, u32[]{:S(2)}, u32[]{:S(2)}) %collective-permute-start.4) | collective-permute-done | bytes 49184 | tf_op jit(solution)/shard_map/ppermute | solution.py:643
  43.5 0.0 collective-permute-done.6.arrived
  43.5 0.0 collective-permute-done.5.theirs
  43.5 0.0 copy-done.1
  43.5 3.6 %final.1 = f32[16,3,128,128]{3,2,1,0:T(8,128)} custom-call(s32[1,2]{1,0:T(1,128)S(1)} %copy-done.2, s32[4,16]{1,0:T(4,128)S(1)} %bitcast.3, f32[512,128]{1,0:T(8,128)S(1)} %get-tuple-element.14.edges, f32[96,128]{1,0:T(8,128)S(1)} %collective-permute-done.3.crossed, f32[96,128]{1,0:T(8,128)S(1)} %collective-permute-done.4.passed, ...), custom_call_target="tpu_custom_call" | custom-call | tf_op jit(solution)/shard_map/final/pallas_call | solution.py:623
  (3 shorter events, 0.0 us)
Async XLA Ops:
  0.0 3.9 %collective-permute-start = (s32[4,16]{1,0:T(4,128)}, s32[4,16]{1,0:T(4,128)S(1)}, u32[]{:S(2)}, u32[]{:S(2)}) collective-permute-start(s32[4,16]{1,0:T(4,128)} %bitcast.1), channel_id=1, source_target_pairs={{0,1},{2,3},{4,5},{6,7},{8,9},{10,11},{12,13},{14,15},{1,0},{3,2},... | collective-permute-start | bytes 776 | tf_op jit(solution)/shard_map/ppermute | solution.py:643
  0.7 0.7 %copy-start = (s32[16,4]{0,1:T(4,128)S(1)}, s32[16,4]{0,1:T(4,128)}, u32[]{:S(2)}) copy-start(s32[16,4]{0,1:T(4,128)} %param.5) | copy-start | bytes 772
  1.4 8.4 %copy-start.2 = (s32[1,2]{1,0:T(1,128)S(1)}, s32[1,2]{1,0:T(1,128)}, u32[]{:S(2)}) copy-start(s32[1,2]{1,0:T(1,128)} %range_ref.5) | copy-start | bytes 28
  3.9 5.8 %collective-permute-start.1 = (f32[80,128]{1,0:T(8,128)S(1)}, f32[80,128]{1,0:T(8,128)S(1)}, u32[]{:S(2)}, u32[]{:S(2)}) collective-permute-start(f32[80,128]{1,0:T(8,128)S(1)} %tables.1.other_ref), channel_id=1, source_target_pairs={{1,2},{3,4},{5,6},{7,8},{9,10},{11,12},{13,14},{2,1},{4,3},{6,5},{... | collective-permute-start | bytes 122888 | tf_op jit(solution)/shard_map/ppermute | solution.py:643
  18.9 24.6 %copy-start.1 = (s32[16,4]{0,1:T(4,128)S(1)}, s32[16,4]{0,1:T(4,128)}, u32[]{:S(2)}) copy-start(s32[16,4]{0,1:T(4,128)} %param.5) | copy-start | bytes 772
  18.9 4.0 %collective-permute-start.2 = (f32[392,128]{1,0:T(8,128)S(1)}, f32[392,128]{1,0:T(8,128)S(1)}, u32[]{:S(2)}, u32[]{:S(2)}) collective-permute-start(f32[392,128]{1,0:T(8,128)S(1)} %get-tuple-element.13.mine), channel_id=1, source_target_pairs={{0,1},{2,3},{4,5},{6,7},{8,9},{10,11},{12,13},{14,15},{1,0},{3,2},... | collective-permute-start | bytes 602120 | tf_op jit(solution)/shard_map/ppermute | solution.py:643
  19.5 24.0 %collective-permute-start.6 = (f32[4,3,128,128]{3,2,1,0:T(8,128)S(1)}, f32[4,3,128,128]{3,2,1,0:T(8,128)S(1)}, u32[]{:S(2)}, u32[]{:S(2)}) collective-permute-start(f32[4,3,128,128]{3,2,1,0:T(8,128)S(1)} %after.3), channel_id=1, source_target_pairs={{1,2},{3,4},{5,6},{7,8},{9,10},{11,12},{13,14},{2,1},{4,3},{6,5},{... | collective-permute-start | bytes 2359304 | tf_op jit(solution)/shard_map/ppermute | solution.py:643
  22.9 20.6 %collective-permute-start.5 = (f32[4,3,128,128]{3,2,1,0:T(8,128)S(1)}, f32[4,3,128,128]{3,2,1,0:T(8,128)S(1)}, u32[]{:S(2)}, u32[]{:S(2)}) collective-permute-start(f32[4,3,128,128]{3,2,1,0:T(8,128)S(1)} %after.2), channel_id=1, source_target_pairs={{0,1},{2,3},{4,5},{6,7},{8,9},{10,11},{12,13},{14,15},{1,0},{3,2},... | collective-permute-start | bytes 2359304 | tf_op jit(solution)/shard_map/ppermute | solution.py:643
  24.2 18.1 %collective-permute-start.3 = (f32[96,128]{1,0:T(8,128)S(1)}, f32[96,128]{1,0:T(8,128)S(1)}, u32[]{:S(2)}, u32[]{:S(2)}) collective-permute-start(f32[96,128]{1,0:T(8,128)S(1)} %get-tuple-element.15), channel_id=1, source_target_pairs={{1,2},{3,4},{5,6},{7,8},{9,10},{11,12},{13,14},{2,1},{4,3},{6,5},{... | collective-permute-start | bytes 147464 | tf_op jit(solution)/shard_map/ppermute | solution.py:643
  42.2 1.2 %collective-permute-start.4 = (f32[96,128]{1,0:T(8,128)S(1)}, f32[96,128]{1,0:T(8,128)S(1)}, u32[]{:S(2)}, u32[]{:S(2)}) collective-permute-start(f32[96,128]{1,0:T(8,128)S(1)} %collective-permute-done.3.crossed), channel_id=1, source_target_pairs={{0,1},{2,3},{4,5},{6,7},{8,9},{10,11},{12,13},{14,15},{1,0},{3,2},... | collective-permute-start | bytes 147464 | tf_op jit(solution)/shard_map/ppermute | solution.py:643

commit v10 on v9

--- a/solution.py
+++ b/solution.py
@@ -211,7 +211,11 @@
 
 
 def cost(patches, side):
-    return pl.CostEstimate(flops=patches * side, bytes_accessed=patches * side, transcendentals=0)
+    return pl.CostEstimate(
+        flops=patches * side * side * 800,
+        bytes_accessed=patches * side * side * 28,
+        transcendentals=patches * side * side,
+    )
 
 
 def room(mebibytes):
@@ -655,7 +659,7 @@
     arrived = swapped(after(rest, bundle), 1)
     shared, inner, own = home_patches(old_range, old_cells, came, margin, per_device)
     their_edges = swapped(shared, 0)
-    theirs = swapped(after(inner, their_edges), 0)
+    theirs = swapped(inner, 0)
     edges, message = answers(old_range, shared, their_edges, came, margin, per_device)
     crossed = swapped(message, 1)
     passed = swapped(crossed, 0)

time: 47.3 us -> 34.8 us (0.74)
  waiting for transfers between devices: 18.9 us -> 6.69 us
    ppermute x7, waiting for transfers between devices: 18.9 us -> 6.69 us  [swapped(): return lax.ppermute(value, AXES, pairs + [(j, i) for i, j in pairs])]
  transfers between devices with their start and end apart: 7 -> 7, of which waited for: 3 -> 4; matrix products, arithmetic and copies ran while one was open for 0% -> 0% of each run, Pallas kernels for 8% -> 37%
where the time goes in v10:
time: 34.8 us; the launch traced here: 34.6 us
  Pallas kernels  16.4 us (47%)
  starting transfers between devices  10.7 us (31%)
  waiting for transfers between devices  6.69 us (19%)
  local copies, waits for them, and re-layouts  0.69 us (2%)
    ppermute x7, starting transfers between devices, swapped(): return lax.ppermute(value, AXES, pairs + [(j, i) for i, j in pairs])  10.7 us
    pallas_call x1, Pallas kernels, home_patches(): pl.pallas_call(functools.partial(home_kernel, margin), in_specs=[SMEM, HB...  9.12 us
    ppermute x7, waiting for transfers between devices, swapped(): return lax.ppermute(value, AXES, pairs + [(j, i) for i, j in pairs])  6.69 us
    pallas_call x1, Pallas kernels, finished(): pl.pallas_call(functools.partial(final_kernel, margin), in_specs=[SMEM] +...  3.56 us
    pallas_call x1, Pallas kernels, outer_patches(): pl.pallas_call(functools.partial(outer_kernel, margin), in_specs=[HBM, VM...  2.51 us
    pallas_call x1, Pallas kernels, answers(): pl.pallas_call(functools.partial(answer_kernel, margin, per_device), in_s...  1.19 us
  transfers between devices with their start and end apart: 7, of which 4 were waited for; matrix products, arithmetic and copies ran while one was open for 0% of the time, Pallas kernels for 37%

profile of v10, /device:TPU:17, one launch (start us, length us, event | category | flops | bytes accessed | tf_op | source)
XLA Modules:
  0.0 34.6 jit_solution(6081491075302544264)
XLA Ops:
  0.0 0.7 %collective-permute-start = (s32[4,16]{1,0:T(4,128)}, s32[4,16]{1,0:T(4,128)S(1)}, u32[]{:S(2)}, u32[]{:S(2)}) collective-permute-start(s32[4,16]{1,0:T(4,128)} %bitcast.1), channel_id=1, source_target_pairs={{0,1},{2,3},{4,5},{6,7},{8,9},{10,11},{12,13},{14,15},{1,0},{3,2},... | collective-permute-start | bytes 776 | tf_op jit(solution)/shard_map/ppermute | solution.py:647
  0.7 0.0 copy-start
  0.7 0.7 %copy-done = s32[16,4]{0,1:T(4,128)S(1)} copy-done((s32[16,4]{0,1:T(4,128)S(1)}, s32[16,4]{0,1:T(4,128)}, u32[]{:S(2)}) %copy-start) | copy-done | bytes 280
  1.4 0.0 copy-start.2
  1.4 2.5 %outer.1 = (f32[4,3,128,128]{3,2,1,0:T(8,128)S(1)}, f32[80,128]{1,0:T(8,128)S(1)}) custom-call(f32[24,4,128,128]{3,2,1,0:T(8,128)} %cells_hbm.3, s32[4,16]{1,0:T(4,128)S(1)} %bitcast.2), custom_call_target="tpu_custom_call" | custom-call | flops 52428800 | bytes 1835008 | tf_op jit(solution)/shard_map/outer/pallas_call | solution.py:227
  3.9 0.0 collective-permute-done.extra_ref
  3.9 3.0 %collective-permute-start.1 = (f32[80,128]{1,0:T(8,128)S(1)}, f32[80,128]{1,0:T(8,128)S(1)}, u32[]{:S(2)}, u32[]{:S(2)}) collective-permute-start(f32[80,128]{1,0:T(8,128)S(1)} %tables.1.other_ref), channel_id=1, source_target_pairs={{1,2},{3,4},{5,6},{7,8},{9,10},{11,12},{13,14},{2,1},{4,3},{6,5},{... | collective-permute-start | bytes 122888 | tf_op jit(solution)/shard_map/ppermute | solution.py:647
  7.0 0.0 copy-start.1
  7.0 2.6 %collective-permute-start.6 = (f32[4,3,128,128]{3,2,1,0:T(8,128)S(1)}, f32[4,3,128,128]{3,2,1,0:T(8,128)S(1)}, u32[]{:S(2)}, u32[]{:S(2)}) collective-permute-start(f32[4,3,128,128]{3,2,1,0:T(8,128)S(1)} %after.1), channel_id=1, source_target_pairs={{1,2},{3,4},{5,6},{7,8},{9,10},{11,12},{13,14},{2,1},{4,3},{6,5},{... | collective-permute-start | bytes 2359304 | tf_op jit(solution)/shard_map/ppermute | solution.py:647
  9.5 0.2 collective-permute-done.1.came
  9.8 0.0 copy-done.2
  9.8 9.1 %home.1 = (f32[392,128]{1,0:T(8,128)S(1)}, f32[4,3,128,128]{3,2,1,0:T(8,128)S(1)}, f32[16,3,128,128]{3,2,1,0:T(8,128)S(1)}) custom-call(s32[1,2]{1,0:T(1,128)S(1)} %copy-done.2, f32[24,4,128,128]{3,2,1,0:T(8,128)} %cells_hbm.3, f32[80,128]{1,0:T(8,128)S(1)} %collective-permute-done.1.came), custom_call_target="tpu_custom_call" | custom-call | flops 262144000 | bytes 9175040 | tf_op jit(solution)/shard_map/home/pallas_call | solution.py:329
  18.9 0.8 %collective-permute-start.5 = (f32[4,3,128,128]{3,2,1,0:T(8,128)S(1)}, f32[4,3,128,128]{3,2,1,0:T(8,128)S(1)}, u32[]{:S(2)}, u32[]{:S(2)}) collective-permute-start(f32[4,3,128,128]{3,2,1,0:T(8,128)S(1)} %get-tuple-element.17), channel_id=1, source_target_pairs={{0,1},{2,3},{4,5},{6,7},{8,9},{10,11},{12,13},{14,15},{1,0},{3,2},... | collective-permute-start | bytes 2359304 | tf_op jit(solution)/shard_map/ppermute | solution.py:647
  19.6 0.1 collective-permute-start.2
  19.7 2.1 %collective-permute-done.2.theirs = f32[392,128]{1,0:T(8,128)S(1)} collective-permute-done((f32[392,128]{1,0:T(8,128)S(1)}, f32[392,128]{1,0:T(8,128)S(1)}, u32[]{:S(2)}, u32[]{:S(2)}) %collective-permute-start.2) | collective-permute-done | bytes 200736 | tf_op jit(solution)/shard_map/ppermute | solution.py:647
  21.8 1.2 %answers.1 = (f32[512,128]{1,0:T(8,128)S(1)}, f32[96,128]{1,0:T(8,128)S(1)}) custom-call(s32[1,2]{1,0:T(1,128)S(1)} %copy-done.2, f32[392,128]{1,0:T(8,128)S(1)} %get-tuple-element.13.mine, f32[392,128]{1,0:T(8,128)S(1)} %collective-permute-done.2.theirs, f32[80,128]{1,0:T(8,128)S(1)} %collective-permute-done.1.came), custom_call_target="tpu_custom_call" | custom-call | tf_op jit(solution)/shard_map/answers/pallas_call | solution.py:459
  23.0 3.5 %collective-permute-start.3 = (f32[96,128]{1,0:T(8,128)S(1)}, f32[96,128]{1,0:T(8,128)S(1)}, u32[]{:S(2)}, u32[]{:S(2)}) collective-permute-start(f32[96,128]{1,0:T(8,128)S(1)} %get-tuple-element.15), channel_id=1, source_target_pairs={{1,2},{3,4},{5,6},{7,8},{9,10},{11,12},{13,14},{2,1},{4,3},{6,5},{... | collective-permute-start | bytes 147464 | tf_op jit(solution)/shard_map/ppermute | solution.py:647
  26.6 3.2 %collective-permute-done.3.crossed = f32[96,128]{1,0:T(8,128)S(1)} collective-permute-done((f32[96,128]{1,0:T(8,128)S(1)}, f32[96,128]{1,0:T(8,128)S(1)}, u32[]{:S(2)}, u32[]{:S(2)}) %collective-permute-start.3) | collective-permute-done | bytes 49184 | tf_op jit(solution)/shard_map/ppermute | solution.py:647
  29.8 0.1 collective-permute-start.4
  29.8 1.1 %collective-permute-done.4.passed = f32[96,128]{1,0:T(8,128)S(1)} collective-permute-done((f32[96,128]{1,0:T(8,128)S(1)}, f32[96,128]{1,0:T(8,128)S(1)}, u32[]{:S(2)}, u32[]{:S(2)}) %collective-permute-start.4) | collective-permute-done | bytes 49184 | tf_op jit(solution)/shard_map/ppermute | solution.py:647
  31.0 0.0 collective-permute-done.6.arrived
  31.0 0.0 collective-permute-done.5.theirs
  31.0 0.0 copy-done.1
  31.0 3.6 %final.1 = f32[16,3,128,128]{3,2,1,0:T(8,128)} custom-call(s32[1,2]{1,0:T(1,128)S(1)} %copy-done.2, s32[4,16]{1,0:T(4,128)S(1)} %bitcast.3, f32[512,128]{1,0:T(8,128)S(1)} %get-tuple-element.14.edges, f32[96,128]{1,0:T(8,128)S(1)} %collective-permute-done.3.crossed, f32[96,128]{1,0:T(8,128)S(1)} %collective-permute-done.4.passed, ...), custom_call_target="tpu_custom_call" | custom-call | tf_op jit(solution)/shard_map/final/pallas_call | solution.py:627
  (2 shorter events, 0.0 us)
Async XLA Ops:
  0.0 3.9 %collective-permute-start = (s32[4,16]{1,0:T(4,128)}, s32[4,16]{1,0:T(4,128)S(1)}, u32[]{:S(2)}, u32[]{:S(2)}) collective-permute-start(s32[4,16]{1,0:T(4,128)} %bitcast.1), channel_id=1, source_target_pairs={{0,1},{2,3},{4,5},{6,7},{8,9},{10,11},{12,13},{14,15},{1,0},{3,2},... | collective-permute-start | bytes 776 | tf_op jit(solution)/shard_map/ppermute | solution.py:647
  0.7 0.7 %copy-start = (s32[16,4]{0,1:T(4,128)S(1)}, s32[16,4]{0,1:T(4,128)}, u32[]{:S(2)}) copy-start(s32[16,4]{0,1:T(4,128)} %param.5) | copy-start | bytes 772
  1.4 8.4 %copy-start.2 = (s32[1,2]{1,0:T(1,128)S(1)}, s32[1,2]{1,0:T(1,128)}, u32[]{:S(2)}) copy-start(s32[1,2]{1,0:T(1,128)} %range_ref.5) | copy-start | bytes 28
  3.9 5.8 %collective-permute-start.1 = (f32[80,128]{1,0:T(8,128)S(1)}, f32[80,128]{1,0:T(8,128)S(1)}, u32[]{:S(2)}, u32[]{:S(2)}) collective-permute-start(f32[80,128]{1,0:T(8,128)S(1)} %tables.1.other_ref), channel_id=1, source_target_pairs={{1,2},{3,4},{5,6},{7,8},{9,10},{11,12},{13,14},{2,1},{4,3},{6,5},{... | collective-permute-start | bytes 122888 | tf_op jit(solution)/shard_map/ppermute | solution.py:647
  7.0 24.0 %copy-start.1 = (s32[16,4]{0,1:T(4,128)S(1)}, s32[16,4]{0,1:T(4,128)}, u32[]{:S(2)}) copy-start(s32[16,4]{0,1:T(4,128)} %param.5) | copy-start | bytes 772
  7.0 24.0 %collective-permute-start.6 = (f32[4,3,128,128]{3,2,1,0:T(8,128)S(1)}, f32[4,3,128,128]{3,2,1,0:T(8,128)S(1)}, u32[]{:S(2)}, u32[]{:S(2)}) collective-permute-start(f32[4,3,128,128]{3,2,1,0:T(8,128)S(1)} %after.1), channel_id=1, source_target_pairs={{1,2},{3,4},{5,6},{7,8},{9,10},{11,12},{13,14},{2,1},{4,3},{6,5},{... | collective-permute-start | bytes 2359304 | tf_op jit(solution)/shard_map/ppermute | solution.py:647
  18.9 12.1 %collective-permute-start.5 = (f32[4,3,128,128]{3,2,1,0:T(8,128)S(1)}, f32[4,3,128,128]{3,2,1,0:T(8,128)S(1)}, u32[]{:S(2)}, u32[]{:S(2)}) collective-permute-start(f32[4,3,128,128]{3,2,1,0:T(8,128)S(1)} %get-tuple-element.17), channel_id=1, source_target_pairs={{0,1},{2,3},{4,5},{6,7},{8,9},{10,11},{12,13},{14,15},{1,0},{3,2},... | collective-permute-start | bytes 2359304 | tf_op jit(solution)/shard_map/ppermute | solution.py:647
  19.6 2.2 %collective-permute-start.2 = (f32[392,128]{1,0:T(8,128)S(1)}, f32[392,128]{1,0:T(8,128)S(1)}, u32[]{:S(2)}, u32[]{:S(2)}) collective-permute-start(f32[392,128]{1,0:T(8,128)S(1)} %get-tuple-element.13.mine), channel_id=1, source_target_pairs={{0,1},{2,3},{4,5},{6,7},{8,9},{10,11},{12,13},{14,15},{1,0},{3,2},... | collective-permute-start | bytes 602120 | tf_op jit(solution)/shard_map/ppermute | solution.py:647
  23.0 6.7 %collective-permute-start.3 = (f32[96,128]{1,0:T(8,128)S(1)}, f32[96,128]{1,0:T(8,128)S(1)}, u32[]{:S(2)}, u32[]{:S(2)}) collective-permute-start(f32[96,128]{1,0:T(8,128)S(1)} %get-tuple-element.15), channel_id=1, source_target_pairs={{1,2},{3,4},{5,6},{7,8},{9,10},{11,12},{13,14},{2,1},{4,3},{6,5},{... | collective-permute-start | bytes 147464 | tf_op jit(solution)/shard_map/ppermute | solution.py:647
  29.8 1.2 %collective-permute-start.4 = (f32[96,128]{1,0:T(8,128)S(1)}, f32[96,128]{1,0:T(8,128)S(1)}, u32[]{:S(2)}, u32[]{:S(2)}) collective-permute-start(f32[96,128]{1,0:T(8,128)S(1)} %collective-permute-done.3.crossed), channel_id=1, source_target_pairs={{0,1},{2,3},{4,5},{6,7},{8,9},{10,11},{12,13},{14,15},{1,0},{3,2},... | collective-permute-start | bytes 147464 | tf_op jit(solution)/shard_map/ppermute | solution.py:647

commit v11 on v10

--- a/solution.py
+++ b/solution.py
@@ -469,7 +469,9 @@
     )(old_range, mine, theirs, came)
 
 
-def ghosts(table, edges, crossed, passed, turn, me, odd):
+def prepare_kernel(table, edges, places, hot, near, walls, turn):
+    me, odd = position()
+    fill_places(places)
     sides, count = table.shape
     side = edges.shape[1]
     total = sides * count
@@ -503,23 +505,50 @@
     index = jnp.where(inside, place.astype(jnp.float32) + twice, across)
     index = jnp.where(wall, own.astype(jnp.float32), index)
     lane = lane.astype(jnp.float32)
-    hot = jnp.concatenate([flag(lane == index), flag(lane + side == index)], axis=1).astype(jnp.bfloat16)
-    hot = jnp.concatenate([hot, hot], axis=1)
-    fields = []
+    walls[...] = flag(wall)
+    far = flag(lane + first == index)
+    hot[...] = jnp.concatenate([far, far], axis=1).astype(jnp.bfloat16)
+    at_home = flag(lane == index)
+    at_home = jnp.concatenate([at_home, at_home], axis=1).astype(jnp.bfloat16)
     for f in range(4):
-        parts = edges_of_field(edges, f)
-        parts += [ref[step * f : step * (f + 1), :] for ref in (crossed, passed)]
-        parts.append(jnp.zeros((2 * side - first - 2 * step, side), jnp.float32))
-        values = jnp.concatenate(parts, axis=0)
-        high = values.astype(jnp.bfloat16)
-        low = (values - high.astype(jnp.float32)).astype(jnp.bfloat16)
-        fields.append(product(hot, jnp.concatenate([high, low], axis=0)))
-    return fields, wall
-
-
-def rim_terms(table, edges, crossed, passed, columns, lines, turn, me, odd):
-    count = table.shape[1]
-    outside, wall = ghosts(table, edges, crossed, passed, turn, me, odd)
+        near[total * f : total * (f + 1), :] = product(at_home, halves(jnp.concatenate(edges_of_field(edges, f), axis=0)))
+
+
+def halves(values):
+    high = values.astype(jnp.bfloat16)
+    low = (values - high.astype(jnp.float32)).astype(jnp.bfloat16)
+    return jnp.concatenate([high, low], axis=0)
+
+
+def prepared(table, edges):
+    side = edges.shape[1]
+    total = table.shape[0] * table.shape[1]
+    return pl.pallas_call(
+        prepare_kernel,
+        in_specs=[VMEM] * 2,
+        out_specs=[VMEM] * 4,
+        out_shape=[
+            jax.ShapeDtypeStruct((2 * side, 6 * side), jnp.bfloat16),
+            jax.ShapeDtypeStruct((total, 2 * side), jnp.bfloat16),
+            jax.ShapeDtypeStruct((4 * total, side), jnp.float32),
+            jax.ShapeDtypeStruct((total, side), jnp.float32),
+        ],
+        scratch_shapes=[pltpu.VMEM((side, side), jnp.float32)],
+        compiler_params=room(4),
+        name="prepare",
+    )(table, edges)
+
+
+def rim_terms(hot, near, walls, edges, crossed, passed, columns, lines, turn, count, odd):
+    side = edges.shape[1]
+    total, step = walls.shape[0], 3 * CAP
+    outside = []
+    for f in range(4):
+        parts = [ref[step * f : step * (f + 1), :] for ref in (crossed, passed)]
+        parts.append(jnp.zeros((side - 2 * step, side), jnp.float32))
+        far = product(hot[...], halves(jnp.concatenate(parts, axis=0)))
+        outside.append(near[total * f : total * (f + 1), :] + far)
+    wall = walls[...] > 0.0
     turn[...] = jnp.zeros_like(turn)
     lines[...] = jnp.zeros_like(lines)
     for s in range(4):
@@ -556,24 +585,25 @@
 
 def fill_places(places):
     side = places.shape[0] // 2
-    row = lax.broadcasted_iota(jnp.int32, (side, side), 0) % 8
+    row = lax.broadcasted_iota(jnp.int32, (side, side), 0) % 16
     lane = lax.broadcasted_iota(jnp.int32, (side, side), 1)
     source = row - jnp.where(lane == 0, 1, jnp.where(lane == side - 1, 0, 1024))
-    for f in range(3):
-        block = jnp.where(source == 2 * f, 1.0, 0.0).astype(jnp.bfloat16)
-        for half in range(2):
-            places[half * side : (half + 1) * side, f * side : (f + 1) * side] = block
+    for u in range(2):
+        for f in range(3):
+            block = jnp.where(source == 8 * u + 2 * f, 1.0, 0.0).astype(jnp.bfloat16)
+            for half in range(2):
+                at = (3 * u + f) * side
+                places[half * side : (half + 1) * side, at : at + side] = block
 
 
 def final_kernel(
-    margin, range_ref, table, edges, crossed, passed, own, theirs, came, arrived, out,
-    result, turn, columns, lines, places, sems,
+    margin, range_ref, places, hot, near, walls, edges, crossed, passed, own, theirs, came, arrived, out,
+    result, turn, columns, lines, sems,
 ):
     count, side = own.shape[0], lines.shape[1]
     me, odd = position()
     even = odd == 0
-    fill_places(places)
-    rim_terms(table, edges, crossed, passed, columns, lines, turn, me, odd)
+    rim_terms(hot, near, walls, edges, crossed, passed, columns, lines, turn, count, odd)
     start, stop = range_ref[0, 0], range_ref[0, 1]
     line = iota(0, side)
     lane = lax.broadcasted_iota(jnp.int32, (side, 2 * side), 1) % side
@@ -586,7 +616,7 @@
     for group in range(0, count, margin):
         patches = range(group, group + margin)
         held = columns[...]
-        masked = [held * jnp.where(lane // 8 == p, 1.0, 0.0).astype(jnp.bfloat16) for p in patches]
+        masked = [held * jnp.where(lane // 16 == p // 2, 1.0, 0.0).astype(jnp.bfloat16) for p in patches[::2]]
         terms = product(jnp.concatenate(masked, axis=0), places[...])
         for m, p in enumerate(patches):
             if group == 0:
@@ -595,7 +625,7 @@
                 taken = me * count + p >= stop
             else:
                 taken = None
-            near = even if group else odd == 1
+            beside = even if group else odd == 1
             for f in range(3):
                 for j in range(steps):
                     rows = slice(ROWS * j, ROWS * (j + 1))
@@ -606,10 +636,11 @@
                             crossing = came[at : at + ROWS, :]
                         else:
                             crossing = arrived[m - FIRST, f, rows, :]
-                        moved = jnp.where(near, theirs[m, f, rows, :], crossing)
+                        moved = jnp.where(beside, theirs[m, f, rows, :], crossing)
                         value = jnp.where(taken, moved, value)
-                    at = side * m + ROWS * j
-                    value = value + terms[at : at + ROWS, f * side : (f + 1) * side]
+                    at = side * (m // 2) + ROWS * j
+                    block = 3 * (m % 2) + f
+                    value = value + terms[at : at + ROWS, block * side : (block + 1) * side]
                     if j == 0:
                         south = lines[8 * p + 2 * f + 1 : 8 * p + 2 * f + 2, :]
                         value = value + jnp.where(line == 0, south, 0.0)
@@ -622,11 +653,11 @@
         copy(p).wait()
 
 
-def finished(old_range, table, edges, crossed, passed, own, theirs, came, arrived, margin):
+def finished(old_range, ready, edges, crossed, passed, own, theirs, came, arrived, margin):
     count, _, side, _ = own.shape
     return pl.pallas_call(
         functools.partial(final_kernel, margin),
-        in_specs=[SMEM] + [VMEM] * 8,
+        in_specs=[SMEM] + [VMEM] * 11,
         out_specs=HBM,
         out_shape=jax.ShapeDtypeStruct(own.shape, jnp.float32),
         scratch_shapes=[
@@ -634,12 +665,11 @@
             pltpu.VMEM((side, side), jnp.float32),
             pltpu.VMEM((side, 2 * side), jnp.bfloat16),
             pltpu.VMEM((side, side), jnp.float32),
-            pltpu.VMEM((2 * side, 3 * side), jnp.bfloat16),
             pltpu.SemaphoreType.DMA((count,)),
         ],
         compiler_params=room(12),
         name="final",
-    )(old_range, table, edges, crossed, passed, own, theirs, came, arrived)
+    )(old_range, *ready, edges, crossed, passed, own, theirs, came, arrived)
 
 
 def swapped(value, first):
@@ -663,7 +693,7 @@
     edges, message = answers(old_range, shared, their_edges, came, margin, per_device)
     crossed = swapped(message, 1)
     passed = swapped(crossed, 0)
-    return finished(old_range, table, edges, crossed, passed, own, theirs, came, arrived, margin)
+    return finished(old_range, prepared(table, edges), edges, crossed, passed, own, theirs, came, arrived, margin)
 
 
 def solution(mesh):

time: 34.8 us -> 34.5 us (level)
  waiting for transfers between devices: 6.69 us -> 6.23 us
    ppermute x7, waiting for transfers between devices: 6.69 us -> 6.23 us  [swapped(): return lax.ppermute(value, AXES, pairs + [(j, i) for i, j in pairs])]
    pallas_call x0 -> x1, Pallas kernels: none -> 0.45 us  [prepared(): pl.pallas_call(prepare_kernel, in_specs=[VMEM] * 2, out_specs=[VMEM] * 4,...]
  transfers between devices with their start and end apart: 7 -> 7, of which waited for: 4 -> 4; matrix products, arithmetic and copies ran while one was open for 0% -> 0% of each run, Pallas kernels for 37% -> 39%
where the time goes in v11:
time: 34.5 us; the launch traced here: 34.3 us
  Pallas kernels  16.6 us (48%)
  starting transfers between devices  10.7 us (31%)
  waiting for transfers between devices  6.23 us (18%)
  local copies, waits for them, and re-layouts  0.69 us (2%)
    ppermute x7, starting transfers between devices, swapped(): return lax.ppermute(value, AXES, pairs + [(j, i) for i, j in pairs])  10.7 us
    pallas_call x1, Pallas kernels, home_patches(): pl.pallas_call(functools.partial(home_kernel, margin), in_specs=[SMEM, HB...  9.12 us
    ppermute x7, waiting for transfers between devices, swapped(): return lax.ppermute(value, AXES, pairs + [(j, i) for i, j in pairs])  6.23 us
    pallas_call x1, Pallas kernels, finished(): pl.pallas_call(functools.partial(final_kernel, margin), in_specs=[SMEM] +...  3.28 us
    pallas_call x1, Pallas kernels, outer_patches(): pl.pallas_call(functools.partial(outer_kernel, margin), in_specs=[HBM, VM...  2.51 us
    pallas_call x1, Pallas kernels, answers(): pl.pallas_call(functools.partial(answer_kernel, margin, per_device), in_s...  1.19 us
    unnamed x6, local copies, waits for them, and re-layouts  0.69 us
  transfers between devices with their start and end apart: 7, of which 4 were waited for; matrix products, arithmetic and copies ran while one was open for 0% of the time, Pallas kernels for 39%

profile of v11, /device:TPU:17, one launch (start us, length us, event | category | flops | bytes accessed | tf_op | source)
XLA Modules:
  0.0 34.3 jit_solution(2072778574278359640)
XLA Ops:
  0.0 0.7 %collective-permute-start = (s32[4,16]{1,0:T(4,128)}, s32[4,16]{1,0:T(4,128)S(1)}, u32[]{:S(2)}, u32[]{:S(2)}) collective-permute-start(s32[4,16]{1,0:T(4,128)} %bitcast.1), channel_id=1, source_target_pairs={{0,1},{2,3},{4,5},{6,7},{8,9},{10,11},{12,13},{14,15},{1,0},{3,2},... | collective-permute-start | bytes 776 | tf_op jit(solution)/shard_map/ppermute | solution.py:677
  0.7 0.0 copy-start
  0.7 0.7 %copy-done = s32[16,4]{0,1:T(4,128)S(1)} copy-done((s32[16,4]{0,1:T(4,128)S(1)}, s32[16,4]{0,1:T(4,128)}, u32[]{:S(2)}) %copy-start) | copy-done | bytes 280
  1.4 0.0 copy-start.2
  1.4 2.5 %outer.1 = (f32[4,3,128,128]{3,2,1,0:T(8,128)S(1)}, f32[80,128]{1,0:T(8,128)S(1)}) custom-call(f32[24,4,128,128]{3,2,1,0:T(8,128)} %cells_hbm.3, s32[4,16]{1,0:T(4,128)S(1)} %bitcast.2), custom_call_target="tpu_custom_call" | custom-call | flops 52428800 | bytes 1835008 | tf_op jit(solution)/shard_map/outer/pallas_call | solution.py:227
  3.9 0.0 collective-permute-done.extra_ref
  3.9 3.0 %collective-permute-start.1 = (f32[80,128]{1,0:T(8,128)S(1)}, f32[80,128]{1,0:T(8,128)S(1)}, u32[]{:S(2)}, u32[]{:S(2)}) collective-permute-start(f32[80,128]{1,0:T(8,128)S(1)} %tables.1.other_ref), channel_id=1, source_target_pairs={{1,2},{3,4},{5,6},{7,8},{9,10},{11,12},{13,14},{2,1},{4,3},{6,5},{... | collective-permute-start | bytes 122888 | tf_op jit(solution)/shard_map/ppermute | solution.py:677
  7.0 0.0 copy-start.1
  7.0 2.6 %collective-permute-start.6 = (f32[4,3,128,128]{3,2,1,0:T(8,128)S(1)}, f32[4,3,128,128]{3,2,1,0:T(8,128)S(1)}, u32[]{:S(2)}, u32[]{:S(2)}) collective-permute-start(f32[4,3,128,128]{3,2,1,0:T(8,128)S(1)} %after.1), channel_id=1, source_target_pairs={{1,2},{3,4},{5,6},{7,8},{9,10},{11,12},{13,14},{2,1},{4,3},{6,5},{... | collective-permute-start | bytes 2359304 | tf_op jit(solution)/shard_map/ppermute | solution.py:677
  9.5 0.2 collective-permute-done.1.came
  9.8 0.0 copy-done.2
  9.8 9.1 %home.1 = (f32[392,128]{1,0:T(8,128)S(1)}, f32[4,3,128,128]{3,2,1,0:T(8,128)S(1)}, f32[16,3,128,128]{3,2,1,0:T(8,128)S(1)}) custom-call(s32[1,2]{1,0:T(1,128)S(1)} %copy-done.2, f32[24,4,128,128]{3,2,1,0:T(8,128)} %cells_hbm.3, f32[80,128]{1,0:T(8,128)S(1)} %collective-permute-done.1.came), custom_call_target="tpu_custom_call" | custom-call | flops 262144000 | bytes 9175040 | tf_op jit(solution)/shard_map/home/pallas_call | solution.py:329
  18.9 0.8 %collective-permute-start.5 = (f32[4,3,128,128]{3,2,1,0:T(8,128)S(1)}, f32[4,3,128,128]{3,2,1,0:T(8,128)S(1)}, u32[]{:S(2)}, u32[]{:S(2)}) collective-permute-start(f32[4,3,128,128]{3,2,1,0:T(8,128)S(1)} %get-tuple-element.25), channel_id=1, source_target_pairs={{0,1},{2,3},{4,5},{6,7},{8,9},{10,11},{12,13},{14,15},{1,0},{3,2},... | collective-permute-start | bytes 2359304 | tf_op jit(solution)/shard_map/ppermute | solution.py:677
  19.6 0.1 collective-permute-start.2
  19.7 2.1 %collective-permute-done.2.theirs = f32[392,128]{1,0:T(8,128)S(1)} collective-permute-done((f32[392,128]{1,0:T(8,128)S(1)}, f32[392,128]{1,0:T(8,128)S(1)}, u32[]{:S(2)}, u32[]{:S(2)}) %collective-permute-start.2) | collective-permute-done | bytes 200736 | tf_op jit(solution)/shard_map/ppermute | solution.py:677
  21.8 1.2 %answers.1 = (f32[512,128]{1,0:T(8,128)S(1)}, f32[96,128]{1,0:T(8,128)S(1)}) custom-call(s32[1,2]{1,0:T(1,128)S(1)} %copy-done.2, f32[392,128]{1,0:T(8,128)S(1)} %get-tuple-element.17.mine, f32[392,128]{1,0:T(8,128)S(1)} %collective-permute-done.2.theirs, f32[80,128]{1,0:T(8,128)S(1)} %collective-permute-done.1.came), custom_call_target="tpu_custom_call" | custom-call | tf_op jit(solution)/shard_map/answers/pallas_call | solution.py:459
  23.0 3.5 %collective-permute-start.3 = (f32[96,128]{1,0:T(8,128)S(1)}, f32[96,128]{1,0:T(8,128)S(1)}, u32[]{:S(2)}, u32[]{:S(2)}) collective-permute-start(f32[96,128]{1,0:T(8,128)S(1)} %get-tuple-element.23), channel_id=1, source_target_pairs={{1,2},{3,4},{5,6},{7,8},{9,10},{11,12},{13,14},{2,1},{4,3},{6,5},{... | collective-permute-start | bytes 147464 | tf_op jit(solution)/shard_map/ppermute | solution.py:677
  26.6 3.2 %collective-permute-done.3.crossed = f32[96,128]{1,0:T(8,128)S(1)} collective-permute-done((f32[96,128]{1,0:T(8,128)S(1)}, f32[96,128]{1,0:T(8,128)S(1)}, u32[]{:S(2)}, u32[]{:S(2)}) %collective-permute-start.3) | collective-permute-done | bytes 49184 | tf_op jit(solution)/shard_map/ppermute | solution.py:677
  29.8 0.1 collective-permute-start.4
  29.8 0.0 copy-done.1
  29.8 0.5 %prepare.1 = (bf16[256,768]{1,0:T(8,128)(2,1)S(1)}, bf16[64,256]{1,0:T(8,128)(2,1)S(1)}, f32[256,128]{1,0:T(8,128)S(1)}, f32[64,128]{1,0:T(8,128)S(1)}) custom-call(s32[4,16]{1,0:T(4,128)S(1)} %bitcast.3, f32[512,128]{1,0:T(8,128)S(1)} %get-tuple-element.18.edges), custom_call_target="tpu_custom_call" | custom-call | tf_op jit(solution)/shard_map/prepare/pallas_call | solution.py:526
  30.3 0.7 %collective-permute-done.4.passed = f32[96,128]{1,0:T(8,128)S(1)} collective-permute-done((f32[96,128]{1,0:T(8,128)S(1)}, f32[96,128]{1,0:T(8,128)S(1)}, u32[]{:S(2)}, u32[]{:S(2)}) %collective-permute-start.4) | collective-permute-done | bytes 49184 | tf_op jit(solution)/shard_map/ppermute | solution.py:677
  31.0 0.0 collective-permute-done.6.arrived
  31.0 0.0 collective-permute-done.5.theirs
  31.0 3.3 %final.1 = f32[16,3,128,128]{3,2,1,0:T(8,128)} custom-call(s32[1,2]{1,0:T(1,128)S(1)} %copy-done.2, bf16[256,768]{1,0:T(8,128)(2,1)S(1)} %get-tuple-element.19.places, bf16[64,256]{1,0:T(8,128)(2,1)S(1)} %get-tuple-element.20.hot, f32[256,128]{1,0:T(8,128)S(1)} %get-tuple-element.21.near, f32[64,128]{1,0:T(8,128)S(1)} %get-tuple-element.22.walls, ...), custom_call_target="tpu_custom_call" | custom-call | tf_op jit(solution)/shard_map/final/pallas_call | solution.py:658
  (2 shorter events, 0.0 us)
Async XLA Ops:
  0.0 3.9 %collective-permute-start = (s32[4,16]{1,0:T(4,128)}, s32[4,16]{1,0:T(4,128)S(1)}, u32[]{:S(2)}, u32[]{:S(2)}) collective-permute-start(s32[4,16]{1,0:T(4,128)} %bitcast.1), channel_id=1, source_target_pairs={{0,1},{2,3},{4,5},{6,7},{8,9},{10,11},{12,13},{14,15},{1,0},{3,2},... | collective-permute-start | bytes 776 | tf_op jit(solution)/shard_map/ppermute | solution.py:677
  0.7 0.7 %copy-start = (s32[16,4]{0,1:T(4,128)S(1)}, s32[16,4]{0,1:T(4,128)}, u32[]{:S(2)}) copy-start(s32[16,4]{0,1:T(4,128)} %param.5) | copy-start | bytes 772
  1.4 8.4 %copy-start.2 = (s32[1,2]{1,0:T(1,128)S(1)}, s32[1,2]{1,0:T(1,128)}, u32[]{:S(2)}) copy-start(s32[1,2]{1,0:T(1,128)} %range_ref.5) | copy-start | bytes 28
  3.9 5.8 %collective-permute-start.1 = (f32[80,128]{1,0:T(8,128)S(1)}, f32[80,128]{1,0:T(8,128)S(1)}, u32[]{:S(2)}, u32[]{:S(2)}) collective-permute-start(f32[80,128]{1,0:T(8,128)S(1)} %tables.1.other_ref), channel_id=1, source_target_pairs={{1,2},{3,4},{5,6},{7,8},{9,10},{11,12},{13,14},{2,1},{4,3},{6,5},{... | collective-permute-start | bytes 122888 | tf_op jit(solution)/shard_map/ppermute | solution.py:677
  7.0 22.9 %copy-start.1 = (s32[16,4]{0,1:T(4,128)S(1)}, s32[16,4]{0,1:T(4,128)}, u32[]{:S(2)}) copy-start(s32[16,4]{0,1:T(4,128)} %param.5) | copy-start | bytes 772
  7.0 24.0 %collective-permute-start.6 = (f32[4,3,128,128]{3,2,1,0:T(8,128)S(1)}, f32[4,3,128,128]{3,2,1,0:T(8,128)S(1)}, u32[]{:S(2)}, u32[]{:S(2)}) collective-permute-start(f32[4,3,128,128]{3,2,1,0:T(8,128)S(1)} %after.1), channel_id=1, source_target_pairs={{1,2},{3,4},{5,6},{7,8},{9,10},{11,12},{13,14},{2,1},{4,3},{6,5},{... | collective-permute-start | bytes 2359304 | tf_op jit(solution)/shard_map/ppermute | solution.py:677
  18.9 12.1 %collective-permute-start.5 = (f32[4,3,128,128]{3,2,1,0:T(8,128)S(1)}, f32[4,3,128,128]{3,2,1,0:T(8,128)S(1)}, u32[]{:S(2)}, u32[]{:S(2)}) collective-permute-start(f32[4,3,128,128]{3,2,1,0:T(8,128)S(1)} %get-tuple-element.25), channel_id=1, source_target_pairs={{0,1},{2,3},{4,5},{6,7},{8,9},{10,11},{12,13},{14,15},{1,0},{3,2},... | collective-permute-start | bytes 2359304 | tf_op jit(solution)/shard_map/ppermute | solution.py:677
  19.6 2.2 %collective-permute-start.2 = (f32[392,128]{1,0:T(8,128)S(1)}, f32[392,128]{1,0:T(8,128)S(1)}, u32[]{:S(2)}, u32[]{:S(2)}) collective-permute-start(f32[392,128]{1,0:T(8,128)S(1)} %get-tuple-element.17.mine), channel_id=1, source_target_pairs={{0,1},{2,3},{4,5},{6,7},{8,9},{10,11},{12,13},{14,15},{1,0},{3,2},... | collective-permute-start | bytes 602120 | tf_op jit(solution)/shard_map/ppermute | solution.py:677
  23.0 6.7 %collective-permute-start.3 = (f32[96,128]{1,0:T(8,128)S(1)}, f32[96,128]{1,0:T(8,128)S(1)}, u32[]{:S(2)}, u32[]{:S(2)}) collective-permute-start(f32[96,128]{1,0:T(8,128)S(1)} %get-tuple-element.23), channel_id=1, source_target_pairs={{1,2},{3,4},{5,6},{7,8},{9,10},{11,12},{13,14},{2,1},{4,3},{6,5},{... | collective-permute-start | bytes 147464 | tf_op jit(solution)/shard_map/ppermute | solution.py:677
  29.8 1.2 %collective-permute-start.4 = (f32[96,128]{1,0:T(8,128)S(1)}, f32[96,128]{1,0:T(8,128)S(1)}, u32[]{:S(2)}, u32[]{:S(2)}) collective-permute-start(f32[96,128]{1,0:T(8,128)S(1)} %collective-permute-done.3.crossed), channel_id=1, source_target_pairs={{0,1},{2,3},{4,5},{6,7},{8,9},{10,11},{12,13},{14,15},{1,0},{3,2},... | collective-permute-start | bytes 147464 | tf_op jit(solution)/shard_map/ppermute | solution.py:677

commit v12 on v11

--- a/solution.py
+++ b/solution.py
@@ -184,15 +184,11 @@
     return tables, tables + 16
 
 
-def outer_kernel(margin, cells_hbm, table, rest, bundle, cells, columns, weights, sems):
+def outer_kernel(margin, cells_hbm, rest, bundle, cells, columns, weights, sems):
     side = columns.shape[0]
-    _, odd = position()
     copy = fetch(cells_hbm, outer_slot(cells_hbm, margin), cells, sems, [(0, margin)])
     fill_weights(weights)
-    tables, results = bundle_layout(margin)
-    sides, count = table.shape
-    bundle[tables:results, :] = jnp.zeros((results - tables, side), jnp.float32)
-    bundle[pl.ds(pl.multiple_of(tables + 8 * odd, 8), sides), 0:count] = table[...].astype(jnp.float32)
+    results = bundle_layout(margin)[1]
     for i in range(0, margin, PAIR):
         for n in range(PAIR):
             copy(i + n).wait()
@@ -222,11 +218,11 @@
     return pltpu.CompilerParams(vmem_limit_bytes=mebibytes << 20)
 
 
-def outer_patches(old_cells, table, margin):
+def outer_patches(old_cells, margin):
     side = old_cells.shape[3]
     return pl.pallas_call(
         functools.partial(outer_kernel, margin),
-        in_specs=[HBM, VMEM],
+        in_specs=[HBM],
         out_specs=[VMEM, VMEM],
         out_shape=[
             jax.ShapeDtypeStruct((margin - FIRST, 3, side, side), jnp.float32),
@@ -241,34 +237,33 @@
         cost_estimate=cost(margin, side),
         compiler_params=room(48),
         name="outer",
-    )(old_cells, table)
-
-
-def placed_rows(rows, start_of, bundle, extra, name):
+    )(old_cells)
+
+
+def with_tables(bundle, table, their_table, margin):
     any_place = pl.BlockSpec(memory_space=pl.ANY)
-    small = rows == 8
-
-    def kernel(bundle_ref, extra_ref, out_ref, held, sem):
-        source = extra_ref
-        if small:
-            held[...] = jnp.zeros_like(held)
-            held[0 : extra_ref.shape[0], 0 : extra_ref.shape[1]] = extra_ref[...].astype(jnp.float32)
-            source = held
-        start = pl.multiple_of(start_of(), 8)
-        copy = pltpu.make_async_copy(source.at[pl.ds(0, rows), :], out_ref.at[pl.ds(start, rows), :], sem)
+    start, end = bundle_layout(margin)
+    sides, count = table.shape
+
+    def kernel(bundle_ref, table_ref, their_ref, out_ref, held, sem):
+        _, odd = position()
+        held[...] = jnp.zeros_like(held)
+        for which, ref in ((odd, table_ref), (1 - odd, their_ref)):
+            held[pl.ds(pl.multiple_of(8 * which, 8), sides), 0:count] = ref[...].astype(jnp.float32)
+        copy = pltpu.make_async_copy(held, out_ref.at[start:end, :], sem)
         copy.start()
         copy.wait()
 
     return pl.pallas_call(
         kernel,
-        in_specs=[any_place, VMEM if small else any_place],
+        in_specs=[any_place, VMEM, VMEM],
         out_specs=any_place,
         out_shape=jax.ShapeDtypeStruct(bundle.shape, bundle.dtype),
-        scratch_shapes=[pltpu.VMEM((8, bundle.shape[1]), jnp.float32), pltpu.SemaphoreType.DMA],
+        scratch_shapes=[pltpu.VMEM((end - start, bundle.shape[1]), jnp.float32), pltpu.SemaphoreType.DMA],
         input_output_aliases={0: 0},
         compiler_params=room(4),
-        name=name,
-    )(bundle, extra)
+        name="tables",
+    )(bundle, table, their_table)
 
 
 def after(value, other):
@@ -682,9 +677,8 @@
     margin = (old_cells.shape[0] - per_device) // 2
     table = neighbours.T
     their_table = swapped(table, 0)
-    rest, bundle = outer_patches(old_cells, table, margin)
-    their_row = lambda: bundle_layout(margin)[0] + 8 * (1 - position()[1])
-    bundle = placed_rows(8, their_row, bundle, their_table, "tables")
+    rest, bundle = outer_patches(old_cells, margin)
+    bundle = with_tables(bundle, table, their_table, margin)
     came = swapped(bundle, 1)
     arrived = swapped(after(rest, bundle), 1)
     shared, inner, own = home_patches(old_range, old_cells, came, margin, per_device)

time: 34.5 us -> 33.8 us (0.980)
  local copies, waits for them, and re-layouts: 0.69 us -> 0.01 us
    unnamed x6 -> x4, local copies, waits for them, and re-layouts: 0.69 us -> 0.01 us
  transfers between devices with their start and end apart: 7 -> 7, of which waited for: 4 -> 4; matrix products, arithmetic and copies ran while one was open for 0% -> 0% of each run, Pallas kernels for 39% -> 40%
where the time goes in v12:
time: 33.8 us; the launch traced here: 33.6 us
  Pallas kernels  16.6 us (49%)
  starting transfers between devices  10.6 us (31%)
  waiting for transfers between devices  6.26 us (19%)
    ppermute x7, starting transfers between devices, swapped(): return lax.ppermute(value, AXES, pairs + [(j, i) for i, j in pairs])  10.6 us
    pallas_call x1, Pallas kernels, home_patches(): pl.pallas_call(functools.partial(home_kernel, margin), in_specs=[SMEM, HB...  9.12 us
    ppermute x7, waiting for transfers between devices, swapped(): return lax.ppermute(value, AXES, pairs + [(j, i) for i, j in pairs])  6.26 us
    pallas_call x1, Pallas kernels, finished(): pl.pallas_call(functools.partial(final_kernel, margin), in_specs=[SMEM] +...  3.28 us
    pallas_call x1, Pallas kernels, outer_patches(): pl.pallas_call(functools.partial(outer_kernel, margin), in_specs=[HBM], o...  2.51 us
    pallas_call x1, Pallas kernels, answers(): pl.pallas_call(functools.partial(answer_kernel, margin, per_device), in_s...  1.19 us
  transfers between devices with their start and end apart: 7, of which 4 were waited for; matrix products, arithmetic and copies ran while one was open for 0% of the time, Pallas kernels for 40%

profile of v12, /device:TPU:17, one launch (start us, length us, event | category | flops | bytes accessed | tf_op | source)
XLA Modules:
  0.0 33.6 jit_solution(17761751710508190898)
XLA Ops:
  0.0 0.0 copy-start
  0.0 0.0 copy-start.1
  0.0 0.7 %collective-permute-start = (s32[4,16]{1,0:T(4,128)}, s32[4,16]{1,0:T(4,128)S(1)}, u32[]{:S(2)}, u32[]{:S(2)}) collective-permute-start(s32[4,16]{1,0:T(4,128)} %bitcast.1), channel_id=1, source_target_pairs={{0,1},{2,3},{4,5},{6,7},{8,9},{10,11},{12,13},{14,15},{1,0},{3,2},... | collective-permute-start | bytes 776 | tf_op jit(solution)/shard_map/ppermute | solution.py:672
  0.7 2.5 %outer.1 = (f32[4,3,128,128]{3,2,1,0:T(8,128)S(1)}, f32[80,128]{1,0:T(8,128)S(1)}) custom-call(f32[24,4,128,128]{3,2,1,0:T(8,128)} %cells_hbm.3), custom_call_target="tpu_custom_call" | custom-call | flops 52428800 | bytes 1835008 | tf_op jit(solution)/shard_map/outer/pallas_call | solution.py:223
  3.2 0.0 collective-permute-done.their_ref
  3.2 0.0 copy-done
  3.3 3.0 %collective-permute-start.1 = (f32[80,128]{1,0:T(8,128)S(1)}, f32[80,128]{1,0:T(8,128)S(1)}, u32[]{:S(2)}, u32[]{:S(2)}) collective-permute-start(f32[80,128]{1,0:T(8,128)S(1)} %tables.1.other_ref), channel_id=1, source_target_pairs={{1,2},{3,4},{5,6},{7,8},{9,10},{11,12},{13,14},{2,1},{4,3},{6,5},{... | collective-permute-start | bytes 122888 | tf_op jit(solution)/shard_map/ppermute | solution.py:672
  6.3 2.5 %collective-permute-start.6 = (f32[4,3,128,128]{3,2,1,0:T(8,128)S(1)}, f32[4,3,128,128]{3,2,1,0:T(8,128)S(1)}, u32[]{:S(2)}, u32[]{:S(2)}) collective-permute-start(f32[4,3,128,128]{3,2,1,0:T(8,128)S(1)} %after.1), channel_id=1, source_target_pairs={{1,2},{3,4},{5,6},{7,8},{9,10},{11,12},{13,14},{2,1},{4,3},{6,5},{... | collective-permute-start | bytes 2359304 | tf_op jit(solution)/shard_map/ppermute | solution.py:672
  8.9 0.2 collective-permute-done.1.came
  9.1 0.0 copy-done.1
  9.1 9.1 %home.1 = (f32[392,128]{1,0:T(8,128)S(1)}, f32[4,3,128,128]{3,2,1,0:T(8,128)S(1)}, f32[16,3,128,128]{3,2,1,0:T(8,128)S(1)}) custom-call(s32[1,2]{1,0:T(1,128)S(1)} %copy-done.1, f32[24,4,128,128]{3,2,1,0:T(8,128)} %cells_hbm.3, f32[80,128]{1,0:T(8,128)S(1)} %collective-permute-done.1.came), custom_call_target="tpu_custom_call" | custom-call | flops 262144000 | bytes 9175040 | tf_op jit(solution)/shard_map/home/pallas_call | solution.py:324
  18.2 0.7 %collective-permute-start.5 = (f32[4,3,128,128]{3,2,1,0:T(8,128)S(1)}, f32[4,3,128,128]{3,2,1,0:T(8,128)S(1)}, u32[]{:S(2)}, u32[]{:S(2)}) collective-permute-start(f32[4,3,128,128]{3,2,1,0:T(8,128)S(1)} %get-tuple-element.25), channel_id=1, source_target_pairs={{0,1},{2,3},{4,5},{6,7},{8,9},{10,11},{12,13},{14,15},{1,0},{3,2},... | collective-permute-start | bytes 2359304 | tf_op jit(solution)/shard_map/ppermute | solution.py:672
  19.0 0.1 collective-permute-start.2
  19.1 2.1 %collective-permute-done.2.theirs = f32[392,128]{1,0:T(8,128)S(1)} collective-permute-done((f32[392,128]{1,0:T(8,128)S(1)}, f32[392,128]{1,0:T(8,128)S(1)}, u32[]{:S(2)}, u32[]{:S(2)}) %collective-permute-start.2) | collective-permute-done | bytes 200736 | tf_op jit(solution)/shard_map/ppermute | solution.py:672
  21.2 1.2 %answers.1 = (f32[512,128]{1,0:T(8,128)S(1)}, f32[96,128]{1,0:T(8,128)S(1)}) custom-call(s32[1,2]{1,0:T(1,128)S(1)} %copy-done.1, f32[392,128]{1,0:T(8,128)S(1)} %get-tuple-element.17.mine, f32[392,128]{1,0:T(8,128)S(1)} %collective-permute-done.2.theirs, f32[80,128]{1,0:T(8,128)S(1)} %collective-permute-done.1.came), custom_call_target="tpu_custom_call" | custom-call | tf_op jit(solution)/shard_map/answers/pallas_call | solution.py:454
  22.4 3.5 %collective-permute-start.3 = (f32[96,128]{1,0:T(8,128)S(1)}, f32[96,128]{1,0:T(8,128)S(1)}, u32[]{:S(2)}, u32[]{:S(2)}) collective-permute-start(f32[96,128]{1,0:T(8,128)S(1)} %get-tuple-element.23), channel_id=1, source_target_pairs={{1,2},{3,4},{5,6},{7,8},{9,10},{11,12},{13,14},{2,1},{4,3},{6,5},{... | collective-permute-start | bytes 147464 | tf_op jit(solution)/shard_map/ppermute | solution.py:672
  25.9 3.2 %collective-permute-done.3.crossed = f32[96,128]{1,0:T(8,128)S(1)} collective-permute-done((f32[96,128]{1,0:T(8,128)S(1)}, f32[96,128]{1,0:T(8,128)S(1)}, u32[]{:S(2)}, u32[]{:S(2)}) %collective-permute-start.3) | collective-permute-done | bytes 49184 | tf_op jit(solution)/shard_map/ppermute | solution.py:672
  29.1 0.1 collective-permute-start.4
  29.2 0.5 %prepare.1 = (bf16[256,768]{1,0:T(8,128)(2,1)S(1)}, bf16[64,256]{1,0:T(8,128)(2,1)S(1)}, f32[256,128]{1,0:T(8,128)S(1)}, f32[64,128]{1,0:T(8,128)S(1)}) custom-call(s32[4,16]{1,0:T(4,128)S(1)} %bitcast.3, f32[512,128]{1,0:T(8,128)S(1)} %get-tuple-element.18.edges), custom_call_target="tpu_custom_call" | custom-call | tf_op jit(solution)/shard_map/prepare/pallas_call | solution.py:521
  29.6 0.7 %collective-permute-done.4.passed = f32[96,128]{1,0:T(8,128)S(1)} collective-permute-done((f32[96,128]{1,0:T(8,128)S(1)}, f32[96,128]{1,0:T(8,128)S(1)}, u32[]{:S(2)}, u32[]{:S(2)}) %collective-permute-start.4) | collective-permute-done | bytes 49184 | tf_op jit(solution)/shard_map/ppermute | solution.py:672
  30.3 0.0 collective-permute-done.6.arrived
  30.3 0.0 collective-permute-done.5.theirs
  30.3 3.3 %final.1 = f32[16,3,128,128]{3,2,1,0:T(8,128)} custom-call(s32[1,2]{1,0:T(1,128)S(1)} %copy-done.1, bf16[256,768]{1,0:T(8,128)(2,1)S(1)} %get-tuple-element.19.places, bf16[64,256]{1,0:T(8,128)(2,1)S(1)} %get-tuple-element.20.hot, f32[256,128]{1,0:T(8,128)S(1)} %get-tuple-element.21.near, f32[64,128]{1,0:T(8,128)S(1)} %get-tuple-element.22.walls, ...), custom_call_target="tpu_custom_call" | custom-call | tf_op jit(solution)/shard_map/final/pallas_call | solution.py:653
  (2 shorter events, 0.0 us)
Async XLA Ops:
  0.0 3.2 %copy-start = (s32[16,4]{0,1:T(4,128)S(1)}, s32[16,4]{0,1:T(4,128)}, u32[]{:S(2)}) copy-start(s32[16,4]{0,1:T(4,128)} %param.5) | copy-start | bytes 772
  0.0 9.1 %copy-start.1 = (s32[1,2]{1,0:T(1,128)S(1)}, s32[1,2]{1,0:T(1,128)}, u32[]{:S(2)}) copy-start(s32[1,2]{1,0:T(1,128)} %range_ref.5) | copy-start | bytes 28
  0.0 3.2 %collective-permute-start = (s32[4,16]{1,0:T(4,128)}, s32[4,16]{1,0:T(4,128)S(1)}, u32[]{:S(2)}, u32[]{:S(2)}) collective-permute-start(s32[4,16]{1,0:T(4,128)} %bitcast.1), channel_id=1, source_target_pairs={{0,1},{2,3},{4,5},{6,7},{8,9},{10,11},{12,13},{14,15},{1,0},{3,2},... | collective-permute-start | bytes 776 | tf_op jit(solution)/shard_map/ppermute | solution.py:672
  3.3 5.8 %collective-permute-start.1 = (f32[80,128]{1,0:T(8,128)S(1)}, f32[80,128]{1,0:T(8,128)S(1)}, u32[]{:S(2)}, u32[]{:S(2)}) collective-permute-start(f32[80,128]{1,0:T(8,128)S(1)} %tables.1.other_ref), channel_id=1, source_target_pairs={{1,2},{3,4},{5,6},{7,8},{9,10},{11,12},{13,14},{2,1},{4,3},{6,5},{... | collective-permute-start | bytes 122888 | tf_op jit(solution)/shard_map/ppermute | solution.py:672
  6.3 24.0 %collective-permute-start.6 = (f32[4,3,128,128]{3,2,1,0:T(8,128)S(1)}, f32[4,3,128,128]{3,2,1,0:T(8,128)S(1)}, u32[]{:S(2)}, u32[]{:S(2)}) collective-permute-start(f32[4,3,128,128]{3,2,1,0:T(8,128)S(1)} %after.1), channel_id=1, source_target_pairs={{1,2},{3,4},{5,6},{7,8},{9,10},{11,12},{13,14},{2,1},{4,3},{6,5},{... | collective-permute-start | bytes 2359304 | tf_op jit(solution)/shard_map/ppermute | solution.py:672
  18.2 12.1 %collective-permute-start.5 = (f32[4,3,128,128]{3,2,1,0:T(8,128)S(1)}, f32[4,3,128,128]{3,2,1,0:T(8,128)S(1)}, u32[]{:S(2)}, u32[]{:S(2)}) collective-permute-start(f32[4,3,128,128]{3,2,1,0:T(8,128)S(1)} %get-tuple-element.25), channel_id=1, source_target_pairs={{0,1},{2,3},{4,5},{6,7},{8,9},{10,11},{12,13},{14,15},{1,0},{3,2},... | collective-permute-start | bytes 2359304 | tf_op jit(solution)/shard_map/ppermute | solution.py:672
  19.0 2.2 %collective-permute-start.2 = (f32[392,128]{1,0:T(8,128)S(1)}, f32[392,128]{1,0:T(8,128)S(1)}, u32[]{:S(2)}, u32[]{:S(2)}) collective-permute-start(f32[392,128]{1,0:T(8,128)S(1)} %get-tuple-element.17.mine), channel_id=1, source_target_pairs={{0,1},{2,3},{4,5},{6,7},{8,9},{10,11},{12,13},{14,15},{1,0},{3,2},... | collective-permute-start | bytes 602120 | tf_op jit(solution)/shard_map/ppermute | solution.py:672
  22.4 6.7 %collective-permute-start.3 = (f32[96,128]{1,0:T(8,128)S(1)}, f32[96,128]{1,0:T(8,128)S(1)}, u32[]{:S(2)}, u32[]{:S(2)}) collective-permute-start(f32[96,128]{1,0:T(8,128)S(1)} %get-tuple-element.23), channel_id=1, source_target_pairs={{1,2},{3,4},{5,6},{7,8},{9,10},{11,12},{13,14},{2,1},{4,3},{6,5},{... | collective-permute-start | bytes 147464 | tf_op jit(solution)/shard_map/ppermute | solution.py:672
  29.1 1.2 %collective-permute-start.4 = (f32[96,128]{1,0:T(8,128)S(1)}, f32[96,128]{1,0:T(8,128)S(1)}, u32[]{:S(2)}, u32[]{:S(2)}) collective-permute-start(f32[96,128]{1,0:T(8,128)S(1)} %collective-permute-done.3.crossed), channel_id=1, source_target_pairs={{0,1},{2,3},{4,5},{6,7},{8,9},{10,11},{12,13},{14,15},{1,0},{3,2},... | collective-permute-start | bytes 147464 | tf_op jit(solution)/shard_map/ppermute | solution.py:672

commit v13 on v12

--- a/solution.py
+++ b/solution.py
@@ -13,6 +13,7 @@
 CAP = 8
 ROWS = 8
 PAIR = 2
+GROUP = 4
 FIRST = 0
 VMEM = pl.BlockSpec(memory_space=pltpu.VMEM)
 SMEM = pl.BlockSpec(memory_space=pltpu.SMEM)
@@ -299,17 +300,17 @@
 
     for at, many, out, row in ((inner_at, margin, inner, 0), (home_at, count, own, home)):
 
-        @pl.loop(0, many // PAIR)
+        @pl.loop(0, many // GROUP)
         def _(step, at=at, out=out):
-            i = step * PAIR
-            for n in range(PAIR):
+            i = step * GROUP
+            for n in range(GROUP):
                 copy(at + i + n).wait()
 
             def put(n, f, row, value):
                 out[i + n, f, row : row + ROWS, :] = value
 
-            gather_columns([loader(cells, at + i + n) for n in range(PAIR)], columns, 8 * i, side)
-            update(cells, at + i, PAIR, weights, put)
+            gather_columns([loader(cells, at + i + n) for n in range(GROUP)], columns, 8 * i, side)
+            update(cells, at + i, GROUP, weights, put)
 
         take_edges(many, cells, lambda p, at=at: at + p, columns, shared, row)
 

time: 33.8 us -> 33.8 us (level)
  no operation moved by 1% of the time
where the time goes in v13:
time: 33.8 us; the launch traced here: 33.6 us
  Pallas kernels  16.7 us (49%)
  starting transfers between devices  10.7 us (32%)
  waiting for transfers between devices  6.16 us (18%)
    ppermute x7, starting transfers between devices, swapped(): return lax.ppermute(value, AXES, pairs + [(j, i) for i, j in pairs])  10.7 us
    pallas_call x1, Pallas kernels, home_patches(): pl.pallas_call(functools.partial(home_kernel, margin), in_specs=[SMEM, HB...  9.17 us
    ppermute x7, waiting for transfers between devices, swapped(): return lax.ppermute(value, AXES, pairs + [(j, i) for i, j in pairs])  6.16 us
    pallas_call x1, Pallas kernels, finished(): pl.pallas_call(functools.partial(final_kernel, margin), in_specs=[SMEM] +...  3.28 us
    pallas_call x1, Pallas kernels, outer_patches(): pl.pallas_call(functools.partial(outer_kernel, margin), in_specs=[HBM], o...  2.51 us
    pallas_call x1, Pallas kernels, answers(): pl.pallas_call(functools.partial(answer_kernel, margin, per_device), in_s...  1.19 us
  transfers between devices with their start and end apart: 7, of which 4 were waited for; matrix products, arithmetic and copies ran while one was open for 0% of the time, Pallas kernels for 40%

profile of v13, /device:TPU:17, one launch (start us, length us, event | category | flops | bytes accessed | tf_op | source)
XLA Modules:
  0.0 33.6 jit_solution(2988035742391319510)
XLA Ops:
  0.0 0.0 copy-start
  0.0 0.0 copy-start.1
  0.0 0.7 %collective-permute-start = (s32[4,16]{1,0:T(4,128)}, s32[4,16]{1,0:T(4,128)S(1)}, u32[]{:S(2)}, u32[]{:S(2)}) collective-permute-start(s32[4,16]{1,0:T(4,128)} %bitcast.1), channel_id=1, source_target_pairs={{0,1},{2,3},{4,5},{6,7},{8,9},{10,11},{12,13},{14,15},{1,0},{3,2},... | collective-permute-start | bytes 776 | tf_op jit(solution)/shard_map/ppermute | solution.py:673
  0.7 2.5 %outer.1 = (f32[4,3,128,128]{3,2,1,0:T(8,128)S(1)}, f32[80,128]{1,0:T(8,128)S(1)}) custom-call(f32[24,4,128,128]{3,2,1,0:T(8,128)} %cells_hbm.3), custom_call_target="tpu_custom_call" | custom-call | flops 52428800 | bytes 1835008 | tf_op jit(solution)/shard_map/outer/pallas_call | solution.py:224
  3.2 0.0 collective-permute-done.their_ref
  3.2 0.0 copy-done
  3.3 3.0 %collective-permute-start.1 = (f32[80,128]{1,0:T(8,128)S(1)}, f32[80,128]{1,0:T(8,128)S(1)}, u32[]{:S(2)}, u32[]{:S(2)}) collective-permute-start(f32[80,128]{1,0:T(8,128)S(1)} %tables.1.other_ref), channel_id=1, source_target_pairs={{1,2},{3,4},{5,6},{7,8},{9,10},{11,12},{13,14},{2,1},{4,3},{6,5},{... | collective-permute-start | bytes 122888 | tf_op jit(solution)/shard_map/ppermute | solution.py:673
  6.3 2.5 %collective-permute-start.6 = (f32[4,3,128,128]{3,2,1,0:T(8,128)S(1)}, f32[4,3,128,128]{3,2,1,0:T(8,128)S(1)}, u32[]{:S(2)}, u32[]{:S(2)}) collective-permute-start(f32[4,3,128,128]{3,2,1,0:T(8,128)S(1)} %after.1), channel_id=1, source_target_pairs={{1,2},{3,4},{5,6},{7,8},{9,10},{11,12},{13,14},{2,1},{4,3},{6,5},{... | collective-permute-start | bytes 2359304 | tf_op jit(solution)/shard_map/ppermute | solution.py:673
  8.9 0.2 collective-permute-done.1.came
  9.1 0.0 copy-done.1
  9.1 9.2 %home.1 = (f32[392,128]{1,0:T(8,128)S(1)}, f32[4,3,128,128]{3,2,1,0:T(8,128)S(1)}, f32[16,3,128,128]{3,2,1,0:T(8,128)S(1)}) custom-call(s32[1,2]{1,0:T(1,128)S(1)} %copy-done.1, f32[24,4,128,128]{3,2,1,0:T(8,128)} %cells_hbm.3, f32[80,128]{1,0:T(8,128)S(1)} %collective-permute-done.1.came), custom_call_target="tpu_custom_call" | custom-call | flops 262144000 | bytes 9175040 | tf_op jit(solution)/shard_map/home/pallas_call | solution.py:325
  18.3 0.7 %collective-permute-start.5 = (f32[4,3,128,128]{3,2,1,0:T(8,128)S(1)}, f32[4,3,128,128]{3,2,1,0:T(8,128)S(1)}, u32[]{:S(2)}, u32[]{:S(2)}) collective-permute-start(f32[4,3,128,128]{3,2,1,0:T(8,128)S(1)} %get-tuple-element.25), channel_id=1, source_target_pairs={{0,1},{2,3},{4,5},{6,7},{8,9},{10,11},{12,13},{14,15},{1,0},{3,2},... | collective-permute-start | bytes 2359304 | tf_op jit(solution)/shard_map/ppermute | solution.py:673
  19.0 0.1 collective-permute-start.2
  19.1 2.1 %collective-permute-done.2.theirs = f32[392,128]{1,0:T(8,128)S(1)} collective-permute-done((f32[392,128]{1,0:T(8,128)S(1)}, f32[392,128]{1,0:T(8,128)S(1)}, u32[]{:S(2)}, u32[]{:S(2)}) %collective-permute-start.2) | collective-permute-done | bytes 200736 | tf_op jit(solution)/shard_map/ppermute | solution.py:673
  21.2 1.2 %answers.1 = (f32[512,128]{1,0:T(8,128)S(1)}, f32[96,128]{1,0:T(8,128)S(1)}) custom-call(s32[1,2]{1,0:T(1,128)S(1)} %copy-done.1, f32[392,128]{1,0:T(8,128)S(1)} %get-tuple-element.17.mine, f32[392,128]{1,0:T(8,128)S(1)} %collective-permute-done.2.theirs, f32[80,128]{1,0:T(8,128)S(1)} %collective-permute-done.1.came), custom_call_target="tpu_custom_call" | custom-call | tf_op jit(solution)/shard_map/answers/pallas_call | solution.py:455
  22.4 3.5 %collective-permute-start.3 = (f32[96,128]{1,0:T(8,128)S(1)}, f32[96,128]{1,0:T(8,128)S(1)}, u32[]{:S(2)}, u32[]{:S(2)}) collective-permute-start(f32[96,128]{1,0:T(8,128)S(1)} %get-tuple-element.23), channel_id=1, source_target_pairs={{1,2},{3,4},{5,6},{7,8},{9,10},{11,12},{13,14},{2,1},{4,3},{6,5},{... | collective-permute-start | bytes 147464 | tf_op jit(solution)/shard_map/ppermute | solution.py:673
  25.9 3.1 %collective-permute-done.3.crossed = f32[96,128]{1,0:T(8,128)S(1)} collective-permute-done((f32[96,128]{1,0:T(8,128)S(1)}, f32[96,128]{1,0:T(8,128)S(1)}, u32[]{:S(2)}, u32[]{:S(2)}) %collective-permute-start.3) | collective-permute-done | bytes 49184 | tf_op jit(solution)/shard_map/ppermute | solution.py:673
  29.1 0.1 collective-permute-start.4
  29.2 0.5 %prepare.1 = (bf16[256,768]{1,0:T(8,128)(2,1)S(1)}, bf16[64,256]{1,0:T(8,128)(2,1)S(1)}, f32[256,128]{1,0:T(8,128)S(1)}, f32[64,128]{1,0:T(8,128)S(1)}) custom-call(s32[4,16]{1,0:T(4,128)S(1)} %bitcast.3, f32[512,128]{1,0:T(8,128)S(1)} %get-tuple-element.18.edges), custom_call_target="tpu_custom_call" | custom-call | tf_op jit(solution)/shard_map/prepare/pallas_call | solution.py:522
  29.7 0.6 %collective-permute-done.4.passed = f32[96,128]{1,0:T(8,128)S(1)} collective-permute-done((f32[96,128]{1,0:T(8,128)S(1)}, f32[96,128]{1,0:T(8,128)S(1)}, u32[]{:S(2)}, u32[]{:S(2)}) %collective-permute-start.4) | collective-permute-done | bytes 49184 | tf_op jit(solution)/shard_map/ppermute | solution.py:673
  30.3 0.0 collective-permute-done.6.arrived
  30.3 0.0 collective-permute-done.5.theirs
  30.3 3.3 %final.1 = f32[16,3,128,128]{3,2,1,0:T(8,128)} custom-call(s32[1,2]{1,0:T(1,128)S(1)} %copy-done.1, bf16[256,768]{1,0:T(8,128)(2,1)S(1)} %get-tuple-element.19.places, bf16[64,256]{1,0:T(8,128)(2,1)S(1)} %get-tuple-element.20.hot, f32[256,128]{1,0:T(8,128)S(1)} %get-tuple-element.21.near, f32[64,128]{1,0:T(8,128)S(1)} %get-tuple-element.22.walls, ...), custom_call_target="tpu_custom_call" | custom-call | tf_op jit(solution)/shard_map/final/pallas_call | solution.py:654
  (2 shorter events, 0.0 us)
Async XLA Ops:
  0.0 3.2 %copy-start = (s32[16,4]{0,1:T(4,128)S(1)}, s32[16,4]{0,1:T(4,128)}, u32[]{:S(2)}) copy-start(s32[16,4]{0,1:T(4,128)} %param.5) | copy-start | bytes 772
  0.0 9.1 %copy-start.1 = (s32[1,2]{1,0:T(1,128)S(1)}, s32[1,2]{1,0:T(1,128)}, u32[]{:S(2)}) copy-start(s32[1,2]{1,0:T(1,128)} %range_ref.5) | copy-start | bytes 28
  0.0 3.2 %collective-permute-start = (s32[4,16]{1,0:T(4,128)}, s32[4,16]{1,0:T(4,128)S(1)}, u32[]{:S(2)}, u32[]{:S(2)}) collective-permute-start(s32[4,16]{1,0:T(4,128)} %bitcast.1), channel_id=1, source_target_pairs={{0,1},{2,3},{4,5},{6,7},{8,9},{10,11},{12,13},{14,15},{1,0},{3,2},... | collective-permute-start | bytes 776 | tf_op jit(solution)/shard_map/ppermute | solution.py:673
  3.3 5.8 %collective-permute-start.1 = (f32[80,128]{1,0:T(8,128)S(1)}, f32[80,128]{1,0:T(8,128)S(1)}, u32[]{:S(2)}, u32[]{:S(2)}) collective-permute-start(f32[80,128]{1,0:T(8,128)S(1)} %tables.1.other_ref), channel_id=1, source_target_pairs={{1,2},{3,4},{5,6},{7,8},{9,10},{11,12},{13,14},{2,1},{4,3},{6,5},{... | collective-permute-start | bytes 122888 | tf_op jit(solution)/shard_map/ppermute | solution.py:673
  6.3 24.0 %collective-permute-start.6 = (f32[4,3,128,128]{3,2,1,0:T(8,128)S(1)}, f32[4,3,128,128]{3,2,1,0:T(8,128)S(1)}, u32[]{:S(2)}, u32[]{:S(2)}) collective-permute-start(f32[4,3,128,128]{3,2,1,0:T(8,128)S(1)} %after.1), channel_id=1, source_target_pairs={{1,2},{3,4},{5,6},{7,8},{9,10},{11,12},{13,14},{2,1},{4,3},{6,5},{... | collective-permute-start | bytes 2359304 | tf_op jit(solution)/shard_map/ppermute | solution.py:673
  18.3 12.0 %collective-permute-start.5 = (f32[4,3,128,128]{3,2,1,0:T(8,128)S(1)}, f32[4,3,128,128]{3,2,1,0:T(8,128)S(1)}, u32[]{:S(2)}, u32[]{:S(2)}) collective-permute-start(f32[4,3,128,128]{3,2,1,0:T(8,128)S(1)} %get-tuple-element.25), channel_id=1, source_target_pairs={{0,1},{2,3},{4,5},{6,7},{8,9},{10,11},{12,13},{14,15},{1,0},{3,2},... | collective-permute-start | bytes 2359304 | tf_op jit(solution)/shard_map/ppermute | solution.py:673
  19.0 2.2 %collective-permute-start.2 = (f32[392,128]{1,0:T(8,128)S(1)}, f32[392,128]{1,0:T(8,128)S(1)}, u32[]{:S(2)}, u32[]{:S(2)}) collective-permute-start(f32[392,128]{1,0:T(8,128)S(1)} %get-tuple-element.17.mine), channel_id=1, source_target_pairs={{0,1},{2,3},{4,5},{6,7},{8,9},{10,11},{12,13},{14,15},{1,0},{3,2},... | collective-permute-start | bytes 602120 | tf_op jit(solution)/shard_map/ppermute | solution.py:673
  22.4 6.7 %collective-permute-start.3 = (f32[96,128]{1,0:T(8,128)S(1)}, f32[96,128]{1,0:T(8,128)S(1)}, u32[]{:S(2)}, u32[]{:S(2)}) collective-permute-start(f32[96,128]{1,0:T(8,128)S(1)} %get-tuple-element.23), channel_id=1, source_target_pairs={{1,2},{3,4},{5,6},{7,8},{9,10},{11,12},{13,14},{2,1},{4,3},{6,5},{... | collective-permute-start | bytes 147464 | tf_op jit(solution)/shard_map/ppermute | solution.py:673
  29.1 1.2 %collective-permute-start.4 = (f32[96,128]{1,0:T(8,128)S(1)}, f32[96,128]{1,0:T(8,128)S(1)}, u32[]{:S(2)}, u32[]{:S(2)}) collective-permute-start(f32[96,128]{1,0:T(8,128)S(1)} %collective-permute-done.3.crossed), channel_id=1, source_target_pairs={{0,1},{2,3},{4,5},{6,7},{8,9},{10,11},{12,13},{14,15},{1,0},{3,2},... | collective-permute-start | bytes 147464 | tf_op jit(solution)/shard_map/ppermute | solution.py:673

commit v14 on v12

--- a/solution.py
+++ b/solution.py
@@ -189,8 +189,8 @@
     copy = fetch(cells_hbm, outer_slot(cells_hbm, margin), cells, sems, [(0, margin)])
     fill_weights(weights)
     results = bundle_layout(margin)[1]
-    for i in range(0, margin, PAIR):
-        for n in range(PAIR):
+    for i in range(0, margin, margin):
+        for n in range(margin):
             copy(i + n).wait()
 
         def put(n, f, row, value, i=i):
@@ -200,8 +200,8 @@
             else:
                 rest[i + n - FIRST, f, row : row + ROWS, :] = value
 
-        gather_columns([loader(cells, i + n) for n in range(PAIR)], columns, 8 * i, side)
-        update(cells, i, PAIR, weights, put)
+        gather_columns([loader(cells, i + n) for n in range(margin)], columns, 8 * i, side)
+        update(cells, i, margin, weights, put)
 
     take_edges(margin, cells, lambda p: p, columns, bundle, 0)
 

time: 33.8 us -> 33.9 us (level)
  no operation moved by 1% of the time
where the time goes in v14:
time: 33.9 us; the launch traced here: 33.7 us
  Pallas kernels  16.7 us (49%)
  starting transfers between devices  10.6 us (31%)
  waiting for transfers between devices  6.3 us (19%)
    ppermute x7, starting transfers between devices, swapped(): return lax.ppermute(value, AXES, pairs + [(j, i) for i, j in pairs])  10.6 us
    pallas_call x1, Pallas kernels, home_patches(): pl.pallas_call(functools.partial(home_kernel, margin), in_specs=[SMEM, HB...  9.12 us
    ppermute x7, waiting for transfers between devices, swapped(): return lax.ppermute(value, AXES, pairs + [(j, i) for i, j in pairs])  6.3 us
    pallas_call x1, Pallas kernels, finished(): pl.pallas_call(functools.partial(final_kernel, margin), in_specs=[SMEM] +...  3.28 us
    pallas_call x1, Pallas kernels, outer_patches(): pl.pallas_call(functools.partial(outer_kernel, margin), in_specs=[HBM], o...  2.6 us
    pallas_call x1, Pallas kernels, answers(): pl.pallas_call(functools.partial(answer_kernel, margin, per_device), in_s...  1.19 us
  transfers between devices with their start and end apart: 7, of which 4 were waited for; matrix products, arithmetic and copies ran while one was open for 0% of the time, Pallas kernels for 40%

profile of v14, /device:TPU:17, one launch (start us, length us, event | category | flops | bytes accessed | tf_op | source)
XLA Modules:
  0.0 33.7 jit_solution(11389955566142224710)
XLA Ops:
  0.0 0.0 copy-start
  0.0 0.0 copy-start.1
  0.0 0.7 %collective-permute-start = (s32[4,16]{1,0:T(4,128)}, s32[4,16]{1,0:T(4,128)S(1)}, u32[]{:S(2)}, u32[]{:S(2)}) collective-permute-start(s32[4,16]{1,0:T(4,128)} %bitcast.1), channel_id=1, source_target_pairs={{0,1},{2,3},{4,5},{6,7},{8,9},{10,11},{12,13},{14,15},{1,0},{3,2},... | collective-permute-start | bytes 776 | tf_op jit(solution)/shard_map/ppermute | solution.py:672
  0.7 2.6 %outer.1 = (f32[4,3,128,128]{3,2,1,0:T(8,128)S(1)}, f32[80,128]{1,0:T(8,128)S(1)}) custom-call(f32[24,4,128,128]{3,2,1,0:T(8,128)} %cells_hbm.3), custom_call_target="tpu_custom_call" | custom-call | flops 52428800 | bytes 1835008 | tf_op jit(solution)/shard_map/outer/pallas_call | solution.py:223
  3.3 0.0 collective-permute-done.their_ref
  3.3 0.0 copy-done
  3.4 3.0 %collective-permute-start.1 = (f32[80,128]{1,0:T(8,128)S(1)}, f32[80,128]{1,0:T(8,128)S(1)}, u32[]{:S(2)}, u32[]{:S(2)}) collective-permute-start(f32[80,128]{1,0:T(8,128)S(1)} %tables.1.other_ref), channel_id=1, source_target_pairs={{1,2},{3,4},{5,6},{7,8},{9,10},{11,12},{13,14},{2,1},{4,3},{6,5},{... | collective-permute-start | bytes 122888 | tf_op jit(solution)/shard_map/ppermute | solution.py:672
  6.4 2.5 %collective-permute-start.6 = (f32[4,3,128,128]{3,2,1,0:T(8,128)S(1)}, f32[4,3,128,128]{3,2,1,0:T(8,128)S(1)}, u32[]{:S(2)}, u32[]{:S(2)}) collective-permute-start(f32[4,3,128,128]{3,2,1,0:T(8,128)S(1)} %after.1), channel_id=1, source_target_pairs={{1,2},{3,4},{5,6},{7,8},{9,10},{11,12},{13,14},{2,1},{4,3},{6,5},{... | collective-permute-start | bytes 2359304 | tf_op jit(solution)/shard_map/ppermute | solution.py:672
  8.9 0.3 collective-permute-done.1.came
  9.2 0.0 copy-done.1
  9.2 9.1 %home.1 = (f32[392,128]{1,0:T(8,128)S(1)}, f32[4,3,128,128]{3,2,1,0:T(8,128)S(1)}, f32[16,3,128,128]{3,2,1,0:T(8,128)S(1)}) custom-call(s32[1,2]{1,0:T(1,128)S(1)} %copy-done.1, f32[24,4,128,128]{3,2,1,0:T(8,128)} %cells_hbm.3, f32[80,128]{1,0:T(8,128)S(1)} %collective-permute-done.1.came), custom_call_target="tpu_custom_call" | custom-call | flops 262144000 | bytes 9175040 | tf_op jit(solution)/shard_map/home/pallas_call | solution.py:324
  18.3 0.7 %collective-permute-start.5 = (f32[4,3,128,128]{3,2,1,0:T(8,128)S(1)}, f32[4,3,128,128]{3,2,1,0:T(8,128)S(1)}, u32[]{:S(2)}, u32[]{:S(2)}) collective-permute-start(f32[4,3,128,128]{3,2,1,0:T(8,128)S(1)} %get-tuple-element.25), channel_id=1, source_target_pairs={{0,1},{2,3},{4,5},{6,7},{8,9},{10,11},{12,13},{14,15},{1,0},{3,2},... | collective-permute-start | bytes 2359304 | tf_op jit(solution)/shard_map/ppermute | solution.py:672
  19.1 0.1 collective-permute-start.2
  19.2 2.1 %collective-permute-done.2.theirs = f32[392,128]{1,0:T(8,128)S(1)} collective-permute-done((f32[392,128]{1,0:T(8,128)S(1)}, f32[392,128]{1,0:T(8,128)S(1)}, u32[]{:S(2)}, u32[]{:S(2)}) %collective-permute-start.2) | collective-permute-done | bytes 200736 | tf_op jit(solution)/shard_map/ppermute | solution.py:672
  21.3 1.2 %answers.1 = (f32[512,128]{1,0:T(8,128)S(1)}, f32[96,128]{1,0:T(8,128)S(1)}) custom-call(s32[1,2]{1,0:T(1,128)S(1)} %copy-done.1, f32[392,128]{1,0:T(8,128)S(1)} %get-tuple-element.17.mine, f32[392,128]{1,0:T(8,128)S(1)} %collective-permute-done.2.theirs, f32[80,128]{1,0:T(8,128)S(1)} %collective-permute-done.1.came), custom_call_target="tpu_custom_call" | custom-call | tf_op jit(solution)/shard_map/answers/pallas_call | solution.py:454
  22.5 3.5 %collective-permute-start.3 = (f32[96,128]{1,0:T(8,128)S(1)}, f32[96,128]{1,0:T(8,128)S(1)}, u32[]{:S(2)}, u32[]{:S(2)}) collective-permute-start(f32[96,128]{1,0:T(8,128)S(1)} %get-tuple-element.23), channel_id=1, source_target_pairs={{1,2},{3,4},{5,6},{7,8},{9,10},{11,12},{13,14},{2,1},{4,3},{6,5},{... | collective-permute-start | bytes 147464 | tf_op jit(solution)/shard_map/ppermute | solution.py:672
  26.0 3.2 %collective-permute-done.3.crossed = f32[96,128]{1,0:T(8,128)S(1)} collective-permute-done((f32[96,128]{1,0:T(8,128)S(1)}, f32[96,128]{1,0:T(8,128)S(1)}, u32[]{:S(2)}, u32[]{:S(2)}) %collective-permute-start.3) | collective-permute-done | bytes 49184 | tf_op jit(solution)/shard_map/ppermute | solution.py:672
  29.2 0.1 collective-permute-start.4
  29.3 0.5 %prepare.1 = (bf16[256,768]{1,0:T(8,128)(2,1)S(1)}, bf16[64,256]{1,0:T(8,128)(2,1)S(1)}, f32[256,128]{1,0:T(8,128)S(1)}, f32[64,128]{1,0:T(8,128)S(1)}) custom-call(s32[4,16]{1,0:T(4,128)S(1)} %bitcast.3, f32[512,128]{1,0:T(8,128)S(1)} %get-tuple-element.18.edges), custom_call_target="tpu_custom_call" | custom-call | tf_op jit(solution)/shard_map/prepare/pallas_call | solution.py:521
  29.7 0.7 %collective-permute-done.4.passed = f32[96,128]{1,0:T(8,128)S(1)} collective-permute-done((f32[96,128]{1,0:T(8,128)S(1)}, f32[96,128]{1,0:T(8,128)S(1)}, u32[]{:S(2)}, u32[]{:S(2)}) %collective-permute-start.4) | collective-permute-done | bytes 49184 | tf_op jit(solution)/shard_map/ppermute | solution.py:672
  30.4 0.0 collective-permute-done.6.arrived
  30.4 0.0 collective-permute-done.5.theirs
  30.4 3.3 %final.1 = f32[16,3,128,128]{3,2,1,0:T(8,128)} custom-call(s32[1,2]{1,0:T(1,128)S(1)} %copy-done.1, bf16[256,768]{1,0:T(8,128)(2,1)S(1)} %get-tuple-element.19.places, bf16[64,256]{1,0:T(8,128)(2,1)S(1)} %get-tuple-element.20.hot, f32[256,128]{1,0:T(8,128)S(1)} %get-tuple-element.21.near, f32[64,128]{1,0:T(8,128)S(1)} %get-tuple-element.22.walls, ...), custom_call_target="tpu_custom_call" | custom-call | tf_op jit(solution)/shard_map/final/pallas_call | solution.py:653
  (2 shorter events, 0.0 us)
Async XLA Ops:
  0.0 3.3 %copy-start = (s32[16,4]{0,1:T(4,128)S(1)}, s32[16,4]{0,1:T(4,128)}, u32[]{:S(2)}) copy-start(s32[16,4]{0,1:T(4,128)} %param.5) | copy-start | bytes 772
  0.0 9.2 %copy-start.1 = (s32[1,2]{1,0:T(1,128)S(1)}, s32[1,2]{1,0:T(1,128)}, u32[]{:S(2)}) copy-start(s32[1,2]{1,0:T(1,128)} %range_ref.5) | copy-start | bytes 28
  0.0 3.3 %collective-permute-start = (s32[4,16]{1,0:T(4,128)}, s32[4,16]{1,0:T(4,128)S(1)}, u32[]{:S(2)}, u32[]{:S(2)}) collective-permute-start(s32[4,16]{1,0:T(4,128)} %bitcast.1), channel_id=1, source_target_pairs={{0,1},{2,3},{4,5},{6,7},{8,9},{10,11},{12,13},{14,15},{1,0},{3,2},... | collective-permute-start | bytes 776 | tf_op jit(solution)/shard_map/ppermute | solution.py:672
  3.4 5.9 %collective-permute-start.1 = (f32[80,128]{1,0:T(8,128)S(1)}, f32[80,128]{1,0:T(8,128)S(1)}, u32[]{:S(2)}, u32[]{:S(2)}) collective-permute-start(f32[80,128]{1,0:T(8,128)S(1)} %tables.1.other_ref), channel_id=1, source_target_pairs={{1,2},{3,4},{5,6},{7,8},{9,10},{11,12},{13,14},{2,1},{4,3},{6,5},{... | collective-permute-start | bytes 122888 | tf_op jit(solution)/shard_map/ppermute | solution.py:672
  6.4 24.0 %collective-permute-start.6 = (f32[4,3,128,128]{3,2,1,0:T(8,128)S(1)}, f32[4,3,128,128]{3,2,1,0:T(8,128)S(1)}, u32[]{:S(2)}, u32[]{:S(2)}) collective-permute-start(f32[4,3,128,128]{3,2,1,0:T(8,128)S(1)} %after.1), channel_id=1, source_target_pairs={{1,2},{3,4},{5,6},{7,8},{9,10},{11,12},{13,14},{2,1},{4,3},{6,5},{... | collective-permute-start | bytes 2359304 | tf_op jit(solution)/shard_map/ppermute | solution.py:672
  18.3 12.1 %collective-permute-start.5 = (f32[4,3,128,128]{3,2,1,0:T(8,128)S(1)}, f32[4,3,128,128]{3,2,1,0:T(8,128)S(1)}, u32[]{:S(2)}, u32[]{:S(2)}) collective-permute-start(f32[4,3,128,128]{3,2,1,0:T(8,128)S(1)} %get-tuple-element.25), channel_id=1, source_target_pairs={{0,1},{2,3},{4,5},{6,7},{8,9},{10,11},{12,13},{14,15},{1,0},{3,2},... | collective-permute-start | bytes 2359304 | tf_op jit(solution)/shard_map/ppermute | solution.py:672
  19.1 2.2 %collective-permute-start.2 = (f32[392,128]{1,0:T(8,128)S(1)}, f32[392,128]{1,0:T(8,128)S(1)}, u32[]{:S(2)}, u32[]{:S(2)}) collective-permute-start(f32[392,128]{1,0:T(8,128)S(1)} %get-tuple-element.17.mine), channel_id=1, source_target_pairs={{0,1},{2,3},{4,5},{6,7},{8,9},{10,11},{12,13},{14,15},{1,0},{3,2},... | collective-permute-start | bytes 602120 | tf_op jit(solution)/shard_map/ppermute | solution.py:672
  22.5 6.7 %collective-permute-start.3 = (f32[96,128]{1,0:T(8,128)S(1)}, f32[96,128]{1,0:T(8,128)S(1)}, u32[]{:S(2)}, u32[]{:S(2)}) collective-permute-start(f32[96,128]{1,0:T(8,128)S(1)} %get-tuple-element.23), channel_id=1, source_target_pairs={{1,2},{3,4},{5,6},{7,8},{9,10},{11,12},{13,14},{2,1},{4,3},{6,5},{... | collective-permute-start | bytes 147464 | tf_op jit(solution)/shard_map/ppermute | solution.py:672
  29.2 1.2 %collective-permute-start.4 = (f32[96,128]{1,0:T(8,128)S(1)}, f32[96,128]{1,0:T(8,128)S(1)}, u32[]{:S(2)}, u32[]{:S(2)}) collective-permute-start(f32[96,128]{1,0:T(8,128)S(1)} %collective-permute-done.3.crossed), channel_id=1, source_target_pairs={{0,1},{2,3},{4,5},{6,7},{8,9},{10,11},{12,13},{14,15},{1,0},{3,2},... | collective-permute-start | bytes 147464 | tf_op jit(solution)/shard_map/ppermute | solution.py:672
